TPU v7x, 32 devices: a whole 2x2x4 slice. The times are simulated.
32 devices in a mesh: parts: 2 (over y), dp: 16 (over z, x, core).
Axes of the slice: x: 2, y: 2, z: 4, core: 2. Of those that a mesh axis runs over, the one named last changes fastest.
Arguments:
- features: bfloat16 [16384, 256], P(('parts', 'dp')), parts along dimension 0, may hold values from -16 to 16
- kernel_map: int32 [16384, 27], P(('parts', 'dp')), parts along dimension 0, may hold values from 384 to 1536, as said below
- occupancy: int32 [32], P(('parts', 'dp')), parts along dimension 0, may hold values from 256 to 512, as said below
- weights: bfloat16 [27, 256, 256], replicated, may hold values from -0.1875 to 0.1875
- bn_gain: float32 [256], replicated, may hold values from 0.5 to 1.5
- bn_shift: float32 [256], replicated, may hold values from -3 to 3
- cotangent: bfloat16 [16384, 256], P(('parts', 'dp')), parts along dimension 0, may hold values from -6 to 6
Outputs:
- block_out: bfloat16 [16384, 256], P(('parts', 'dp')), parts along dimension 0
- grad_features: bfloat16 [16384, 256], P(('parts', 'dp')), parts along dimension 0
- grad_weights: bfloat16 [54, 256, 256], P('parts'), parts along dimension 0
- grad_gain: float32 [512], P('parts'), parts along dimension 0
- grad_shift: float32 [512], P('parts'), parts along dimension 0
There are 2 independent parts, one for each index of `parts`. A program takes and returns all parts, laid end to end along the dimension named above; an argument that names none is the same for every part. Nothing has to cross between parts.
Inputs may be any that keep to these rules, and one draw needn't show every extreme that they name: `kernel_map`: entry [r, k] names, for an occupied row r of device d, its neighbour at offset k as a row of the rows of devices d - 1, d and d + 1 laid end to end, or 1536 for none; column 13 names r itself. A row in block b of its device (128 rows a block) names only rows of blocks b - 1, b and b + 1, counted in that concatenation around d's own rows; so neighbours on device d - 1 lie in its last 128 rows and are named only by the first 128 rows of d, and neighbours on d + 1 lie in its first 128 rows and are named only by the last 128 rows of d; the first and last device name none beyond the slab. Only occupied rows are named, and unoccupied rows name none. `occupancy`: a multiple of 128; a device's occupied rows are its first 128, its last 128, and the occupancy - 256 rows after its first 128.
All inputs are finite; a program needn't handle non-finite values.
Results may differ from a plain program's by a relative error of at most 0.0056.
Values may be sent and summed in bfloat16 or wider, within the bound.
No kernel may reach another device: no remote copies, remote signals or barrier semaphores. Data moves between devices by JAX's collectives and lax.ppermute only.
A program may use at most 64 MiB of HBM per device.

v0:
```python
import jax
import jax.numpy as jnp
from jax import lax
from jax.sharding import PartitionSpec as P

K = 27
BLOCK = 128


EPSILON = 1e-05


def with_halo(shard, sides, width):
    for axis, dim in sides:
        peers, length = (lax.axis_size(axis), shard.shape[dim])
        up = [(i, (i + 1) % peers) for i in range(peers - 1)]
        down = [(j, i) for i, j in up]
        last = lax.slice_in_dim(shard, length - width, length, axis=dim)
        initial = lax.slice_in_dim(shard, 0, width, axis=dim)
        before = lax.ppermute(last, axis, up)
        after = lax.ppermute(initial, axis, down)
        shard = jnp.concatenate([before, shard, after], axis=dim)
    return shard


def from_behind(shard, axis, by):
    peers = lax.axis_size(axis)
    pairs = [(i, i + by) for i in range(peers) if 0 <= i + by < peers]
    return lax.ppermute(shard, axis, pairs)


def summed_rows(values):
    return jnp.sum(values, axis=0)


def per_device(features, kernel_map, occupancy, weights, bn_gain, bn_shift, cotangent):
    row_count = features.shape[0]
    channels = features.shape[1]
    block_count = row_count // BLOCK
    position = lax.iota(jnp.int32, row_count)
    filled = occupancy[0]
    occupied = ((position < filled - BLOCK) | (position >= row_count - BLOCK))[:, None]
    window = with_halo(features, (("dp", 0),), row_count)
    trimmed = window[row_count - BLOCK : 2 * row_count + BLOCK]
    span = row_count + 2 * BLOCK
    lookup = jnp.minimum(kernel_map - row_count + BLOCK, span)
    block_start = (position // BLOCK * BLOCK)[:, None]
    local_index = jnp.where(lookup >= span, -1, lookup - block_start)
    local_index = jnp.transpose(local_index.reshape(block_count, BLOCK, K), (2, 0, 1))
    tiles = trimmed.reshape(block_count + 2, BLOCK, channels)
    stacked = jnp.concatenate([tiles[:block_count], tiles[1 : block_count + 1], tiles[2:]], axis=1)
    slots = lax.iota(jnp.int32, 3 * BLOCK)

    def selector(index_block):
        return (index_block[:, :, None] == slots[None, None, :]).astype(jnp.bfloat16)

    def forward_step(summed, inputs):
        index_block, kernel = inputs
        chosen = selector(index_block)
        picked = jnp.einsum("bij,bjc->bic", chosen, stacked, preferred_element_type=jnp.float32)
        picked = picked.astype(jnp.bfloat16).reshape(row_count, channels)
        return (summed + jnp.dot(picked, kernel, preferred_element_type=jnp.float32), picked)

    conv, picked_all = lax.scan(
        forward_step, jnp.zeros((row_count, channels), jnp.float32), (local_index, weights)
    )
    local_total = filled.astype(jnp.float32)
    masked_conv = jnp.where(occupied, conv, 0.0)
    sums, total = lax.psum((summed_rows(masked_conv), local_total), "dp")
    center = sums / total
    spread = (
        lax.psum(summed_rows(jnp.where(occupied, jnp.square(conv - center), 0.0)), "dp") / total
    )
    inverse = lax.rsqrt(spread + EPSILON)
    normed = (conv - center) * inverse
    affine = bn_gain * normed + bn_shift
    block_out = jnp.where(
        occupied, jnp.maximum(affine, 0.0) + features.astype(jnp.float32), 0.0
    ).astype(jnp.bfloat16)
    upstream = jnp.where(occupied & (affine > 0.0), cotangent.astype(jnp.float32), 0.0)
    grad_gain, grad_shift = lax.psum((summed_rows(upstream * normed), summed_rows(upstream)), "dp")
    grad_conv = jnp.where(
        occupied,
        bn_gain * inverse * (upstream - grad_shift / total - normed * grad_gain / total),
        0.0,
    ).astype(jnp.bfloat16)

    def backward_step(sink, inputs):
        index_block, kernel, picked = inputs
        slice_grad = lax.dot_general(
            picked, grad_conv, (((0,), (0,)), ((), ())), preferred_element_type=jnp.float32
        )
        pushed = lax.dot_general(
            grad_conv, kernel, (((1,), (1,)), ((), ())), preferred_element_type=jnp.float32
        )
        pushed = pushed.astype(jnp.bfloat16).reshape(block_count, BLOCK, channels)
        chosen = selector(index_block)
        return (
            sink + jnp.einsum("bij,bic->bjc", chosen, pushed, preferred_element_type=jnp.float32),
            slice_grad,
        )

    stacked_sink, kernel_grads = lax.scan(
        backward_step,
        jnp.zeros((block_count, 3 * BLOCK, channels), jnp.float32),
        (local_index, weights, picked_all),
    )
    kernel_grads = lax.psum(kernel_grads, "dp").astype(jnp.bfloat16)
    thirds = stacked_sink.reshape(block_count, 3, BLOCK, channels)
    sink_tiles = jnp.pad(thirds[:, 0], ((0, 2), (0, 0), (0, 0)))
    sink_tiles = sink_tiles + jnp.pad(thirds[:, 1], ((1, 1), (0, 0), (0, 0)))
    sink_tiles = sink_tiles + jnp.pad(thirds[:, 2], ((2, 0), (0, 0), (0, 0)))
    sink = sink_tiles.reshape(span, channels)
    full_sink = jnp.pad(sink, ((row_count - BLOCK, row_count - BLOCK), (0, 0)))
    from_next = from_behind(full_sink[:row_count].astype(jnp.bfloat16), "dp", -1).astype(
        jnp.float32
    )
    from_prev = from_behind(
        full_sink[2 * row_count : 3 * row_count].astype(jnp.bfloat16), "dp", 1
    ).astype(jnp.float32)
    received = full_sink[row_count : 2 * row_count] + from_next + from_prev
    grad_features = (jnp.where(occupied, cotangent.astype(jnp.float32), 0.0) + received).astype(
        jnp.bfloat16
    )
    return (block_out, grad_features, kernel_grads, grad_gain, grad_shift)


def solution(mesh):
    in_specs = (
        P(("parts", "dp"), None),
        P(("parts", "dp"), None),
        P(("parts", "dp")),
        P(),
        P(),
        P(),
        P(("parts", "dp"), None),
    )
    out_specs = (
        P(("parts", "dp"), None),
        P(("parts", "dp"), None),
        P("parts", None, None),
        P("parts"),
        P("parts"),
    )
    return jax.shard_map(
        per_device, mesh=mesh, in_specs=in_specs, out_specs=out_specs, check_vma=False
    )
```

profile of v0, /device:TPU:1, one launch (start us, length us, event | category | flops | bytes accessed | tf_op | source)
XLA Modules:
  0.0 439.3 jit_solution(11842741033498674163)
XLA Ops:
  0.6 2.0 collective-permute-start.1
  2.6 4.5 %collective-permute-start = (bf16[512,256]{1,0:T(8,128)(2,1)}, bf16[512,256]{1,0:T(8,128)(2,1)S(1)}, u32[]{:S(2)}, u32[]{:S(2)}) collective-permute-start(bf16[512,256]{1,0:T(8,128)(2,1)} %param.11), channel_id=1, source_target_pairs={{0,1},{1,2},{2,3},{3,4},{4,5},{5,6},{6,7},{7,8},{8,9},{9,10},{10,1... | collective-permute-start | bytes 786440 | tf_op jit(solution)/shard_map/ppermute | solution.py:20
  9.4 3.1 collective-permute-done
  14.6 61.8 %while.26 = (s32[]{:T(128)}, f32[512,256]{1,0:T(8,128)S(1)}, bf16[27,512,256]{2,1,0:T(8,128)(2,1)}, s32[27,4,128]{2,1,0:T(4,128)S(1)}, bf16[4,384,256]{2,1,0:T(8...) while((s32[]{:T(128)}, f32[512,256]{1,0:T(8,128)S(1)}, ...), condition=%wide.region_1.2_spmd.clone, body=%wide.region_0.1_spmd.clone.sunk | while | flops 168361984 | bytes 3020915 | solution.py:64
  76.6 29.7 %all-reduce.5 = (f32[256]{0:T(256)S(1)}, f32[]{:T(128)}) all-reduce(f32[256]{0:T(256)S(1)} %select_reduce_fusion.1, f32[]{:T(128)} %bitcast.5), channel_id=1, replica_groups=mesh['parts'=2,'dp'=16] {'dp'}, use_global_device_ids=true, to_apply=%region_3.4 | all-reduce | flops 257 | bytes 2056 | tf_op jit(solution)/shard_map/psum | solution.py:69
  107.1 30.3 %psum.44 = f32[256]{0:T(256)S(1)} all-reduce(f32[256]{0:T(256)S(1)} %select_reduce_fusion), channel_id=1, replica_groups=mesh['parts'=2,'dp'=16] {'dp'}, use_global_device_ids=true, to_apply=%region_6.7 | all-reduce | flops 256 | bytes 2048 | tf_op jit(solution)/shard_map/psum | solution.py:72
  138.3 29.5 %all-reduce.4 = (f32[256]{0:T(256)S(1)}, f32[256]{0:T(256)S(1)}) all-reduce(f32[256]{0:T(256)S(1)} %get-tuple-element.140, f32[256]{0:T(256)S(1)} %get-tuple-element.139), channel_id=1, replica_groups=mesh['parts'=2,'dp'=16] {'dp'}, use_global_device_ids=true, to_apply=%region_10.11 | all-reduce | flops 512 | bytes 4096 | tf_op jit(solution)/shard_map/psum | solution.py:81
  170.2 105.2 %while.27 = (s32[]{:T(128)}, f32[4,384,256]{2,1,0:T(8,128)S(1)}, f32[27,256,256]{2,1,0:T(8,128)}, s32[27,4,128]{2,1,0:T(4,128)S(1)}, bf16[27,256,256]{2,1,0:T(8,...) while((s32[]{:T(128)}, f32[4,384,256]{2,1,0:T(8,128)S(1)}, ...), condition=%wide.region_12.13_spmd.clone, body=%wide.region_11.12_spmd.clone.sunk | while | flops 235995136 | bytes 5381239 | solution.py:103
  183.8 1.9 fusion.58
  187.7 1.9 fusion.58
  191.6 1.9 fusion.58
  199.4 1.9 fusion.58
  203.3 1.9 fusion.58
  215.0 1.9 fusion.58
  218.9 1.9 fusion.58
  222.8 1.9 fusion.58
  230.6 1.9 fusion.58
  246.1 1.9 fusion.58
  253.9 1.9 fusion.58
  261.7 1.9 fusion.58
  273.4 1.9 fusion.58
  275.6 2.6 collective-permute-start.2
  278.2 3.0 collective-permute-start.3
  281.2 157.1 %all-reduce.7 = bf16[27,256,256]{2,1,0:T(8,128)(2,1)} all-reduce(f32[27,256,256]{2,1,0:T(8,128)} %get-tuple-element.89), channel_id=1, replica_groups=mesh['parts'=2,'dp'=16] {'dp'}, use_global_device_ids=true, to_apply=%region_13.14 | all-reduce | flops 1769472 | bytes 10616832 | tf_op jit(solution)/shard_map/psum | solution.py:108
  (267 shorter events, 149.8 us)
Async XLA Ops:
  0.6 8.8 %collective-permute-start.1 = (bf16[512,256]{1,0:T(8,128)(2,1)}, bf16[512,256]{1,0:T(8,128)(2,1)S(1)}, u32[]{:S(2)}, u32[]{:S(2)}) collective-permute-start(bf16[512,256]{1,0:T(8,128)(2,1)} %param.11), channel_id=1, source_target_pairs={{1,0},{2,1},{3,2},{4,3},{5,4},{6,5},{7,6},{8,7},{9,8},{10,9},{11,1... | collective-permute-start | bytes 786440 | tf_op jit(solution)/shard_map/ppermute | solution.py:21
  2.6 9.9 %collective-permute-start = (bf16[512,256]{1,0:T(8,128)(2,1)}, bf16[512,256]{1,0:T(8,128)(2,1)S(1)}, u32[]{:S(2)}, u32[]{:S(2)}) collective-permute-start(bf16[512,256]{1,0:T(8,128)(2,1)} %param.11), channel_id=1, source_target_pairs={{0,1},{1,2},{2,3},{3,4},{4,5},{5,6},{6,7},{7,8},{8,9},{9,10},{10,1... | collective-permute-start | bytes 786440 | tf_op jit(solution)/shard_map/ppermute | solution.py:20
  14.6 122.8 %copy-start.2 = (f32[256]{0:T(256)S(1)}, f32[256]{0:T(256)}, u32[]{:S(2)}) copy-start(f32[256]{0:T(256)} %param.15) | copy-start | bytes 3076
  14.6 123.4 %copy-start.1 = (bf16[512,256]{1,0:T(8,128)(2,1)S(1)}, bf16[512,256]{1,0:T(8,128)(2,1)}, u32[]{:S(2)}) copy-start(bf16[512,256]{1,0:T(8,128)(2,1)} %param.17) | copy-start | bytes 786436
  14.6 123.4 %copy-start.3 = (f32[256]{0:T(256)S(1)}, f32[256]{0:T(256)}, u32[]{:S(2)}) copy-start(f32[256]{0:T(256)} %param.16) | copy-start | bytes 3076
  14.6 153.8 %copy-start = (bf16[512,256]{1,0:T(8,128)(2,1)S(1)}, bf16[512,256]{1,0:T(8,128)(2,1)}, u32[]{:S(2)}) copy-start(bf16[512,256]{1,0:T(8,128)(2,1)} %param.11) | copy-start | bytes 786436
  167.8 2.4 copy-start.4
  167.8 2.4 copy-start.5
  275.6 162.8 %collective-permute-start.2 = (bf16[512,256]{1,0:T(8,128)(2,1)S(1)}, bf16[512,256]{1,0:T(8,128)(2,1)S(1)}, u32[]{:S(2)}, u32[]{:S(2)}) collective-permute-start(bf16[512,256]{1,0:T(8,128)(2,1)S(1)} %get-tuple-element.176), channel_id=1, source_target_pairs={{1,0},{2,1},{3,2},{4,3},{5,4},{6,5},{7,6},{8,7},{9,8},{10,9},{11,1... | collective-permute-start | bytes 786440 | tf_op jit(solution)/shard_map/ppermute | solution.py:29
  278.2 160.2 %collective-permute-start.3 = (bf16[512,256]{1,0:T(8,128)(2,1)S(1)}, bf16[512,256]{1,0:T(8,128)(2,1)S(1)}, u32[]{:S(2)}, u32[]{:S(2)}) collective-permute-start(bf16[512,256]{1,0:T(8,128)(2,1)S(1)} %get-tuple-element.177), channel_id=1, source_target_pairs={{0,1},{1,2},{2,3},{3,4},{4,5},{5,6},{6,7},{7,8},{8,9},{9,10},{10,1... | collective-permute-start | bytes 786440 | tf_op jit(solution)/shard_map/ppermute | solution.py:29
where the time goes:
time: 442 us; the launch traced here: 439 us
  blocking collectives  247 us (56%)
  matrix products  143 us (32%)
  local copies, waits for them, and re-layouts  23.6 us (5%)
  starting transfers between devices  12 us (3%)
  other arithmetic  8.14 us (2%)
    psum x1, blocking collectives, per_device(): kernel_grads = lax.psum(kernel_grads, 'dp').astype(jnp.bfloat16)  157 us
    dot_general x27, matrix products, backward_step(): lax.dot_general(picked, grad_conv, (((0,), (0,)), ((), ())), preferred_el...  52.2 us
    dot_general x27, matrix products, forward_step(): jnp.dot(picked, kernel, preferred_element_type=jnp.float32)  32.3 us
    dot_general x27, matrix products, backward_step(): lax.dot_general(grad_conv, kernel, (((1,), (1,)), ((), ())), preferred_el...  31.4 us
    psum x1, blocking collectives, per_device(): lax.psum(summed_rows(jnp.where(occupied, jnp.square(conv - center), 0.0))...  30.3 us
    psum x1, blocking collectives, per_device(): sums, total = lax.psum((summed_rows(masked_conv), local_total), 'dp')  29.7 us
    psum x1, blocking collectives, per_device(): lax.psum((summed_rows(upstream * normed), summed_rows(upstream)), 'dp')  29.5 us
    dynamic_update_slice x27, local copies, waits for them, and re-layouts, per_device(): lax.scan(forward_step, jnp.zeros((row_count, channels), jnp.float32), (lo...  19.7 us
  transfers between devices with their start and end apart: 4, of which 2 were waited for; matrix products, arithmetic and copies ran while one was open for 0% of the time, Pallas kernels for 0%

commit v1 on v0

v1 whole, which is shorter than its diff:
```python
import functools

import jax
import jax.numpy as jnp
from jax import lax
from jax.experimental import pallas as pl
from jax.experimental.pallas import tpu as pltpu
from jax.sharding import PartitionSpec as P

K = 27
BLOCK = 128
GROUP = 3
K_ONE = 18
EPSILON = 1e-05
F32 = jnp.float32
BF16 = jnp.bfloat16
VMEM_LIMIT = 24 * 1024 * 1024


def dot(a, b, contract):
    return lax.dot_general(a, b, ((contract[0], contract[1]), ((), ())), preferred_element_type=F32)


def full(shape):
    return pl.BlockSpec(shape, lambda *_: (0,) * len(shape))


def params(**more):
    return pltpu.CompilerParams(vmem_limit_bytes=VMEM_LIMIT, **more)


def cost(flops, moved):
    return pl.CostEstimate(flops=int(flops), bytes_accessed=int(moved), transcendentals=0)


def occupied_rows(filled, rows):
    position = lax.broadcasted_iota(jnp.int32, (rows, 1), 0)
    return (position < filled - BLOCK) | (position >= rows - BLOCK)


def select_and_multiply(index_ref, tiles, weight_ref, conv_ref, picked_ref):
    step = pl.program_id(0)
    index = pltpu.roll(index_ref[...], lax.rem(BLOCK - step * GROUP, BLOCK), 1)
    slots = lax.broadcasted_iota(jnp.int32, (BLOCK, 3 * BLOCK), 1)
    for b, stacked in enumerate(tiles):
        rows = slice(b * BLOCK, (b + 1) * BLOCK)
        chosen = jnp.concatenate(
            [
                jnp.where(index[rows, j : j + 1] == slots, 1.0, 0.0).astype(BF16)
                for j in range(GROUP)
            ],
            axis=0,
        )
        picked = dot(chosen, stacked, ((1,), (0,))).astype(BF16)
        for j in range(GROUP):
            picked_ref[j, rows, :] = picked[j * BLOCK : (j + 1) * BLOCK]
    total = jnp.where(step == 0, 0.0, conv_ref[...])
    for j in range(GROUP):
        total = total + dot(picked_ref[j], weight_ref[j], ((1,), (0,)))
    conv_ref[...] = total


def inner_kernel(index_ref, own_ref, weight_ref, conv_ref, picked_ref):
    tiles = [own_ref[0 : 3 * BLOCK, :], own_ref[BLOCK : 4 * BLOCK, :]]
    select_and_multiply(index_ref, tiles, weight_ref, conv_ref, picked_ref)


def outer_kernel(
    filled_ref, index_ref, before_ref, own_ref, after_ref, inner_ref, weight_ref,
    conv_ref, picked_ref, stats_ref,
):
    tiles = [
        jnp.concatenate([before_ref[...], own_ref[0 : 2 * BLOCK, :]], axis=0),
        jnp.concatenate([own_ref[2 * BLOCK : 4 * BLOCK, :], after_ref[...]], axis=0),
    ]
    select_and_multiply(index_ref, tiles, weight_ref, conv_ref, picked_ref)

    @pl.when(pl.program_id(0) == pl.num_programs(0) - 1)
    def _():
        filled = filled_ref[0]
        count = filled.astype(F32)
        conv = jnp.concatenate([conv_ref[0:BLOCK, :], inner_ref[...], conv_ref[BLOCK:, :]], axis=0)
        occupied = occupied_rows(filled, conv.shape[0])
        sums = jnp.sum(jnp.where(occupied, conv, 0.0), axis=0, keepdims=True)
        off = jnp.where(occupied, conv - sums / count, 0.0)
        squares = jnp.sum(off * off, axis=0, keepdims=True)
        line = jnp.concatenate([sums, squares, jnp.full_like(sums, count)], axis=0)
        stats_ref[...] = jnp.broadcast_to(line[None], stats_ref.shape)


def moments(stats):
    sums, squares, counts = stats[:, 0, :], stats[:, 1, :], stats[:, 2, :]
    total = jnp.sum(counts, axis=0, keepdims=True)
    center = jnp.sum(sums, axis=0, keepdims=True) / total
    away = sums / counts - center
    spread = jnp.sum(squares + counts * away * away, axis=0, keepdims=True) / total
    return center, lax.rsqrt(spread + EPSILON), total


def normalised(filled, inner_ref, outer_ref, stats_ref, gain_ref, shift_ref, cotangent_ref):
    conv = jnp.concatenate([outer_ref[0:BLOCK, :], inner_ref[...], outer_ref[BLOCK:, :]], axis=0)
    center, inverse, total = moments(stats_ref[...])
    occupied = occupied_rows(filled, conv.shape[0])
    normed = (conv - center) * inverse
    affine = gain_ref[...] * normed + shift_ref[...]
    upstream = jnp.where(occupied & (affine > 0.0), cotangent_ref[...].astype(F32), 0.0)
    return occupied, normed, affine, upstream, inverse, total


def norm_kernel(
    filled_ref, inner_ref, outer_ref, stats_ref, gain_ref, shift_ref, cotangent_ref, feature_ref,
    out_ref, sums_ref,
):
    occupied, normed, affine, upstream, _, _ = normalised(
        filled_ref[0], inner_ref, outer_ref, stats_ref, gain_ref, shift_ref, cotangent_ref
    )
    out = jnp.maximum(affine, 0.0) + feature_ref[...].astype(F32)
    out_ref[...] = jnp.where(occupied, out, 0.0).astype(BF16)
    line = jnp.concatenate(
        [jnp.sum(upstream * normed, axis=0, keepdims=True), jnp.sum(upstream, axis=0, keepdims=True)],
        axis=0,
    )
    sums_ref[...] = jnp.broadcast_to(line[None], sums_ref.shape)


def kernel_gradient(place, inner_ref, outer_ref, grad_ref, product, keep_ref, send_ref):
    rows = product.shape[0] // 16
    half = keep_ref.shape[0]
    product[...] = dot(
        inner_ref[0], grad_ref[BLOCK : 3 * BLOCK, :], ((0,), (0,))
    ) + dot(
        outer_ref[0],
        jnp.concatenate([grad_ref[0:BLOCK, :], grad_ref[3 * BLOCK :, :]], axis=0),
        ((0,), (0,)),
    )
    for piece in range(16):
        start = pl.multiple_of(lax.bitwise_xor(jnp.int32(piece), place) * rows, rows)
        value = product[pl.ds(start, rows), :]
        if piece < half:
            keep_ref[piece, 0] = value
        else:
            send_ref[piece - half, 0] = value.astype(BF16)


def first_gradient_kernel(
    scalars_ref, inner_ref, outer_ref, stats_ref, grads_ref, gain_ref, shift_ref, cotangent_ref,
    picked_in_ref, picked_out_ref,
    keep_ref, send_ref, grad_ref, grad_gain_ref, grad_shift_ref, product,
):
    @pl.when(pl.program_id(0) == 0)
    def _():
        occupied, normed, _, upstream, inverse, total = normalised(
            scalars_ref[0], inner_ref, outer_ref, stats_ref, gain_ref, shift_ref, cotangent_ref
        )
        grads = grads_ref[...]
        grad_gain = jnp.sum(grads[:, 0, :], axis=0, keepdims=True)
        grad_shift = jnp.sum(grads[:, 1, :], axis=0, keepdims=True)
        grad_gain_ref[...] = grad_gain
        grad_shift_ref[...] = grad_shift
        grad_conv = gain_ref[...] * inverse * (
            upstream - grad_shift / total - normed * grad_gain / total
        )
        grad_ref[...] = jnp.where(occupied, grad_conv, 0.0).astype(BF16)

    kernel_gradient(
        scalars_ref[1], picked_in_ref, picked_out_ref, grad_ref, product, keep_ref, send_ref
    )


def second_gradient_kernel(
    scalars_ref, grad_ref, picked_in_ref, picked_out_ref, keep_ref, send_ref, product
):
    kernel_gradient(
        scalars_ref[1], picked_in_ref, picked_out_ref, grad_ref, product, keep_ref, send_ref
    )


def push_kernel(grad_ref, index_ref, weight_ref, before_ref, own_ref, after_ref, sink):
    step = pl.program_id(0)

    @pl.when(step == 0)
    def _():
        sink[...] = jnp.zeros_like(sink)

    blocks = grad_ref.shape[0] // BLOCK
    slots = lax.broadcasted_iota(jnp.int32, (3 * BLOCK, BLOCK), 0)
    pushed = [
        dot(grad_ref[...], weight_ref[j], ((1,), (1,))).astype(BF16) for j in range(GROUP)
    ]
    for b in range(blocks):
        rows = slice(b * BLOCK, (b + 1) * BLOCK)
        chosen = jnp.concatenate(
            [
                jnp.where(index_ref[step * GROUP + j, :][None, rows] == slots, 1.0, 0.0).astype(BF16)
                for j in range(GROUP)
            ],
            axis=1,
        )
        stacked = jnp.concatenate([pushed[j][rows] for j in range(GROUP)], axis=0)
        window = slice(b * BLOCK, (b + 3) * BLOCK)
        sink[window, :] = sink[window, :] + dot(chosen, stacked, ((1,), (0,)))

    @pl.when(step == pl.num_programs(0) - 1)
    def _():
        before_ref[...] = sink[0:BLOCK, :].astype(BF16)
        own_ref[...] = sink[BLOCK : (blocks + 1) * BLOCK, :]
        after_ref[...] = sink[(blocks + 1) * BLOCK :, :].astype(BF16)


def place_kernel(places_ref, own_one, other_one, own_two, other_two, out_ref, sems):
    rows = own_one.shape[2]
    half = own_one.shape[0]
    split = own_one.shape[1]
    copies = []
    for piece in range(16):
        for part, (own, other) in enumerate(((own_one, other_one), (own_two, other_two))):
            source = own if piece < half else other
            place = lax.bitwise_xor(jnp.int32(piece), places_ref[part])
            start = pl.multiple_of(place * rows, rows)
            first = 0 if part == 0 else split
            copies.append(
                pltpu.make_async_copy(
                    source.at[piece % half],
                    out_ref.at[pl.ds(first, source.shape[1]), pl.ds(start, rows), :],
                    sems.at[len(copies)],
                )
            )
    for copy in copies:
        copy.start()
    for copy in copies:
        copy.wait()


def swap(value, by):
    peers = lax.axis_size("dp")
    return lax.ppermute(value, "dp", [(i, i ^ by) for i in range(peers)])


STAGES = {"c": (1,), "x": (2,), "z": (4, 8, 12)}


def reduce_start(total, stage):
    partners = STAGES[stage]
    size = total.shape[0] // (len(partners) + 1)
    return [
        swap(total[(i + 1) * size : (i + 2) * size].astype(BF16), by)
        for i, by in enumerate(partners)
    ]


def reduce_end(total, received):
    size = received[0].shape[0]
    return functools.reduce(lambda a, b: a + b.astype(F32), received, total[:size])


def gather_start(piece, stage):
    return [swap(piece, by) for by in STAGES[stage]]


def lockstep(pieces, starts, ends):
    received = [start(piece) for piece, start in zip(pieces, starts)]
    received, pieces = lax.optimization_barrier((received, pieces))
    return [end(piece, got) for piece, got, end in zip(pieces, received, ends)]


def summed_over_devices(one, two):
    pieces = [keep + swap(send, 1).astype(F32) for keep, send in (one, two)]
    for stages in ("xz", "zx"):
        starts = [functools.partial(reduce_start, stage=stage) for stage in stages]
        pieces = lockstep(pieces, starts, [reduce_end] * 2)
    by = 16
    while by < lax.axis_size("dp"):
        pieces = [piece + swap(piece, by) for piece in pieces]
        by *= 2
    pieces = [piece.astype(BF16) for piece in pieces]

    def joined(piece, received):
        return jnp.concatenate([piece] + received, axis=0)

    for stages in ("zx", "xz"):
        starts = [functools.partial(gather_start, stage=stage) for stage in stages]
        pieces = lockstep(pieces, starts, [joined] * 2)
    return [(piece, swap(piece, 1)) for piece in pieces]


def per_device(features, kernel_map, occupancy, weights, bn_gain, bn_shift, cotangent):
    rows, channels = features.shape
    peers = lax.axis_size("dp")
    me = lax.axis_index("dp")
    blocks = rows // BLOCK
    inner_rows = rows - 2 * BLOCK
    steps = K // GROUP

    up = [(i, i + 1) for i in range(peers - 1)]
    down = [(i + 1, i) for i in range(peers - 1)]
    before = lax.ppermute(features[rows - BLOCK :], "dp", up)
    after = lax.ppermute(features[:BLOCK], "dp", down)

    block_of = lax.broadcasted_iota(jnp.int32, kernel_map.shape, 0) // BLOCK
    index = kernel_map - (rows - BLOCK) - block_of * BLOCK
    index_wide = jnp.pad(index, ((0, 0), (0, BLOCK - K)), constant_values=-1)
    index_flat = jnp.transpose(index)

    gain = bn_gain.reshape(1, channels)
    shift = bn_shift.reshape(1, channels)
    smem = pl.BlockSpec(memory_space=pltpu.SMEM)
    weight_spec = pl.BlockSpec((GROUP, channels, channels), lambda s: (s, 0, 0))
    picked_spec = pl.BlockSpec((GROUP, 2 * BLOCK, channels), lambda s: (s, 0, 0))
    half_conv = jax.ShapeDtypeStruct((2 * BLOCK, channels), F32)
    half_picked = jax.ShapeDtypeStruct((K, 2 * BLOCK, channels), BF16)
    work = K * 2 * BLOCK * channels * 2 * (3 * BLOCK + channels)
    moved = K * channels * channels * 2 * 2

    inner, picked_in = pl.pallas_call(
        inner_kernel,
        grid=(steps,),
        in_specs=[full((inner_rows, BLOCK)), full((rows, channels)), weight_spec],
        out_specs=[full((inner_rows, channels)), picked_spec],
        out_shape=[half_conv, half_picked],
        compiler_params=params(),
        cost_estimate=cost(work, moved),
        name="conv_inner",
    )(index_wide[BLOCK : rows - BLOCK], features, weights)

    index_outer = jnp.concatenate([index_wide[:BLOCK], index_wide[rows - BLOCK :]], axis=0)
    outer, picked_out, stats = pl.pallas_call(
        outer_kernel,
        grid=(steps,),
        in_specs=[
            smem,
            full((2 * BLOCK, BLOCK)),
            full((BLOCK, channels)),
            full((rows, channels)),
            full((BLOCK, channels)),
            full((inner_rows, channels)),
            weight_spec,
        ],
        out_specs=[full((2 * BLOCK, channels)), picked_spec, full((peers, 3, channels))],
        out_shape=[half_conv, half_picked, jax.ShapeDtypeStruct((peers, 3, channels), F32)],
        compiler_params=params(),
        cost_estimate=cost(work, moved),
        name="conv_outer",
    )(occupancy, index_outer, before, features, after, inner, weights)

    stats = lax.all_to_all(stats, "dp", 0, 0, tiled=True)

    block_out, sums = pl.pallas_call(
        norm_kernel,
        in_specs=[smem] + [pl.BlockSpec(memory_space=pltpu.VMEM)] * 7,
        out_shape=[
            jax.ShapeDtypeStruct((rows, channels), BF16),
            jax.ShapeDtypeStruct((peers, 2, channels), F32),
        ],
        compiler_params=params(),
        cost_estimate=cost(rows * channels * 20, rows * channels * 10),
        name="norm",
    )(occupancy, inner, outer, stats, gain, shift, cotangent, features)

    grads = lax.all_to_all(sums, "dp", 0, 0, tiled=True)

    core, lane, depth = me & 1, (me >> 1) & 1, (me >> 2) & 3
    place_one = core * 8 + lane * 4 + depth
    place_two = core * 8 + depth * 2 + lane
    piece_rows = channels // 16
    picked_one = pl.BlockSpec((1, 2 * BLOCK, channels), lambda s: (s, 0, 0))
    picked_two = pl.BlockSpec((1, 2 * BLOCK, channels), lambda s: (s + K_ONE, 0, 0))
    piece_spec = pl.BlockSpec((8, 1, piece_rows, channels), lambda s: (0, s, 0, 0))

    def pieces(count):
        shape = (8, count, piece_rows, channels)
        return [jax.ShapeDtypeStruct(shape, F32), jax.ShapeDtypeStruct(shape, BF16)]

    product = pltpu.VMEM((channels, channels), F32)
    line = jax.ShapeDtypeStruct((1, channels), F32)
    keep_one, send_one, grad_conv, grad_gain, grad_shift = pl.pallas_call(
        first_gradient_kernel,
        grid=(K_ONE,),
        in_specs=[
            smem,
            full((2 * BLOCK, channels)),
            full((2 * BLOCK, channels)),
            full((peers, 3, channels)),
            full((peers, 2, channels)),
            full((1, channels)),
            full((1, channels)),
            full((rows, channels)),
            picked_one,
            picked_one,
        ],
        out_specs=[
            piece_spec,
            piece_spec,
            full((rows, channels)),
            full((1, channels)),
            full((1, channels)),
        ],
        out_shape=pieces(K_ONE) + [jax.ShapeDtypeStruct((rows, channels), BF16), line, line],
        scratch_shapes=[product],
        compiler_params=params(),
        cost_estimate=cost(K_ONE * rows * channels * channels * 2, K_ONE * channels * channels * 8),
        name="weight_gradient_one",
    )(
        jnp.stack([occupancy[0], place_one]),
        inner, outer, stats, grads, gain, shift, cotangent, picked_in, picked_out,
    )

    keep_two, send_two = pl.pallas_call(
        second_gradient_kernel,
        grid=(K - K_ONE,),
        in_specs=[smem, full((rows, channels)), picked_two, picked_two],
        out_specs=[piece_spec, piece_spec],
        out_shape=pieces(K - K_ONE),
        scratch_shapes=[product],
        compiler_params=params(),
        cost_estimate=cost(
            (K - K_ONE) * rows * channels * channels * 2, (K - K_ONE) * channels * channels * 8
        ),
        name="weight_gradient_two",
    )(jnp.stack([occupancy[0], place_two]), grad_conv, picked_in, picked_out)

    (own_one, other_one), (own_two, other_two) = summed_over_devices(
        (keep_one, send_one), (keep_two, send_two)
    )
    anywhere = pl.BlockSpec(memory_space=pl.ANY)
    grad_weights = pl.pallas_call(
        place_kernel,
        in_specs=[smem] + [anywhere] * 4,
        out_specs=anywhere,
        out_shape=jax.ShapeDtypeStruct(weights.shape, BF16),
        scratch_shapes=[pltpu.SemaphoreType.DMA((32,))],
        compiler_params=params(),
        cost_estimate=cost(0, K * channels * channels * 4),
        name="place",
    )(jnp.stack([place_one, place_two]), own_one, other_one, own_two, other_two)

    sink_before, sink_own, sink_after = pl.pallas_call(
        push_kernel,
        grid=(steps,),
        in_specs=[full((rows, channels)), full((K, rows)), weight_spec],
        out_specs=[full((BLOCK, channels)), full((rows, channels)), full((BLOCK, channels))],
        out_shape=[
            jax.ShapeDtypeStruct((BLOCK, channels), BF16),
            jax.ShapeDtypeStruct((rows, channels), F32),
            jax.ShapeDtypeStruct((BLOCK, channels), BF16),
        ],
        scratch_shapes=[pltpu.VMEM((rows + 2 * BLOCK, channels), F32)],
        compiler_params=params(),
        cost_estimate=cost(2 * work, moved),
        name="push",
    )(grad_conv, index_flat, weights)
    from_next = lax.ppermute(sink_before, "dp", down).astype(F32)
    from_prev = lax.ppermute(sink_after, "dp", up).astype(F32)
    occupied = occupied_rows(occupancy[0], rows)
    received = jnp.concatenate(
        [
            sink_own[:BLOCK] + from_prev,
            sink_own[BLOCK : rows - BLOCK],
            sink_own[rows - BLOCK :] + from_next,
        ],
        axis=0,
    )
    grad_features = (jnp.where(occupied, cotangent.astype(F32), 0.0) + received).astype(BF16)
    return (
        block_out,
        grad_features,
        grad_weights,
        grad_gain.reshape(channels),
        grad_shift.reshape(channels),
    )


def solution(mesh):
    in_specs = (
        P(("parts", "dp"), None),
        P(("parts", "dp"), None),
        P(("parts", "dp")),
        P(),
        P(),
        P(),
        P(("parts", "dp"), None),
    )
    out_specs = (
        P(("parts", "dp"), None),
        P(("parts", "dp"), None),
        P("parts", None, None),
        P("parts"),
        P("parts"),
    )
    return jax.shard_map(
        per_device, mesh=mesh, in_specs=in_specs, out_specs=out_specs, check_vma=False
    )
```

time: 442 us -> 188 us (0.43)
  blocking collectives: 247 us -> 0 us
  matrix products: 143 us -> 0 us
  waiting for transfers between devices: 3.8 us -> 53.1 us
  Pallas kernels: 0 us -> 44.6 us
  starting transfers between devices: 12 us -> 48.5 us
  local copies, waits for them, and re-layouts: 23.6 us -> 31.8 us
    psum x4 -> x0, blocking collectives: 247 us -> none  [the longest x1 157 us: per_device(): kernel_grads = lax.psum(kernel_grads, 'dp').astype(jnp.bfloat16)]
    dot_general x135 -> x0, matrix products: 143 us -> none  [the longest x27 52.2 us: backward_step(): lax.dot_general(picked, grad_conv, (((0,), (0,)), ((), ())), preferred_el...]
    pallas_call x0 -> x7, Pallas kernels: none -> 44.6 us  [the longest x1 11.4 us: per_device(): pl.pallas_call(push_kernel, grid=(steps,), in_specs=[full((rows, channels...]
    ppermute x4 -> x24, waiting for transfers between devices: 3.8 us -> 41 us  [the longest x20 37.3 us: swap(): return lax.ppermute(value, 'dp', [(i, i ^ by) for i in range(peers)])]
    unnamed x12 -> x82, local copies, waits for them, and re-layouts: 0.03 us -> 27 us
    ppermute x4 -> x24, starting transfers between devices: 12 us -> 37.3 us  [the longest x20 26 us: swap(): return lax.ppermute(value, 'dp', [(i, i ^ by) for i in range(peers)])]
    dynamic_update_slice x27 -> x0, local copies, waits for them, and re-layouts: 19.7 us -> none  [per_device(): lax.scan(forward_step, jnp.zeros((row_count, channels), jnp.float32), (lo...]
    all_to_all x0 -> x2, waiting for transfers between devices: none -> 12.2 us  [the longest x1 6.15 us: per_device(): stats = lax.all_to_all(stats, 'dp', 0, 0, tiled=True)]
  transfers between devices with their start and end apart: 4 -> 26, of which waited for: 2 -> 13; matrix products, arithmetic and copies ran while one was open for 0% -> 4% of each run, Pallas kernels for 0% -> 12%
where the time goes in v1:
time: 188 us; the launch traced here: 185 us
  waiting for transfers between devices  53.1 us (28%)
  starting transfers between devices  48.5 us (26%)
  Pallas kernels  44.6 us (24%)
  local copies, waits for them, and re-layouts  31.8 us (17%)
  other arithmetic  4.95 us (3%)
    ppermute x20, waiting for transfers between devices, swap(): return lax.ppermute(value, 'dp', [(i, i ^ by) for i in range(peers)])  37.3 us
    unnamed x82, local copies, waits for them, and re-layouts  27 us
    ppermute x20, starting transfers between devices, swap(): return lax.ppermute(value, 'dp', [(i, i ^ by) for i in range(peers)])  26 us
    pallas_call x1, Pallas kernels, per_device(): pl.pallas_call(push_kernel, grid=(steps,), in_specs=[full((rows, channels...  11.4 us
    pallas_call x1, Pallas kernels, per_device(): pl.pallas_call(first_gradient_kernel, grid=(K_ONE,), in_specs=[smem, full...  9.96 us
    pallas_call x1, Pallas kernels, per_device(): pl.pallas_call(outer_kernel, grid=(steps,), in_specs=[smem, full((2 * BLO...  8.17 us
    pallas_call x1, Pallas kernels, per_device(): pl.pallas_call(inner_kernel, grid=(steps,), in_specs=[full((inner_rows, B...  7.06 us
    all_to_all x1, starting transfers between devices, per_device(): stats = lax.all_to_all(stats, 'dp', 0, 0, tiled=True)  6.46 us
  transfers between devices with their start and end apart: 26, of which 13 were waited for; matrix products, arithmetic and copies ran while one was open for 4% of the time, Pallas kernels for 12%

profile of v1, /device:TPU:1, one launch (start us, length us, event | category | flops | bytes accessed | tf_op | source)
XLA Modules:
  0.0 184.7 jit_solution(7697559036203561129)
XLA Ops:
  2.2 4.5 %collective-permute-start = (bf16[128,256]{1,0:T(8,128)(2,1)}, bf16[128,256]{1,0:T(8,128)(2,1)}, u32[]{:S(2)}, u32[]{:S(2)}) collective-permute-start(bf16[128,256]{1,0:T(8,128)(2,1)} %get-tuple-element.100), channel_id=1, source_target_pairs={{0,1},{1,2},{2,3},{3,4},{4,5},{5,6},{6,7},{7,8},{8,9},{9,10},{10,1... | collective-permute-start | bytes 196616 | tf_op jit(solution)/shard_map/ppermute | solution.py:296
  14.8 7.1 %conv_inner.1 = (f32[256,256]{1,0:T(8,128)S(1)}, bf16[27,256,256]{2,1,0:T(8,128)(2,1)S(1)}) custom-call(s32[256,128]{1,0:T(8,128)S(1)} %copy-done.22, bf16[512,256]{1,0:T(8,128)(2,1)S(1)} %copy-done.15, bf16[27,256,256]{2,1,0:T(8,128)(2,1)S(1)} %copy-done.27), custom_call_target="tpu_custom_call" | custom-call | flops 2264924160 | bytes 7077888 | tf_op jit(solution)/shard_map/conv_inner/pallas_call | solution.py:314
  30.4 8.2 %conv_outer.1 = (f32[256,256]{1,0:T(8,128)S(1)}, bf16[27,256,256]{2,1,0:T(8,128)(2,1)S(1)}, f32[16,3,256]{2,1,0:T(4,128)S(1)}) custom-call(s32[1]{0:T(128)S(6)} %copy.22.filled_ref, s32[256,128]{1,0:T(8,128)S(1)} %copy-done.21, bf16[128,256]{1,0:T(8,128)(2,1)} %collective-permute-done.before_ref, bf16[512,256]{1,0:T(8,128)(2,1)S(1)} %copy-done.16, ...), custom_call_target="tpu_custom_call" | custom-call | flops 2264924160 | bytes 7077888 | tf_op jit(solution)/shard_map/conv_outer/pallas_call | solution.py:326
  41.7 6.5 %all-to-all-start = ((f32[16,3,256]{2,1,0:T(4,128)}), f32[16,3,256]{2,1,0:T(4,128)}, u32[]{:S(2)}, u32[]{:S(2)}) async-start(f32[16,3,256]{2,1,0:T(4,128)} %copy-done.23), calls=%async_computation | async-start | bytes 131072 | tf_op jit(solution)/shard_map/all_to_all | solution.py:345
  48.2 6.1 %all-to-all-done.stats_ref = f32[16,3,256]{2,1,0:T(4,128)} async-done(((f32[16,3,256]{2,1,0:T(4,128)}), f32[16,3,256]{2,1,0:T(4,128)}, u32[]{:S(2)}, u32[]{:S(2)}) %all-to-all-start) | async-done | bytes 49184 | tf_op jit(solution)/shard_map/all_to_all | solution.py:345
  60.6 4.8 %all-to-all-start.1 = ((f32[16,2,256]{2,1,0:T(2,128)}), f32[16,2,256]{2,1,0:T(2,128)}, u32[]{:S(2)}, u32[]{:S(2)}) async-start(f32[16,2,256]{2,1,0:T(2,128)} %copy-done.24), calls=%async_computation.1 | async-start | bytes 65536 | tf_op jit(solution)/shard_map/all_to_all | solution.py:359
  65.5 6.0 %all-to-all-done.1.grads_ref = f32[16,2,256]{2,1,0:T(2,128)} async-done(((f32[16,2,256]{2,1,0:T(2,128)}), f32[16,2,256]{2,1,0:T(2,128)}, u32[]{:S(2)}, u32[]{:S(2)}) %all-to-all-start.1) | async-done | bytes 32800 | tf_op jit(solution)/shard_map/all_to_all | solution.py:359
  76.4 10.0 %weight_gradient_one.1 = (f32[8,18,16,256]{3,2,1,0:T(8,128)S(1)}, bf16[8,18,16,256]{3,2,1,0:T(8,128)(2,1)}, bf16[512,256]{1,0:T(8,128)(2,1)S(1)}, f32[1,256]{1,0:T(1,128)}, f32[1,256]{1,0:T(1,128)}) custom-call(s32[2]{0:T(128)S(1)} %pad_add_fusion.1.scalars_ref, f32[256,256]{1,0:T(8,128)S(1)} %copy-done.11, f32[256,256]{1,0:T(8,128)S(1)} %copy-done.14, ...), custom_call_target="tpu_custom_call" | custom-call | flops 1207959552 | bytes 9437184 | tf_op jit(solution)/shard_map/weight_gradient_one/pallas_call | solution.py:375
  92.3 3.5 %weight_gradient_two.1 = (f32[8,9,16,256]{3,2,1,0:T(8,128)S(1)}, bf16[8,9,16,256]{3,2,1,0:T(8,128)(2,1)S(1)}) custom-call(s32[2]{0:T(128)S(1)} %pad_add_fusion.3.scalars_ref, bf16[512,256]{1,0:T(8,128)(2,1)S(1)} %copy-done.19, bf16[27,256,256]{2,1,0:T(8,128)(2,1)S(1)} %get-tuple-element.51.picked_in_ref, bf16[27,256,256]{2,1,0:T(8,128)(2,1)S(1)} %copy-done.2), custom_call_target="tpu_custom_call" | custom-call | flops 603979776 | bytes 4718592 | tf_op jit(solution)/shard_map/weight_gradient_two/pallas_call | solution.py:407
  99.0 2.8 %collective-permute-start.9 = (bf16[2,9,16,256]{3,2,1,0:T(8,128)(2,1)S(1)}, bf16[2,9,16,256]{3,2,1,0:T(8,128)(2,1)S(1)}, u32[]{:S(2)}, u32[]{:S(2)}) collective-permute-start(bf16[2,9,16,256]{3,2,1,0:T(8,128)(2,1)S(1)} %get-tuple-element.94), channel_id=1, source_target_pairs={{0,12},{1,13},{2,14},{3,15},{4,8},{5,9},{6,10},{7,11},{8,4},{9,5},... | collective-permute-start | bytes 442376 | tf_op jit(solution)/shard_map/ppermute | solution.py:236
  101.8 2.9 %collective-permute-done.7 = bf16[2,9,16,256]{3,2,1,0:T(8,128)(2,1)S(1)} collective-permute-done((bf16[2,9,16,256]{3,2,1,0:T(8,128)(2,1)S(1)}, bf16[2,9,16,256]{3,2,1,0:T(8,128)(2,1)S(1)}, u32[]{:S(2)}, u32[]{:S(2)}) %collective-permute-start.7) | collective-permute-done | bytes 147488 | tf_op jit(solution)/shard_map/ppermute | solution.py:236
  105.2 4.2 %collective-permute-done.9 = bf16[2,9,16,256]{3,2,1,0:T(8,128)(2,1)S(1)} collective-permute-done((bf16[2,9,16,256]{3,2,1,0:T(8,128)(2,1)S(1)}, bf16[2,9,16,256]{3,2,1,0:T(8,128)(2,1)S(1)}, u32[]{:S(2)}, u32[]{:S(2)}) %collective-permute-start.9) | collective-permute-done | bytes 147488 | tf_op jit(solution)/shard_map/ppermute | solution.py:236
  109.4 2.7 %collective-permute-done.5 = bf16[4,18,16,256]{3,2,1,0:T(8,128)(2,1)S(1)} collective-permute-done((bf16[4,18,16,256]{3,2,1,0:T(8,128)(2,1)S(1)}, bf16[4,18,16,256]{3,2,1,0:T(8,128)(2,1)S(1)}, u32[]{:S(2)}, u32[]{:S(2)}) %collective-permute-start.5) | collective-permute-done | bytes 589856 | tf_op jit(solution)/shard_map/ppermute | solution.py:236
  114.2 2.2 %collective-permute-start.12 = (bf16[1,18,16,256]{3,2,1,0:T(8,128)(2,1)S(1)}, bf16[1,18,16,256]{3,2,1,0:T(8,128)(2,1)S(1)}, u32[]{:S(2)}, u32[]{:S(2)}) collective-permute-start(bf16[1,18,16,256]{3,2,1,0:T(8,128)(2,1)S(1)} %get-tuple-element.91), channel_id=1, source_target_pairs={{0,12},{1,13},{2,14},{3,15},{4,8},{5,9},{6,10},{7,11},{8,4},{9,5},... | collective-permute-start | bytes 442376 | tf_op jit(solution)/shard_map/ppermute | solution.py:236
  119.8 6.6 %collective-permute-done.11 = bf16[1,18,16,256]{3,2,1,0:T(8,128)(2,1)S(1)} collective-permute-done((bf16[1,18,16,256]{3,2,1,0:T(8,128)(2,1)S(1)}, bf16[1,18,16,256]{3,2,1,0:T(8,128)(2,1)S(1)}, u32[]{:S(2)}, u32[]{:S(2)}) %collective-permute-start.11) | collective-permute-done | bytes 147488 | tf_op jit(solution)/shard_map/ppermute | solution.py:236
  126.5 3.5 %collective-permute-start.14 = (bf16[1,18,16,256]{3,2,1,0:T(8,128)(2,1)S(1)}, bf16[1,18,16,256]{3,2,1,0:T(8,128)(2,1)S(1)}, u32[]{:S(2)}, u32[]{:S(2)}) collective-permute-start(bf16[1,18,16,256]{3,2,1,0:T(8,128)(2,1)S(1)} %add_convert_fusion), channel_id=1, source_target_pairs={{0,4},{1,5},{2,6},{3,7},{4,0},{5,1},{6,2},{7,3},{8,12},{9,13},{10,... | collective-permute-start | bytes 442376 | tf_op jit(solution)/shard_map/ppermute | solution.py:236
  135.4 6.6 %collective-permute-done.15 = bf16[1,18,16,256]{3,2,1,0:T(8,128)(2,1)S(1)} collective-permute-done((bf16[1,18,16,256]{3,2,1,0:T(8,128)(2,1)S(1)}, bf16[1,18,16,256]{3,2,1,0:T(8,128)(2,1)S(1)}, u32[]{:S(2)}, u32[]{:S(2)}) %collective-permute-start.15) | collective-permute-done | bytes 147488 | tf_op jit(solution)/shard_map/ppermute | solution.py:236
  143.3 3.5 %collective-permute-start.19 = (bf16[2,9,16,256]{3,2,1,0:T(8,128)(2,1)S(1)}, bf16[2,9,16,256]{3,2,1,0:T(8,128)(2,1)S(1)}, u32[]{:S(2)}, u32[]{:S(2)}) collective-permute-start(bf16[2,9,16,256]{3,2,1,0:T(8,128)(2,1)S(1)} %constant_dynamic-update-slice_fusion.4), channel_id=1, source_target_pairs={{0,4},{1,5},{2,6},{3,7},{4,0},{5,1},{6,2},{7,3},{8,12},{9,13},{10,... | collective-permute-start | bytes 442376 | tf_op jit(solution)/shard_map/ppermute | solution.py:236
  149.6 9.1 %collective-permute-done.20 = bf16[2,9,16,256]{3,2,1,0:T(8,128)(2,1)S(1)} collective-permute-done((bf16[2,9,16,256]{3,2,1,0:T(8,128)(2,1)S(1)}, bf16[2,9,16,256]{3,2,1,0:T(8,128)(2,1)S(1)}, u32[]{:S(2)}, u32[]{:S(2)}) %collective-permute-start.20) | collective-permute-done | bytes 147488 | tf_op jit(solution)/shard_map/ppermute | solution.py:236
  158.9 2.3 %collective-permute-start.22 = (bf16[8,18,16,256]{3,2,1,0:T(8,128)(2,1)S(1)}, bf16[8,18,16,256]{3,2,1,0:T(8,128)(2,1)S(1)}, u32[]{:S(2)}, u32[]{:S(2)}) collective-permute-start(bf16[8,18,16,256]{3,2,1,0:T(8,128)(2,1)S(1)} %constant_dynamic-update-slice_fusion.6.own_one), channel_id=1, source_target_pairs={{0,1},{1,0},{2,3},{3,2},{4,5},{5,4},{6,7},{7,6},{8,9},{9,8},{10,11... | collective-permute-start | bytes 3538952 | tf_op jit(solution)/shard_map/ppermute | solution.py:236
  161.3 11.4 %push.1 = (bf16[128,256]{1,0:T(8,128)(2,1)S(1)}, f32[512,256]{1,0:T(8,128)S(1)}, bf16[128,256]{1,0:T(8,128)(2,1)S(1)}) custom-call(bf16[512,256]{1,0:T(8,128)(2,1)S(1)} %copy-done.20, s32[27,512]{1,0:T(8,128)S(1)} %fusion.10.index_ref, bf16[27,256,256]{2,1,0:T(8,128)(2,1)S(1)} %copy-done.29), custom_call_target="tpu_custom_call" | custom-call | flops 4529848320 | bytes 7077888 | tf_op jit(solution)/shard_map/push/pallas_call | solution.py:436
  172.7 2.9 %collective-permute-start.2 = (bf16[128,256]{1,0:T(8,128)(2,1)S(1)}, bf16[128,256]{1,0:T(8,128)(2,1)S(1)}, u32[]{:S(2)}, u32[]{:S(2)}) collective-permute-start(bf16[128,256]{1,0:T(8,128)(2,1)S(1)} %get-tuple-element.55), channel_id=1, source_target_pairs={{0,1},{1,2},{2,3},{3,4},{4,5},{5,6},{6,7},{7,8},{8,9},{9,10},{10,1... | collective-permute-start | bytes 196616 | tf_op jit(solution)/shard_map/ppermute | solution.py:452
  177.6 3.6 %collective-permute-done.3 = bf16[128,256]{1,0:T(8,128)(2,1)S(1)} collective-permute-done((bf16[128,256]{1,0:T(8,128)(2,1)S(1)}, bf16[128,256]{1,0:T(8,128)(2,1)S(1)}, u32[]{:S(2)}, u32[]{:S(2)}) %collective-permute-start.3) | collective-permute-done | bytes 65568 | tf_op jit(solution)/shard_map/ppermute | solution.py:451
  182.1 2.6 %place.1 = bf16[27,256,256]{2,1,0:T(8,128)(2,1)} custom-call(s32[2]{0:T(128)S(1)} %pad_add_fusion.2.places_ref, bf16[8,18,16,256]{3,2,1,0:T(8,128)(2,1)S(1)} %constant_dynamic-update-slice_fusion.6.own_one, bf16[8,18,16,256]{3,2,1,0:T(8,128)(2,1)S(1)} %collective-permute-done.22.other_one, ...), custom_call_target="tpu_custom_call" | custom-call | bytes 7077888 | tf_op jit(solution)/shard_map/place/pallas_call | solution.py:425
  (148 shorter events, 59.4 us)
Async XLA Ops:
  2.2 23.4 %collective-permute-start = (bf16[128,256]{1,0:T(8,128)(2,1)}, bf16[128,256]{1,0:T(8,128)(2,1)}, u32[]{:S(2)}, u32[]{:S(2)}) collective-permute-start(bf16[128,256]{1,0:T(8,128)(2,1)} %get-tuple-element.100), channel_id=1, source_target_pairs={{0,1},{1,2},{2,3},{3,4},{4,5},{5,6},{6,7},{7,8},{8,9},{9,10},{10,1... | collective-permute-start | bytes 196616 | tf_op jit(solution)/shard_map/ppermute | solution.py:296
  6.7 18.9 %collective-permute-start.1 = (bf16[128,256]{1,0:T(8,128)(2,1)}, bf16[128,256]{1,0:T(8,128)(2,1)}, u32[]{:S(2)}, u32[]{:S(2)}) collective-permute-start(bf16[128,256]{1,0:T(8,128)(2,1)} %get-tuple-element.99), channel_id=1, source_target_pairs={{1,0},{2,1},{3,2},{4,3},{5,4},{6,5},{7,6},{8,7},{9,8},{10,9},{11,1... | collective-permute-start | bytes 196616 | tf_op jit(solution)/shard_map/ppermute | solution.py:297
  41.7 12.6 %all-to-all-start = ((f32[16,3,256]{2,1,0:T(4,128)}), f32[16,3,256]{2,1,0:T(4,128)}, u32[]{:S(2)}, u32[]{:S(2)}) async-start(f32[16,3,256]{2,1,0:T(4,128)} %copy-done.23), calls=%async_computation | async-start | bytes 131072 | tf_op jit(solution)/shard_map/all_to_all | solution.py:345
  60.6 10.9 %all-to-all-start.1 = ((f32[16,2,256]{2,1,0:T(2,128)}), f32[16,2,256]{2,1,0:T(2,128)}, u32[]{:S(2)}, u32[]{:S(2)}) async-start(f32[16,2,256]{2,1,0:T(2,128)} %copy-done.24), calls=%async_computation.1 | async-start | bytes 65536 | tf_op jit(solution)/shard_map/all_to_all | solution.py:359
  88.4 7.5 %collective-permute-start.4 = (bf16[8,18,16,256]{3,2,1,0:T(8,128)(2,1)}, bf16[8,18,16,256]{3,2,1,0:T(8,128)(2,1)}, u32[]{:S(2)}, u32[]{:S(2)}) collective-permute-start(bf16[8,18,16,256]{3,2,1,0:T(8,128)(2,1)} %get-tuple-element.58), channel_id=1, source_target_pairs={{0,1},{1,0},{2,3},{3,2},{4,5},{5,4},{6,7},{7,6},{8,9},{9,8},{10,11... | collective-permute-start | bytes 3538952 | tf_op jit(solution)/shard_map/ppermute | solution.py:236
  97.7 14.5 %collective-permute-start.5 = (bf16[4,18,16,256]{3,2,1,0:T(8,128)(2,1)S(1)}, bf16[4,18,16,256]{3,2,1,0:T(8,128)(2,1)S(1)}, u32[]{:S(2)}, u32[]{:S(2)}) collective-permute-start(bf16[4,18,16,256]{3,2,1,0:T(8,128)(2,1)S(1)} %slice.107), channel_id=1, source_target_pairs={{0,2},{1,3},{2,0},{3,1},{4,6},{5,7},{6,4},{7,5},{8,10},{9,11},{10,... | collective-permute-start | bytes 1769480 | tf_op jit(solution)/shard_map/ppermute | solution.py:236
  98.2 6.5 %collective-permute-start.7 = (bf16[2,9,16,256]{3,2,1,0:T(8,128)(2,1)S(1)}, bf16[2,9,16,256]{3,2,1,0:T(8,128)(2,1)S(1)}, u32[]{:S(2)}, u32[]{:S(2)}) collective-permute-start(bf16[2,9,16,256]{3,2,1,0:T(8,128)(2,1)S(1)} %get-tuple-element.96), channel_id=1, source_target_pairs={{0,4},{1,5},{2,6},{3,7},{4,0},{5,1},{6,2},{7,3},{8,12},{9,13},{10,... | collective-permute-start | bytes 442376 | tf_op jit(solution)/shard_map/ppermute | solution.py:236
  98.5 6.6 %collective-permute-start.8 = (bf16[2,9,16,256]{3,2,1,0:T(8,128)(2,1)S(1)}, bf16[2,9,16,256]{3,2,1,0:T(8,128)(2,1)S(1)}, u32[]{:S(2)}, u32[]{:S(2)}) collective-permute-start(bf16[2,9,16,256]{3,2,1,0:T(8,128)(2,1)S(1)} %get-tuple-element.95), channel_id=1, source_target_pairs={{0,8},{1,9},{2,10},{3,11},{4,12},{5,13},{6,14},{7,15},{8,0},{9,1},... | collective-permute-start | bytes 442376 | tf_op jit(solution)/shard_map/ppermute | solution.py:236
  99.0 10.4 %collective-permute-start.9 = (bf16[2,9,16,256]{3,2,1,0:T(8,128)(2,1)S(1)}, bf16[2,9,16,256]{3,2,1,0:T(8,128)(2,1)S(1)}, u32[]{:S(2)}, u32[]{:S(2)}) collective-permute-start(bf16[2,9,16,256]{3,2,1,0:T(8,128)(2,1)S(1)} %get-tuple-element.94), channel_id=1, source_target_pairs={{0,12},{1,13},{2,14},{3,15},{4,8},{5,9},{6,10},{7,11},{8,4},{9,5},... | collective-permute-start | bytes 442376 | tf_op jit(solution)/shard_map/ppermute | solution.py:236
  112.4 7.3 %collective-permute-start.10 = (bf16[1,18,16,256]{3,2,1,0:T(8,128)(2,1)S(1)}, bf16[1,18,16,256]{3,2,1,0:T(8,128)(2,1)S(1)}, u32[]{:S(2)}, u32[]{:S(2)}) collective-permute-start(bf16[1,18,16,256]{3,2,1,0:T(8,128)(2,1)S(1)} %get-tuple-element.93), channel_id=1, source_target_pairs={{0,4},{1,5},{2,6},{3,7},{4,0},{5,1},{6,2},{7,3},{8,12},{9,13},{10,... | collective-permute-start | bytes 442376 | tf_op jit(solution)/shard_map/ppermute | solution.py:236
  114.2 12.1 %collective-permute-start.11 = (bf16[1,18,16,256]{3,2,1,0:T(8,128)(2,1)S(1)}, bf16[1,18,16,256]{3,2,1,0:T(8,128)(2,1)S(1)}, u32[]{:S(2)}, u32[]{:S(2)}) collective-permute-start(bf16[1,18,16,256]{3,2,1,0:T(8,128)(2,1)S(1)} %get-tuple-element.92), channel_id=1, source_target_pairs={{0,8},{1,9},{2,10},{3,11},{4,12},{5,13},{6,14},{7,15},{8,0},{9,1},... | collective-permute-start | bytes 442376 | tf_op jit(solution)/shard_map/ppermute | solution.py:236
  114.2 12.1 %collective-permute-start.12 = (bf16[1,18,16,256]{3,2,1,0:T(8,128)(2,1)S(1)}, bf16[1,18,16,256]{3,2,1,0:T(8,128)(2,1)S(1)}, u32[]{:S(2)}, u32[]{:S(2)}) collective-permute-start(bf16[1,18,16,256]{3,2,1,0:T(8,128)(2,1)S(1)} %get-tuple-element.91), channel_id=1, source_target_pairs={{0,12},{1,13},{2,14},{3,15},{4,8},{5,9},{6,10},{7,11},{8,4},{9,5},... | collective-permute-start | bytes 442376 | tf_op jit(solution)/shard_map/ppermute | solution.py:236
  116.5 3.3 %collective-permute-start.13 = (bf16[1,9,16,256]{3,2,1,0:T(8,128)(2,1)S(1)}, bf16[1,9,16,256]{3,2,1,0:T(8,128)(2,1)S(1)}, u32[]{:S(2)}, u32[]{:S(2)}) collective-permute-start(bf16[1,9,16,256]{3,2,1,0:T(8,128)(2,1)S(1)} %slice.108), channel_id=1, source_target_pairs={{0,2},{1,3},{2,0},{3,1},{4,6},{5,7},{6,4},{7,5},{8,10},{9,11},{10,... | collective-permute-start | bytes 221192 | tf_op jit(solution)/shard_map/ppermute | solution.py:236
  126.5 9.0 %collective-permute-start.14 = (bf16[1,18,16,256]{3,2,1,0:T(8,128)(2,1)S(1)}, bf16[1,18,16,256]{3,2,1,0:T(8,128)(2,1)S(1)}, u32[]{:S(2)}, u32[]{:S(2)}) collective-permute-start(bf16[1,18,16,256]{3,2,1,0:T(8,128)(2,1)S(1)} %add_convert_fusion), channel_id=1, source_target_pairs={{0,4},{1,5},{2,6},{3,7},{4,0},{5,1},{6,2},{7,3},{8,12},{9,13},{10,... | collective-permute-start | bytes 442376 | tf_op jit(solution)/shard_map/ppermute | solution.py:236
  130.0 12.0 %collective-permute-start.15 = (bf16[1,18,16,256]{3,2,1,0:T(8,128)(2,1)S(1)}, bf16[1,18,16,256]{3,2,1,0:T(8,128)(2,1)S(1)}, u32[]{:S(2)}, u32[]{:S(2)}) collective-permute-start(bf16[1,18,16,256]{3,2,1,0:T(8,128)(2,1)S(1)} %add_convert_fusion), channel_id=1, source_target_pairs={{0,8},{1,9},{2,10},{3,11},{4,12},{5,13},{6,14},{7,15},{8,0},{9,1},... | collective-permute-start | bytes 442376 | tf_op jit(solution)/shard_map/ppermute | solution.py:236
  130.0 12.0 %collective-permute-start.16 = (bf16[1,18,16,256]{3,2,1,0:T(8,128)(2,1)S(1)}, bf16[1,18,16,256]{3,2,1,0:T(8,128)(2,1)S(1)}, u32[]{:S(2)}, u32[]{:S(2)}) collective-permute-start(bf16[1,18,16,256]{3,2,1,0:T(8,128)(2,1)S(1)} %add_convert_fusion), channel_id=1, source_target_pairs={{0,12},{1,13},{2,14},{3,15},{4,8},{5,9},{6,10},{7,11},{8,4},{9,5},... | collective-permute-start | bytes 442376 | tf_op jit(solution)/shard_map/ppermute | solution.py:236
  142.1 16.7 %collective-permute-start.18 = (bf16[4,18,16,256]{3,2,1,0:T(8,128)(2,1)S(1)}, bf16[4,18,16,256]{3,2,1,0:T(8,128)(2,1)S(1)}, u32[]{:S(2)}, u32[]{:S(2)}) collective-permute-start(bf16[4,18,16,256]{3,2,1,0:T(8,128)(2,1)S(1)} %constant_dynamic-update-slice_fusion), channel_id=1, source_target_pairs={{0,2},{1,3},{2,0},{3,1},{4,6},{5,7},{6,4},{7,5},{8,10},{9,11},{10,... | collective-permute-start | bytes 1769480 | tf_op jit(solution)/shard_map/ppermute | solution.py:236
  143.3 6.3 %collective-permute-start.19 = (bf16[2,9,16,256]{3,2,1,0:T(8,128)(2,1)S(1)}, bf16[2,9,16,256]{3,2,1,0:T(8,128)(2,1)S(1)}, u32[]{:S(2)}, u32[]{:S(2)}) collective-permute-start(bf16[2,9,16,256]{3,2,1,0:T(8,128)(2,1)S(1)} %constant_dynamic-update-slice_fusion.4), channel_id=1, source_target_pairs={{0,4},{1,5},{2,6},{3,7},{4,0},{5,1},{6,2},{7,3},{8,12},{9,13},{10,... | collective-permute-start | bytes 442376 | tf_op jit(solution)/shard_map/ppermute | solution.py:236
  146.8 12.0 %collective-permute-start.20 = (bf16[2,9,16,256]{3,2,1,0:T(8,128)(2,1)S(1)}, bf16[2,9,16,256]{3,2,1,0:T(8,128)(2,1)S(1)}, u32[]{:S(2)}, u32[]{:S(2)}) collective-permute-start(bf16[2,9,16,256]{3,2,1,0:T(8,128)(2,1)S(1)} %constant_dynamic-update-slice_fusion.4), channel_id=1, source_target_pairs={{0,8},{1,9},{2,10},{3,11},{4,12},{5,13},{6,14},{7,15},{8,0},{9,1},... | collective-permute-start | bytes 442376 | tf_op jit(solution)/shard_map/ppermute | solution.py:236
  146.8 12.0 %collective-permute-start.21 = (bf16[2,9,16,256]{3,2,1,0:T(8,128)(2,1)S(1)}, bf16[2,9,16,256]{3,2,1,0:T(8,128)(2,1)S(1)}, u32[]{:S(2)}, u32[]{:S(2)}) collective-permute-start(bf16[2,9,16,256]{3,2,1,0:T(8,128)(2,1)S(1)} %constant_dynamic-update-slice_fusion.4), channel_id=1, source_target_pairs={{0,12},{1,13},{2,14},{3,15},{4,8},{5,9},{6,10},{7,11},{8,4},{9,5},... | collective-permute-start | bytes 442376 | tf_op jit(solution)/shard_map/ppermute | solution.py:236
  158.9 23.2 %collective-permute-start.22 = (bf16[8,18,16,256]{3,2,1,0:T(8,128)(2,1)S(1)}, bf16[8,18,16,256]{3,2,1,0:T(8,128)(2,1)S(1)}, u32[]{:S(2)}, u32[]{:S(2)}) collective-permute-start(bf16[8,18,16,256]{3,2,1,0:T(8,128)(2,1)S(1)} %constant_dynamic-update-slice_fusion.6.own_one), channel_id=1, source_target_pairs={{0,1},{1,0},{2,3},{3,2},{4,5},{5,4},{6,7},{7,6},{8,9},{9,8},{10,11... | collective-permute-start | bytes 3538952 | tf_op jit(solution)/shard_map/ppermute | solution.py:236
  161.2 20.9 %collective-permute-start.23 = (bf16[8,9,16,256]{3,2,1,0:T(8,128)(2,1)S(1)}, bf16[8,9,16,256]{3,2,1,0:T(8,128)(2,1)S(1)}, u32[]{:S(2)}, u32[]{:S(2)}) collective-permute-start(bf16[8,9,16,256]{3,2,1,0:T(8,128)(2,1)S(1)} %constant_dynamic-update-slice_fusion.8.own_two), channel_id=1, source_target_pairs={{0,1},{1,0},{2,3},{3,2},{4,5},{5,4},{6,7},{7,6},{8,9},{9,8},{10,11... | collective-permute-start | bytes 1769480 | tf_op jit(solution)/shard_map/ppermute | solution.py:236
  172.7 4.9 %collective-permute-start.2 = (bf16[128,256]{1,0:T(8,128)(2,1)S(1)}, bf16[128,256]{1,0:T(8,128)(2,1)S(1)}, u32[]{:S(2)}, u32[]{:S(2)}) collective-permute-start(bf16[128,256]{1,0:T(8,128)(2,1)S(1)} %get-tuple-element.55), channel_id=1, source_target_pairs={{0,1},{1,2},{2,3},{3,4},{4,5},{5,6},{6,7},{7,8},{8,9},{9,10},{10,1... | collective-permute-start | bytes 196616 | tf_op jit(solution)/shard_map/ppermute | solution.py:452
  175.6 5.6 %collective-permute-start.3 = (bf16[128,256]{1,0:T(8,128)(2,1)S(1)}, bf16[128,256]{1,0:T(8,128)(2,1)S(1)}, u32[]{:S(2)}, u32[]{:S(2)}) collective-permute-start(bf16[128,256]{1,0:T(8,128)(2,1)S(1)} %get-tuple-element.56), channel_id=1, source_target_pairs={{1,0},{2,1},{3,2},{4,3},{5,4},{6,5},{7,6},{8,7},{9,8},{10,9},{11,1... | collective-permute-start | bytes 196616 | tf_op jit(solution)/shard_map/ppermute | solution.py:451
  (39 other events, 199.8 us)

commit v2 on v1

v2 whole, which is shorter than its diff:
```python
import functools

import jax
import jax.numpy as jnp
from jax import lax
from jax.experimental import pallas as pl
from jax.experimental.pallas import tpu as pltpu
from jax.sharding import PartitionSpec as P

K = 27
BLOCK = 128
GROUP = 9
K_ONE = 18
EPSILON = 1e-05
F32 = jnp.float32
BF16 = jnp.bfloat16
LARGE = 58 * 1024 * 1024
SMALL = 12 * 1024 * 1024


def dot(a, b, contract):
    return lax.dot_general(a, b, ((contract[0], contract[1]), ((), ())), preferred_element_type=F32)


def full(shape):
    return pl.BlockSpec(shape, lambda *_: (0,) * len(shape))


def params(limit):
    return pltpu.CompilerParams(vmem_limit_bytes=limit)


def cost(flops, moved):
    return pl.CostEstimate(flops=int(flops), bytes_accessed=int(moved), transcendentals=0)


def occupied_rows(filled, rows):
    position = lax.broadcasted_iota(jnp.int32, (rows, 1), 0)
    return (position < filled - BLOCK) | (position >= rows - BLOCK)


def convolve(blocks, map_ref, tiles, weight_hbm, conv_ref, picked_hbm, rows_of, scratch):
    weight, picked, index, weight_sem, picked_sem = scratch
    groups = K // GROUP

    def fetch(g):
        here = pl.ds(g * GROUP, GROUP)
        return pltpu.make_async_copy(weight_hbm.at[here], weight.at[here], weight_sem.at[g])

    def keep(g, b):
        here = pl.ds(g * GROUP, GROUP)
        return pltpu.make_async_copy(
            picked.at[here, pl.ds(b * BLOCK, BLOCK)],
            picked_hbm.at[here, pl.ds(rows_of[b], BLOCK)],
            picked_sem.at[g, b],
        )

    for g in range(groups):
        fetch(g).start()
    spare = jnp.zeros((BLOCK - K, blocks * BLOCK), jnp.int32)
    index[...] = jnp.transpose(jnp.concatenate([map_ref[...], spare], axis=0))
    conv_ref[...] = jnp.zeros_like(conv_ref)
    slots = lax.broadcasted_iota(jnp.int32, (BLOCK, 3 * BLOCK), 1)

    def group(g, carry):
        local = pltpu.roll(index[...], lax.rem(BLOCK - g * GROUP, BLOCK), 1)
        fetch(g).wait()
        for b in range(blocks):
            rows = slice(b * BLOCK, (b + 1) * BLOCK)
            here = local[rows] - (2 * BLOCK + rows_of[b] + BLOCK)
            for j in range(GROUP):
                chosen = jnp.where(here[:, j : j + 1] == slots, 1.0, 0.0).astype(BF16)
                picked[g * GROUP + j, rows, :] = dot(chosen, tiles[b][...], ((1,), (0,))).astype(BF16)
            keep(g, b).start()
        total = conv_ref[...]
        for j in range(GROUP):
            k = g * GROUP + j
            total = total + dot(picked[k], weight[k], ((1,), (0,)))
        conv_ref[...] = total
        return carry

    lax.fori_loop(0, groups, group, 0)

    def finish():
        for g in range(groups):
            for b in range(blocks):
                keep(g, b).wait()

    return finish


def inner_kernel(map_ref, own_ref, weight_hbm, conv_ref, picked_hbm, *scratch):
    tiles = [own_ref.at[0 : 3 * BLOCK], own_ref.at[BLOCK : 4 * BLOCK]]
    finish = convolve(
        2, map_ref, tiles, weight_hbm, conv_ref, picked_hbm, (BLOCK, 2 * BLOCK), scratch
    )
    finish()


def outer_kernel(
    filled_ref, map_ref, before_ref, own_ref, after_ref, inner_ref, weight_hbm, _,
    conv_ref, stats_ref, picked_hbm, first, last, *scratch,
):
    first[0:BLOCK, :] = before_ref[...]
    first[BLOCK:, :] = own_ref[0 : 2 * BLOCK, :]
    last[0 : 2 * BLOCK, :] = own_ref[2 * BLOCK :, :]
    last[2 * BLOCK :, :] = after_ref[...]
    finish = convolve(
        2, map_ref, [first, last], weight_hbm, conv_ref, picked_hbm, (0, 3 * BLOCK), scratch
    )
    filled = filled_ref[0]
    count = filled.astype(F32)
    conv = jnp.concatenate([conv_ref[0:BLOCK, :], inner_ref[...], conv_ref[BLOCK:, :]], axis=0)
    occupied = occupied_rows(filled, conv.shape[0])
    sums = jnp.sum(jnp.where(occupied, conv, 0.0), axis=0, keepdims=True)
    off = jnp.where(occupied, conv - sums / count, 0.0)
    squares = jnp.sum(off * off, axis=0, keepdims=True)
    stats_ref[...] = jnp.concatenate([sums, squares, jnp.full_like(sums, count)], axis=0)
    finish()


def normalised(filled, inner_ref, outer_ref, stats_ref, gain_ref, shift_ref, cotangent_ref):
    conv = jnp.concatenate([outer_ref[0:BLOCK, :], inner_ref[...], outer_ref[BLOCK:, :]], axis=0)
    total = stats_ref[2:3, :]
    center = stats_ref[0:1, :] / total
    inverse = lax.rsqrt(stats_ref[1:2, :] / total + EPSILON)
    occupied = occupied_rows(filled, conv.shape[0])
    normed = (conv - center) * inverse
    affine = gain_ref[...] * normed + shift_ref[...]
    upstream = jnp.where(occupied & (affine > 0.0), cotangent_ref[...].astype(F32), 0.0)
    return occupied, normed, affine, upstream, inverse, total


def norm_kernel(
    filled_ref, inner_ref, outer_ref, stats_ref, gain_ref, shift_ref, cotangent_ref, feature_ref,
    out_ref, sums_ref,
):
    occupied, normed, affine, upstream, _, _ = normalised(
        filled_ref[0], inner_ref, outer_ref, stats_ref, gain_ref, shift_ref, cotangent_ref
    )
    out = jnp.maximum(affine, 0.0) + feature_ref[...].astype(F32)
    out_ref[...] = jnp.where(occupied, out, 0.0).astype(BF16)
    sums_ref[...] = jnp.concatenate(
        [jnp.sum(upstream * normed, axis=0, keepdims=True), jnp.sum(upstream, axis=0, keepdims=True)],
        axis=0,
    )


def kernel_gradient(place, picked_ref, grad_ref, product, keep_ref, send_ref):
    rows = product.shape[1] // 16
    half = keep_ref.shape[0]
    for j in range(GROUP):
        product[j] = dot(picked_ref[j], grad_ref[...], ((0,), (0,)))
        for piece in range(16):
            start = pl.multiple_of(lax.bitwise_xor(jnp.int32(piece), place) * rows, rows)
            value = product[j, pl.ds(start, rows), :]
            if piece < half:
                keep_ref[piece, j] = value
            else:
                send_ref[piece - half, j] = value.astype(BF16)


def first_gradient_kernel(
    filled_ref, place_ref, inner_ref, outer_ref, stats_ref, grads_ref, gain_ref, shift_ref,
    cotangent_ref, picked_ref, keep_ref, send_ref, grad_ref, product,
):
    @pl.when(pl.program_id(0) == 0)
    def _():
        occupied, normed, _, upstream, inverse, total = normalised(
            filled_ref[0], inner_ref, outer_ref, stats_ref, gain_ref, shift_ref, cotangent_ref
        )
        grad_conv = gain_ref[...] * inverse * (
            upstream - grads_ref[1:2, :] / total - normed * grads_ref[0:1, :] / total
        )
        grad_ref[...] = jnp.where(occupied, grad_conv, 0.0).astype(BF16)

    kernel_gradient(place_ref[0], picked_ref, grad_ref, product, keep_ref, send_ref)


def second_gradient_kernel(place_ref, grad_ref, picked_ref, keep_ref, send_ref, product):
    kernel_gradient(place_ref[0], picked_ref, grad_ref, product, keep_ref, send_ref)


def push_kernel(grad_ref, index_ref, weight_ref, before_ref, own_ref, after_ref, sink):
    step = pl.program_id(0)

    @pl.when(step == 0)
    def _():
        sink[...] = jnp.zeros_like(sink)

    blocks = grad_ref.shape[0] // BLOCK
    here = jnp.concatenate([index_ref[step * GROUP + j, :][None] for j in range(GROUP)], axis=0)
    block_of = lax.broadcasted_iota(jnp.int32, here.shape, 1) // BLOCK
    local = here - (3 + block_of) * BLOCK
    slots = lax.broadcasted_iota(jnp.int32, (3 * BLOCK, BLOCK), 0)
    pushed = [
        dot(grad_ref[...], weight_ref[j], ((1,), (1,))).astype(BF16) for j in range(GROUP)
    ]
    for b in range(blocks):
        rows = slice(b * BLOCK, (b + 1) * BLOCK)
        chosen = jnp.concatenate(
            [
                jnp.where(local[j : j + 1, rows] == slots, 1.0, 0.0).astype(BF16)
                for j in range(GROUP)
            ],
            axis=1,
        )
        stacked = jnp.concatenate([pushed[j][rows] for j in range(GROUP)], axis=0)
        window = slice(b * BLOCK, (b + 3) * BLOCK)
        sink[window, :] = sink[window, :] + dot(chosen, stacked, ((1,), (0,)))

    @pl.when(step == pl.num_programs(0) - 1)
    def _():
        before_ref[...] = sink[0:BLOCK, :].astype(BF16)
        own_ref[...] = sink[BLOCK : (blocks + 1) * BLOCK, :]
        after_ref[...] = sink[(blocks + 1) * BLOCK :, :].astype(BF16)


def place_kernel(places_ref, own_one, other_one, own_two, other_two, out_ref, sems):
    rows = own_one.shape[2]
    half = own_one.shape[0]
    split = own_one.shape[1]
    copies = []
    for piece in range(16):
        for part, (own, other) in enumerate(((own_one, other_one), (own_two, other_two))):
            source = own if piece < half else other
            place = lax.bitwise_xor(jnp.int32(piece), places_ref[part])
            start = pl.multiple_of(place * rows, rows)
            first = 0 if part == 0 else split
            copies.append(
                pltpu.make_async_copy(
                    source.at[piece % half],
                    out_ref.at[pl.ds(first, source.shape[1]), pl.ds(start, rows), :],
                    sems.at[len(copies)],
                )
            )
    for copy in copies:
        copy.start()
    for copy in copies:
        copy.wait()


def swap(value, by):
    peers = lax.axis_size("dp")
    return lax.ppermute(value, "dp", [(i, i ^ by) for i in range(peers)])


STAGES = {"c": (1,), "x": (2,), "z": (4, 8, 12)}


def reduce_start(total, stage):
    partners = STAGES[stage]
    size = total.shape[0] // (len(partners) + 1)
    return [
        swap(total[(i + 1) * size : (i + 2) * size].astype(BF16), by)
        for i, by in enumerate(partners)
    ]


def reduce_end(total, received):
    size = received[0].shape[0]
    return functools.reduce(lambda a, b: a + b.astype(F32), received, total[:size])


def gather_start(piece, stage):
    return [swap(piece, by) for by in STAGES[stage]]


def summed_over_devices(one, two, grad_conv, push):
    pieces = [keep + swap(send, 1).astype(F32) for keep, send in (one, two)]
    pieces, grad_conv = lax.optimization_barrier((pieces, grad_conv))
    beside = push(grad_conv)
    for stages in ("xz", "zx"):
        received = [reduce_start(piece, stage) for piece, stage in zip(pieces, stages)]
        received, pieces, beside = lax.optimization_barrier((received, pieces, beside))
        pieces = [reduce_end(piece, got) for piece, got in zip(pieces, received)]
    by = 16
    while by < lax.axis_size("dp"):
        pieces = [piece + swap(piece, by) for piece in pieces]
        by *= 2
    pieces = [piece.astype(BF16) for piece in pieces]
    for stages in ("zx", "xz"):
        received = [gather_start(piece, stage) for piece, stage in zip(pieces, stages)]
        received, pieces = lax.optimization_barrier((received, pieces))
        pieces = [
            jnp.concatenate([piece] + got, axis=0) for piece, got in zip(pieces, received)
        ]
    return [(piece, swap(piece, 1)) for piece in pieces], beside


def exchanged(value, merge):
    for partners in ((1, 2, 3), (4, 8, 12)):
        received = [swap(value, by) for by in partners]
        received, value = lax.optimization_barrier((received, value))
        value = merge(merge(value, received[0]), merge(received[1], received[2]))
    by = 16
    while by < lax.axis_size("dp"):
        value = merge(value, swap(value, by))
        by *= 2
    return value


def merged_moments(one, two):
    (sum_one, square_one, count_one), (sum_two, square_two, count_two) = one, two
    away = sum_one / count_one - sum_two / count_two
    count = count_one + count_two
    square = (square_one + square_two) + away * away * (count_one * count_two / count)
    return jnp.stack([sum_one + sum_two, square, count])


def per_device(features, kernel_map, occupancy, weights, bn_gain, bn_shift, cotangent):
    rows, channels = features.shape
    peers = lax.axis_size("dp")
    me = lax.axis_index("dp")
    blocks = rows // BLOCK
    inner_rows = rows - 2 * BLOCK
    steps = K // GROUP

    up = [(i, i + 1) for i in range(peers - 1)]
    down = [(i + 1, i) for i in range(peers - 1)]
    before = lax.ppermute(features[rows - BLOCK :], "dp", up)
    after = lax.ppermute(features[:BLOCK], "dp", down)

    map_rows = jnp.transpose(kernel_map)
    map_outer = jnp.concatenate([map_rows[:, :BLOCK], map_rows[:, rows - BLOCK :]], axis=1)

    gain = bn_gain.reshape(1, channels)
    shift = bn_shift.reshape(1, channels)
    smem = pl.BlockSpec(memory_space=pltpu.SMEM)
    vmem = pl.BlockSpec(memory_space=pltpu.VMEM)
    hbm = pl.BlockSpec(memory_space=pltpu.HBM)
    groups = K // GROUP
    half_conv = jax.ShapeDtypeStruct((2 * BLOCK, channels), F32)
    all_picked = jax.ShapeDtypeStruct((K, rows, channels), BF16)
    work = K * 2 * BLOCK * channels * 2 * (3 * BLOCK + channels)
    moved = K * channels * channels * 2 * 2
    scratch = [
        pltpu.VMEM((K, channels, channels), BF16),
        pltpu.VMEM((K, 2 * BLOCK, channels), BF16),
        pltpu.VMEM((2 * BLOCK, BLOCK), jnp.int32),
        pltpu.SemaphoreType.DMA((groups,)),
        pltpu.SemaphoreType.DMA((groups, 2)),
    ]

    inner, picked = pl.pallas_call(
        inner_kernel,
        in_specs=[vmem, vmem, hbm],
        out_specs=[vmem, hbm],
        out_shape=[half_conv, all_picked],
        scratch_shapes=scratch,
        compiler_params=params(LARGE),
        cost_estimate=cost(work, moved),
        name="conv_inner",
    )(map_rows[:, BLOCK : rows - BLOCK], features, weights)

    outer, stats, picked = pl.pallas_call(
        outer_kernel,
        in_specs=[smem, vmem, vmem, vmem, vmem, vmem, hbm, hbm],
        out_specs=[vmem, vmem, hbm],
        out_shape=[half_conv, jax.ShapeDtypeStruct((3, channels), F32), all_picked],
        scratch_shapes=[pltpu.VMEM((3 * BLOCK, channels), BF16)] * 2 + scratch,
        input_output_aliases={7: 2},
        compiler_params=params(LARGE),
        cost_estimate=cost(work, moved),
        name="conv_outer",
    )(occupancy, map_outer, before, features, after, inner, weights, picked)

    stats = exchanged(stats, merged_moments)

    block_out, sums = pl.pallas_call(
        norm_kernel,
        in_specs=[smem] + [vmem] * 7,
        out_shape=[
            jax.ShapeDtypeStruct((rows, channels), BF16),
            jax.ShapeDtypeStruct((2, channels), F32),
        ],
        compiler_params=params(LARGE),
        cost_estimate=cost(rows * channels * 20, rows * channels * 10),
        name="norm",
    )(occupancy, inner, outer, stats, gain, shift, cotangent, features)

    grads = exchanged(sums, jnp.add)

    core, lane, depth = me & 1, (me >> 1) & 1, (me >> 2) & 3
    place_one = (core * 8 + lane * 4 + depth).reshape(1)
    place_two = (core * 8 + depth * 2 + lane).reshape(1)
    piece_rows = channels // 16
    piece_spec = pl.BlockSpec((8, GROUP, piece_rows, channels), lambda s: (0, s, 0, 0))

    def picked_spec(first):
        return pl.BlockSpec((GROUP, rows, channels), lambda s: (s + first // GROUP, 0, 0))

    def pieces(count):
        shape = (8, count, piece_rows, channels)
        return [jax.ShapeDtypeStruct(shape, F32), jax.ShapeDtypeStruct(shape, BF16)]

    product = pltpu.VMEM((GROUP, channels, channels), F32)
    keep_one, send_one, grad_conv = pl.pallas_call(
        first_gradient_kernel,
        grid=(K_ONE // GROUP,),
        in_specs=[
            smem,
            smem,
            full((2 * BLOCK, channels)),
            full((2 * BLOCK, channels)),
            full((3, channels)),
            full((2, channels)),
            full((1, channels)),
            full((1, channels)),
            full((rows, channels)),
            picked_spec(0),
        ],
        out_specs=[piece_spec, piece_spec, full((rows, channels))],
        out_shape=pieces(K_ONE) + [jax.ShapeDtypeStruct((rows, channels), BF16)],
        scratch_shapes=[product],
        compiler_params=params(LARGE),
        cost_estimate=cost(K_ONE * rows * channels * channels * 2, K_ONE * channels * channels * 8),
        name="weight_gradient_one",
    )(occupancy, place_one, inner, outer, stats, grads, gain, shift, cotangent, picked)

    keep_two, send_two = pl.pallas_call(
        second_gradient_kernel,
        grid=((K - K_ONE) // GROUP,),
        in_specs=[smem, full((rows, channels)), picked_spec(K_ONE)],
        out_specs=[piece_spec, piece_spec],
        out_shape=pieces(K - K_ONE),
        scratch_shapes=[product],
        compiler_params=params(LARGE),
        cost_estimate=cost(
            (K - K_ONE) * rows * channels * channels * 2, (K - K_ONE) * channels * channels * 8
        ),
        name="weight_gradient_two",
    )(place_two, grad_conv, picked)

    weight_spec = pl.BlockSpec((GROUP, channels, channels), lambda s: (s, 0, 0))

    def push(grad_conv):
        sink_before, sink_own, sink_after = pl.pallas_call(
            push_kernel,
            grid=(groups,),
            in_specs=[full((rows, channels)), full((K, rows)), weight_spec],
            out_specs=[full((BLOCK, channels)), full((rows, channels)), full((BLOCK, channels))],
            out_shape=[
                jax.ShapeDtypeStruct((BLOCK, channels), BF16),
                jax.ShapeDtypeStruct((rows, channels), F32),
                jax.ShapeDtypeStruct((BLOCK, channels), BF16),
            ],
            scratch_shapes=[pltpu.VMEM((rows + 2 * BLOCK, channels), F32)],
            compiler_params=params(SMALL),
            cost_estimate=cost(2 * work, moved),
            name="push",
        )(grad_conv, map_rows, weights)
        return sink_before, sink_own, sink_after

    ((own_one, other_one), (own_two, other_two)), (sink_before, sink_own, sink_after) = (
        summed_over_devices((keep_one, send_one), (keep_two, send_two), grad_conv, push)
    )
    anywhere = pl.BlockSpec(memory_space=pl.ANY)
    grad_weights = pl.pallas_call(
        place_kernel,
        in_specs=[smem] + [anywhere] * 4,
        out_specs=anywhere,
        out_shape=jax.ShapeDtypeStruct(weights.shape, BF16),
        scratch_shapes=[pltpu.SemaphoreType.DMA((32,))],
        compiler_params=params(SMALL),
        cost_estimate=cost(0, K * channels * channels * 4),
        name="place",
    )(jnp.concatenate([place_one, place_two]), own_one, other_one, own_two, other_two)

    from_next = lax.ppermute(sink_before, "dp", down).astype(F32)
    from_prev = lax.ppermute(sink_after, "dp", up).astype(F32)
    occupied = occupied_rows(occupancy[0], rows)
    received = jnp.concatenate(
        [
            sink_own[:BLOCK] + from_prev,
            sink_own[BLOCK : rows - BLOCK],
            sink_own[rows - BLOCK :] + from_next,
        ],
        axis=0,
    )
    grad_features = (jnp.where(occupied, cotangent.astype(F32), 0.0) + received).astype(BF16)
    return (
        block_out,
        grad_features,
        grad_weights,
        grads[0],
        grads[1],
    )


def solution(mesh):
    in_specs = (
        P(("parts", "dp"), None),
        P(("parts", "dp"), None),
        P(("parts", "dp")),
        P(),
        P(),
        P(),
        P(("parts", "dp"), None),
    )
    out_specs = (
        P(("parts", "dp"), None),
        P(("parts", "dp"), None),
        P("parts", None, None),
        P("parts"),
        P("parts"),
    )
    return jax.shard_map(
        per_device, mesh=mesh, in_specs=in_specs, out_specs=out_specs, check_vma=False
    )
```

time: 188 us -> 151 us (0.80)
  local copies, waits for them, and re-layouts: 31.8 us -> 4.99 us
  waiting for transfers between devices: 53.1 us -> 39.4 us
  starting transfers between devices: 48.5 us -> 58.1 us
  Pallas kernels: 44.6 us -> 37.9 us
  other arithmetic: 4.95 us -> 6.84 us
    unnamed x82 -> x24, local copies, waits for them, and re-layouts: 27 us -> 1.18 us
    ppermute x20 -> x32, starting transfers between devices: 26 us -> 47.2 us  [swap(): return lax.ppermute(value, 'dp', [(i, i ^ by) for i in range(peers)])]
    all_to_all x2 -> x0, waiting for transfers between devices: 12.2 us -> none  [the longest x1 6.15 us: per_device(): stats = lax.all_to_all(stats, 'dp', 0, 0, tiled=True)]
    all_to_all x2 -> x0, starting transfers between devices: 11.3 us -> none  [the longest x1 6.46 us: per_device(): stats = lax.all_to_all(stats, 'dp', 0, 0, tiled=True)]
    pallas_call x6, Pallas kernels: 42 us -> 35.3 us  [the longest x1 9.28 us: push(): pl.pallas_call(push_kernel, grid=(groups,), in_specs=[full((rows, channel...]
    add x0 -> x4, other arithmetic: none -> 2.12 us  [the longest x2 1.28 us: exchanged(): value = merge(merge(value, received[0]), merge(received[1], received[2]))]
    ppermute x20 -> x32, waiting for transfers between devices: 37.3 us -> 36.8 us  [swap(): return lax.ppermute(value, 'dp', [(i, i ^ by) for i in range(peers)])]
  transfers between devices with their start and end apart: 26 -> 36, of which waited for: 13 -> 17; matrix products, arithmetic and copies ran while one was open for 4% -> 4% of each run, Pallas kernels for 12% -> 14%
where the time goes in v2:
time: 151 us; the launch traced here: 149 us
  starting transfers between devices  58.1 us (38%)
  waiting for transfers between devices  39.4 us (26%)
  Pallas kernels  37.9 us (25%)
  other arithmetic  6.84 us (5%)
  local copies, waits for them, and re-layouts  4.99 us (3%)
  between operations  1.66 us (1%)
    ppermute x32, starting transfers between devices, swap(): return lax.ppermute(value, 'dp', [(i, i ^ by) for i in range(peers)])  47.2 us
    ppermute x32, waiting for transfers between devices, swap(): return lax.ppermute(value, 'dp', [(i, i ^ by) for i in range(peers)])  36.8 us
    pallas_call x1, Pallas kernels, push(): pl.pallas_call(push_kernel, grid=(groups,), in_specs=[full((rows, channel...  9.28 us
    pallas_call x1, Pallas kernels, per_device(): pl.pallas_call(outer_kernel, in_specs=[smem, vmem, vmem, vmem, vmem, vmem...  7.37 us
    pallas_call x1, Pallas kernels, per_device(): pl.pallas_call(inner_kernel, in_specs=[vmem, vmem, hbm], out_specs=[vmem,...  7.27 us
    pallas_call x1, Pallas kernels, per_device(): pl.pallas_call(first_gradient_kernel, grid=(K_ONE // GROUP,), in_specs=[s...  5.32 us
    ppermute x1, starting transfers between devices, per_device(): before = lax.ppermute(features[rows - BLOCK:], 'dp', up)  4.51 us
    pallas_call x1, Pallas kernels, per_device(): pl.pallas_call(second_gradient_kernel, grid=((K - K_ONE) // GROUP,), in_s...  3.89 us
  transfers between devices with their start and end apart: 36, of which 17 were waited for; matrix products, arithmetic and copies ran while one was open for 4% of the time, Pallas kernels for 14%

profile of v2, /device:TPU:1, one launch (start us, length us, event | category | flops | bytes accessed | tf_op | source)
XLA Modules:
  0.0 149.0 jit_solution(10831435892376689103)
XLA Ops:
  1.5 4.5 %collective-permute-start = (bf16[128,256]{1,0:T(8,128)(2,1)S(1)}, bf16[128,256]{1,0:T(8,128)(2,1)S(1)}, u32[]{:S(2)}, u32[]{:S(2)}) collective-permute-start(bf16[128,256]{1,0:T(8,128)(2,1)S(1)} %get-tuple-element.148), channel_id=1, source_target_pairs={{0,1},{1,2},{2,3},{3,4},{4,5},{5,6},{6,7},{7,8},{8,9},{9,10},{10,1... | collective-permute-start | bytes 196616 | tf_op jit(solution)/shard_map/ppermute | solution.py:321
  10.7 7.3 %conv_inner.1 = (f32[256,256]{1,0:T(8,128)}, bf16[27,512,256]{2,1,0:T(8,128)(2,1)}) custom-call(s32[27,256]{1,0:T(8,128)} %slice.96.map_ref, bf16[512,256]{1,0:T(8,128)(2,1)} %feature_ref.1, bf16[27,256,256]{2,1,0:T(8,128)(2,1)} %weight_ref.1), custom_call_target="tpu_custom_call" | custom-call | flops 2264924160 | bytes 7077888 | tf_op jit(solution)/shard_map/conv_inner/pallas_call | solution.py:345
  19.3 7.4 %conv_outer.1 = (f32[256,256]{1,0:T(8,128)}, f32[3,256]{1,0:T(4,128)}, bf16[27,512,256]{2,1,0:T(8,128)(2,1)}) custom-call(s32[1]{0:T(128)S(6)} %copy.22.filled_ref, s32[27,256]{1,0:T(8,128)} %pad_add_fusion.map_ref, bf16[128,256]{1,0:T(8,128)(2,1)} %copy-done.5, bf16[512,256]{1,0:T(8,128)(2,1)} %feature_ref.1, ...), custom_call_target="tpu_custom_call", output_to_operand_aliasing={{2}: (7, {})} | custom-call | flops 2264924160 | bytes 7077888 | tf_op jit(solution)/shard_map/conv_outer/pallas_call | solution.py:356
  34.0 2.3 %collective-permute-start.6 = (f32[3,256]{1,0:T(4,128)S(1)}, f32[3,256]{1,0:T(4,128)S(1)}, u32[]{:S(2)}, u32[]{:S(2)}) collective-permute-start(f32[3,256]{1,0:T(4,128)S(1)} %pad_maximum_fusion), channel_id=1, source_target_pairs={{0,8},{1,9},{2,10},{3,11},{4,12},{5,13},{6,14},{7,15},{8,0},{9,1},... | collective-permute-start | bytes 9224 | tf_op jit(solution)/shard_map/ppermute | solution.py:245
  37.4 3.2 %collective-permute-done.7 = f32[3,256]{1,0:T(4,128)S(1)} collective-permute-done((f32[3,256]{1,0:T(4,128)S(1)}, f32[3,256]{1,0:T(4,128)S(1)}, u32[]{:S(2)}, u32[]{:S(2)}) %collective-permute-start.7) | collective-permute-done | bytes 3104 | tf_op jit(solution)/shard_map/ppermute | solution.py:245
  43.4 3.1 %collective-permute-start.10 = (f32[2,256]{1,0:T(2,128)}, f32[2,256]{1,0:T(2,128)S(1)}, u32[]{:S(2)}, u32[]{:S(2)}) collective-permute-start(f32[2,256]{1,0:T(2,128)} %get-tuple-element.83), channel_id=1, source_target_pairs={{0,3},{1,2},{2,1},{3,0},{4,7},{5,6},{6,5},{7,4},{8,11},{9,10},{10,... | collective-permute-start | bytes 6152 | tf_op jit(solution)/shard_map/ppermute | solution.py:245
  49.9 3.5 %collective-permute-start.13 = (f32[2,256]{1,0:T(2,128)S(1)}, f32[2,256]{1,0:T(2,128)S(1)}, u32[]{:S(2)}, u32[]{:S(2)}) collective-permute-start(f32[2,256]{1,0:T(2,128)S(1)} %add_add_fusion.1), channel_id=1, source_target_pairs={{0,12},{1,13},{2,14},{3,15},{4,8},{5,9},{6,10},{7,11},{8,4},{9,5},... | collective-permute-start | bytes 6152 | tf_op jit(solution)/shard_map/ppermute | solution.py:245
  55.0 5.3 %weight_gradient_one.1 = (f32[8,18,16,256]{3,2,1,0:T(8,128)}, bf16[8,18,16,256]{3,2,1,0:T(8,128)(2,1)}, bf16[512,256]{1,0:T(8,128)(2,1)}) custom-call(s32[1]{0:T(128)S(6)} %copy.22.filled_ref, s32[1]{0:T(128)} %bitcast.4.place_ref, f32[256,256]{1,0:T(8,128)} %get-tuple-element.69.inner_ref, f32[256,256]{1,0:T(8,128)} %get-tuple-element.71.outer_ref, ...), custom_call_target="tpu_custom_call" | custom-call | flops 1207959552 | bytes 9437184 | tf_op jit(solution)/shard_map/weight_gradient_one/pallas_call | solution.py:398
  60.3 3.2 %collective-permute-start.14 = (bf16[8,18,16,256]{3,2,1,0:T(8,128)(2,1)}, bf16[8,18,16,256]{3,2,1,0:T(8,128)(2,1)S(1)}, u32[]{:S(2)}, u32[]{:S(2)}) collective-permute-start(bf16[8,18,16,256]{3,2,1,0:T(8,128)(2,1)} %get-tuple-element.93), channel_id=1, source_target_pairs={{0,1},{1,0},{2,3},{3,2},{4,5},{5,4},{6,7},{7,6},{8,9},{9,8},{10,11... | collective-permute-start | bytes 3538952 | tf_op jit(solution)/shard_map/ppermute | solution.py:245
  63.5 3.9 %weight_gradient_two.1 = (f32[8,9,16,256]{3,2,1,0:T(8,128)}, bf16[8,9,16,256]{3,2,1,0:T(8,128)(2,1)}) custom-call(s32[1]{0:T(128)} %bitcast.5.place_ref, bf16[512,256]{1,0:T(8,128)(2,1)} %get-tuple-element.99.grad_ref, bf16[27,512,256]{2,1,0:T(8,128)(2,1)} %get-tuple-element.91.picked_ref), custom_call_target="tpu_custom_call" | custom-call | flops 603979776 | bytes 4718592 | tf_op jit(solution)/shard_map/weight_gradient_two/pallas_call | solution.py:421
  73.0 3.6 %collective-permute-start.18 = (bf16[2,9,16,256]{3,2,1,0:T(8,128)(2,1)S(1)}, bf16[2,9,16,256]{3,2,1,0:T(8,128)(2,1)S(1)}, u32[]{:S(2)}, u32[]{:S(2)}) collective-permute-start(bf16[2,9,16,256]{3,2,1,0:T(8,128)(2,1)S(1)} %get-tuple-element.143), channel_id=1, source_target_pairs={{0,8},{1,9},{2,10},{3,11},{4,12},{5,13},{6,14},{7,15},{8,0},{9,1},... | collective-permute-start | bytes 442376 | tf_op jit(solution)/shard_map/ppermute | solution.py:245
  76.6 9.3 %push.1 = (bf16[128,256]{1,0:T(8,128)(2,1)S(1)}, f32[512,256]{1,0:T(8,128)S(1)}, bf16[128,256]{1,0:T(8,128)(2,1)S(1)}) custom-call(bf16[512,256]{1,0:T(8,128)(2,1)S(1)} %copy-done.1, s32[27,512]{1,0:T(8,128)S(1)} %bitcast.10, bf16[27,256,256]{2,1,0:T(8,128)(2,1)S(1)} %copy-done), custom_call_target="tpu_custom_call" | custom-call | flops 4529848320 | bytes 7077888 | tf_op jit(solution)/shard_map/push/pallas_call | solution.py:438
  87.4 2.9 %collective-permute-start.20 = (bf16[1,18,16,256]{3,2,1,0:T(8,128)(2,1)S(1)}, bf16[1,18,16,256]{3,2,1,0:T(8,128)(2,1)S(1)}, u32[]{:S(2)}, u32[]{:S(2)}) collective-permute-start(bf16[1,18,16,256]{3,2,1,0:T(8,128)(2,1)S(1)} %get-tuple-element.141), channel_id=1, source_target_pairs={{0,4},{1,5},{2,6},{3,7},{4,0},{5,1},{6,2},{7,3},{8,12},{9,13},{10,... | collective-permute-start | bytes 442376 | tf_op jit(solution)/shard_map/ppermute | solution.py:245
  93.7 2.4 %collective-permute-done.23 = bf16[1,9,16,256]{3,2,1,0:T(8,128)(2,1)S(1)} collective-permute-done((bf16[1,9,16,256]{3,2,1,0:T(8,128)(2,1)S(1)}, bf16[1,9,16,256]{3,2,1,0:T(8,128)(2,1)S(1)}, u32[]{:S(2)}, u32[]{:S(2)}) %collective-permute-start.23) | collective-permute-done | bytes 73760 | tf_op jit(solution)/shard_map/ppermute | solution.py:245
  96.1 5.0 %collective-permute-done.22 = bf16[1,18,16,256]{3,2,1,0:T(8,128)(2,1)S(1)} collective-permute-done((bf16[1,18,16,256]{3,2,1,0:T(8,128)(2,1)S(1)}, bf16[1,18,16,256]{3,2,1,0:T(8,128)(2,1)S(1)}, u32[]{:S(2)}, u32[]{:S(2)}) %collective-permute-start.22) | collective-permute-done | bytes 147488 | tf_op jit(solution)/shard_map/ppermute | solution.py:245
  101.1 4.0 %collective-permute-start.26 = (bf16[1,18,16,256]{3,2,1,0:T(8,128)(2,1)S(1)}, bf16[1,18,16,256]{3,2,1,0:T(8,128)(2,1)S(1)}, u32[]{:S(2)}, u32[]{:S(2)}) collective-permute-start(bf16[1,18,16,256]{3,2,1,0:T(8,128)(2,1)S(1)} %add_convert_fusion), channel_id=1, source_target_pairs={{0,4},{1,5},{2,6},{3,7},{4,0},{5,1},{6,2},{7,3},{8,12},{9,13},{10,... | collective-permute-start | bytes 442376 | tf_op jit(solution)/shard_map/ppermute | solution.py:245
  109.2 2.4 %collective-permute-done.29 = bf16[1,9,16,256]{3,2,1,0:T(8,128)(2,1)S(1)} collective-permute-done((bf16[1,9,16,256]{3,2,1,0:T(8,128)(2,1)S(1)}, bf16[1,9,16,256]{3,2,1,0:T(8,128)(2,1)S(1)}, u32[]{:S(2)}, u32[]{:S(2)}) %collective-permute-start.29) | collective-permute-done | bytes 73760 | tf_op jit(solution)/shard_map/ppermute | solution.py:245
  111.6 4.8 %collective-permute-done.28 = bf16[1,18,16,256]{3,2,1,0:T(8,128)(2,1)S(1)} collective-permute-done((bf16[1,18,16,256]{3,2,1,0:T(8,128)(2,1)S(1)}, bf16[1,18,16,256]{3,2,1,0:T(8,128)(2,1)S(1)}, u32[]{:S(2)}, u32[]{:S(2)}) %collective-permute-start.28) | collective-permute-done | bytes 147488 | tf_op jit(solution)/shard_map/ppermute | solution.py:245
  117.6 4.1 %collective-permute-start.31 = (bf16[2,9,16,256]{3,2,1,0:T(8,128)(2,1)S(1)}, bf16[2,9,16,256]{3,2,1,0:T(8,128)(2,1)S(1)}, u32[]{:S(2)}, u32[]{:S(2)}) collective-permute-start(bf16[2,9,16,256]{3,2,1,0:T(8,128)(2,1)S(1)} %constant_dynamic-update-slice_fusion.4), channel_id=1, source_target_pairs={{0,4},{1,5},{2,6},{3,7},{4,0},{5,1},{6,2},{7,3},{8,12},{9,13},{10,... | collective-permute-start | bytes 442376 | tf_op jit(solution)/shard_map/ppermute | solution.py:245
  126.7 6.5 %collective-permute-done.33 = bf16[2,9,16,256]{3,2,1,0:T(8,128)(2,1)S(1)} collective-permute-done((bf16[2,9,16,256]{3,2,1,0:T(8,128)(2,1)S(1)}, bf16[2,9,16,256]{3,2,1,0:T(8,128)(2,1)S(1)}, u32[]{:S(2)}, u32[]{:S(2)}) %collective-permute-start.33) | collective-permute-done | bytes 147488 | tf_op jit(solution)/shard_map/ppermute | solution.py:245
  133.3 4.2 %collective-permute-start.34 = (bf16[8,18,16,256]{3,2,1,0:T(8,128)(2,1)S(1)}, bf16[8,18,16,256]{3,2,1,0:T(8,128)(2,1)S(1)}, u32[]{:S(2)}, u32[]{:S(2)}) collective-permute-start(bf16[8,18,16,256]{3,2,1,0:T(8,128)(2,1)S(1)} %constant_dynamic-update-slice_fusion.6.own_one), channel_id=1, source_target_pairs={{0,1},{1,0},{2,3},{3,2},{4,5},{5,4},{6,7},{7,6},{8,9},{9,8},{10,11... | collective-permute-start | bytes 3538952 | tf_op jit(solution)/shard_map/ppermute | solution.py:245
  137.6 2.3 %collective-permute-start.24 = (bf16[128,256]{1,0:T(8,128)(2,1)S(1)}, bf16[128,256]{1,0:T(8,128)(2,1)S(1)}, u32[]{:S(2)}, u32[]{:S(2)}) collective-permute-start(bf16[128,256]{1,0:T(8,128)(2,1)S(1)} %get-tuple-element.113), channel_id=1, source_target_pairs={{0,1},{1,2},{2,3},{3,4},{4,5},{5,6},{6,7},{7,8},{8,9},{9,10},{10,1... | collective-permute-start | bytes 196616 | tf_op jit(solution)/shard_map/ppermute | solution.py:471
  142.8 2.7 %collective-permute-done.25 = bf16[128,256]{1,0:T(8,128)(2,1)S(1)} collective-permute-done((bf16[128,256]{1,0:T(8,128)(2,1)S(1)}, bf16[128,256]{1,0:T(8,128)(2,1)S(1)}, u32[]{:S(2)}, u32[]{:S(2)}) %collective-permute-start.25) | collective-permute-done | bytes 65568 | tf_op jit(solution)/shard_map/ppermute | solution.py:470
  146.4 2.6 %place.1 = bf16[27,256,256]{2,1,0:T(8,128)(2,1)} custom-call(s32[2]{0:T(128)S(1)} %pad_add_fusion.1.places_ref, bf16[8,18,16,256]{3,2,1,0:T(8,128)(2,1)S(1)} %constant_dynamic-update-slice_fusion.6.own_one, bf16[8,18,16,256]{3,2,1,0:T(8,128)(2,1)S(1)} %collective-permute-done.34.other_one, ...), custom_call_target="tpu_custom_call" | custom-call | bytes 7077888 | tf_op jit(solution)/shard_map/place/pallas_call | solution.py:459
  (110 shorter events, 47.1 us)
Async XLA Ops:
  1.5 17.1 %collective-permute-start = (bf16[128,256]{1,0:T(8,128)(2,1)S(1)}, bf16[128,256]{1,0:T(8,128)(2,1)S(1)}, u32[]{:S(2)}, u32[]{:S(2)}) collective-permute-start(bf16[128,256]{1,0:T(8,128)(2,1)S(1)} %get-tuple-element.148), channel_id=1, source_target_pairs={{0,1},{1,2},{2,3},{3,4},{4,5},{5,6},{6,7},{7,8},{8,9},{9,10},{10,1... | collective-permute-start | bytes 196616 | tf_op jit(solution)/shard_map/ppermute | solution.py:321
  6.0 12.6 %collective-permute-start.1 = (bf16[128,256]{1,0:T(8,128)(2,1)S(1)}, bf16[128,256]{1,0:T(8,128)(2,1)S(1)}, u32[]{:S(2)}, u32[]{:S(2)}) collective-permute-start(bf16[128,256]{1,0:T(8,128)(2,1)S(1)} %get-tuple-element.147), channel_id=1, source_target_pairs={{1,0},{2,1},{3,2},{4,3},{5,4},{6,5},{7,6},{8,7},{9,8},{10,9},{11,1... | collective-permute-start | bytes 196616 | tf_op jit(solution)/shard_map/ppermute | solution.py:322
  36.3 4.3 %collective-permute-start.7 = (f32[3,256]{1,0:T(4,128)S(1)}, f32[3,256]{1,0:T(4,128)S(1)}, u32[]{:S(2)}, u32[]{:S(2)}) collective-permute-start(f32[3,256]{1,0:T(4,128)S(1)} %pad_maximum_fusion), channel_id=1, source_target_pairs={{0,12},{1,13},{2,14},{3,15},{4,8},{5,9},{6,10},{7,11},{8,4},{9,5},... | collective-permute-start | bytes 9224 | tf_op jit(solution)/shard_map/ppermute | solution.py:245
  43.4 4.6 %collective-permute-start.10 = (f32[2,256]{1,0:T(2,128)}, f32[2,256]{1,0:T(2,128)S(1)}, u32[]{:S(2)}, u32[]{:S(2)}) collective-permute-start(f32[2,256]{1,0:T(2,128)} %get-tuple-element.83), channel_id=1, source_target_pairs={{0,3},{1,2},{2,1},{3,0},{4,7},{5,6},{6,5},{7,4},{8,11},{9,10},{10,... | collective-permute-start | bytes 6152 | tf_op jit(solution)/shard_map/ppermute | solution.py:245
  49.9 4.5 %collective-permute-start.13 = (f32[2,256]{1,0:T(2,128)S(1)}, f32[2,256]{1,0:T(2,128)S(1)}, u32[]{:S(2)}, u32[]{:S(2)}) collective-permute-start(f32[2,256]{1,0:T(2,128)S(1)} %add_add_fusion.1), channel_id=1, source_target_pairs={{0,12},{1,13},{2,14},{3,15},{4,8},{5,9},{6,10},{7,11},{8,4},{9,5},... | collective-permute-start | bytes 6152 | tf_op jit(solution)/shard_map/ppermute | solution.py:245
  60.3 10.9 %collective-permute-start.14 = (bf16[8,18,16,256]{3,2,1,0:T(8,128)(2,1)}, bf16[8,18,16,256]{3,2,1,0:T(8,128)(2,1)S(1)}, u32[]{:S(2)}, u32[]{:S(2)}) collective-permute-start(bf16[8,18,16,256]{3,2,1,0:T(8,128)(2,1)} %get-tuple-element.93), channel_id=1, source_target_pairs={{0,1},{1,0},{2,3},{3,2},{4,5},{5,4},{6,7},{7,6},{8,9},{9,8},{10,11... | collective-permute-start | bytes 3538952 | tf_op jit(solution)/shard_map/ppermute | solution.py:245
  72.2 14.9 %collective-permute-start.16 = (bf16[4,18,16,256]{3,2,1,0:T(8,128)(2,1)S(1)}, bf16[4,18,16,256]{3,2,1,0:T(8,128)(2,1)S(1)}, u32[]{:S(2)}, u32[]{:S(2)}) collective-permute-start(bf16[4,18,16,256]{3,2,1,0:T(8,128)(2,1)S(1)} %slice.117), channel_id=1, source_target_pairs={{0,2},{1,3},{2,0},{3,1},{4,6},{5,7},{6,4},{7,5},{8,10},{9,11},{10,... | collective-permute-start | bytes 1769480 | tf_op jit(solution)/shard_map/ppermute | solution.py:245
  72.8 13.0 %collective-permute-start.17 = (bf16[2,9,16,256]{3,2,1,0:T(8,128)(2,1)S(1)}, bf16[2,9,16,256]{3,2,1,0:T(8,128)(2,1)S(1)}, u32[]{:S(2)}, u32[]{:S(2)}) collective-permute-start(bf16[2,9,16,256]{3,2,1,0:T(8,128)(2,1)S(1)} %get-tuple-element.144), channel_id=1, source_target_pairs={{0,4},{1,5},{2,6},{3,7},{4,0},{5,1},{6,2},{7,3},{8,12},{9,13},{10,... | collective-permute-start | bytes 442376 | tf_op jit(solution)/shard_map/ppermute | solution.py:245
  73.0 12.9 %collective-permute-start.18 = (bf16[2,9,16,256]{3,2,1,0:T(8,128)(2,1)S(1)}, bf16[2,9,16,256]{3,2,1,0:T(8,128)(2,1)S(1)}, u32[]{:S(2)}, u32[]{:S(2)}) collective-permute-start(bf16[2,9,16,256]{3,2,1,0:T(8,128)(2,1)S(1)} %get-tuple-element.143), channel_id=1, source_target_pairs={{0,8},{1,9},{2,10},{3,11},{4,12},{5,13},{6,14},{7,15},{8,0},{9,1},... | collective-permute-start | bytes 442376 | tf_op jit(solution)/shard_map/ppermute | solution.py:245
  76.5 9.9 %collective-permute-start.19 = (bf16[2,9,16,256]{3,2,1,0:T(8,128)(2,1)S(1)}, bf16[2,9,16,256]{3,2,1,0:T(8,128)(2,1)S(1)}, u32[]{:S(2)}, u32[]{:S(2)}) collective-permute-start(bf16[2,9,16,256]{3,2,1,0:T(8,128)(2,1)S(1)} %get-tuple-element.142), channel_id=1, source_target_pairs={{0,12},{1,13},{2,14},{3,15},{4,8},{5,9},{6,10},{7,11},{8,4},{9,5},... | collective-permute-start | bytes 442376 | tf_op jit(solution)/shard_map/ppermute | solution.py:245
  87.4 8.7 %collective-permute-start.20 = (bf16[1,18,16,256]{3,2,1,0:T(8,128)(2,1)S(1)}, bf16[1,18,16,256]{3,2,1,0:T(8,128)(2,1)S(1)}, u32[]{:S(2)}, u32[]{:S(2)}) collective-permute-start(bf16[1,18,16,256]{3,2,1,0:T(8,128)(2,1)S(1)} %get-tuple-element.141), channel_id=1, source_target_pairs={{0,4},{1,5},{2,6},{3,7},{4,0},{5,1},{6,2},{7,3},{8,12},{9,13},{10,... | collective-permute-start | bytes 442376 | tf_op jit(solution)/shard_map/ppermute | solution.py:245
  90.2 5.8 %collective-permute-start.21 = (bf16[1,18,16,256]{3,2,1,0:T(8,128)(2,1)S(1)}, bf16[1,18,16,256]{3,2,1,0:T(8,128)(2,1)S(1)}, u32[]{:S(2)}, u32[]{:S(2)}) collective-permute-start(bf16[1,18,16,256]{3,2,1,0:T(8,128)(2,1)S(1)} %get-tuple-element.140), channel_id=1, source_target_pairs={{0,8},{1,9},{2,10},{3,11},{4,12},{5,13},{6,14},{7,15},{8,0},{9,1},... | collective-permute-start | bytes 442376 | tf_op jit(solution)/shard_map/ppermute | solution.py:245
  91.3 9.7 %collective-permute-start.22 = (bf16[1,18,16,256]{3,2,1,0:T(8,128)(2,1)S(1)}, bf16[1,18,16,256]{3,2,1,0:T(8,128)(2,1)S(1)}, u32[]{:S(2)}, u32[]{:S(2)}) collective-permute-start(bf16[1,18,16,256]{3,2,1,0:T(8,128)(2,1)S(1)} %get-tuple-element.139), channel_id=1, source_target_pairs={{0,12},{1,13},{2,14},{3,15},{4,8},{5,9},{6,10},{7,11},{8,4},{9,5},... | collective-permute-start | bytes 442376 | tf_op jit(solution)/shard_map/ppermute | solution.py:245
  101.1 10.4 %collective-permute-start.26 = (bf16[1,18,16,256]{3,2,1,0:T(8,128)(2,1)S(1)}, bf16[1,18,16,256]{3,2,1,0:T(8,128)(2,1)S(1)}, u32[]{:S(2)}, u32[]{:S(2)}) collective-permute-start(bf16[1,18,16,256]{3,2,1,0:T(8,128)(2,1)S(1)} %add_convert_fusion), channel_id=1, source_target_pairs={{0,4},{1,5},{2,6},{3,7},{4,0},{5,1},{6,2},{7,3},{8,12},{9,13},{10,... | collective-permute-start | bytes 442376 | tf_op jit(solution)/shard_map/ppermute | solution.py:245
  105.1 6.5 %collective-permute-start.27 = (bf16[1,18,16,256]{3,2,1,0:T(8,128)(2,1)S(1)}, bf16[1,18,16,256]{3,2,1,0:T(8,128)(2,1)S(1)}, u32[]{:S(2)}, u32[]{:S(2)}) collective-permute-start(bf16[1,18,16,256]{3,2,1,0:T(8,128)(2,1)S(1)} %add_convert_fusion), channel_id=1, source_target_pairs={{0,8},{1,9},{2,10},{3,11},{4,12},{5,13},{6,14},{7,15},{8,0},{9,1},... | collective-permute-start | bytes 442376 | tf_op jit(solution)/shard_map/ppermute | solution.py:245
  106.9 9.5 %collective-permute-start.28 = (bf16[1,18,16,256]{3,2,1,0:T(8,128)(2,1)S(1)}, bf16[1,18,16,256]{3,2,1,0:T(8,128)(2,1)S(1)}, u32[]{:S(2)}, u32[]{:S(2)}) collective-permute-start(bf16[1,18,16,256]{3,2,1,0:T(8,128)(2,1)S(1)} %add_convert_fusion), channel_id=1, source_target_pairs={{0,12},{1,13},{2,14},{3,15},{4,8},{5,9},{6,10},{7,11},{8,4},{9,5},... | collective-permute-start | bytes 442376 | tf_op jit(solution)/shard_map/ppermute | solution.py:245
  116.4 16.8 %collective-permute-start.30 = (bf16[4,18,16,256]{3,2,1,0:T(8,128)(2,1)S(1)}, bf16[4,18,16,256]{3,2,1,0:T(8,128)(2,1)S(1)}, u32[]{:S(2)}, u32[]{:S(2)}) collective-permute-start(bf16[4,18,16,256]{3,2,1,0:T(8,128)(2,1)S(1)} %constant_dynamic-update-slice_fusion), channel_id=1, source_target_pairs={{0,2},{1,3},{2,0},{3,1},{4,6},{5,7},{6,4},{7,5},{8,10},{9,11},{10,... | collective-permute-start | bytes 1769480 | tf_op jit(solution)/shard_map/ppermute | solution.py:245
  117.6 7.3 %collective-permute-start.31 = (bf16[2,9,16,256]{3,2,1,0:T(8,128)(2,1)S(1)}, bf16[2,9,16,256]{3,2,1,0:T(8,128)(2,1)S(1)}, u32[]{:S(2)}, u32[]{:S(2)}) collective-permute-start(bf16[2,9,16,256]{3,2,1,0:T(8,128)(2,1)S(1)} %constant_dynamic-update-slice_fusion.4), channel_id=1, source_target_pairs={{0,4},{1,5},{2,6},{3,7},{4,0},{5,1},{6,2},{7,3},{8,12},{9,13},{10,... | collective-permute-start | bytes 442376 | tf_op jit(solution)/shard_map/ppermute | solution.py:245
  121.7 5.0 %collective-permute-start.32 = (bf16[2,9,16,256]{3,2,1,0:T(8,128)(2,1)S(1)}, bf16[2,9,16,256]{3,2,1,0:T(8,128)(2,1)S(1)}, u32[]{:S(2)}, u32[]{:S(2)}) collective-permute-start(bf16[2,9,16,256]{3,2,1,0:T(8,128)(2,1)S(1)} %constant_dynamic-update-slice_fusion.4), channel_id=1, source_target_pairs={{0,8},{1,9},{2,10},{3,11},{4,12},{5,13},{6,14},{7,15},{8,0},{9,1},... | collective-permute-start | bytes 442376 | tf_op jit(solution)/shard_map/ppermute | solution.py:245
  123.7 9.5 %collective-permute-start.33 = (bf16[2,9,16,256]{3,2,1,0:T(8,128)(2,1)S(1)}, bf16[2,9,16,256]{3,2,1,0:T(8,128)(2,1)S(1)}, u32[]{:S(2)}, u32[]{:S(2)}) collective-permute-start(bf16[2,9,16,256]{3,2,1,0:T(8,128)(2,1)S(1)} %constant_dynamic-update-slice_fusion.4), channel_id=1, source_target_pairs={{0,12},{1,13},{2,14},{3,15},{4,8},{5,9},{6,10},{7,11},{8,4},{9,5},... | collective-permute-start | bytes 442376 | tf_op jit(solution)/shard_map/ppermute | solution.py:245
  133.3 13.0 %collective-permute-start.34 = (bf16[8,18,16,256]{3,2,1,0:T(8,128)(2,1)S(1)}, bf16[8,18,16,256]{3,2,1,0:T(8,128)(2,1)S(1)}, u32[]{:S(2)}, u32[]{:S(2)}) collective-permute-start(bf16[8,18,16,256]{3,2,1,0:T(8,128)(2,1)S(1)} %constant_dynamic-update-slice_fusion.6.own_one), channel_id=1, source_target_pairs={{0,1},{1,0},{2,3},{3,2},{4,5},{5,4},{6,7},{7,6},{8,9},{9,8},{10,11... | collective-permute-start | bytes 3538952 | tf_op jit(solution)/shard_map/ppermute | solution.py:245
  137.6 5.2 %collective-permute-start.24 = (bf16[128,256]{1,0:T(8,128)(2,1)S(1)}, bf16[128,256]{1,0:T(8,128)(2,1)S(1)}, u32[]{:S(2)}, u32[]{:S(2)}) collective-permute-start(bf16[128,256]{1,0:T(8,128)(2,1)S(1)} %get-tuple-element.113), channel_id=1, source_target_pairs={{0,1},{1,2},{2,3},{3,4},{4,5},{5,6},{6,7},{7,8},{8,9},{9,10},{10,1... | collective-permute-start | bytes 196616 | tf_op jit(solution)/shard_map/ppermute | solution.py:471
  139.9 5.6 %collective-permute-start.25 = (bf16[128,256]{1,0:T(8,128)(2,1)S(1)}, bf16[128,256]{1,0:T(8,128)(2,1)S(1)}, u32[]{:S(2)}, u32[]{:S(2)}) collective-permute-start(bf16[128,256]{1,0:T(8,128)(2,1)S(1)} %get-tuple-element.114), channel_id=1, source_target_pairs={{1,0},{2,1},{3,2},{4,3},{5,4},{6,5},{7,6},{8,7},{9,8},{10,9},{11,1... | collective-permute-start | bytes 196616 | tf_op jit(solution)/shard_map/ppermute | solution.py:470
  142.1 4.2 %collective-permute-start.35 = (bf16[8,9,16,256]{3,2,1,0:T(8,128)(2,1)S(1)}, bf16[8,9,16,256]{3,2,1,0:T(8,128)(2,1)S(1)}, u32[]{:S(2)}, u32[]{:S(2)}) collective-permute-start(bf16[8,9,16,256]{3,2,1,0:T(8,128)(2,1)S(1)} %constant_dynamic-update-slice_fusion.8.own_two), channel_id=1, source_target_pairs={{0,1},{1,0},{2,3},{3,2},{4,5},{5,4},{6,7},{7,6},{8,9},{9,8},{10,11... | collective-permute-start | bytes 1769480 | tf_op jit(solution)/shard_map/ppermute | solution.py:245
  (20 other events, 70.1 us)

commit v3 on v2

v3 whole, which is shorter than its diff:
```python
import functools

import jax
import jax.numpy as jnp
from jax import lax
from jax.experimental import pallas as pl
from jax.experimental.pallas import tpu as pltpu
from jax.sharding import PartitionSpec as P

K = 27
BLOCK = 128
GROUP = 9
PART = 3
EPSILON = 1e-05
F32 = jnp.float32
BF16 = jnp.bfloat16
LIMIT = 24 * 1024 * 1024


def dot(a, b, contract):
    return lax.dot_general(a, b, ((contract[0], contract[1]), ((), ())), preferred_element_type=F32)


def full(shape):
    return pl.BlockSpec(shape, lambda *_: (0,) * len(shape))


def params(limit):
    return pltpu.CompilerParams(vmem_limit_bytes=limit)


def cost(flops, moved):
    return pl.CostEstimate(flops=int(flops), bytes_accessed=int(moved), transcendentals=0)


def occupied_rows(filled, rows):
    position = lax.broadcasted_iota(jnp.int32, (rows, 1), 0)
    return (position < filled - BLOCK) | (position >= rows - BLOCK)


def convolve(map_ref, tiles, weight_hbm, conv_ref, picked_any, scratch):
    weight, picked, index, weight_sem, picked_sem = scratch
    groups = K // GROUP
    rows = conv_ref.shape[0]

    def fetch(g):
        here = pl.ds(g * GROUP, GROUP)
        return pltpu.make_async_copy(weight_hbm.at[here], weight.at[here], weight_sem.at[g])

    def keep(g):
        here = pl.ds(g * GROUP, GROUP)
        return pltpu.make_async_copy(picked.at[here], picked_any.at[here], picked_sem.at[g])

    for g in range(groups):
        fetch(g).start()
    spare = jnp.zeros((BLOCK - K, rows), jnp.int32)
    index[...] = jnp.transpose(jnp.concatenate([map_ref[...], spare], axis=0))
    conv_ref[...] = jnp.zeros_like(conv_ref)
    slots = lax.broadcasted_iota(jnp.int32, (BLOCK, 3 * BLOCK), 1)

    def group(g, carry):
        local = pltpu.roll(index[...], lax.rem(BLOCK - g * GROUP, BLOCK), 1)
        fetch(g).wait()
        for b, tile in enumerate(tiles):
            here = slice(b * BLOCK, (b + 1) * BLOCK)
            slot = local[here] - (rows - BLOCK + b * BLOCK)
            for j in range(GROUP):
                chosen = jnp.where(slot[:, j : j + 1] == slots, 1.0, 0.0).astype(BF16)
                picked[g * GROUP + j, here, :] = dot(chosen, tile[...], ((1,), (0,))).astype(BF16)
        keep(g).start()
        total = conv_ref[...]
        for j in range(GROUP):
            k = g * GROUP + j
            total = total + dot(picked[k], weight[k], ((1,), (0,)))
        conv_ref[...] = total
        return carry

    lax.fori_loop(0, groups, group, 0)

    def finish():
        for g in range(groups):
            keep(g).wait()

    return finish


def conv_kernel(
    filled_ref, odd_ref, map_ref, own_ref, even_ref, other_ref, weight_hbm,
    conv_ref, stats_ref, picked_any, first, last, *scratch,
):
    rows = own_ref.shape[0]
    odd = odd_ref[0] == 1
    first[0:BLOCK, :] = jnp.where(odd, even_ref[...], other_ref[...])
    first[BLOCK:, :] = own_ref[0 : 2 * BLOCK, :]
    last[0 : 2 * BLOCK, :] = own_ref[rows - 2 * BLOCK :, :]
    last[2 * BLOCK :, :] = jnp.where(odd, other_ref[...], even_ref[...])
    middle = [
        own_ref.at[b * BLOCK : (b + 3) * BLOCK] for b in range(rows // BLOCK - 2)
    ]
    tiles = [first] + middle + [last]
    finish = convolve(map_ref, tiles, weight_hbm, conv_ref, picked_any, scratch)
    filled = filled_ref[0]
    count = filled.astype(F32)
    conv = conv_ref[...]
    occupied = occupied_rows(filled, rows)
    sums = jnp.sum(jnp.where(occupied, conv, 0.0), axis=0, keepdims=True)
    off = jnp.where(occupied, conv - sums / count, 0.0)
    squares = jnp.sum(off * off, axis=0, keepdims=True)
    stats_ref[...] = jnp.concatenate([sums, squares, jnp.full_like(sums, count)], axis=0)
    finish()


def normalised(filled, conv_ref, stats_ref, gain_ref, shift_ref, cotangent_ref):
    conv = conv_ref[...]
    total = stats_ref[2:3, :]
    center = stats_ref[0:1, :] / total
    inverse = lax.rsqrt(stats_ref[1:2, :] / total + EPSILON)
    occupied = occupied_rows(filled, conv.shape[0])
    normed = (conv - center) * inverse
    affine = gain_ref[...] * normed + shift_ref[...]
    upstream = jnp.where(occupied & (affine > 0.0), cotangent_ref[...].astype(F32), 0.0)
    return occupied, normed, affine, upstream, inverse, total


def norm_kernel(
    filled_ref, conv_ref, stats_ref, gain_ref, shift_ref, cotangent_ref, feature_ref,
    out_ref, sums_ref,
):
    occupied, normed, affine, upstream, _, _ = normalised(
        filled_ref[0], conv_ref, stats_ref, gain_ref, shift_ref, cotangent_ref
    )
    out = jnp.maximum(affine, 0.0) + feature_ref[...].astype(F32)
    out_ref[...] = jnp.where(occupied, out, 0.0).astype(BF16)
    sums_ref[...] = jnp.concatenate(
        [jnp.sum(upstream * normed, axis=0, keepdims=True), jnp.sum(upstream, axis=0, keepdims=True)],
        axis=0,
    )


def kernel_gradient(first, place, picked_any, grad, keep_any, send_any, scratch):
    picked, product, keep, send, in_sem, out_sem = scratch
    rows = product.shape[1] // 16
    half = keep.shape[0]

    def fetch(j):
        return pltpu.make_async_copy(picked_any.at[first + j], picked.at[j], in_sem.at[j])

    def store(t):
        here = pl.ds(t * PART, PART)
        return [
            pltpu.make_async_copy(keep.at[:, here], keep_any.at[:, here], out_sem.at[0, t]),
            pltpu.make_async_copy(send.at[:, here], send_any.at[:, here], out_sem.at[1, t]),
        ]

    for j in range(GROUP):
        fetch(j).start()
    grad = grad()
    for j in range(GROUP):
        fetch(j).wait()
        product[j] = dot(picked[j], grad, ((0,), (0,)))
        for piece in range(16):
            start = pl.multiple_of(lax.bitwise_xor(jnp.int32(piece), place) * rows, rows)
            value = product[j, pl.ds(start, rows), :]
            if piece < half:
                keep[piece, j] = value
            else:
                send[piece - half, j] = value.astype(BF16)
        if j % PART == PART - 1:
            for copy in store(j // PART):
                copy.start()
    for t in range(GROUP // PART):
        for copy in store(t):
            copy.wait()


def first_gradient_kernel(
    filled_ref, place_ref, conv_ref, stats_ref, grads_ref, gain_ref, shift_ref, cotangent_ref,
    picked_any, grad_ref, keep_any, send_any, *scratch,
):
    def grad():
        occupied, normed, _, upstream, inverse, total = normalised(
            filled_ref[0], conv_ref, stats_ref, gain_ref, shift_ref, cotangent_ref
        )
        grad_conv = gain_ref[...] * inverse * (
            upstream - grads_ref[1:2, :] / total - normed * grads_ref[0:1, :] / total
        )
        value = jnp.where(occupied, grad_conv, 0.0).astype(BF16)
        grad_ref[...] = value
        return value

    kernel_gradient(0, place_ref[0], picked_any, grad, keep_any, send_any, scratch)


def later_gradient_kernel(
    first, place_ref, grad_ref, picked_any, keep_any, send_any, *scratch
):
    def grad():
        return grad_ref[...]

    kernel_gradient(first, place_ref[0], picked_any, grad, keep_any, send_any, scratch)


def push_kernel(grad_ref, index_ref, weight_ref, before_ref, own_ref, after_ref, sink):
    step = pl.program_id(0)

    @pl.when(step == 0)
    def _():
        sink[...] = jnp.zeros_like(sink)

    blocks = grad_ref.shape[0] // BLOCK
    here = jnp.concatenate([index_ref[step * GROUP + j, :][None] for j in range(GROUP)], axis=0)
    block_of = lax.broadcasted_iota(jnp.int32, here.shape, 1) // BLOCK
    local = here - (3 + block_of) * BLOCK
    slots = lax.broadcasted_iota(jnp.int32, (3 * BLOCK, BLOCK), 0)
    pushed = [
        dot(grad_ref[...], weight_ref[j], ((1,), (1,))).astype(BF16) for j in range(GROUP)
    ]
    for b in range(blocks):
        rows = slice(b * BLOCK, (b + 1) * BLOCK)
        chosen = jnp.concatenate(
            [
                jnp.where(local[j : j + 1, rows] == slots, 1.0, 0.0).astype(BF16)
                for j in range(GROUP)
            ],
            axis=1,
        )
        stacked = jnp.concatenate([pushed[j][rows] for j in range(GROUP)], axis=0)
        window = slice(b * BLOCK, (b + 3) * BLOCK)
        sink[window, :] = sink[window, :] + dot(chosen, stacked, ((1,), (0,)))

    @pl.when(step == pl.num_programs(0) - 1)
    def _():
        before_ref[...] = sink[0:BLOCK, :].astype(BF16)
        own_ref[...] = sink[BLOCK : (blocks + 1) * BLOCK, :]
        after_ref[...] = sink[(blocks + 1) * BLOCK :, :].astype(BF16)


def place_kernel(other, places_ref, one, two, *refs):
    out_ref, sems = refs[-2:]
    half, split, rows = two.shape[:3]
    copies = []
    for piece in range(half):
        for part, source in enumerate((one, two)):
            relative = jnp.int32(piece + half * other)
            place = lax.bitwise_xor(relative, places_ref[part])
            start = pl.multiple_of(place * rows, rows)
            first = split if part == 0 else 0
            copies.append(
                pltpu.make_async_copy(
                    source.at[piece],
                    out_ref.at[pl.ds(first, source.shape[1]), pl.ds(start, rows), :],
                    sems.at[len(copies)],
                )
            )
    for copy in copies:
        copy.start()
    for copy in copies:
        copy.wait()


def swap(value, by):
    peers = lax.axis_size("dp")
    return lax.ppermute(value, "dp", [(i, i ^ by) for i in range(peers)])


STAGES = {"c": (1,), "x": (2,), "z": (4, 8, 12)}


def reduce_start(total, stage):
    partners = STAGES[stage]
    size = total.shape[0] // (len(partners) + 1)
    return [
        swap(total[(i + 1) * size : (i + 2) * size].astype(BF16), by)
        for i, by in enumerate(partners)
    ]


def reduce_end(total, received):
    size = received[0].shape[0]
    return functools.reduce(lambda a, b: a + b.astype(F32), received, total[:size])


def gather_start(piece, stage):
    return [swap(piece, by) for by in STAGES[stage]]


def core_reduced(keep, send):
    return keep + swap(send, 1).astype(F32)


def summed_over_devices(one, two, beside, then):
    pieces = [one, two]
    for stages, work in (("xz", beside), ("zx", then)):
        received = [reduce_start(piece, stage) for piece, stage in zip(pieces, stages)]
        received, pieces, result = lax.optimization_barrier((received, pieces, work()))
        pieces = [reduce_end(piece, got) for piece, got in zip(pieces, received)]
    by = 16
    while by < lax.axis_size("dp"):
        pieces = [piece + swap(piece, by) for piece in pieces]
        by *= 2
    pieces = [piece.astype(BF16) for piece in pieces]
    for stages in ("zx", "xz"):
        received = [gather_start(piece, stage) for piece, stage in zip(pieces, stages)]
        received, pieces = lax.optimization_barrier((received, pieces))
        pieces = [
            jnp.concatenate([piece] + got, axis=0) for piece, got in zip(pieces, received)
        ]
    return pieces, result


def exchanged(value, merge):
    for partners in ((1, 2, 3), (4, 8, 12)):
        received = [swap(value, by) for by in partners]
        received, value = lax.optimization_barrier((received, value))
        value = merge(merge(value, received[0]), merge(received[1], received[2]))
    by = 16
    while by < lax.axis_size("dp"):
        value = merge(value, swap(value, by))
        by *= 2
    return value


def merged_moments(one, two):
    (sum_one, square_one, count_one), (sum_two, square_two, count_two) = one, two
    away = sum_one / count_one - sum_two / count_two
    count = count_one + count_two
    square = (square_one + square_two) + away * away * (count_one * count_two / count)
    return jnp.stack([sum_one + sum_two, square, count])


def per_device(features, kernel_map, occupancy, weights, bn_gain, bn_shift, cotangent):
    rows, channels = features.shape
    peers = lax.axis_size("dp")
    me = lax.axis_index("dp")
    blocks = rows // BLOCK
    inner_rows = rows - 2 * BLOCK
    steps = K // GROUP

    odd = me & 1
    even_pairs = [(i, i ^ 1) for i in range(peers)]
    other_pairs = [(i, ((i + 1) ^ 1) - 1) for i in range(1, peers - 1)]

    def neighbours_swap(to_before, to_after):
        even = lax.ppermute(jnp.where(odd == 1, to_before, to_after), "dp", even_pairs)
        other = lax.ppermute(jnp.where(odd == 1, to_after, to_before), "dp", other_pairs)
        return even, other

    even, other = neighbours_swap(features[:BLOCK], features[rows - BLOCK :])
    map_rows = jnp.transpose(kernel_map)
    odd_flag = odd.reshape(1)

    gain = bn_gain.reshape(1, channels)
    shift = bn_shift.reshape(1, channels)
    smem = pl.BlockSpec(memory_space=pltpu.SMEM)
    vmem = pl.BlockSpec(memory_space=pltpu.VMEM)
    hbm = pl.BlockSpec(memory_space=pltpu.HBM)
    anywhere = pl.BlockSpec(memory_space=pl.ANY)
    groups = K // GROUP
    work = K * rows * channels * 2 * (3 * BLOCK + channels)
    moved = K * channels * channels * 2 * 3

    conv, stats, picked = pl.pallas_call(
        conv_kernel,
        in_specs=[smem, smem, vmem, vmem, vmem, vmem, hbm],
        out_specs=[vmem, vmem, anywhere],
        out_shape=[
            jax.ShapeDtypeStruct((rows, channels), F32),
            jax.ShapeDtypeStruct((3, channels), F32),
            jax.ShapeDtypeStruct((K, rows, channels), BF16),
        ],
        scratch_shapes=[pltpu.VMEM((3 * BLOCK, channels), BF16)] * 2
        + [
            pltpu.VMEM((K, channels, channels), BF16),
            pltpu.VMEM((K, rows, channels), BF16),
            pltpu.VMEM((rows, BLOCK), jnp.int32),
            pltpu.SemaphoreType.DMA((groups,)),
            pltpu.SemaphoreType.DMA((groups,)),
        ],
        compiler_params=params(LIMIT),
        cost_estimate=cost(work, moved),
        name="conv",
    )(occupancy, odd_flag, map_rows, features, even, other, weights)

    stats = exchanged(stats, merged_moments)

    block_out, sums = pl.pallas_call(
        norm_kernel,
        in_specs=[smem] + [vmem] * 6,
        out_shape=[
            jax.ShapeDtypeStruct((rows, channels), BF16),
            jax.ShapeDtypeStruct((2, channels), F32),
        ],
        compiler_params=params(LIMIT),
        cost_estimate=cost(rows * channels * 20, rows * channels * 10),
        name="norm",
    )(occupancy, conv, stats, gain, shift, cotangent, features)

    grads = exchanged(sums, jnp.add)

    core, lane, depth = me & 1, (me >> 1) & 1, (me >> 2) & 3
    place_one = (core * 8 + lane * 4 + depth).reshape(1)
    place_two = (core * 8 + depth * 2 + lane).reshape(1)
    piece_rows = channels // 16
    piece_shape = (8, GROUP, piece_rows, channels)
    piece_types = [
        jax.ShapeDtypeStruct(piece_shape, F32),
        jax.ShapeDtypeStruct(piece_shape, BF16),
    ]
    gradient_scratch = [
        pltpu.VMEM((GROUP, rows, channels), BF16),
        pltpu.VMEM((GROUP, channels, channels), F32),
        pltpu.VMEM(piece_shape, F32),
        pltpu.VMEM(piece_shape, BF16),
        pltpu.SemaphoreType.DMA((GROUP,)),
        pltpu.SemaphoreType.DMA((2, GROUP // PART)),
    ]
    gradient_cost = cost(
        GROUP * rows * channels * channels * 2, GROUP * channels * (channels * 5 + rows * 2)
    )
    grad_conv, *pair_two = pl.pallas_call(
        first_gradient_kernel,
        in_specs=[smem, smem] + [vmem] * 6 + [anywhere],
        out_specs=[vmem, anywhere, anywhere],
        out_shape=[jax.ShapeDtypeStruct((rows, channels), BF16)] + piece_types,
        scratch_shapes=gradient_scratch,
        compiler_params=params(LIMIT),
        cost_estimate=gradient_cost,
        name="weight_gradient_first",
    )(occupancy, place_two, conv, stats, grads, gain, shift, cotangent, picked)
    two = core_reduced(*pair_two)

    def later_gradient(first):
        return pl.pallas_call(
            functools.partial(later_gradient_kernel, first),
            in_specs=[smem, vmem, anywhere],
            out_specs=[anywhere, anywhere],
            out_shape=piece_types,
            scratch_shapes=gradient_scratch,
            compiler_params=params(LIMIT),
            cost_estimate=gradient_cost,
            name="weight_gradient_later",
        )(place_one, grad_conv, picked)

    one = [core_reduced(*later_gradient(first)) for first in (GROUP, 2 * GROUP)]
    one = jnp.concatenate(one, axis=1)

    weight_spec = pl.BlockSpec((GROUP, channels, channels), lambda s: (s, 0, 0))
    one, grad_conv_later = lax.optimization_barrier((one, grad_conv))
    sink_before, sink_own, sink_after = pl.pallas_call(
        push_kernel,
        grid=(groups,),
        in_specs=[full((rows, channels)), full((K, rows)), weight_spec],
        out_specs=[full((BLOCK, channels)), full((rows, channels)), full((BLOCK, channels))],
        out_shape=[
            jax.ShapeDtypeStruct((BLOCK, channels), BF16),
            jax.ShapeDtypeStruct((rows, channels), F32),
            jax.ShapeDtypeStruct((BLOCK, channels), BF16),
        ],
        scratch_shapes=[pltpu.VMEM((rows + 2 * BLOCK, channels), F32)],
        compiler_params=params(LIMIT),
        cost_estimate=cost(work, moved),
        name="push",
    )(grad_conv_later, map_rows, weights)

    def spread_gradient():
        even, other = neighbours_swap(sink_before, sink_after)
        from_prev = jnp.where(odd == 1, even, other).astype(F32)
        from_next = jnp.where(odd == 1, other, even).astype(F32)
        occupied = occupied_rows(occupancy[0], rows)
        received = jnp.concatenate(
            [
                sink_own[:BLOCK] + from_prev,
                sink_own[BLOCK : rows - BLOCK],
                sink_own[rows - BLOCK :] + from_next,
            ],
            axis=0,
        )
        return (jnp.where(occupied, cotangent.astype(F32), 0.0) + received).astype(BF16)

    (own_one, own_two), grad_features = summed_over_devices(
        one, two, lambda: (sink_before, sink_own, sink_after), spread_gradient
    )
    places = jnp.concatenate([place_one, place_two])

    def placed(other, sources, *into):
        return pl.pallas_call(
            functools.partial(place_kernel, other),
            in_specs=[smem, anywhere, anywhere] + [hbm] * len(into),
            out_specs=hbm,
            out_shape=jax.ShapeDtypeStruct(weights.shape, BF16),
            scratch_shapes=[pltpu.SemaphoreType.DMA((16,))],
            input_output_aliases={3: 0} if into else {},
            compiler_params=params(LIMIT),
            cost_estimate=cost(0, K * channels * channels * 2),
            name="place",
        )(places, *sources, *into)

    others = [swap(own_one, 1), swap(own_two, 1)]
    grad_weights = placed(1, others, placed(0, (own_one, own_two)))
    return block_out, grad_features, grad_weights, grads[0], grads[1]


def solution(mesh):
    in_specs = (
        P(("parts", "dp"), None),
        P(("parts", "dp"), None),
        P(("parts", "dp")),
        P(),
        P(),
        P(),
        P(("parts", "dp"), None),
    )
    out_specs = (
        P(("parts", "dp"), None),
        P(("parts", "dp"), None),
        P("parts", None, None),
        P("parts"),
        P("parts"),
    )
    return jax.shard_map(
        per_device, mesh=mesh, in_specs=in_specs, out_specs=out_specs, check_vma=False
    )
```

time: 151 us -> 153 us (1.013)
  local copies, waits for them, and re-layouts: 4.99 us -> 11.1 us
  waiting for transfers between devices: 39.4 us -> 45.2 us
  Pallas kernels: 37.9 us -> 33.2 us
  other arithmetic: 6.84 us -> 3.2 us
    unnamed x24 -> x30, local copies, waits for them, and re-layouts: 1.18 us -> 10.2 us
    ppermute x32 -> x33, waiting for transfers between devices: 36.8 us -> 43.9 us  [swap(): return lax.ppermute(value, 'dp', [(i, i ^ by) for i in range(peers)])]
    pallas_call x7 -> x8, Pallas kernels: 37.9 us -> 33.2 us  [the longest x1 9.29 us: per_device(): pl.pallas_call(push_kernel, grid=(groups,), in_specs=[full((rows, channel...]
    slice x4 -> x1, local copies, waits for them, and re-layouts: 3.02 us -> 0.02 us  [spread_gradient(): sink_own[BLOCK:rows - BLOCK]]
    ppermute x4, starting transfers between devices: 10.9 us -> 8.04 us  [the longest x2 7.72 us: neighbours_swap(): lax.ppermute(jnp.where(odd == 1, to_after, to_before), 'dp', other_pairs)]
    ppermute x32 -> x33, starting transfers between devices: 47.2 us -> 49.5 us  [swap(): return lax.ppermute(value, 'dp', [(i, i ^ by) for i in range(peers)])]
    add x3, other arithmetic: 2.06 us -> 0.4 us  [the longest x2 0.38 us: core_reduced(): return keep + swap(send, 1).astype(F32)]
  transfers between devices with their start and end apart: 36 -> 37, of which waited for: 17 -> 18; matrix products, arithmetic and copies ran while one was open for 4% -> 2% of each run, Pallas kernels for 14% -> 10%
where the time goes in v3:
time: 153 us; the launch traced here: 152 us
  starting transfers between devices  57.6 us (38%)
  waiting for transfers between devices  45.2 us (30%)
  Pallas kernels  33.2 us (22%)
  local copies, waits for them, and re-layouts  11.1 us (7%)
  other arithmetic  3.2 us (2%)
  between operations  1.82 us (1%)
    ppermute x33, starting transfers between devices, swap(): return lax.ppermute(value, 'dp', [(i, i ^ by) for i in range(peers)])  49.5 us
    ppermute x33, waiting for transfers between devices, swap(): return lax.ppermute(value, 'dp', [(i, i ^ by) for i in range(peers)])  43.9 us
    unnamed x30, local copies, waits for them, and re-layouts  10.2 us
    pallas_call x1, Pallas kernels, per_device(): pl.pallas_call(push_kernel, grid=(groups,), in_specs=[full((rows, channel...  9.29 us
    pallas_call x1, Pallas kernels, per_device(): pl.pallas_call(conv_kernel, in_specs=[smem, smem, vmem, vmem, vmem, vmem,...  8.75 us
    ppermute x2, starting transfers between devices, neighbours_swap(): lax.ppermute(jnp.where(odd == 1, to_after, to_before), 'dp', other_pairs)  7.72 us
    pallas_call x2, Pallas kernels, later_gradient(): pl.pallas_call(functools.partial(later_gradient_kernel, first), in_specs=...  6.77 us
    pallas_call x2, Pallas kernels, placed(): pl.pallas_call(functools.partial(place_kernel, other), in_specs=[smem, an...  3.75 us
  transfers between devices with their start and end apart: 37, of which 18 were waited for; matrix products, arithmetic and copies ran while one was open for 2% of the time, Pallas kernels for 10%

profile of v3, /device:TPU:1, one launch (start us, length us, event | category | flops | bytes accessed | tf_op | source)
XLA Modules:
  0.0 152.0 jit_solution(10691932996360454044)
XLA Ops:
  1.6 4.5 %collective-permute-start.1 = (bf16[128,256]{1,0:T(8,128)(2,1)S(1)}, bf16[128,256]{1,0:T(8,128)(2,1)S(1)}, u32[]{:S(2)}, u32[]{:S(2)}) collective-permute-start(bf16[128,256]{1,0:T(8,128)(2,1)S(1)} %get-tuple-element.137), channel_id=1, source_target_pairs={{1,2},{2,1},{3,4},{4,3},{5,6},{6,5},{7,8},{8,7},{9,10},{10,9},{11,... | collective-permute-start | bytes 196616 | tf_op jit(solution)/shard_map/ppermute | solution.py:345
  11.9 8.7 %conv.1 = (f32[512,256]{1,0:T(8,128)S(1)}, f32[3,256]{1,0:T(4,128)S(1)}, bf16[27,512,256]{2,1,0:T(8,128)(2,1)S(1)}) custom-call(s32[1]{0:T(128)S(6)} %copy.22.filled_ref, s32[1]{0:T(128)} %bitcast.odd_ref, s32[27,512]{1,0:T(8,128)S(1)} %bitcast.13, bf16[512,256]{1,0:T(8,128)(2,1)S(1)} %copy-done.4, bf16[128,256]{1,0:T(8,128)(2,1)S(1)} %collective-permute-done.even_ref, ...), custom_call_target="tpu_custom_call" | custom-call | flops 4529848320 | bytes 10616832 | tf_op jit(solution)/shard_map/conv/pallas_call | solution.py:362
  20.6 2.8 %copy-done = bf16[27,512,256]{2,1,0:T(8,128)(2,1)} copy-done((bf16[27,512,256]{2,1,0:T(8,128)(2,1)}, bf16[27,512,256]{2,1,0:T(8,128)(2,1)S(1)}, u32[]{:S(2)}) %copy-start) | copy-done | bytes 7077912
  23.4 2.7 %collective-permute-start.3 = (f32[3,256]{1,0:T(4,128)S(1)}, f32[3,256]{1,0:T(4,128)S(1)}, u32[]{:S(2)}, u32[]{:S(2)}) collective-permute-start(f32[3,256]{1,0:T(4,128)S(1)} %get-tuple-element.65), channel_id=1, source_target_pairs={{0,2},{1,3},{2,0},{3,1},{4,6},{5,7},{6,4},{7,5},{8,10},{9,11},{10,... | collective-permute-start | bytes 9224 | tf_op jit(solution)/shard_map/ppermute | solution.py:263
  34.0 2.5 %collective-permute-done.7 = f32[3,256]{1,0:T(4,128)S(1)} collective-permute-done((f32[3,256]{1,0:T(4,128)S(1)}, f32[3,256]{1,0:T(4,128)S(1)}, u32[]{:S(2)}, u32[]{:S(2)}) %collective-permute-start.7) | collective-permute-done | bytes 3104 | tf_op jit(solution)/shard_map/ppermute | solution.py:263
  37.5 2.1 %collective-permute-start.8 = (f32[2,256]{1,0:T(2,128)S(1)}, f32[2,256]{1,0:T(2,128)S(1)}, u32[]{:S(2)}, u32[]{:S(2)}) collective-permute-start(f32[2,256]{1,0:T(2,128)S(1)} %get-tuple-element.75), channel_id=1, source_target_pairs={{0,1},{1,0},{2,3},{3,2},{4,5},{5,4},{6,7},{7,6},{8,9},{9,8},{10,11... | collective-permute-start | bytes 6152 | tf_op jit(solution)/shard_map/ppermute | solution.py:263
  44.3 3.1 %collective-permute-start.13 = (f32[2,256]{1,0:T(2,128)S(1)}, f32[2,256]{1,0:T(2,128)S(1)}, u32[]{:S(2)}, u32[]{:S(2)}) collective-permute-start(f32[2,256]{1,0:T(2,128)S(1)} %add_add_fusion.1), channel_id=1, source_target_pairs={{0,12},{1,13},{2,14},{3,15},{4,8},{5,9},{6,10},{7,11},{8,4},{9,5},... | collective-permute-start | bytes 6152 | tf_op jit(solution)/shard_map/ppermute | solution.py:263
  48.5 3.0 %copy-done.1 = bf16[27,512,256]{2,1,0:T(8,128)(2,1)S(1)} copy-done((bf16[27,512,256]{2,1,0:T(8,128)(2,1)S(1)}, bf16[27,512,256]{2,1,0:T(8,128)(2,1)}, u32[]{:S(2)}) %copy-start.1) | copy-done | bytes 7077912
  51.5 3.7 %weight_gradient_first.1 = (bf16[512,256]{1,0:T(8,128)(2,1)S(1)}, f32[8,9,16,256]{3,2,1,0:T(8,128)S(1)}, bf16[8,9,16,256]{3,2,1,0:T(8,128)(2,1)S(1)}) custom-call(s32[1]{0:T(128)S(6)} %copy.22.filled_ref, s32[1]{0:T(128)} %bitcast.5.place_ref, f32[512,256]{1,0:T(8,128)S(1)} %get-tuple-element.63.conv_ref, f32[3,256]{1,0:T(4,128)S(1)} %pad_maximum_fusion.2.stats_ref, ...), custom_call_target="tpu_custom_call" | custom-call | flops 603979776 | bytes 5308416 | tf_op jit(solution)/shard_map/weight_gradient_first/pallas_call | solution.py:420
  55.2 3.4 %weight_gradient_later.3 = (f32[8,9,16,256]{3,2,1,0:T(8,128)S(1)}, bf16[8,9,16,256]{3,2,1,0:T(8,128)(2,1)S(1)}) custom-call(s32[1]{0:T(128)} %bitcast.4.place_ref, bf16[512,256]{1,0:T(8,128)(2,1)S(1)} %get-tuple-element.92.grad_ref, bf16[27,512,256]{2,1,0:T(8,128)(2,1)S(1)} %copy-done.2), custom_call_target="tpu_custom_call" | custom-call | flops 603979776 | bytes 5308416 | tf_op jit(solution)/shard_map/weight_gradient_later/pallas_call | solution.py:433
  58.6 2.1 %collective-permute-start.15 = (bf16[8,9,16,256]{3,2,1,0:T(8,128)(2,1)S(1)}, bf16[8,9,16,256]{3,2,1,0:T(8,128)(2,1)S(1)}, u32[]{:S(2)}, u32[]{:S(2)}) collective-permute-start(bf16[8,9,16,256]{3,2,1,0:T(8,128)(2,1)S(1)} %get-tuple-element.88), channel_id=1, source_target_pairs={{0,1},{1,0},{2,3},{3,2},{4,5},{5,4},{6,7},{7,6},{8,9},{9,8},{10,11... | collective-permute-start | bytes 1769480 | tf_op jit(solution)/shard_map/ppermute | solution.py:263
  60.7 3.4 %weight_gradient_later.2 = (f32[8,9,16,256]{3,2,1,0:T(8,128)S(1)}, bf16[8,9,16,256]{3,2,1,0:T(8,128)(2,1)S(1)}) custom-call(s32[1]{0:T(128)} %bitcast.4.place_ref, bf16[512,256]{1,0:T(8,128)(2,1)S(1)} %get-tuple-element.92.grad_ref, bf16[27,512,256]{2,1,0:T(8,128)(2,1)S(1)} %copy-done.2), custom_call_target="tpu_custom_call" | custom-call | flops 603979776 | bytes 5308416 | tf_op jit(solution)/shard_map/weight_gradient_later/pallas_call | solution.py:433
  68.4 9.3 %push.1 = (bf16[128,256]{1,0:T(8,128)(2,1)S(1)}, f32[512,256]{1,0:T(8,128)S(1)}, bf16[128,256]{1,0:T(8,128)(2,1)S(1)}) custom-call(bf16[512,256]{1,0:T(8,128)(2,1)S(1)} %get-tuple-element.92.grad_ref, s32[27,512]{1,0:T(8,128)S(1)} %bitcast.14, bf16[27,256,256]{2,1,0:T(8,128)(2,1)S(1)} %copy-done.8), custom_call_target="tpu_custom_call" | custom-call | flops 4529848320 | bytes 10616832 | tf_op jit(solution)/shard_map/push/pallas_call | solution.py:449
  77.9 3.3 %collective-permute-start.26 = (bf16[128,256]{1,0:T(8,128)(2,1)S(1)}, bf16[128,256]{1,0:T(8,128)(2,1)S(1)}, u32[]{:S(2)}, u32[]{:S(2)}) collective-permute-start(bf16[128,256]{1,0:T(8,128)(2,1)S(1)} %get-tuple-element.140), channel_id=1, source_target_pairs={{1,2},{2,1},{3,4},{4,3},{5,6},{6,5},{7,8},{8,7},{9,10},{10,9},{11,... | collective-permute-start | bytes 196616 | tf_op jit(solution)/shard_map/ppermute | solution.py:345
  81.6 2.6 %collective-permute-start.19 = (bf16[2,9,16,256]{3,2,1,0:T(8,128)(2,1)S(1)}, bf16[2,9,16,256]{3,2,1,0:T(8,128)(2,1)S(1)}, u32[]{:S(2)}, u32[]{:S(2)}) collective-permute-start(bf16[2,9,16,256]{3,2,1,0:T(8,128)(2,1)S(1)} %get-tuple-element.135), channel_id=1, source_target_pairs={{0,8},{1,9},{2,10},{3,11},{4,12},{5,13},{6,14},{7,15},{8,0},{9,1},... | collective-permute-start | bytes 442376 | tf_op jit(solution)/shard_map/ppermute | solution.py:263
  85.2 4.3 %collective-permute-done.18 = bf16[2,9,16,256]{3,2,1,0:T(8,128)(2,1)S(1)} collective-permute-done((bf16[2,9,16,256]{3,2,1,0:T(8,128)(2,1)S(1)}, bf16[2,9,16,256]{3,2,1,0:T(8,128)(2,1)S(1)}, u32[]{:S(2)}, u32[]{:S(2)}) %collective-permute-start.18) | collective-permute-done | bytes 147488 | tf_op jit(solution)/shard_map/ppermute | solution.py:263
  89.6 5.0 %collective-permute-done.20 = bf16[2,9,16,256]{3,2,1,0:T(8,128)(2,1)S(1)} collective-permute-done((bf16[2,9,16,256]{3,2,1,0:T(8,128)(2,1)S(1)}, bf16[2,9,16,256]{3,2,1,0:T(8,128)(2,1)S(1)}, u32[]{:S(2)}, u32[]{:S(2)}) %collective-permute-start.20) | collective-permute-done | bytes 147488 | tf_op jit(solution)/shard_map/ppermute | solution.py:263
  94.9 2.8 %collective-permute-start.21 = (bf16[1,18,16,256]{3,2,1,0:T(8,128)(2,1)S(1)}, bf16[1,18,16,256]{3,2,1,0:T(8,128)(2,1)S(1)}, u32[]{:S(2)}, u32[]{:S(2)}) collective-permute-start(bf16[1,18,16,256]{3,2,1,0:T(8,128)(2,1)S(1)} %get-tuple-element.133), channel_id=1, source_target_pairs={{0,4},{1,5},{2,6},{3,7},{4,0},{5,1},{6,2},{7,3},{8,12},{9,13},{10,... | collective-permute-start | bytes 442376 | tf_op jit(solution)/shard_map/ppermute | solution.py:263
  104.4 6.1 %collective-permute-done.23 = bf16[1,18,16,256]{3,2,1,0:T(8,128)(2,1)S(1)} collective-permute-done((bf16[1,18,16,256]{3,2,1,0:T(8,128)(2,1)S(1)}, bf16[1,18,16,256]{3,2,1,0:T(8,128)(2,1)S(1)}, u32[]{:S(2)}, u32[]{:S(2)}) %collective-permute-start.23) | collective-permute-done | bytes 147488 | tf_op jit(solution)/shard_map/ppermute | solution.py:263
  110.6 3.0 %collective-permute-start.27 = (bf16[1,18,16,256]{3,2,1,0:T(8,128)(2,1)S(1)}, bf16[1,18,16,256]{3,2,1,0:T(8,128)(2,1)S(1)}, u32[]{:S(2)}, u32[]{:S(2)}) collective-permute-start(bf16[1,18,16,256]{3,2,1,0:T(8,128)(2,1)S(1)} %add_convert_fusion), channel_id=1, source_target_pairs={{0,4},{1,5},{2,6},{3,7},{4,0},{5,1},{6,2},{7,3},{8,12},{9,13},{10,... | collective-permute-start | bytes 442376 | tf_op jit(solution)/shard_map/ppermute | solution.py:263
  120.3 5.1 %collective-permute-done.29 = bf16[1,18,16,256]{3,2,1,0:T(8,128)(2,1)S(1)} collective-permute-done((bf16[1,18,16,256]{3,2,1,0:T(8,128)(2,1)S(1)}, bf16[1,18,16,256]{3,2,1,0:T(8,128)(2,1)S(1)}, u32[]{:S(2)}, u32[]{:S(2)}) %collective-permute-start.29) | collective-permute-done | bytes 147488 | tf_op jit(solution)/shard_map/ppermute | solution.py:263
  127.2 3.7 %collective-permute-start.32 = (bf16[2,9,16,256]{3,2,1,0:T(8,128)(2,1)S(1)}, bf16[2,9,16,256]{3,2,1,0:T(8,128)(2,1)S(1)}, u32[]{:S(2)}, u32[]{:S(2)}) collective-permute-start(bf16[2,9,16,256]{3,2,1,0:T(8,128)(2,1)S(1)} %constant_dynamic-update-slice_fusion.4), channel_id=1, source_target_pairs={{0,4},{1,5},{2,6},{3,7},{4,0},{5,1},{6,2},{7,3},{8,12},{9,13},{10,... | collective-permute-start | bytes 442376 | tf_op jit(solution)/shard_map/ppermute | solution.py:263
  135.9 6.2 %collective-permute-done.34 = bf16[2,9,16,256]{3,2,1,0:T(8,128)(2,1)S(1)} collective-permute-done((bf16[2,9,16,256]{3,2,1,0:T(8,128)(2,1)S(1)}, bf16[2,9,16,256]{3,2,1,0:T(8,128)(2,1)S(1)}, u32[]{:S(2)}, u32[]{:S(2)}) %collective-permute-start.34) | collective-permute-done | bytes 147488 | tf_op jit(solution)/shard_map/ppermute | solution.py:263
  142.2 4.4 %collective-permute-start.35 = (bf16[8,18,16,256]{3,2,1,0:T(8,128)(2,1)S(1)}, bf16[8,18,16,256]{3,2,1,0:T(8,128)(2,1)S(1)}, u32[]{:S(2)}, u32[]{:S(2)}) collective-permute-start(bf16[8,18,16,256]{3,2,1,0:T(8,128)(2,1)S(1)} %constant_dynamic-update-slice_fusion.6.one), channel_id=1, source_target_pairs={{0,1},{1,0},{2,3},{3,2},{4,5},{5,4},{6,7},{7,6},{8,9},{9,8},{10,11... | collective-permute-start | bytes 3538952 | tf_op jit(solution)/shard_map/ppermute | solution.py:263
  (118 shorter events, 52.5 us)
Async XLA Ops:
  1.5 5.2 %collective-permute-start = (bf16[128,256]{1,0:T(8,128)(2,1)S(1)}, bf16[128,256]{1,0:T(8,128)(2,1)S(1)}, u32[]{:S(2)}, u32[]{:S(2)}) collective-permute-start(bf16[128,256]{1,0:T(8,128)(2,1)S(1)} %get-tuple-element.138), channel_id=1, source_target_pairs={{0,1},{1,0},{2,3},{3,2},{4,5},{5,4},{6,7},{7,6},{8,9},{9,8},{10,11... | collective-permute-start | bytes 196616 | tf_op jit(solution)/shard_map/ppermute | solution.py:344
  1.6 6.4 %collective-permute-start.1 = (bf16[128,256]{1,0:T(8,128)(2,1)S(1)}, bf16[128,256]{1,0:T(8,128)(2,1)S(1)}, u32[]{:S(2)}, u32[]{:S(2)}) collective-permute-start(bf16[128,256]{1,0:T(8,128)(2,1)S(1)} %get-tuple-element.137), channel_id=1, source_target_pairs={{1,2},{2,1},{3,4},{4,3},{5,6},{6,5},{7,8},{8,7},{9,10},{10,9},{11,... | collective-permute-start | bytes 196616 | tf_op jit(solution)/shard_map/ppermute | solution.py:345
  32.2 4.3 %collective-permute-start.7 = (f32[3,256]{1,0:T(4,128)S(1)}, f32[3,256]{1,0:T(4,128)S(1)}, u32[]{:S(2)}, u32[]{:S(2)}) collective-permute-start(f32[3,256]{1,0:T(4,128)S(1)} %pad_maximum_fusion.1), channel_id=1, source_target_pairs={{0,12},{1,13},{2,14},{3,15},{4,8},{5,9},{6,10},{7,11},{8,4},{9,5},... | collective-permute-start | bytes 9224 | tf_op jit(solution)/shard_map/ppermute | solution.py:263
  37.5 3.7 %collective-permute-start.8 = (f32[2,256]{1,0:T(2,128)S(1)}, f32[2,256]{1,0:T(2,128)S(1)}, u32[]{:S(2)}, u32[]{:S(2)}) collective-permute-start(f32[2,256]{1,0:T(2,128)S(1)} %get-tuple-element.75), channel_id=1, source_target_pairs={{0,1},{1,0},{2,3},{3,2},{4,5},{5,4},{6,7},{7,6},{8,9},{9,8},{10,11... | collective-permute-start | bytes 6152 | tf_op jit(solution)/shard_map/ppermute | solution.py:263
  44.3 4.2 %collective-permute-start.13 = (f32[2,256]{1,0:T(2,128)S(1)}, f32[2,256]{1,0:T(2,128)S(1)}, u32[]{:S(2)}, u32[]{:S(2)}) collective-permute-start(f32[2,256]{1,0:T(2,128)S(1)} %add_add_fusion.1), channel_id=1, source_target_pairs={{0,12},{1,13},{2,14},{3,15},{4,8},{5,9},{6,10},{7,11},{8,4},{9,5},... | collective-permute-start | bytes 6152 | tf_op jit(solution)/shard_map/ppermute | solution.py:263
  58.6 6.1 %collective-permute-start.15 = (bf16[8,9,16,256]{3,2,1,0:T(8,128)(2,1)S(1)}, bf16[8,9,16,256]{3,2,1,0:T(8,128)(2,1)S(1)}, u32[]{:S(2)}, u32[]{:S(2)}) collective-permute-start(bf16[8,9,16,256]{3,2,1,0:T(8,128)(2,1)S(1)} %get-tuple-element.88), channel_id=1, source_target_pairs={{0,1},{1,0},{2,3},{3,2},{4,5},{5,4},{6,7},{7,6},{8,9},{9,8},{10,11... | collective-permute-start | bytes 1769480 | tf_op jit(solution)/shard_map/ppermute | solution.py:263
  64.2 17.0 %collective-permute-start.17 = (bf16[8,9,16,256]{3,2,1,0:T(8,128)(2,1)S(1)}, bf16[8,9,16,256]{3,2,1,0:T(8,128)(2,1)S(1)}, u32[]{:S(2)}, u32[]{:S(2)}) collective-permute-start(bf16[8,9,16,256]{3,2,1,0:T(8,128)(2,1)S(1)} %get-tuple-element.91), channel_id=1, source_target_pairs={{0,1},{1,0},{2,3},{3,2},{4,5},{5,4},{6,7},{7,6},{8,9},{9,8},{10,11... | collective-permute-start | bytes 1769480 | tf_op jit(solution)/shard_map/ppermute | solution.py:263
  66.7 27.9 %collective-permute-start.16 = (bf16[4,18,16,256]{3,2,1,0:T(8,128)(2,1)S(1)}, bf16[4,18,16,256]{3,2,1,0:T(8,128)(2,1)S(1)}, u32[]{:S(2)}, u32[]{:S(2)}) collective-permute-start(bf16[4,18,16,256]{3,2,1,0:T(8,128)(2,1)S(1)} %slice.106), channel_id=1, source_target_pairs={{0,2},{1,3},{2,0},{3,1},{4,6},{5,7},{6,4},{7,5},{8,10},{9,11},{10,... | collective-permute-start | bytes 1769480 | tf_op jit(solution)/shard_map/ppermute | solution.py:263
  77.7 6.5 %collective-permute-start.25 = (bf16[128,256]{1,0:T(8,128)(2,1)S(1)}, bf16[128,256]{1,0:T(8,128)(2,1)S(1)}, u32[]{:S(2)}, u32[]{:S(2)}) collective-permute-start(bf16[128,256]{1,0:T(8,128)(2,1)S(1)} %get-tuple-element.139), channel_id=1, source_target_pairs={{0,1},{1,0},{2,3},{3,2},{4,5},{5,4},{6,7},{7,6},{8,9},{9,8},{10,11... | collective-permute-start | bytes 196616 | tf_op jit(solution)/shard_map/ppermute | solution.py:344
  77.9 7.3 %collective-permute-start.26 = (bf16[128,256]{1,0:T(8,128)(2,1)S(1)}, bf16[128,256]{1,0:T(8,128)(2,1)S(1)}, u32[]{:S(2)}, u32[]{:S(2)}) collective-permute-start(bf16[128,256]{1,0:T(8,128)(2,1)S(1)} %get-tuple-element.140), channel_id=1, source_target_pairs={{1,2},{2,1},{3,4},{4,3},{5,6},{6,5},{7,8},{8,7},{9,10},{10,9},{11,... | collective-permute-start | bytes 196616 | tf_op jit(solution)/shard_map/ppermute | solution.py:345
  81.5 8.1 %collective-permute-start.18 = (bf16[2,9,16,256]{3,2,1,0:T(8,128)(2,1)S(1)}, bf16[2,9,16,256]{3,2,1,0:T(8,128)(2,1)S(1)}, u32[]{:S(2)}, u32[]{:S(2)}) collective-permute-start(bf16[2,9,16,256]{3,2,1,0:T(8,128)(2,1)S(1)} %get-tuple-element.136), channel_id=1, source_target_pairs={{0,4},{1,5},{2,6},{3,7},{4,0},{5,1},{6,2},{7,3},{8,12},{9,13},{10,... | collective-permute-start | bytes 442376 | tf_op jit(solution)/shard_map/ppermute | solution.py:263
  81.6 8.0 %collective-permute-start.19 = (bf16[2,9,16,256]{3,2,1,0:T(8,128)(2,1)S(1)}, bf16[2,9,16,256]{3,2,1,0:T(8,128)(2,1)S(1)}, u32[]{:S(2)}, u32[]{:S(2)}) collective-permute-start(bf16[2,9,16,256]{3,2,1,0:T(8,128)(2,1)S(1)} %get-tuple-element.135), channel_id=1, source_target_pairs={{0,8},{1,9},{2,10},{3,11},{4,12},{5,13},{6,14},{7,15},{8,0},{9,1},... | collective-permute-start | bytes 442376 | tf_op jit(solution)/shard_map/ppermute | solution.py:263
  84.2 10.4 %collective-permute-start.20 = (bf16[2,9,16,256]{3,2,1,0:T(8,128)(2,1)S(1)}, bf16[2,9,16,256]{3,2,1,0:T(8,128)(2,1)S(1)}, u32[]{:S(2)}, u32[]{:S(2)}) collective-permute-start(bf16[2,9,16,256]{3,2,1,0:T(8,128)(2,1)S(1)} %get-tuple-element.134), channel_id=1, source_target_pairs={{0,12},{1,13},{2,14},{3,15},{4,8},{5,9},{6,10},{7,11},{8,4},{9,5},... | collective-permute-start | bytes 442376 | tf_op jit(solution)/shard_map/ppermute | solution.py:263
  94.9 9.5 %collective-permute-start.21 = (bf16[1,18,16,256]{3,2,1,0:T(8,128)(2,1)S(1)}, bf16[1,18,16,256]{3,2,1,0:T(8,128)(2,1)S(1)}, u32[]{:S(2)}, u32[]{:S(2)}) collective-permute-start(bf16[1,18,16,256]{3,2,1,0:T(8,128)(2,1)S(1)} %get-tuple-element.133), channel_id=1, source_target_pairs={{0,4},{1,5},{2,6},{3,7},{4,0},{5,1},{6,2},{7,3},{8,12},{9,13},{10,... | collective-permute-start | bytes 442376 | tf_op jit(solution)/shard_map/ppermute | solution.py:263
  97.6 6.8 %collective-permute-start.22 = (bf16[1,18,16,256]{3,2,1,0:T(8,128)(2,1)S(1)}, bf16[1,18,16,256]{3,2,1,0:T(8,128)(2,1)S(1)}, u32[]{:S(2)}, u32[]{:S(2)}) collective-permute-start(bf16[1,18,16,256]{3,2,1,0:T(8,128)(2,1)S(1)} %get-tuple-element.132), channel_id=1, source_target_pairs={{0,8},{1,9},{2,10},{3,11},{4,12},{5,13},{6,14},{7,15},{8,0},{9,1},... | collective-permute-start | bytes 442376 | tf_op jit(solution)/shard_map/ppermute | solution.py:263
  99.6 10.9 %collective-permute-start.23 = (bf16[1,18,16,256]{3,2,1,0:T(8,128)(2,1)S(1)}, bf16[1,18,16,256]{3,2,1,0:T(8,128)(2,1)S(1)}, u32[]{:S(2)}, u32[]{:S(2)}) collective-permute-start(bf16[1,18,16,256]{3,2,1,0:T(8,128)(2,1)S(1)} %get-tuple-element.131), channel_id=1, source_target_pairs={{0,12},{1,13},{2,14},{3,15},{4,8},{5,9},{6,10},{7,11},{8,4},{9,5},... | collective-permute-start | bytes 442376 | tf_op jit(solution)/shard_map/ppermute | solution.py:263
  110.6 9.8 %collective-permute-start.27 = (bf16[1,18,16,256]{3,2,1,0:T(8,128)(2,1)S(1)}, bf16[1,18,16,256]{3,2,1,0:T(8,128)(2,1)S(1)}, u32[]{:S(2)}, u32[]{:S(2)}) collective-permute-start(bf16[1,18,16,256]{3,2,1,0:T(8,128)(2,1)S(1)} %add_convert_fusion), channel_id=1, source_target_pairs={{0,4},{1,5},{2,6},{3,7},{4,0},{5,1},{6,2},{7,3},{8,12},{9,13},{10,... | collective-permute-start | bytes 442376 | tf_op jit(solution)/shard_map/ppermute | solution.py:263
  113.5 6.8 %collective-permute-start.28 = (bf16[1,18,16,256]{3,2,1,0:T(8,128)(2,1)S(1)}, bf16[1,18,16,256]{3,2,1,0:T(8,128)(2,1)S(1)}, u32[]{:S(2)}, u32[]{:S(2)}) collective-permute-start(bf16[1,18,16,256]{3,2,1,0:T(8,128)(2,1)S(1)} %add_convert_fusion), channel_id=1, source_target_pairs={{0,8},{1,9},{2,10},{3,11},{4,12},{5,13},{6,14},{7,15},{8,0},{9,1},... | collective-permute-start | bytes 442376 | tf_op jit(solution)/shard_map/ppermute | solution.py:263
  115.5 9.9 %collective-permute-start.29 = (bf16[1,18,16,256]{3,2,1,0:T(8,128)(2,1)S(1)}, bf16[1,18,16,256]{3,2,1,0:T(8,128)(2,1)S(1)}, u32[]{:S(2)}, u32[]{:S(2)}) collective-permute-start(bf16[1,18,16,256]{3,2,1,0:T(8,128)(2,1)S(1)} %add_convert_fusion), channel_id=1, source_target_pairs={{0,12},{1,13},{2,14},{3,15},{4,8},{5,9},{6,10},{7,11},{8,4},{9,5},... | collective-permute-start | bytes 442376 | tf_op jit(solution)/shard_map/ppermute | solution.py:263
  125.5 16.6 %collective-permute-start.31 = (bf16[4,18,16,256]{3,2,1,0:T(8,128)(2,1)S(1)}, bf16[4,18,16,256]{3,2,1,0:T(8,128)(2,1)S(1)}, u32[]{:S(2)}, u32[]{:S(2)}) collective-permute-start(bf16[4,18,16,256]{3,2,1,0:T(8,128)(2,1)S(1)} %constant_dynamic-update-slice_fusion), channel_id=1, source_target_pairs={{0,2},{1,3},{2,0},{3,1},{4,6},{5,7},{6,4},{7,5},{8,10},{9,11},{10,... | collective-permute-start | bytes 1769480 | tf_op jit(solution)/shard_map/ppermute | solution.py:263
  127.2 6.7 %collective-permute-start.32 = (bf16[2,9,16,256]{3,2,1,0:T(8,128)(2,1)S(1)}, bf16[2,9,16,256]{3,2,1,0:T(8,128)(2,1)S(1)}, u32[]{:S(2)}, u32[]{:S(2)}) collective-permute-start(bf16[2,9,16,256]{3,2,1,0:T(8,128)(2,1)S(1)} %constant_dynamic-update-slice_fusion.4), channel_id=1, source_target_pairs={{0,4},{1,5},{2,6},{3,7},{4,0},{5,1},{6,2},{7,3},{8,12},{9,13},{10,... | collective-permute-start | bytes 442376 | tf_op jit(solution)/shard_map/ppermute | solution.py:263
  130.9 5.0 %collective-permute-start.33 = (bf16[2,9,16,256]{3,2,1,0:T(8,128)(2,1)S(1)}, bf16[2,9,16,256]{3,2,1,0:T(8,128)(2,1)S(1)}, u32[]{:S(2)}, u32[]{:S(2)}) collective-permute-start(bf16[2,9,16,256]{3,2,1,0:T(8,128)(2,1)S(1)} %constant_dynamic-update-slice_fusion.4), channel_id=1, source_target_pairs={{0,8},{1,9},{2,10},{3,11},{4,12},{5,13},{6,14},{7,15},{8,0},{9,1},... | collective-permute-start | bytes 442376 | tf_op jit(solution)/shard_map/ppermute | solution.py:263
  132.8 9.4 %collective-permute-start.34 = (bf16[2,9,16,256]{3,2,1,0:T(8,128)(2,1)S(1)}, bf16[2,9,16,256]{3,2,1,0:T(8,128)(2,1)S(1)}, u32[]{:S(2)}, u32[]{:S(2)}) collective-permute-start(bf16[2,9,16,256]{3,2,1,0:T(8,128)(2,1)S(1)} %constant_dynamic-update-slice_fusion.4), channel_id=1, source_target_pairs={{0,12},{1,13},{2,14},{3,15},{4,8},{5,9},{6,10},{7,11},{8,4},{9,5},... | collective-permute-start | bytes 442376 | tf_op jit(solution)/shard_map/ppermute | solution.py:263
  142.2 7.7 %collective-permute-start.35 = (bf16[8,18,16,256]{3,2,1,0:T(8,128)(2,1)S(1)}, bf16[8,18,16,256]{3,2,1,0:T(8,128)(2,1)S(1)}, u32[]{:S(2)}, u32[]{:S(2)}) collective-permute-start(bf16[8,18,16,256]{3,2,1,0:T(8,128)(2,1)S(1)} %constant_dynamic-update-slice_fusion.6.one), channel_id=1, source_target_pairs={{0,1},{1,0},{2,3},{3,2},{4,5},{5,4},{6,7},{7,6},{8,9},{9,8},{10,11... | collective-permute-start | bytes 3538952 | tf_op jit(solution)/shard_map/ppermute | solution.py:263
  (24 other events, 133.0 us)

commit v4 on v3

v4 whole, which is shorter than its diff:
```python
import functools

import jax
import jax.numpy as jnp
from jax import lax
from jax.experimental import pallas as pl
from jax.experimental.pallas import tpu as pltpu
from jax.sharding import PartitionSpec as P

K = 27
BLOCK = 128
GROUP = 9
K_ONE = 18
EPSILON = 1e-05
F32 = jnp.float32
BF16 = jnp.bfloat16
LARGE = 58 * 1024 * 1024
SMALL = 24 * 1024 * 1024


def merged(merge, values):
    return merge(merge(values[0], values[1]), merge(values[2], values[3]))


def merged_moments(one, two):
    (sum_one, square_one, count_one), (sum_two, square_two, count_two) = one, two
    away = sum_one / count_one - sum_two / count_two
    count = count_one + count_two
    square = (square_one + square_two) + away * away * (count_one * count_two / count)
    return sum_one + sum_two, square, count


def dot(a, b, contract):
    return lax.dot_general(a, b, ((contract[0], contract[1]), ((), ())), preferred_element_type=F32)


def full(shape):
    return pl.BlockSpec(shape, lambda *_: (0,) * len(shape))


def params(limit):
    return pltpu.CompilerParams(vmem_limit_bytes=limit)


def cost(flops, moved):
    return pl.CostEstimate(flops=int(flops), bytes_accessed=int(moved), transcendentals=0)


def occupied_rows(filled, rows):
    position = lax.broadcasted_iota(jnp.int32, (rows, 1), 0)
    return (position < filled - BLOCK) | (position >= rows - BLOCK)


def chosen_slots(slot, slots):
    return jnp.where(slot == slots, 1.0, 0.0).astype(BF16)


def transposed_map(map_ref):
    spare = jnp.zeros((BLOCK - K, map_ref.shape[1]), jnp.int32)
    return jnp.transpose(jnp.concatenate([map_ref[...], spare], axis=0))


def convolve(map_ref, tiles, first_slots, weight_hbm, conv_ref, scratch):
    weight, picked, index, weight_sem = scratch
    groups = K // GROUP

    def fetch(g):
        here = pl.ds(g * GROUP, GROUP)
        return pltpu.make_async_copy(weight_hbm.at[here], weight.at[here], weight_sem.at[g])

    for g in range(groups):
        fetch(g).start()
    index[...] = transposed_map(map_ref)
    conv_ref[...] = jnp.zeros_like(conv_ref)
    slots = lax.broadcasted_iota(jnp.int32, (BLOCK, 3 * BLOCK), 1)

    def group(g, carry):
        local = pltpu.roll(index[...], lax.rem(BLOCK - g * GROUP, BLOCK), 1)
        for b, tile in enumerate(tiles):
            here = slice(b * BLOCK, (b + 1) * BLOCK)
            slot = local[here] - first_slots[b]
            for j in range(GROUP):
                chosen = chosen_slots(slot[:, j : j + 1], slots)
                picked[j, here, :] = dot(chosen, tile[...], ((1,), (0,))).astype(BF16)
        fetch(g).wait()
        total = conv_ref[...]
        for j in range(GROUP):
            total = total + dot(picked[j], weight[g * GROUP + j], ((1,), (0,)))
        conv_ref[...] = total
        return carry

    lax.fori_loop(0, groups, group, 0)


def inner_kernel(map_ref, own_ref, weight_hbm, conv_ref, chosen_map, *scratch):
    rows = own_ref.shape[0]
    chosen_map[...] = map_ref[:, BLOCK : rows - BLOCK]
    blocks = range(1, rows // BLOCK - 1)
    tiles = [own_ref.at[(b - 1) * BLOCK : (b + 2) * BLOCK] for b in blocks]
    first_slots = [rows - BLOCK + b * BLOCK for b in blocks]
    convolve(chosen_map, tiles, first_slots, weight_hbm, conv_ref, scratch)


def outer_kernel(
    filled_ref, odd_ref, map_ref, own_ref, even_ref, other_ref, inner_ref, weight_hbm,
    conv_ref, stats_ref, window_ref, chosen_map, *scratch,
):
    rows = own_ref.shape[0]
    odd = odd_ref[0] == 1
    window_ref[0:BLOCK, :] = jnp.where(odd, even_ref[...], other_ref[...])
    window_ref[BLOCK : rows + BLOCK, :] = own_ref[...]
    window_ref[rows + BLOCK :, :] = jnp.where(odd, other_ref[...], even_ref[...])
    chosen_map[:, 0:BLOCK] = map_ref[:, 0:BLOCK]
    chosen_map[:, BLOCK:] = map_ref[:, rows - BLOCK :]
    tiles = [window_ref.at[0 : 3 * BLOCK], window_ref.at[rows - BLOCK :]]
    first_slots = [rows - BLOCK, 2 * rows - 2 * BLOCK]
    convolve(chosen_map, tiles, first_slots, weight_hbm, conv_ref, scratch)
    filled = filled_ref[0]
    count = filled.astype(F32)
    conv = whole(inner_ref, conv_ref)
    occupied = occupied_rows(filled, rows)
    sums = jnp.sum(jnp.where(occupied, conv, 0.0), axis=0, keepdims=True)
    off = jnp.where(occupied, conv - sums / count, 0.0)
    squares = jnp.sum(off * off, axis=0, keepdims=True)
    stats_ref[...] = jnp.concatenate([sums, squares, jnp.full_like(sums, count)], axis=0)


def whole(inner_ref, outer_ref):
    return jnp.concatenate([outer_ref[0:BLOCK, :], inner_ref[...], outer_ref[BLOCK:, :]], axis=0)


def normalised(filled, inner_ref, outer_ref, stats_refs, gain_ref, shift_ref, cotangent_ref):
    conv = whole(inner_ref, outer_ref)
    sums, squares, total = merged(
        merged_moments, [[ref[i : i + 1, :] for i in range(3)] for ref in stats_refs]
    )
    center = sums / total
    inverse = lax.rsqrt(squares / total + EPSILON)
    occupied = occupied_rows(filled, conv.shape[0])
    normed = (conv - center) * inverse
    affine = gain_ref[...] * normed + shift_ref[...]
    upstream = jnp.where(occupied & (affine > 0.0), cotangent_ref[...].astype(F32), 0.0)
    return occupied, normed, affine, upstream, inverse, total


def norm_kernel(
    filled_ref, inner_ref, outer_ref, gain_ref, shift_ref, cotangent_ref, feature_ref, *refs
):
    *stats_refs, out_ref, sums_ref = refs
    occupied, normed, affine, upstream, _, _ = normalised(
        filled_ref[0], inner_ref, outer_ref, stats_refs, gain_ref, shift_ref, cotangent_ref
    )
    out = jnp.maximum(affine, 0.0) + feature_ref[...].astype(F32)
    out_ref[...] = jnp.where(occupied, out, 0.0).astype(BF16)
    sums_ref[...] = jnp.concatenate(
        [jnp.sum(upstream * normed, axis=0, keepdims=True), jnp.sum(upstream, axis=0, keepdims=True)],
        axis=0,
    )


def kernel_gradient(first, place, map_ref, window_ref, grad, keep_any, send_any, scratch):
    index, picked, product, keep, send, out_sem = scratch
    half, count, rows = keep.shape[:3]
    index[...] = transposed_map(map_ref)
    slots = lax.broadcasted_iota(jnp.int32, (BLOCK, 3 * BLOCK), 1)

    def store(g):
        here = pl.ds(g * GROUP, GROUP)
        return [
            pltpu.make_async_copy(keep.at[:, here], keep_any.at[:, here], out_sem.at[0, g]),
            pltpu.make_async_copy(send.at[:, here], send_any.at[:, here], out_sem.at[1, g]),
        ]

    def group(g, carry):
        local = pltpu.roll(index[...], lax.rem(BLOCK - first - g * GROUP, BLOCK), 1)
        for j in range(GROUP):
            for b in range(grad.shape[0] // BLOCK):
                here = slice(b * BLOCK, (b + 1) * BLOCK)
                slot = local[here, j : j + 1] - (grad.shape[0] + (b - 1) * BLOCK)
                tile = window_ref[b * BLOCK : (b + 3) * BLOCK, :]
                chosen = chosen_slots(slot, slots)
                picked[j, here, :] = dot(chosen, tile, ((1,), (0,))).astype(BF16)
        for j in range(GROUP):
            product[j] = dot(picked[j], grad[...], ((0,), (0,)))
            for piece in range(16):
                start = pl.multiple_of(lax.bitwise_xor(jnp.int32(piece), place) * rows, rows)
                value = product[j, pl.ds(start, rows), :]
                if piece < half:
                    keep[piece, g * GROUP + j] = value
                else:
                    send[piece - half, g * GROUP + j] = value.astype(BF16)
        for copy in store(g):
            copy.start()
        return carry

    lax.fori_loop(0, count // GROUP, group, 0)
    for g in range(count // GROUP):
        for copy in store(g):
            copy.wait()


def first_gradient_kernel(
    parts, filled_ref, place_ref, inner_ref, outer_ref, gain_ref, shift_ref, cotangent_ref,
    map_ref, window_ref, *refs,
):
    stats_refs, grads_refs, refs = refs[:parts], refs[parts : 2 * parts], refs[2 * parts :]
    grad_ref, sums_ref, keep_any, send_any, *scratch = refs
    occupied, normed, _, upstream, inverse, total = normalised(
        filled_ref[0], inner_ref, outer_ref, stats_refs, gain_ref, shift_ref, cotangent_ref
    )
    sums = merged(jnp.add, [ref[...] for ref in grads_refs])
    sums_ref[...] = sums
    grad_conv = gain_ref[...] * inverse * (
        upstream - sums[1:2, :] / total - normed * sums[0:1, :] / total
    )
    grad_ref[...] = jnp.where(occupied, grad_conv, 0.0).astype(BF16)
    kernel_gradient(0, place_ref[0], map_ref, window_ref, grad_ref, keep_any, send_any, scratch)


def second_gradient_kernel(
    place_ref, grad_ref, map_ref, window_ref, keep_any, send_any, *scratch
):
    kernel_gradient(
        K_ONE, place_ref[0], map_ref, window_ref, grad_ref, keep_any, send_any, scratch
    )


def push_kernel(grad_ref, index_ref, weight_ref, before_ref, own_ref, after_ref, sink):
    step = pl.program_id(0)

    @pl.when(step == 0)
    def _():
        sink[...] = jnp.zeros_like(sink)

    blocks = grad_ref.shape[0] // BLOCK
    here = jnp.concatenate([index_ref[step * GROUP + j, :][None] for j in range(GROUP)], axis=0)
    block_of = lax.broadcasted_iota(jnp.int32, here.shape, 1) // BLOCK
    local = here - (3 + block_of) * BLOCK
    slots = lax.broadcasted_iota(jnp.int32, (3 * BLOCK, BLOCK), 0)
    pushed = [
        dot(grad_ref[...], weight_ref[j], ((1,), (1,))).astype(BF16) for j in range(GROUP)
    ]
    for b in range(blocks):
        rows = slice(b * BLOCK, (b + 1) * BLOCK)
        chosen = jnp.concatenate(
            [
                jnp.where(local[j : j + 1, rows] == slots, 1.0, 0.0).astype(BF16)
                for j in range(GROUP)
            ],
            axis=1,
        )
        stacked = jnp.concatenate([pushed[j][rows] for j in range(GROUP)], axis=0)
        window = slice(b * BLOCK, (b + 3) * BLOCK)
        sink[window, :] = sink[window, :] + dot(chosen, stacked, ((1,), (0,)))

    @pl.when(step == pl.num_programs(0) - 1)
    def _():
        before_ref[...] = sink[0:BLOCK, :].astype(BF16)
        own_ref[...] = sink[BLOCK : (blocks + 1) * BLOCK, :]
        after_ref[...] = sink[(blocks + 1) * BLOCK :, :].astype(BF16)


def place_kernel(other, places_ref, one, two, *refs):
    out_ref, sems = refs[-2:]
    half, split, rows = one.shape[:3]
    copies = []
    for piece in range(half):
        for part, source in enumerate((one, two)):
            relative = jnp.int32(piece + half * other)
            place = lax.bitwise_xor(relative, places_ref[part])
            start = pl.multiple_of(place * rows, rows)
            first = 0 if part == 0 else split
            copies.append(
                pltpu.make_async_copy(
                    source.at[piece],
                    out_ref.at[pl.ds(first, source.shape[1]), pl.ds(start, rows), :],
                    sems.at[len(copies)],
                )
            )
    for copy in copies:
        copy.start()
    for copy in copies:
        copy.wait()


def swap(value, by):
    peers = lax.axis_size("dp")
    return lax.ppermute(value, "dp", [(i, i ^ by) for i in range(peers)])


STAGES = {"c": (1,), "x": (2,), "z": (4, 8, 12)}


def split(total, stage):
    size = total.shape[0] // (len(STAGES[stage]) + 1)
    sends = [
        total[(i + 1) * size : (i + 2) * size].astype(BF16) for i in range(len(STAGES[stage]))
    ]
    return total[:size], sends


def swapped(sends, stage):
    return [swap(send, by) for send, by in zip(sends, STAGES[stage])]


def added(kept, received):
    return functools.reduce(lambda a, b: a + b.astype(F32), received, kept)


def gather_start(piece, stage):
    return [swap(piece, by) for by in STAGES[stage]]


def core_reduced(keep, send):
    return keep + swap(send, 1).astype(F32)


def summed_over_devices(one, two, grad_conv, push, spread):
    parts = [split(one, "x"), split(two, "z")]
    parts, grad_conv = lax.optimization_barrier((parts, grad_conv))
    received = [swapped(sends, stage) for (_, sends), stage in zip(parts, "xz")]
    received, sinks = lax.optimization_barrier((received, push(grad_conv)))
    pieces = [added(kept, got) for (kept, _), got in zip(parts, received)]
    parts = [split(piece, stage) for piece, stage in zip(pieces, "zx")]
    received = [swapped(sends, stage) for (_, sends), stage in zip(parts, "zx")]
    received, result = lax.optimization_barrier((received, spread(*sinks)))
    pieces = [added(kept, got) for (kept, _), got in zip(parts, received)]
    by = 16
    while by < lax.axis_size("dp"):
        pieces = [piece + swap(piece, by) for piece in pieces]
        by *= 2
    pieces = [piece.astype(BF16) for piece in pieces]
    for stages in ("zx", "xz"):
        received = [gather_start(piece, stage) for piece, stage in zip(pieces, stages)]
        received, pieces = lax.optimization_barrier((received, pieces))
        pieces = [
            jnp.concatenate([piece] + got, axis=0) for piece, got in zip(pieces, received)
        ]
    return pieces, result


def exchanged(value, merge):
    received = [swap(value, by) for by in (1, 2, 3)]
    value = merged(merge, [value] + received)
    by = 16
    while by < lax.axis_size("dp"):
        value = merge(value, swap(value, by))
        by *= 2
    return [value] + [swap(value, by) for by in (4, 8, 12)]


def stacked_moments(one, two):
    return jnp.stack(merged_moments(one, two))


def per_device(features, kernel_map, occupancy, weights, bn_gain, bn_shift, cotangent):
    rows, channels = features.shape
    peers = lax.axis_size("dp")
    me = lax.axis_index("dp")
    blocks = rows // BLOCK
    inner_rows = rows - 2 * BLOCK
    steps = K // GROUP

    odd = me & 1
    even_pairs = [(i, i ^ 1) for i in range(peers)]
    other_pairs = [(i, ((i + 1) ^ 1) - 1) for i in range(1, peers - 1)]

    def neighbours_swap(to_before, to_after):
        even = lax.ppermute(jnp.where(odd == 1, to_before, to_after), "dp", even_pairs)
        other = lax.ppermute(jnp.where(odd == 1, to_after, to_before), "dp", other_pairs)
        return even, other

    even, other = neighbours_swap(features[:BLOCK], features[rows - BLOCK :])
    map_rows = jnp.transpose(kernel_map)
    odd_flag = odd.reshape(1)

    gain = bn_gain.reshape(1, channels)
    shift = bn_shift.reshape(1, channels)
    smem = pl.BlockSpec(memory_space=pltpu.SMEM)
    vmem = pl.BlockSpec(memory_space=pltpu.VMEM)
    hbm = pl.BlockSpec(memory_space=pltpu.HBM)
    anywhere = pl.BlockSpec(memory_space=pl.ANY)
    groups = K // GROUP
    work = K * rows * channels * 2 * (3 * BLOCK + channels)
    moved = K * channels * channels * 2 * 3

    half_conv = jax.ShapeDtypeStruct((2 * BLOCK, channels), F32)
    scratch = [
        pltpu.VMEM((K, 2 * BLOCK), jnp.int32),
        pltpu.VMEM((K, channels, channels), BF16),
        pltpu.VMEM((GROUP, 2 * BLOCK, channels), BF16),
        pltpu.VMEM((2 * BLOCK, BLOCK), jnp.int32),
        pltpu.SemaphoreType.DMA((groups,)),
    ]

    inner = pl.pallas_call(
        inner_kernel,
        in_specs=[vmem, vmem, hbm],
        out_specs=vmem,
        out_shape=half_conv,
        scratch_shapes=scratch,
        compiler_params=params(LARGE),
        cost_estimate=cost(work / 2, moved),
        name="conv_inner",
    )(map_rows, features, weights)

    outer, stats, window = pl.pallas_call(
        outer_kernel,
        in_specs=[smem, smem, vmem, vmem, vmem, vmem, vmem, hbm],
        out_specs=[vmem, vmem, vmem],
        out_shape=[
            half_conv,
            jax.ShapeDtypeStruct((3, channels), F32),
            jax.ShapeDtypeStruct((rows + 2 * BLOCK, channels), BF16),
        ],
        scratch_shapes=scratch,
        compiler_params=params(LARGE),
        cost_estimate=cost(work / 2, moved),
        name="conv_outer",
    )(occupancy, odd_flag, map_rows, features, even, other, inner, weights)

    stats = exchanged(stats, stacked_moments)

    block_out, sums = pl.pallas_call(
        norm_kernel,
        in_specs=[smem] + [vmem] * 10,
        out_shape=[
            jax.ShapeDtypeStruct((rows, channels), BF16),
            jax.ShapeDtypeStruct((2, channels), F32),
        ],
        compiler_params=params(SMALL),
        cost_estimate=cost(rows * channels * 20, rows * channels * 10),
        name="norm",
    )(occupancy, inner, outer, gain, shift, cotangent, features, *stats)

    grads = exchanged(sums, jnp.add)

    core, lane, depth = me & 1, (me >> 1) & 1, (me >> 2) & 3
    place_one = (core * 8 + lane * 4 + depth).reshape(1)
    place_two = (core * 8 + depth * 2 + lane).reshape(1)
    piece_rows = channels // 16

    def gradient(kernel, count, in_specs, out_specs, out_shape, name):
        shape = (8, count, piece_rows, channels)
        return pl.pallas_call(
            kernel,
            in_specs=in_specs,
            out_specs=out_specs + [anywhere, anywhere],
            out_shape=out_shape
            + [jax.ShapeDtypeStruct(shape, F32), jax.ShapeDtypeStruct(shape, BF16)],
            scratch_shapes=[
                pltpu.VMEM((rows, BLOCK), jnp.int32),
                pltpu.VMEM((GROUP, rows, channels), BF16),
                pltpu.VMEM((GROUP, channels, channels), F32),
                pltpu.VMEM(shape, F32),
                pltpu.VMEM(shape, BF16),
                pltpu.SemaphoreType.DMA((2, count // GROUP)),
            ],
            compiler_params=params(SMALL),
            cost_estimate=cost(work * count / K, count * channels * channels * 6),
            name=name,
        )

    grad_conv, sums, *pair_one = gradient(
        functools.partial(first_gradient_kernel, len(stats)),
        K_ONE,
        [smem, smem] + [vmem] * 15,
        [vmem, vmem],
        [
            jax.ShapeDtypeStruct((rows, channels), BF16),
            jax.ShapeDtypeStruct((2, channels), F32),
        ],
        "weight_gradient_one",
    )(
        occupancy, place_one, inner, outer, gain, shift, cotangent, map_rows, window,
        *stats, *grads,
    )
    one = core_reduced(*pair_one)
    pair_two = gradient(
        second_gradient_kernel, K - K_ONE, [smem] + [vmem] * 3, [], [], "weight_gradient_two"
    )(place_two, grad_conv, map_rows, window)
    two = core_reduced(*pair_two)

    weight_spec = pl.BlockSpec((GROUP, channels, channels), lambda s: (s, 0, 0))

    def push(grad_conv):
        return pl.pallas_call(
            push_kernel,
            grid=(groups,),
            in_specs=[full((rows, channels)), full((K, rows)), weight_spec],
            out_specs=[full((BLOCK, channels)), full((rows, channels)), full((BLOCK, channels))],
            out_shape=[
                jax.ShapeDtypeStruct((BLOCK, channels), BF16),
                jax.ShapeDtypeStruct((rows, channels), F32),
                jax.ShapeDtypeStruct((BLOCK, channels), BF16),
            ],
            scratch_shapes=[pltpu.VMEM((rows + 2 * BLOCK, channels), F32)],
            compiler_params=params(SMALL),
            cost_estimate=cost(work, moved),
            name="push",
        )(grad_conv, map_rows, weights)

    def spread_gradient(sink_before, sink_own, sink_after):
        even, other = neighbours_swap(sink_before, sink_after)
        from_prev = jnp.where(odd == 1, even, other).astype(F32)
        from_next = jnp.where(odd == 1, other, even).astype(F32)
        occupied = occupied_rows(occupancy[0], rows)
        received = jnp.concatenate(
            [
                sink_own[:BLOCK] + from_prev,
                sink_own[BLOCK : rows - BLOCK],
                sink_own[rows - BLOCK :] + from_next,
            ],
            axis=0,
        )
        return (jnp.where(occupied, cotangent.astype(F32), 0.0) + received).astype(BF16)

    (own_one, own_two), grad_features = summed_over_devices(
        one, two, grad_conv, push, spread_gradient
    )
    places = jnp.concatenate([place_one, place_two])

    def placed(other, sources, *into):
        return pl.pallas_call(
            functools.partial(place_kernel, other),
            in_specs=[smem, anywhere, anywhere] + [hbm] * len(into),
            out_specs=hbm,
            out_shape=jax.ShapeDtypeStruct(weights.shape, BF16),
            scratch_shapes=[pltpu.SemaphoreType.DMA((16,))],
            input_output_aliases={3: 0} if into else {},
            compiler_params=params(SMALL),
            cost_estimate=cost(0, K * channels * channels * 2),
            name="place",
        )(places, *sources, *into)

    others = [swap(own_one, 1), swap(own_two, 1)]
    grad_weights = placed(1, others, placed(0, (own_one, own_two)))
    return block_out, grad_features, grad_weights, sums[0], sums[1]


def solution(mesh):
    in_specs = (
        P(("parts", "dp"), None),
        P(("parts", "dp"), None),
        P(("parts", "dp")),
        P(),
        P(),
        P(),
        P(("parts", "dp"), None),
    )
    out_specs = (
        P(("parts", "dp"), None),
        P(("parts", "dp"), None),
        P("parts", None, None),
        P("parts"),
        P("parts"),
    )
    return jax.shard_map(
        per_device, mesh=mesh, in_specs=in_specs, out_specs=out_specs, check_vma=False
    )
```

time: 153 us -> 136 us (0.89)
  starting transfers between devices: 57.6 us -> 45.6 us
  local copies, waits for them, and re-layouts: 11.1 us -> 5.8 us
  waiting for transfers between devices: 45.2 us -> 41.8 us
  Pallas kernels: 33.2 us -> 36 us
    ppermute x33 -> x32, starting transfers between devices: 49.5 us -> 36.7 us  [swap(): return lax.ppermute(value, 'dp', [(i, i ^ by) for i in range(peers)])]
    unnamed x30 -> x36, local copies, waits for them, and re-layouts: 10.2 us -> 4.97 us
    pallas_call x6, Pallas kernels: 29.5 us -> 32.2 us  [the longest x1 9.26 us: push(): pl.pallas_call(push_kernel, grid=(groups,), in_specs=[full((rows, channel...]
    ppermute x2, starting transfers between devices: 0.32 us -> 2.4 us  [neighbours_swap(): lax.ppermute(jnp.where(odd == 1, to_before, to_after), 'dp', even_pairs)]
    ppermute x33 -> x32, waiting for transfers between devices: 43.9 us -> 41.8 us  [swap(): return lax.ppermute(value, 'dp', [(i, i ^ by) for i in range(peers)])]
  transfers between devices with their start and end apart: 37 -> 36, of which waited for: 18 -> 18; matrix products, arithmetic and copies ran while one was open for 2% -> 2% of each run, Pallas kernels for 10% -> 15%
where the time goes in v4:
time: 136 us; the launch traced here: 135 us
  starting transfers between devices  45.6 us (34%)
  waiting for transfers between devices  41.8 us (31%)
  Pallas kernels  36 us (26%)
  local copies, waits for them, and re-layouts  5.8 us (4%)
  other arithmetic  3.75 us (3%)
  between operations  1.86 us (1%)
    ppermute x32, waiting for transfers between devices, swap(): return lax.ppermute(value, 'dp', [(i, i ^ by) for i in range(peers)])  41.8 us
    ppermute x32, starting transfers between devices, swap(): return lax.ppermute(value, 'dp', [(i, i ^ by) for i in range(peers)])  36.7 us
    pallas_call x1, Pallas kernels, push(): pl.pallas_call(push_kernel, grid=(groups,), in_specs=[full((rows, channel...  9.26 us
    pallas_call x1, Pallas kernels, per_device(): pl.pallas_call(outer_kernel, in_specs=[smem, smem, vmem, vmem, vmem, vmem...  6.82 us
    ppermute x2, starting transfers between devices, neighbours_swap(): lax.ppermute(jnp.where(odd == 1, to_after, to_before), 'dp', other_pairs)  6.51 us
    pallas_call x1, Pallas kernels, per_device(): pl.pallas_call(inner_kernel, in_specs=[vmem, vmem, hbm], out_specs=vmem,...  6.4 us
    pallas_call x1, Pallas kernels, per_device(): gradient(functools.partial(first_gradient_kernel, len(stats)), K_ONE, [sm...  5.79 us
    unnamed x36, local copies, waits for them, and re-layouts  4.97 us
  transfers between devices with their start and end apart: 36, of which 18 were waited for; matrix products, arithmetic and copies ran while one was open for 2% of the time, Pallas kernels for 15%

profile of v4, /device:TPU:1, one launch (start us, length us, event | category | flops | bytes accessed | tf_op | source)
XLA Modules:
  0.0 134.8 jit_solution(1208247540834011318)
XLA Ops:
  1.5 4.5 %collective-permute-start.1 = (bf16[128,256]{1,0:T(8,128)(2,1)S(1)}, bf16[128,256]{1,0:T(8,128)(2,1)S(1)}, u32[]{:S(2)}, u32[]{:S(2)}) collective-permute-start(bf16[128,256]{1,0:T(8,128)(2,1)S(1)} %get-tuple-element.109), channel_id=1, source_target_pairs={{1,2},{2,1},{3,4},{4,3},{5,6},{6,5},{7,8},{8,7},{9,10},{10,9},{11,... | collective-permute-start | bytes 196616 | tf_op jit(solution)/shard_map/ppermute | solution.py:370
  6.1 6.4 %conv_inner.1.inner_ref = f32[256,256]{1,0:T(8,128)} custom-call(s32[27,512]{1,0:T(8,128)} %bitcast.13, bf16[512,256]{1,0:T(8,128)(2,1)} %feature_ref.1, bf16[27,256,256]{2,1,0:T(8,128)(2,1)} %weight_ref.1), custom_call_target="tpu_custom_call" | custom-call | flops 2264924160 | bytes 10616832 | tf_op jit(solution)/shard_map/conv_inner/pallas_call | solution.py:396
  13.9 6.8 %conv_outer.1 = (f32[256,256]{1,0:T(8,128)}, f32[3,256]{1,0:T(4,128)}, bf16[768,256]{1,0:T(8,128)(2,1)}) custom-call(s32[1]{0:T(128)S(6)} %copy.22.filled_ref, s32[1]{0:T(128)} %bitcast.1.odd_ref, s32[27,512]{1,0:T(8,128)} %bitcast.14, bf16[512,256]{1,0:T(8,128)(2,1)} %feature_ref.1, bf16[128,256]{1,0:T(8,128)(2,1)} %copy-done.13, ...), custom_call_target="tpu_custom_call" | custom-call | flops 2264924160 | bytes 10616832 | tf_op jit(solution)/shard_map/conv_outer/pallas_call | solution.py:407
  25.9 2.4 %collective-permute-start.7 = (f32[3,256]{1,0:T(4,128)S(1)}, f32[3,256]{1,0:T(4,128)S(1)}, u32[]{:S(2)}, u32[]{:S(2)}) collective-permute-start(f32[3,256]{1,0:T(4,128)S(1)} %pad_maximum_fusion.refs_0_), channel_id=1, source_target_pairs={{0,12},{1,13},{2,14},{3,15},{4,8},{5,9},{6,10},{7,11},{8,4},{9,5},... | collective-permute-start | bytes 9224 | tf_op jit(solution)/shard_map/ppermute | solution.py:288
  30.2 1.8 %collective-permute-done.6.refs_2_ = f32[3,256]{1,0:T(4,128)S(1)} collective-permute-done((f32[3,256]{1,0:T(4,128)S(1)}, f32[3,256]{1,0:T(4,128)S(1)}, u32[]{:S(2)}, u32[]{:S(2)}) %collective-permute-start.6) | collective-permute-done | bytes 3104 | tf_op jit(solution)/shard_map/ppermute | solution.py:288
  34.0 3.4 %collective-permute-start.10 = (f32[2,256]{1,0:T(2,128)S(1)}, f32[2,256]{1,0:T(2,128)S(1)}, u32[]{:S(2)}, u32[]{:S(2)}) collective-permute-start(f32[2,256]{1,0:T(2,128)S(1)} %get-tuple-element.54), channel_id=1, source_target_pairs={{0,3},{1,2},{2,1},{3,0},{4,7},{5,6},{6,5},{7,4},{8,11},{9,10},{10,... | collective-permute-start | bytes 6152 | tf_op jit(solution)/shard_map/ppermute | solution.py:288
  46.8 5.8 %weight_gradient_one.1 = (bf16[512,256]{1,0:T(8,128)(2,1)S(1)}, f32[2,256]{1,0:T(2,128)S(1)}, f32[8,18,16,256]{3,2,1,0:T(8,128)S(1)}, bf16[8,18,16,256]{3,2,1,0:T(8,128)(2,1)S(1)}) custom-call(s32[1]{0:T(128)S(6)} %copy.22.filled_ref, s32[1]{0:T(128)} %bitcast.4.place_ref, f32[256,256]{1,0:T(8,128)S(1)} %copy-done.2, f32[256,256]{1,0:T(8,128)S(1)} %copy-done.4, ...), custom_call_target="tpu_custom_call" | custom-call | flops 3019898880 | bytes 7077888 | tf_op jit(solution)/shard_map/weight_gradient_one/pallas_call | solution.py:464
  54.3 3.0 %weight_gradient_two.1 = (f32[8,9,16,256]{3,2,1,0:T(8,128)S(1)}, bf16[8,9,16,256]{3,2,1,0:T(8,128)(2,1)S(1)}) custom-call(s32[1]{0:T(128)} %bitcast.5.place_ref, bf16[512,256]{1,0:T(8,128)(2,1)S(1)} %get-tuple-element.65.grad_ref, s32[27,512]{1,0:T(8,128)S(1)} %bitcast.16, bf16[768,256]{1,0:T(8,128)(2,1)S(1)} %copy-done.10), custom_call_target="tpu_custom_call" | custom-call | flops 1509949440 | bytes 3538944 | tf_op jit(solution)/shard_map/weight_gradient_two/pallas_call | solution.py:479
  57.3 2.0 %collective-permute-done.15 = bf16[8,9,16,256]{3,2,1,0:T(8,128)(2,1)S(1)} collective-permute-done((bf16[8,9,16,256]{3,2,1,0:T(8,128)(2,1)S(1)}, bf16[8,9,16,256]{3,2,1,0:T(8,128)(2,1)S(1)}, u32[]{:S(2)}, u32[]{:S(2)}) %collective-permute-start.15) | collective-permute-done | bytes 589856 | tf_op jit(solution)/shard_map/ppermute | solution.py:288
  66.0 9.3 %push.1 = (bf16[128,256]{1,0:T(8,128)(2,1)S(1)}, f32[512,256]{1,0:T(8,128)S(1)}, bf16[128,256]{1,0:T(8,128)(2,1)S(1)}) custom-call(bf16[512,256]{1,0:T(8,128)(2,1)S(1)} %get-tuple-element.65.grad_ref, s32[27,512]{1,0:T(8,128)S(1)} %bitcast.17, bf16[27,256,256]{2,1,0:T(8,128)(2,1)S(1)} %copy-done.7), custom_call_target="tpu_custom_call" | custom-call | flops 4529848320 | bytes 10616832 | tf_op jit(solution)/shard_map/push/pallas_call | solution.py:487
  76.2 2.3 %collective-permute-start.24 = (bf16[128,256]{1,0:T(8,128)(2,1)S(1)}, bf16[128,256]{1,0:T(8,128)(2,1)S(1)}, u32[]{:S(2)}, u32[]{:S(2)}) collective-permute-start(bf16[128,256]{1,0:T(8,128)(2,1)S(1)} %get-tuple-element.111), channel_id=1, source_target_pairs={{0,1},{1,0},{2,3},{3,2},{4,5},{5,4},{6,7},{7,6},{8,9},{9,8},{10,11... | collective-permute-start | bytes 196616 | tf_op jit(solution)/shard_map/ppermute | solution.py:369
  78.6 2.0 %collective-permute-start.25 = (bf16[128,256]{1,0:T(8,128)(2,1)S(1)}, bf16[128,256]{1,0:T(8,128)(2,1)S(1)}, u32[]{:S(2)}, u32[]{:S(2)}) collective-permute-start(bf16[128,256]{1,0:T(8,128)(2,1)S(1)} %get-tuple-element.112), channel_id=1, source_target_pairs={{1,2},{2,1},{3,4},{4,3},{5,6},{6,5},{7,8},{8,7},{9,10},{10,9},{11,... | collective-permute-start | bytes 196616 | tf_op jit(solution)/shard_map/ppermute | solution.py:370
  81.0 3.4 %collective-permute-start.23 = (bf16[1,9,16,256]{3,2,1,0:T(8,128)(2,1)S(1)}, bf16[1,9,16,256]{3,2,1,0:T(8,128)(2,1)S(1)}, u32[]{:S(2)}, u32[]{:S(2)}) collective-permute-start(bf16[1,9,16,256]{3,2,1,0:T(8,128)(2,1)S(1)} %slice.115), channel_id=1, source_target_pairs={{0,2},{1,3},{2,0},{3,1},{4,6},{5,7},{6,4},{7,5},{8,10},{9,11},{10,... | collective-permute-start | bytes 221192 | tf_op jit(solution)/shard_map/ppermute | solution.py:288
  85.9 2.1 %collective-permute-start.20 = (bf16[1,18,16,256]{3,2,1,0:T(8,128)(2,1)S(1)}, bf16[1,18,16,256]{3,2,1,0:T(8,128)(2,1)S(1)}, u32[]{:S(2)}, u32[]{:S(2)}) collective-permute-start(bf16[1,18,16,256]{3,2,1,0:T(8,128)(2,1)S(1)} %get-tuple-element.105), channel_id=1, source_target_pairs={{0,4},{1,5},{2,6},{3,7},{4,0},{5,1},{6,2},{7,3},{8,12},{9,13},{10,... | collective-permute-start | bytes 442376 | tf_op jit(solution)/shard_map/ppermute | solution.py:288
  88.9 3.0 %collective-permute-done.22 = bf16[1,18,16,256]{3,2,1,0:T(8,128)(2,1)S(1)} collective-permute-done((bf16[1,18,16,256]{3,2,1,0:T(8,128)(2,1)S(1)}, bf16[1,18,16,256]{3,2,1,0:T(8,128)(2,1)S(1)}, u32[]{:S(2)}, u32[]{:S(2)}) %collective-permute-start.22) | collective-permute-done | bytes 147488 | tf_op jit(solution)/shard_map/ppermute | solution.py:288
  91.9 6.8 %collective-permute-done.21 = bf16[1,18,16,256]{3,2,1,0:T(8,128)(2,1)S(1)} collective-permute-done((bf16[1,18,16,256]{3,2,1,0:T(8,128)(2,1)S(1)}, bf16[1,18,16,256]{3,2,1,0:T(8,128)(2,1)S(1)}, u32[]{:S(2)}, u32[]{:S(2)}) %collective-permute-start.21) | collective-permute-done | bytes 147488 | tf_op jit(solution)/shard_map/ppermute | solution.py:288
  99.8 2.6 %collective-permute-start.26 = (bf16[1,18,16,256]{3,2,1,0:T(8,128)(2,1)S(1)}, bf16[1,18,16,256]{3,2,1,0:T(8,128)(2,1)S(1)}, u32[]{:S(2)}, u32[]{:S(2)}) collective-permute-start(bf16[1,18,16,256]{3,2,1,0:T(8,128)(2,1)S(1)} %fusion.3), channel_id=1, source_target_pairs={{0,4},{1,5},{2,6},{3,7},{4,0},{5,1},{6,2},{7,3},{8,12},{9,13},{10,... | collective-permute-start | bytes 442376 | tf_op jit(solution)/shard_map/ppermute | solution.py:288
  103.0 2.9 %collective-permute-done.29 = bf16[1,9,16,256]{3,2,1,0:T(8,128)(2,1)S(1)} collective-permute-done((bf16[1,9,16,256]{3,2,1,0:T(8,128)(2,1)S(1)}, bf16[1,9,16,256]{3,2,1,0:T(8,128)(2,1)S(1)}, u32[]{:S(2)}, u32[]{:S(2)}) %collective-permute-start.29) | collective-permute-done | bytes 73760 | tf_op jit(solution)/shard_map/ppermute | solution.py:288
  106.0 6.8 %collective-permute-done.27 = bf16[1,18,16,256]{3,2,1,0:T(8,128)(2,1)S(1)} collective-permute-done((bf16[1,18,16,256]{3,2,1,0:T(8,128)(2,1)S(1)}, bf16[1,18,16,256]{3,2,1,0:T(8,128)(2,1)S(1)}, u32[]{:S(2)}, u32[]{:S(2)}) %collective-permute-start.27) | collective-permute-done | bytes 147488 | tf_op jit(solution)/shard_map/ppermute | solution.py:288
  113.7 2.2 %collective-permute-start.33 = (bf16[2,9,16,256]{3,2,1,0:T(8,128)(2,1)S(1)}, bf16[2,9,16,256]{3,2,1,0:T(8,128)(2,1)S(1)}, u32[]{:S(2)}, u32[]{:S(2)}) collective-permute-start(bf16[2,9,16,256]{3,2,1,0:T(8,128)(2,1)S(1)} %constant_dynamic-update-slice_fusion.4), channel_id=1, source_target_pairs={{0,12},{1,13},{2,14},{3,15},{4,8},{5,9},{6,10},{7,11},{8,4},{9,5},... | collective-permute-start | bytes 442376 | tf_op jit(solution)/shard_map/ppermute | solution.py:288
  117.3 2.4 %collective-permute-done.33 = bf16[2,9,16,256]{3,2,1,0:T(8,128)(2,1)S(1)} collective-permute-done((bf16[2,9,16,256]{3,2,1,0:T(8,128)(2,1)S(1)}, bf16[2,9,16,256]{3,2,1,0:T(8,128)(2,1)S(1)}, u32[]{:S(2)}, u32[]{:S(2)}) %collective-permute-start.33) | collective-permute-done | bytes 147488 | tf_op jit(solution)/shard_map/ppermute | solution.py:288
  119.8 8.2 %collective-permute-done.32 = bf16[2,9,16,256]{3,2,1,0:T(8,128)(2,1)S(1)} collective-permute-done((bf16[2,9,16,256]{3,2,1,0:T(8,128)(2,1)S(1)}, bf16[2,9,16,256]{3,2,1,0:T(8,128)(2,1)S(1)}, u32[]{:S(2)}, u32[]{:S(2)}) %collective-permute-start.32) | collective-permute-done | bytes 147488 | tf_op jit(solution)/shard_map/ppermute | solution.py:288
  130.3 1.9 %place.2.refs_0_ = bf16[27,256,256]{2,1,0:T(8,128)(2,1)} custom-call(s32[2]{0:T(128)S(1)} %pad_add_fusion.places_ref, bf16[8,18,16,256]{3,2,1,0:T(8,128)(2,1)S(1)} %constant_dynamic-update-slice_fusion.6.one, bf16[8,9,16,256]{3,2,1,0:T(8,128)(2,1)S(1)} %constant_dynamic-update-slice_fusion.8.two), custom_call_target="tpu_custom_call" | custom-call | bytes 3538944 | tf_op jit(solution)/shard_map/place/pallas_call | solution.py:524
  132.8 1.9 %place.3 = bf16[27,256,256]{2,1,0:T(8,128)(2,1)} custom-call(s32[2]{0:T(128)S(1)} %pad_add_fusion.places_ref, bf16[8,18,16,256]{3,2,1,0:T(8,128)(2,1)S(1)} %collective-permute-done.34.one, bf16[8,9,16,256]{3,2,1,0:T(8,128)(2,1)S(1)} %collective-permute-done.35.two, bf16[27,256,256]{2,1,0:T(8,128)(2,1)} %place.2.refs_0_), custom_call_target="tpu_custom_call", output_to_operand_aliasing={{}: (3, {})} | custom-call | bytes 3538944 | tf_op jit(solution)/shard_map/place/pallas_call | solution.py:524
  (120 shorter events, 39.2 us)
Async XLA Ops:
  1.5 11.7 %collective-permute-start.1 = (bf16[128,256]{1,0:T(8,128)(2,1)S(1)}, bf16[128,256]{1,0:T(8,128)(2,1)S(1)}, u32[]{:S(2)}, u32[]{:S(2)}) collective-permute-start(bf16[128,256]{1,0:T(8,128)(2,1)S(1)} %get-tuple-element.109), channel_id=1, source_target_pairs={{1,2},{2,1},{3,4},{4,3},{5,6},{6,5},{7,8},{8,7},{9,10},{10,9},{11,... | collective-permute-start | bytes 196616 | tf_op jit(solution)/shard_map/ppermute | solution.py:370
  6.0 7.2 %collective-permute-start = (bf16[128,256]{1,0:T(8,128)(2,1)S(1)}, bf16[128,256]{1,0:T(8,128)(2,1)S(1)}, u32[]{:S(2)}, u32[]{:S(2)}) collective-permute-start(bf16[128,256]{1,0:T(8,128)(2,1)S(1)} %get-tuple-element.110), channel_id=1, source_target_pairs={{0,1},{1,0},{2,3},{3,2},{4,5},{5,4},{6,7},{7,6},{8,9},{9,8},{10,11... | collective-permute-start | bytes 196616 | tf_op jit(solution)/shard_map/ppermute | solution.py:369
  25.9 4.3 %collective-permute-start.7 = (f32[3,256]{1,0:T(4,128)S(1)}, f32[3,256]{1,0:T(4,128)S(1)}, u32[]{:S(2)}, u32[]{:S(2)}) collective-permute-start(f32[3,256]{1,0:T(4,128)S(1)} %pad_maximum_fusion.refs_0_), channel_id=1, source_target_pairs={{0,12},{1,13},{2,14},{3,15},{4,8},{5,9},{6,10},{7,11},{8,4},{9,5},... | collective-permute-start | bytes 9224 | tf_op jit(solution)/shard_map/ppermute | solution.py:288
  34.0 4.8 %collective-permute-start.10 = (f32[2,256]{1,0:T(2,128)S(1)}, f32[2,256]{1,0:T(2,128)S(1)}, u32[]{:S(2)}, u32[]{:S(2)}) collective-permute-start(f32[2,256]{1,0:T(2,128)S(1)} %get-tuple-element.54), channel_id=1, source_target_pairs={{0,3},{1,2},{2,1},{3,0},{4,7},{5,6},{6,5},{7,4},{8,11},{9,10},{10,... | collective-permute-start | bytes 6152 | tf_op jit(solution)/shard_map/ppermute | solution.py:288
  39.8 4.3 %collective-permute-start.13 = (f32[2,256]{1,0:T(2,128)S(1)}, f32[2,256]{1,0:T(2,128)S(1)}, u32[]{:S(2)}, u32[]{:S(2)}) collective-permute-start(f32[2,256]{1,0:T(2,128)S(1)} %add_add_fusion.refs_4_), channel_id=1, source_target_pairs={{0,12},{1,13},{2,14},{3,15},{4,8},{5,9},{6,10},{7,11},{8,4},{9,5},... | collective-permute-start | bytes 6152 | tf_op jit(solution)/shard_map/ppermute | solution.py:288
  52.6 7.0 %collective-permute-start.14 = (bf16[8,18,16,256]{3,2,1,0:T(8,128)(2,1)S(1)}, bf16[8,18,16,256]{3,2,1,0:T(8,128)(2,1)S(1)}, u32[]{:S(2)}, u32[]{:S(2)}) collective-permute-start(bf16[8,18,16,256]{3,2,1,0:T(8,128)(2,1)S(1)} %get-tuple-element.56), channel_id=1, source_target_pairs={{0,1},{1,0},{2,3},{3,2},{4,5},{5,4},{6,7},{7,6},{8,9},{9,8},{10,11... | collective-permute-start | bytes 3538952 | tf_op jit(solution)/shard_map/ppermute | solution.py:288
  61.4 14.8 %collective-permute-start.16 = (bf16[4,18,16,256]{3,2,1,0:T(8,128)(2,1)S(1)}, bf16[4,18,16,256]{3,2,1,0:T(8,128)(2,1)S(1)}, u32[]{:S(2)}, u32[]{:S(2)}) collective-permute-start(bf16[4,18,16,256]{3,2,1,0:T(8,128)(2,1)S(1)} %slice.114), channel_id=1, source_target_pairs={{0,2},{1,3},{2,0},{3,1},{4,6},{5,7},{6,4},{7,5},{8,10},{9,11},{10,... | collective-permute-start | bytes 1769480 | tf_op jit(solution)/shard_map/ppermute | solution.py:288
  62.1 13.2 %collective-permute-start.17 = (bf16[2,9,16,256]{3,2,1,0:T(8,128)(2,1)S(1)}, bf16[2,9,16,256]{3,2,1,0:T(8,128)(2,1)S(1)}, u32[]{:S(2)}, u32[]{:S(2)}) collective-permute-start(bf16[2,9,16,256]{3,2,1,0:T(8,128)(2,1)S(1)} %get-tuple-element.62), channel_id=1, source_target_pairs={{0,4},{1,5},{2,6},{3,7},{4,0},{5,1},{6,2},{7,3},{8,12},{9,13},{10,... | collective-permute-start | bytes 442376 | tf_op jit(solution)/shard_map/ppermute | solution.py:288
  63.8 12.0 %collective-permute-start.18 = (bf16[2,9,16,256]{3,2,1,0:T(8,128)(2,1)S(1)}, bf16[2,9,16,256]{3,2,1,0:T(8,128)(2,1)S(1)}, u32[]{:S(2)}, u32[]{:S(2)}) collective-permute-start(bf16[2,9,16,256]{3,2,1,0:T(8,128)(2,1)S(1)} %get-tuple-element.63), channel_id=1, source_target_pairs={{0,8},{1,9},{2,10},{3,11},{4,12},{5,13},{6,14},{7,15},{8,0},{9,1},... | collective-permute-start | bytes 442376 | tf_op jit(solution)/shard_map/ppermute | solution.py:288
  64.7 11.2 %collective-permute-start.19 = (bf16[2,9,16,256]{3,2,1,0:T(8,128)(2,1)S(1)}, bf16[2,9,16,256]{3,2,1,0:T(8,128)(2,1)S(1)}, u32[]{:S(2)}, u32[]{:S(2)}) collective-permute-start(bf16[2,9,16,256]{3,2,1,0:T(8,128)(2,1)S(1)} %get-tuple-element.64), channel_id=1, source_target_pairs={{0,12},{1,13},{2,14},{3,15},{4,8},{5,9},{6,10},{7,11},{8,4},{9,5},... | collective-permute-start | bytes 442376 | tf_op jit(solution)/shard_map/ppermute | solution.py:288
  76.2 9.7 %collective-permute-start.24 = (bf16[128,256]{1,0:T(8,128)(2,1)S(1)}, bf16[128,256]{1,0:T(8,128)(2,1)S(1)}, u32[]{:S(2)}, u32[]{:S(2)}) collective-permute-start(bf16[128,256]{1,0:T(8,128)(2,1)S(1)} %get-tuple-element.111), channel_id=1, source_target_pairs={{0,1},{1,0},{2,3},{3,2},{4,5},{5,4},{6,7},{7,6},{8,9},{9,8},{10,11... | collective-permute-start | bytes 196616 | tf_op jit(solution)/shard_map/ppermute | solution.py:369
  78.6 9.4 %collective-permute-start.25 = (bf16[128,256]{1,0:T(8,128)(2,1)S(1)}, bf16[128,256]{1,0:T(8,128)(2,1)S(1)}, u32[]{:S(2)}, u32[]{:S(2)}) collective-permute-start(bf16[128,256]{1,0:T(8,128)(2,1)S(1)} %get-tuple-element.112), channel_id=1, source_target_pairs={{1,2},{2,1},{3,4},{4,3},{5,6},{6,5},{7,8},{8,7},{9,10},{10,9},{11,... | collective-permute-start | bytes 196616 | tf_op jit(solution)/shard_map/ppermute | solution.py:370
  81.0 7.9 %collective-permute-start.23 = (bf16[1,9,16,256]{3,2,1,0:T(8,128)(2,1)S(1)}, bf16[1,9,16,256]{3,2,1,0:T(8,128)(2,1)S(1)}, u32[]{:S(2)}, u32[]{:S(2)}) collective-permute-start(bf16[1,9,16,256]{3,2,1,0:T(8,128)(2,1)S(1)} %slice.115), channel_id=1, source_target_pairs={{0,2},{1,3},{2,0},{3,1},{4,6},{5,7},{6,4},{7,5},{8,10},{9,11},{10,... | collective-permute-start | bytes 221192 | tf_op jit(solution)/shard_map/ppermute | solution.py:288
  84.4 7.5 %collective-permute-start.22 = (bf16[1,18,16,256]{3,2,1,0:T(8,128)(2,1)S(1)}, bf16[1,18,16,256]{3,2,1,0:T(8,128)(2,1)S(1)}, u32[]{:S(2)}, u32[]{:S(2)}) collective-permute-start(bf16[1,18,16,256]{3,2,1,0:T(8,128)(2,1)S(1)} %get-tuple-element.103), channel_id=1, source_target_pairs={{0,12},{1,13},{2,14},{3,15},{4,8},{5,9},{6,10},{7,11},{8,4},{9,5},... | collective-permute-start | bytes 442376 | tf_op jit(solution)/shard_map/ppermute | solution.py:288
  84.5 14.2 %collective-permute-start.21 = (bf16[1,18,16,256]{3,2,1,0:T(8,128)(2,1)S(1)}, bf16[1,18,16,256]{3,2,1,0:T(8,128)(2,1)S(1)}, u32[]{:S(2)}, u32[]{:S(2)}) collective-permute-start(bf16[1,18,16,256]{3,2,1,0:T(8,128)(2,1)S(1)} %get-tuple-element.104), channel_id=1, source_target_pairs={{0,8},{1,9},{2,10},{3,11},{4,12},{5,13},{6,14},{7,15},{8,0},{9,1},... | collective-permute-start | bytes 442376 | tf_op jit(solution)/shard_map/ppermute | solution.py:288
  85.9 12.8 %collective-permute-start.20 = (bf16[1,18,16,256]{3,2,1,0:T(8,128)(2,1)S(1)}, bf16[1,18,16,256]{3,2,1,0:T(8,128)(2,1)S(1)}, u32[]{:S(2)}, u32[]{:S(2)}) collective-permute-start(bf16[1,18,16,256]{3,2,1,0:T(8,128)(2,1)S(1)} %get-tuple-element.105), channel_id=1, source_target_pairs={{0,4},{1,5},{2,6},{3,7},{4,0},{5,1},{6,2},{7,3},{8,12},{9,13},{10,... | collective-permute-start | bytes 442376 | tf_op jit(solution)/shard_map/ppermute | solution.py:288
  98.8 7.2 %collective-permute-start.28 = (bf16[1,18,16,256]{3,2,1,0:T(8,128)(2,1)S(1)}, bf16[1,18,16,256]{3,2,1,0:T(8,128)(2,1)S(1)}, u32[]{:S(2)}, u32[]{:S(2)}) collective-permute-start(bf16[1,18,16,256]{3,2,1,0:T(8,128)(2,1)S(1)} %fusion.3), channel_id=1, source_target_pairs={{0,12},{1,13},{2,14},{3,15},{4,8},{5,9},{6,10},{7,11},{8,4},{9,5},... | collective-permute-start | bytes 442376 | tf_op jit(solution)/shard_map/ppermute | solution.py:288
  99.8 13.0 %collective-permute-start.27 = (bf16[1,18,16,256]{3,2,1,0:T(8,128)(2,1)S(1)}, bf16[1,18,16,256]{3,2,1,0:T(8,128)(2,1)S(1)}, u32[]{:S(2)}, u32[]{:S(2)}) collective-permute-start(bf16[1,18,16,256]{3,2,1,0:T(8,128)(2,1)S(1)} %fusion.3), channel_id=1, source_target_pairs={{0,8},{1,9},{2,10},{3,11},{4,12},{5,13},{6,14},{7,15},{8,0},{9,1},... | collective-permute-start | bytes 442376 | tf_op jit(solution)/shard_map/ppermute | solution.py:288
  99.8 13.0 %collective-permute-start.26 = (bf16[1,18,16,256]{3,2,1,0:T(8,128)(2,1)S(1)}, bf16[1,18,16,256]{3,2,1,0:T(8,128)(2,1)S(1)}, u32[]{:S(2)}, u32[]{:S(2)}) collective-permute-start(bf16[1,18,16,256]{3,2,1,0:T(8,128)(2,1)S(1)} %fusion.3), channel_id=1, source_target_pairs={{0,4},{1,5},{2,6},{3,7},{4,0},{5,1},{6,2},{7,3},{8,12},{9,13},{10,... | collective-permute-start | bytes 442376 | tf_op jit(solution)/shard_map/ppermute | solution.py:288
  112.9 15.1 %collective-permute-start.30 = (bf16[4,18,16,256]{3,2,1,0:T(8,128)(2,1)S(1)}, bf16[4,18,16,256]{3,2,1,0:T(8,128)(2,1)S(1)}, u32[]{:S(2)}, u32[]{:S(2)}) collective-permute-start(bf16[4,18,16,256]{3,2,1,0:T(8,128)(2,1)S(1)} %constant_dynamic-update-slice_fusion), channel_id=1, source_target_pairs={{0,2},{1,3},{2,0},{3,1},{4,6},{5,7},{6,4},{7,5},{8,10},{9,11},{10,... | collective-permute-start | bytes 1769480 | tf_op jit(solution)/shard_map/ppermute | solution.py:288
  113.7 6.1 %collective-permute-start.33 = (bf16[2,9,16,256]{3,2,1,0:T(8,128)(2,1)S(1)}, bf16[2,9,16,256]{3,2,1,0:T(8,128)(2,1)S(1)}, u32[]{:S(2)}, u32[]{:S(2)}) collective-permute-start(bf16[2,9,16,256]{3,2,1,0:T(8,128)(2,1)S(1)} %constant_dynamic-update-slice_fusion.4), channel_id=1, source_target_pairs={{0,12},{1,13},{2,14},{3,15},{4,8},{5,9},{6,10},{7,11},{8,4},{9,5},... | collective-permute-start | bytes 442376 | tf_op jit(solution)/shard_map/ppermute | solution.py:288
  115.9 12.0 %collective-permute-start.32 = (bf16[2,9,16,256]{3,2,1,0:T(8,128)(2,1)S(1)}, bf16[2,9,16,256]{3,2,1,0:T(8,128)(2,1)S(1)}, u32[]{:S(2)}, u32[]{:S(2)}) collective-permute-start(bf16[2,9,16,256]{3,2,1,0:T(8,128)(2,1)S(1)} %constant_dynamic-update-slice_fusion.4), channel_id=1, source_target_pairs={{0,8},{1,9},{2,10},{3,11},{4,12},{5,13},{6,14},{7,15},{8,0},{9,1},... | collective-permute-start | bytes 442376 | tf_op jit(solution)/shard_map/ppermute | solution.py:288
  115.9 12.0 %collective-permute-start.31 = (bf16[2,9,16,256]{3,2,1,0:T(8,128)(2,1)S(1)}, bf16[2,9,16,256]{3,2,1,0:T(8,128)(2,1)S(1)}, u32[]{:S(2)}, u32[]{:S(2)}) collective-permute-start(bf16[2,9,16,256]{3,2,1,0:T(8,128)(2,1)S(1)} %constant_dynamic-update-slice_fusion.4), channel_id=1, source_target_pairs={{0,4},{1,5},{2,6},{3,7},{4,0},{5,1},{6,2},{7,3},{8,12},{9,13},{10,... | collective-permute-start | bytes 442376 | tf_op jit(solution)/shard_map/ppermute | solution.py:288
  128.0 4.7 %collective-permute-start.34 = (bf16[8,18,16,256]{3,2,1,0:T(8,128)(2,1)S(1)}, bf16[8,18,16,256]{3,2,1,0:T(8,128)(2,1)S(1)}, u32[]{:S(2)}, u32[]{:S(2)}) collective-permute-start(bf16[8,18,16,256]{3,2,1,0:T(8,128)(2,1)S(1)} %constant_dynamic-update-slice_fusion.6.one), channel_id=1, source_target_pairs={{0,1},{1,0},{2,3},{3,2},{4,5},{5,4},{6,7},{7,6},{8,9},{9,8},{10,11... | collective-permute-start | bytes 3538952 | tf_op jit(solution)/shard_map/ppermute | solution.py:288
  (27 other events, 195.3 us)

commit v5 on v4

--- a/solution.py
+++ b/solution.py
@@ -14,8 +14,7 @@
 EPSILON = 1e-05
 F32 = jnp.float32
 BF16 = jnp.bfloat16
-LARGE = 58 * 1024 * 1024
-SMALL = 24 * 1024 * 1024
+LIMIT = 24 * 1024 * 1024
 
 
 def merged(merge, values):
@@ -291,28 +290,25 @@
 STAGES = {"c": (1,), "x": (2,), "z": (4, 8, 12)}
 
 
-def split(total, stage):
-    size = total.shape[0] // (len(STAGES[stage]) + 1)
-    sends = [
-        total[(i + 1) * size : (i + 2) * size].astype(BF16) for i in range(len(STAGES[stage]))
-    ]
-    return total[:size], sends
+def part(terms, first, size):
+    return functools.reduce(
+        jnp.add, [term[first : first + size].astype(F32) for term in terms]
+    )
+
+
+def split(terms, stage):
+    partners = STAGES[stage]
+    size = terms[0].shape[0] // (len(partners) + 1)
+    sends = [part(terms, (i + 1) * size, size).astype(BF16) for i in range(len(partners))]
+    return part(terms, 0, size), sends
 
 
 def swapped(sends, stage):
     return [swap(send, by) for send, by in zip(sends, STAGES[stage])]
 
 
-def added(kept, received):
-    return functools.reduce(lambda a, b: a + b.astype(F32), received, kept)
-
-
 def gather_start(piece, stage):
     return [swap(piece, by) for by in STAGES[stage]]
-
-
-def core_reduced(keep, send):
-    return keep + swap(send, 1).astype(F32)
 
 
 def summed_over_devices(one, two, grad_conv, push, spread):
@@ -320,11 +316,14 @@
     parts, grad_conv = lax.optimization_barrier((parts, grad_conv))
     received = [swapped(sends, stage) for (_, sends), stage in zip(parts, "xz")]
     received, sinks = lax.optimization_barrier((received, push(grad_conv)))
-    pieces = [added(kept, got) for (kept, _), got in zip(parts, received)]
-    parts = [split(piece, stage) for piece, stage in zip(pieces, "zx")]
+    parts = [
+        split([kept] + got, stage) for (kept, _), got, stage in zip(parts, received, "zx")
+    ]
+    parts, sinks = lax.optimization_barrier((parts, sinks))
     received = [swapped(sends, stage) for (_, sends), stage in zip(parts, "zx")]
-    received, result = lax.optimization_barrier((received, spread(*sinks)))
-    pieces = [added(kept, got) for (kept, _), got in zip(parts, received)]
+    halo = spread(sinks)
+    received, halo = lax.optimization_barrier((received, halo))
+    pieces = [part([kept] + got, 0, 1) for (kept, _), got in zip(parts, received)]
     by = 16
     while by < lax.axis_size("dp"):
         pieces = [piece + swap(piece, by) for piece in pieces]
@@ -336,7 +335,7 @@
         pieces = [
             jnp.concatenate([piece] + got, axis=0) for piece, got in zip(pieces, received)
         ]
-    return pieces, result
+    return pieces, halo
 
 
 def exchanged(value, merge):
@@ -393,16 +392,19 @@
         pltpu.SemaphoreType.DMA((groups,)),
     ]
 
+    def in_hbm(value):
+        return pltpu.with_memory_space_constraint(value, pltpu.HBM)
+
     inner = pl.pallas_call(
         inner_kernel,
         in_specs=[vmem, vmem, hbm],
         out_specs=vmem,
         out_shape=half_conv,
         scratch_shapes=scratch,
-        compiler_params=params(LARGE),
+        compiler_params=params(LIMIT),
         cost_estimate=cost(work / 2, moved),
         name="conv_inner",
-    )(map_rows, features, weights)
+    )(in_hbm(map_rows), in_hbm(features), in_hbm(weights))
 
     outer, stats, window = pl.pallas_call(
         outer_kernel,
@@ -414,10 +416,10 @@
             jax.ShapeDtypeStruct((rows + 2 * BLOCK, channels), BF16),
         ],
         scratch_shapes=scratch,
-        compiler_params=params(LARGE),
+        compiler_params=params(LIMIT),
         cost_estimate=cost(work / 2, moved),
         name="conv_outer",
-    )(occupancy, odd_flag, map_rows, features, even, other, inner, weights)
+    )(occupancy, odd_flag, map_rows, features, even, other, inner, in_hbm(weights))
 
     stats = exchanged(stats, stacked_moments)
 
@@ -428,7 +430,7 @@
             jax.ShapeDtypeStruct((rows, channels), BF16),
             jax.ShapeDtypeStruct((2, channels), F32),
         ],
-        compiler_params=params(SMALL),
+        compiler_params=params(LIMIT),
         cost_estimate=cost(rows * channels * 20, rows * channels * 10),
         name="norm",
     )(occupancy, inner, outer, gain, shift, cotangent, features, *stats)
@@ -456,7 +458,7 @@
                 pltpu.VMEM(shape, BF16),
                 pltpu.SemaphoreType.DMA((2, count // GROUP)),
             ],
-            compiler_params=params(SMALL),
+            compiler_params=params(LIMIT),
             cost_estimate=cost(work * count / K, count * channels * channels * 6),
             name=name,
         )
@@ -475,11 +477,11 @@
         occupancy, place_one, inner, outer, gain, shift, cotangent, map_rows, window,
         *stats, *grads,
     )
-    one = core_reduced(*pair_one)
+    one = [pair_one[0], swap(pair_one[1], 1)]
     pair_two = gradient(
         second_gradient_kernel, K - K_ONE, [smem] + [vmem] * 3, [], [], "weight_gradient_two"
     )(place_two, grad_conv, map_rows, window)
-    two = core_reduced(*pair_two)
+    two = [pair_two[0], swap(pair_two[1], 1)]
 
     weight_spec = pl.BlockSpec((GROUP, channels, channels), lambda s: (s, 0, 0))
 
@@ -495,29 +497,30 @@
                 jax.ShapeDtypeStruct((BLOCK, channels), BF16),
             ],
             scratch_shapes=[pltpu.VMEM((rows + 2 * BLOCK, channels), F32)],
-            compiler_params=params(SMALL),
-            cost_estimate=cost(work, moved),
+            compiler_params=params(LIMIT),
+            cost_estimate=cost(1000, 1000),
             name="push",
         )(grad_conv, map_rows, weights)
 
-    def spread_gradient(sink_before, sink_own, sink_after):
-        even, other = neighbours_swap(sink_before, sink_after)
-        from_prev = jnp.where(odd == 1, even, other).astype(F32)
-        from_next = jnp.where(odd == 1, other, even).astype(F32)
-        occupied = occupied_rows(occupancy[0], rows)
-        received = jnp.concatenate(
-            [
-                sink_own[:BLOCK] + from_prev,
-                sink_own[BLOCK : rows - BLOCK],
-                sink_own[rows - BLOCK :] + from_next,
-            ],
-            axis=0,
-        )
-        return (jnp.where(occupied, cotangent.astype(F32), 0.0) + received).astype(BF16)
-
-    (own_one, own_two), grad_features = summed_over_devices(
+    def spread_gradient(sinks):
+        sink_before, sink_own, sink_after = sinks
+        return neighbours_swap(sink_before, sink_after), sink_own
+
+    (own_one, own_two), ((even, other), sink_own) = summed_over_devices(
         one, two, grad_conv, push, spread_gradient
     )
+    from_prev = jnp.where(odd == 1, even, other).astype(F32)
+    from_next = jnp.where(odd == 1, other, even).astype(F32)
+    occupied = occupied_rows(occupancy[0], rows)
+    received = jnp.concatenate(
+        [
+            sink_own[:BLOCK] + from_prev,
+            sink_own[BLOCK : rows - BLOCK],
+            sink_own[rows - BLOCK :] + from_next,
+        ],
+        axis=0,
+    )
+    grad_features = (jnp.where(occupied, cotangent.astype(F32), 0.0) + received).astype(BF16)
     places = jnp.concatenate([place_one, place_two])
 
     def placed(other, sources, *into):
@@ -528,7 +531,7 @@
             out_shape=jax.ShapeDtypeStruct(weights.shape, BF16),
             scratch_shapes=[pltpu.SemaphoreType.DMA((16,))],
             input_output_aliases={3: 0} if into else {},
-            compiler_params=params(SMALL),
+            compiler_params=params(LIMIT),
             cost_estimate=cost(0, K * channels * channels * 2),
             name="place",
         )(places, *sources, *into)

time: 136 us -> 129 us (0.949)
  waiting for transfers between devices: 41.8 us -> 33.1 us
  starting transfers between devices: 45.6 us -> 52 us
  local copies, waits for them, and re-layouts: 5.8 us -> 2.81 us
  Pallas kernels: 36 us -> 34 us
    ppermute x32, waiting for transfers between devices: 41.8 us -> 31.4 us  [swap(): return lax.ppermute(value, 'dp', [(i, i ^ by) for i in range(peers)])]
    ppermute x32, starting transfers between devices: 36.7 us -> 43.3 us  [swap(): return lax.ppermute(value, 'dp', [(i, i ^ by) for i in range(peers)])]
    unnamed x36 -> x26, local copies, waits for them, and re-layouts: 4.97 us -> 2.15 us
    ppermute x2, starting transfers between devices: 2.4 us -> 0.07 us  [neighbours_swap(): lax.ppermute(jnp.where(odd == 1, to_before, to_after), 'dp', even_pairs)]
    convert_element_type x1 -> x5, other arithmetic: 0.84 us -> 3.12 us  [the longest x4 2.27 us: split(): part(terms, (i + 1) * size, size).astype(BF16)]
    ppermute x2, starting transfers between devices: 6.51 us -> 8.56 us  [neighbours_swap(): lax.ppermute(jnp.where(odd == 1, to_after, to_before), 'dp', other_pairs)]
    pallas_call x1, Pallas kernels: 6.82 us -> 4.91 us  [per_device(): pl.pallas_call(outer_kernel, in_specs=[smem, smem, vmem, vmem, vmem, vmem...]
  transfers between devices with their start and end apart: 36 -> 36, of which waited for: 18 -> 18; matrix products, arithmetic and copies ran while one was open for 2% -> 1% of each run, Pallas kernels for 15% -> 15%
where the time goes in v5:
time: 129 us; the launch traced here: 128 us
  starting transfers between devices  52 us (40%)
  Pallas kernels  34 us (26%)
  waiting for transfers between devices  33.1 us (26%)
  other arithmetic  4.27 us (3%)
  local copies, waits for them, and re-layouts  2.81 us (2%)
  between operations  1.83 us (1%)
    ppermute x32, starting transfers between devices, swap(): return lax.ppermute(value, 'dp', [(i, i ^ by) for i in range(peers)])  43.3 us
    ppermute x32, waiting for transfers between devices, swap(): return lax.ppermute(value, 'dp', [(i, i ^ by) for i in range(peers)])  31.4 us
    pallas_call x1, Pallas kernels, push(): pl.pallas_call(push_kernel, grid=(groups,), in_specs=[full((rows, channel...  9.26 us
    ppermute x2, starting transfers between devices, neighbours_swap(): lax.ppermute(jnp.where(odd == 1, to_after, to_before), 'dp', other_pairs)  8.56 us
    pallas_call x1, Pallas kernels, per_device(): gradient(functools.partial(first_gradient_kernel, len(stats)), K_ONE, [sm...  6.37 us
    pallas_call x1, Pallas kernels, per_device(): pl.pallas_call(inner_kernel, in_specs=[vmem, vmem, hbm], out_specs=vmem,...  5.73 us
    pallas_call x1, Pallas kernels, per_device(): pl.pallas_call(outer_kernel, in_specs=[smem, smem, vmem, vmem, vmem, vmem...  4.91 us
    pallas_call x2, Pallas kernels, placed(): pl.pallas_call(functools.partial(place_kernel, other), in_specs=[smem, an...  3.76 us
  transfers between devices with their start and end apart: 36, of which 18 were waited for; matrix products, arithmetic and copies ran while one was open for 1% of the time, Pallas kernels for 15%

profile of v5, /device:TPU:1, one launch (start us, length us, event | category | flops | bytes accessed | tf_op | source)
XLA Modules:
  0.0 127.9 jit_solution(18225431609108135371)
XLA Ops:
  1.5 4.5 %collective-permute-start.1 = (bf16[128,256]{1,0:T(8,128)(2,1)S(1)}, bf16[128,256]{1,0:T(8,128)(2,1)S(1)}, u32[]{:S(2)}, u32[]{:S(2)}) collective-permute-start(bf16[128,256]{1,0:T(8,128)(2,1)S(1)} %get-tuple-element.133), channel_id=1, source_target_pairs={{1,2},{2,1},{3,4},{4,3},{5,6},{6,5},{7,8},{8,7},{9,10},{10,9},{11,... | collective-permute-start | bytes 196616 | tf_op jit(solution)/shard_map/ppermute | solution.py:369
  6.1 5.7 %conv_inner.1.inner_ref = f32[256,256]{1,0:T(8,128)S(1)} custom-call(s32[27,512]{1,0:T(8,128)} %bitcast.9, bf16[512,256]{1,0:T(8,128)(2,1)} %feature_ref.1, bf16[27,256,256]{2,1,0:T(8,128)(2,1)} %weight_ref.1), custom_call_target="tpu_custom_call" | custom-call | flops 2264924160 | bytes 10616832 | tf_op jit(solution)/shard_map/conv_inner/pallas_call | solution.py:398
  12.6 4.9 %conv_outer.1 = (f32[256,256]{1,0:T(8,128)S(1)}, f32[3,256]{1,0:T(4,128)S(1)}, bf16[768,256]{1,0:T(8,128)(2,1)S(1)}) custom-call(s32[1]{0:T(128)S(6)} %copy.22.filled_ref, s32[1]{0:T(128)} %bitcast.1.odd_ref, s32[27,512]{1,0:T(8,128)S(1)} %bitcast.10, bf16[512,256]{1,0:T(8,128)(2,1)S(1)} %copy-done.2, bf16[128,256]{1,0:T(8,128)(2,1)S(1)} %collective-permute-done.even_ref, ...), custom_call_target="tpu_custom_call" | custom-call | flops 2264924160 | bytes 10616832 | tf_op jit(solution)/shard_map/conv_outer/pallas_call | solution.py:409
  21.7 2.4 %collective-permute-start.7 = (f32[3,256]{1,0:T(4,128)S(1)}, f32[3,256]{1,0:T(4,128)S(1)}, u32[]{:S(2)}, u32[]{:S(2)}) collective-permute-start(f32[3,256]{1,0:T(4,128)S(1)} %pad_maximum_fusion.refs_0_), channel_id=1, source_target_pairs={{0,12},{1,13},{2,14},{3,15},{4,8},{5,9},{6,10},{7,11},{8,4},{9,5},... | collective-permute-start | bytes 9224 | tf_op jit(solution)/shard_map/ppermute | solution.py:287
  28.8 3.4 %collective-permute-start.10 = (f32[2,256]{1,0:T(2,128)S(1)}, f32[2,256]{1,0:T(2,128)S(1)}, u32[]{:S(2)}, u32[]{:S(2)}) collective-permute-start(f32[2,256]{1,0:T(2,128)S(1)} %get-tuple-element.65), channel_id=1, source_target_pairs={{0,3},{1,2},{2,1},{3,0},{4,7},{5,6},{6,5},{7,4},{8,11},{9,10},{10,... | collective-permute-start | bytes 6152 | tf_op jit(solution)/shard_map/ppermute | solution.py:287
  40.7 6.4 %weight_gradient_one.1 = (bf16[512,256]{1,0:T(8,128)(2,1)S(1)}, f32[2,256]{1,0:T(2,128)S(1)}, f32[8,18,16,256]{3,2,1,0:T(8,128)S(1)}, bf16[8,18,16,256]{3,2,1,0:T(8,128)(2,1)}) custom-call(s32[1]{0:T(128)S(6)} %copy.22.filled_ref, s32[1]{0:T(128)} %bitcast.5.place_ref, f32[256,256]{1,0:T(8,128)S(1)} %conv_inner.1.inner_ref, ...), custom_call_target="tpu_custom_call" | custom-call | flops 3019898880 | bytes 7077888 | tf_op jit(solution)/shard_map/weight_gradient_one/pallas_call | solution.py:466
  49.7 2.9 %weight_gradient_two.1 = (f32[8,9,16,256]{3,2,1,0:T(8,128)S(1)}, bf16[8,9,16,256]{3,2,1,0:T(8,128)(2,1)S(1)}) custom-call(s32[1]{0:T(128)} %bitcast.6.place_ref, bf16[512,256]{1,0:T(8,128)(2,1)S(1)} %get-tuple-element.76.grad_ref, s32[27,512]{1,0:T(8,128)S(1)} %bitcast.12, bf16[768,256]{1,0:T(8,128)(2,1)S(1)} %copy-done.8), custom_call_target="tpu_custom_call" | custom-call | flops 1509949440 | bytes 3538944 | tf_op jit(solution)/shard_map/weight_gradient_two/pallas_call | solution.py:481
  52.8 2.0 %collective-permute-done.15 = bf16[8,9,16,256]{3,2,1,0:T(8,128)(2,1)S(1)} collective-permute-done((bf16[8,9,16,256]{3,2,1,0:T(8,128)(2,1)S(1)}, bf16[8,9,16,256]{3,2,1,0:T(8,128)(2,1)S(1)}, u32[]{:S(2)}, u32[]{:S(2)}) %collective-permute-start.15) | collective-permute-done | bytes 589856 | tf_op jit(solution)/shard_map/ppermute | solution.py:287
  61.4 9.3 %push.1 = (bf16[128,256]{1,0:T(8,128)(2,1)S(1)}, f32[512,256]{1,0:T(8,128)S(1)}, bf16[128,256]{1,0:T(8,128)(2,1)S(1)}) custom-call(bf16[512,256]{1,0:T(8,128)(2,1)S(1)} %get-tuple-element.76.grad_ref, s32[27,512]{1,0:T(8,128)S(1)} %bitcast.13, bf16[27,256,256]{2,1,0:T(8,128)(2,1)S(1)} %copy-done), custom_call_target="tpu_custom_call" | custom-call | flops 1000 | bytes 1000 | tf_op jit(solution)/shard_map/push/pallas_call | solution.py:489
  71.9 3.1 %collective-permute-start.20 = (bf16[1,18,16,256]{3,2,1,0:T(8,128)(2,1)S(1)}, bf16[1,18,16,256]{3,2,1,0:T(8,128)(2,1)S(1)}, u32[]{:S(2)}, u32[]{:S(2)}) collective-permute-start(bf16[1,18,16,256]{3,2,1,0:T(8,128)(2,1)S(1)} %get-tuple-element.88), channel_id=1, source_target_pairs={{0,4},{1,5},{2,6},{3,7},{4,0},{5,1},{6,2},{7,3},{8,12},{9,13},{10,... | collective-permute-start | bytes 442376 | tf_op jit(solution)/shard_map/ppermute | solution.py:287
  75.2 2.1 %collective-permute-start.22 = (bf16[1,18,16,256]{3,2,1,0:T(8,128)(2,1)S(1)}, bf16[1,18,16,256]{3,2,1,0:T(8,128)(2,1)S(1)}, u32[]{:S(2)}, u32[]{:S(2)}) collective-permute-start(bf16[1,18,16,256]{3,2,1,0:T(8,128)(2,1)S(1)} %get-tuple-element.90), channel_id=1, source_target_pairs={{0,12},{1,13},{2,14},{3,15},{4,8},{5,9},{6,10},{7,11},{8,4},{9,5},... | collective-permute-start | bytes 442376 | tf_op jit(solution)/shard_map/ppermute | solution.py:287
  77.3 4.0 %collective-permute-start.25 = (bf16[128,256]{1,0:T(8,128)(2,1)S(1)}, bf16[128,256]{1,0:T(8,128)(2,1)S(1)}, u32[]{:S(2)}, u32[]{:S(2)}) collective-permute-start(bf16[128,256]{1,0:T(8,128)(2,1)S(1)} %get-tuple-element.135), channel_id=1, source_target_pairs={{1,2},{2,1},{3,4},{4,3},{5,6},{6,5},{7,8},{8,7},{9,10},{10,9},{11,... | collective-permute-start | bytes 196616 | tf_op jit(solution)/shard_map/ppermute | solution.py:369
  81.3 1.8 %collective-permute-start.23 = (bf16[1,9,16,256]{3,2,1,0:T(8,128)(2,1)S(1)}, bf16[1,9,16,256]{3,2,1,0:T(8,128)(2,1)S(1)}, u32[]{:S(2)}, u32[]{:S(2)}) collective-permute-start(bf16[1,9,16,256]{3,2,1,0:T(8,128)(2,1)S(1)} %get-tuple-element.91), channel_id=1, source_target_pairs={{0,2},{1,3},{2,0},{3,1},{4,6},{5,7},{6,4},{7,5},{8,10},{9,11},{10,... | collective-permute-start | bytes 221192 | tf_op jit(solution)/shard_map/ppermute | solution.py:287
  85.2 1.8 %collective-permute-done.21 = bf16[1,18,16,256]{3,2,1,0:T(8,128)(2,1)S(1)} collective-permute-done((bf16[1,18,16,256]{3,2,1,0:T(8,128)(2,1)S(1)}, bf16[1,18,16,256]{3,2,1,0:T(8,128)(2,1)S(1)}, u32[]{:S(2)}, u32[]{:S(2)}) %collective-permute-start.21) | collective-permute-done | bytes 147488 | tf_op jit(solution)/shard_map/ppermute | solution.py:287
  88.7 6.7 %collective-permute-start.27 = (bf16[1,18,16,256]{3,2,1,0:T(8,128)(2,1)S(1)}, bf16[1,18,16,256]{3,2,1,0:T(8,128)(2,1)S(1)}, u32[]{:S(2)}, u32[]{:S(2)}) collective-permute-start(bf16[1,18,16,256]{3,2,1,0:T(8,128)(2,1)S(1)} %add_convert_fusion.1), channel_id=1, source_target_pairs={{0,8},{1,9},{2,10},{3,11},{4,12},{5,13},{6,14},{7,15},{8,0},{9,1},... | collective-permute-start | bytes 442376 | tf_op jit(solution)/shard_map/ppermute | solution.py:287
  95.6 1.9 %collective-permute-start.29 = (bf16[1,9,16,256]{3,2,1,0:T(8,128)(2,1)S(1)}, bf16[1,9,16,256]{3,2,1,0:T(8,128)(2,1)S(1)}, u32[]{:S(2)}, u32[]{:S(2)}) collective-permute-start(bf16[1,9,16,256]{3,2,1,0:T(8,128)(2,1)S(1)} %add_convert_fusion.8), channel_id=1, source_target_pairs={{0,2},{1,3},{2,0},{3,1},{4,6},{5,7},{6,4},{7,5},{8,10},{9,11},{10,... | collective-permute-start | bytes 221192 | tf_op jit(solution)/shard_map/ppermute | solution.py:287
  97.5 2.0 %collective-permute-done.29 = bf16[1,9,16,256]{3,2,1,0:T(8,128)(2,1)S(1)} collective-permute-done((bf16[1,9,16,256]{3,2,1,0:T(8,128)(2,1)S(1)}, bf16[1,9,16,256]{3,2,1,0:T(8,128)(2,1)S(1)}, u32[]{:S(2)}, u32[]{:S(2)}) %collective-permute-start.29) | collective-permute-done | bytes 73760 | tf_op jit(solution)/shard_map/ppermute | solution.py:287
  99.5 6.0 %collective-permute-done.27 = bf16[1,18,16,256]{3,2,1,0:T(8,128)(2,1)S(1)} collective-permute-done((bf16[1,18,16,256]{3,2,1,0:T(8,128)(2,1)S(1)}, bf16[1,18,16,256]{3,2,1,0:T(8,128)(2,1)S(1)}, u32[]{:S(2)}, u32[]{:S(2)}) %collective-permute-start.27) | collective-permute-done | bytes 147488 | tf_op jit(solution)/shard_map/ppermute | solution.py:287
  105.6 2.0 %collective-permute-start.30 = (bf16[4,18,16,256]{3,2,1,0:T(8,128)(2,1)S(1)}, bf16[4,18,16,256]{3,2,1,0:T(8,128)(2,1)S(1)}, u32[]{:S(2)}, u32[]{:S(2)}) collective-permute-start(bf16[4,18,16,256]{3,2,1,0:T(8,128)(2,1)S(1)} %constant_dynamic-update-slice_fusion), channel_id=1, source_target_pairs={{0,2},{1,3},{2,0},{3,1},{4,6},{5,7},{6,4},{7,5},{8,10},{9,11},{10,... | collective-permute-start | bytes 1769480 | tf_op jit(solution)/shard_map/ppermute | solution.py:287
  108.9 2.4 %collective-permute-start.31 = (bf16[2,9,16,256]{3,2,1,0:T(8,128)(2,1)S(1)}, bf16[2,9,16,256]{3,2,1,0:T(8,128)(2,1)S(1)}, u32[]{:S(2)}, u32[]{:S(2)}) collective-permute-start(bf16[2,9,16,256]{3,2,1,0:T(8,128)(2,1)S(1)} %constant_dynamic-update-slice_fusion.4), channel_id=1, source_target_pairs={{0,4},{1,5},{2,6},{3,7},{4,0},{5,1},{6,2},{7,3},{8,12},{9,13},{10,... | collective-permute-start | bytes 442376 | tf_op jit(solution)/shard_map/ppermute | solution.py:287
  111.4 2.4 %collective-permute-done.33 = bf16[2,9,16,256]{3,2,1,0:T(8,128)(2,1)S(1)} collective-permute-done((bf16[2,9,16,256]{3,2,1,0:T(8,128)(2,1)S(1)}, bf16[2,9,16,256]{3,2,1,0:T(8,128)(2,1)S(1)}, u32[]{:S(2)}, u32[]{:S(2)}) %collective-permute-start.33) | collective-permute-done | bytes 147488 | tf_op jit(solution)/shard_map/ppermute | solution.py:287
  113.8 7.9 %collective-permute-done.32 = bf16[2,9,16,256]{3,2,1,0:T(8,128)(2,1)S(1)} collective-permute-done((bf16[2,9,16,256]{3,2,1,0:T(8,128)(2,1)S(1)}, bf16[2,9,16,256]{3,2,1,0:T(8,128)(2,1)S(1)}, u32[]{:S(2)}, u32[]{:S(2)}) %collective-permute-start.32) | collective-permute-done | bytes 147488 | tf_op jit(solution)/shard_map/ppermute | solution.py:287
  124.0 1.9 %place.2.refs_0_ = bf16[27,256,256]{2,1,0:T(8,128)(2,1)} custom-call(s32[2]{0:T(128)S(1)} %pad_add_fusion.places_ref, bf16[8,18,16,256]{3,2,1,0:T(8,128)(2,1)S(1)} %constant_dynamic-update-slice_fusion.6.one, bf16[8,9,16,256]{3,2,1,0:T(8,128)(2,1)S(1)} %constant_dynamic-update-slice_fusion.8.two), custom_call_target="tpu_custom_call" | custom-call | bytes 3538944 | tf_op jit(solution)/shard_map/place/pallas_call | solution.py:527
  125.9 1.9 %place.3 = bf16[27,256,256]{2,1,0:T(8,128)(2,1)} custom-call(s32[2]{0:T(128)S(1)} %pad_add_fusion.places_ref, bf16[8,18,16,256]{3,2,1,0:T(8,128)(2,1)S(1)} %collective-permute-done.34.one, bf16[8,9,16,256]{3,2,1,0:T(8,128)(2,1)S(1)} %collective-permute-done.35.two, bf16[27,256,256]{2,1,0:T(8,128)(2,1)} %place.2.refs_0_), custom_call_target="tpu_custom_call", output_to_operand_aliasing={{}: (3, {})} | custom-call | bytes 3538944 | tf_op jit(solution)/shard_map/place/pallas_call | solution.py:527
  (103 shorter events, 36.5 us)
Async XLA Ops:
  1.5 11.0 %collective-permute-start.1 = (bf16[128,256]{1,0:T(8,128)(2,1)S(1)}, bf16[128,256]{1,0:T(8,128)(2,1)S(1)}, u32[]{:S(2)}, u32[]{:S(2)}) collective-permute-start(bf16[128,256]{1,0:T(8,128)(2,1)S(1)} %get-tuple-element.133), channel_id=1, source_target_pairs={{1,2},{2,1},{3,4},{4,3},{5,6},{6,5},{7,8},{8,7},{9,10},{10,9},{11,... | collective-permute-start | bytes 196616 | tf_op jit(solution)/shard_map/ppermute | solution.py:369
  6.0 6.5 %collective-permute-start = (bf16[128,256]{1,0:T(8,128)(2,1)S(1)}, bf16[128,256]{1,0:T(8,128)(2,1)S(1)}, u32[]{:S(2)}, u32[]{:S(2)}) collective-permute-start(bf16[128,256]{1,0:T(8,128)(2,1)S(1)} %get-tuple-element.134), channel_id=1, source_target_pairs={{0,1},{1,0},{2,3},{3,2},{4,5},{5,4},{6,7},{7,6},{8,9},{9,8},{10,11... | collective-permute-start | bytes 196616 | tf_op jit(solution)/shard_map/ppermute | solution.py:368
  21.7 4.3 %collective-permute-start.7 = (f32[3,256]{1,0:T(4,128)S(1)}, f32[3,256]{1,0:T(4,128)S(1)}, u32[]{:S(2)}, u32[]{:S(2)}) collective-permute-start(f32[3,256]{1,0:T(4,128)S(1)} %pad_maximum_fusion.refs_0_), channel_id=1, source_target_pairs={{0,12},{1,13},{2,14},{3,15},{4,8},{5,9},{6,10},{7,11},{8,4},{9,5},... | collective-permute-start | bytes 9224 | tf_op jit(solution)/shard_map/ppermute | solution.py:287
  28.8 4.8 %collective-permute-start.10 = (f32[2,256]{1,0:T(2,128)S(1)}, f32[2,256]{1,0:T(2,128)S(1)}, u32[]{:S(2)}, u32[]{:S(2)}) collective-permute-start(f32[2,256]{1,0:T(2,128)S(1)} %get-tuple-element.65), channel_id=1, source_target_pairs={{0,3},{1,2},{2,1},{3,0},{4,7},{5,6},{6,5},{7,4},{8,11},{9,10},{10,... | collective-permute-start | bytes 6152 | tf_op jit(solution)/shard_map/ppermute | solution.py:287
  34.6 4.3 %collective-permute-start.13 = (f32[2,256]{1,0:T(2,128)S(1)}, f32[2,256]{1,0:T(2,128)S(1)}, u32[]{:S(2)}, u32[]{:S(2)}) collective-permute-start(f32[2,256]{1,0:T(2,128)S(1)} %add_add_fusion.refs_4_), channel_id=1, source_target_pairs={{0,12},{1,13},{2,14},{3,15},{4,8},{5,9},{6,10},{7,11},{8,4},{9,5},... | collective-permute-start | bytes 6152 | tf_op jit(solution)/shard_map/ppermute | solution.py:287
  47.1 7.9 %collective-permute-start.14 = (bf16[8,18,16,256]{3,2,1,0:T(8,128)(2,1)}, bf16[8,18,16,256]{3,2,1,0:T(8,128)(2,1)}, u32[]{:S(2)}, u32[]{:S(2)}) collective-permute-start(bf16[8,18,16,256]{3,2,1,0:T(8,128)(2,1)} %get-tuple-element.67), channel_id=1, source_target_pairs={{0,1},{1,0},{2,3},{3,2},{4,5},{5,4},{6,7},{7,6},{8,9},{9,8},{10,11... | collective-permute-start | bytes 3538952 | tf_op jit(solution)/shard_map/ppermute | solution.py:287
  56.8 14.9 %collective-permute-start.16 = (bf16[4,18,16,256]{3,2,1,0:T(8,128)(2,1)S(1)}, bf16[4,18,16,256]{3,2,1,0:T(8,128)(2,1)S(1)}, u32[]{:S(2)}, u32[]{:S(2)}) collective-permute-start(bf16[4,18,16,256]{3,2,1,0:T(8,128)(2,1)S(1)} %get-tuple-element.72), channel_id=1, source_target_pairs={{0,2},{1,3},{2,0},{3,1},{4,6},{5,7},{6,4},{7,5},{8,10},{9,11},{10,... | collective-permute-start | bytes 1769480 | tf_op jit(solution)/shard_map/ppermute | solution.py:287
  57.6 13.1 %collective-permute-start.17 = (bf16[2,9,16,256]{3,2,1,0:T(8,128)(2,1)S(1)}, bf16[2,9,16,256]{3,2,1,0:T(8,128)(2,1)S(1)}, u32[]{:S(2)}, u32[]{:S(2)}) collective-permute-start(bf16[2,9,16,256]{3,2,1,0:T(8,128)(2,1)S(1)} %get-tuple-element.73), channel_id=1, source_target_pairs={{0,4},{1,5},{2,6},{3,7},{4,0},{5,1},{6,2},{7,3},{8,12},{9,13},{10,... | collective-permute-start | bytes 442376 | tf_op jit(solution)/shard_map/ppermute | solution.py:287
  59.3 11.4 %collective-permute-start.18 = (bf16[2,9,16,256]{3,2,1,0:T(8,128)(2,1)S(1)}, bf16[2,9,16,256]{3,2,1,0:T(8,128)(2,1)S(1)}, u32[]{:S(2)}, u32[]{:S(2)}) collective-permute-start(bf16[2,9,16,256]{3,2,1,0:T(8,128)(2,1)S(1)} %get-tuple-element.74), channel_id=1, source_target_pairs={{0,8},{1,9},{2,10},{3,11},{4,12},{5,13},{6,14},{7,15},{8,0},{9,1},... | collective-permute-start | bytes 442376 | tf_op jit(solution)/shard_map/ppermute | solution.py:287
  60.1 10.5 %collective-permute-start.19 = (bf16[2,9,16,256]{3,2,1,0:T(8,128)(2,1)S(1)}, bf16[2,9,16,256]{3,2,1,0:T(8,128)(2,1)S(1)}, u32[]{:S(2)}, u32[]{:S(2)}) collective-permute-start(bf16[2,9,16,256]{3,2,1,0:T(8,128)(2,1)S(1)} %get-tuple-element.75), channel_id=1, source_target_pairs={{0,12},{1,13},{2,14},{3,15},{4,8},{5,9},{6,10},{7,11},{8,4},{9,5},... | collective-permute-start | bytes 442376 | tf_op jit(solution)/shard_map/ppermute | solution.py:287
  71.9 13.2 %collective-permute-start.20 = (bf16[1,18,16,256]{3,2,1,0:T(8,128)(2,1)S(1)}, bf16[1,18,16,256]{3,2,1,0:T(8,128)(2,1)S(1)}, u32[]{:S(2)}, u32[]{:S(2)}) collective-permute-start(bf16[1,18,16,256]{3,2,1,0:T(8,128)(2,1)S(1)} %get-tuple-element.88), channel_id=1, source_target_pairs={{0,4},{1,5},{2,6},{3,7},{4,0},{5,1},{6,2},{7,3},{8,12},{9,13},{10,... | collective-permute-start | bytes 442376 | tf_op jit(solution)/shard_map/ppermute | solution.py:287
  75.1 11.9 %collective-permute-start.21 = (bf16[1,18,16,256]{3,2,1,0:T(8,128)(2,1)S(1)}, bf16[1,18,16,256]{3,2,1,0:T(8,128)(2,1)S(1)}, u32[]{:S(2)}, u32[]{:S(2)}) collective-permute-start(bf16[1,18,16,256]{3,2,1,0:T(8,128)(2,1)S(1)} %get-tuple-element.89), channel_id=1, source_target_pairs={{0,8},{1,9},{2,10},{3,11},{4,12},{5,13},{6,14},{7,15},{8,0},{9,1},... | collective-permute-start | bytes 442376 | tf_op jit(solution)/shard_map/ppermute | solution.py:287
  75.2 11.9 %collective-permute-start.22 = (bf16[1,18,16,256]{3,2,1,0:T(8,128)(2,1)S(1)}, bf16[1,18,16,256]{3,2,1,0:T(8,128)(2,1)S(1)}, u32[]{:S(2)}, u32[]{:S(2)}) collective-permute-start(bf16[1,18,16,256]{3,2,1,0:T(8,128)(2,1)S(1)} %get-tuple-element.90), channel_id=1, source_target_pairs={{0,12},{1,13},{2,14},{3,15},{4,8},{5,9},{6,10},{7,11},{8,4},{9,5},... | collective-permute-start | bytes 442376 | tf_op jit(solution)/shard_map/ppermute | solution.py:287
  77.3 6.3 %collective-permute-start.25 = (bf16[128,256]{1,0:T(8,128)(2,1)S(1)}, bf16[128,256]{1,0:T(8,128)(2,1)S(1)}, u32[]{:S(2)}, u32[]{:S(2)}) collective-permute-start(bf16[128,256]{1,0:T(8,128)(2,1)S(1)} %get-tuple-element.135), channel_id=1, source_target_pairs={{1,2},{2,1},{3,4},{4,3},{5,6},{6,5},{7,8},{8,7},{9,10},{10,9},{11,... | collective-permute-start | bytes 196616 | tf_op jit(solution)/shard_map/ppermute | solution.py:369
  81.3 3.9 %collective-permute-start.23 = (bf16[1,9,16,256]{3,2,1,0:T(8,128)(2,1)S(1)}, bf16[1,9,16,256]{3,2,1,0:T(8,128)(2,1)S(1)}, u32[]{:S(2)}, u32[]{:S(2)}) collective-permute-start(bf16[1,9,16,256]{3,2,1,0:T(8,128)(2,1)S(1)} %get-tuple-element.91), channel_id=1, source_target_pairs={{0,2},{1,3},{2,0},{3,1},{4,6},{5,7},{6,4},{7,5},{8,10},{9,11},{10,... | collective-permute-start | bytes 221192 | tf_op jit(solution)/shard_map/ppermute | solution.py:287
  87.1 12.4 %collective-permute-start.28 = (bf16[1,18,16,256]{3,2,1,0:T(8,128)(2,1)S(1)}, bf16[1,18,16,256]{3,2,1,0:T(8,128)(2,1)S(1)}, u32[]{:S(2)}, u32[]{:S(2)}) collective-permute-start(bf16[1,18,16,256]{3,2,1,0:T(8,128)(2,1)S(1)} %add_convert_fusion.1), channel_id=1, source_target_pairs={{0,12},{1,13},{2,14},{3,15},{4,8},{5,9},{6,10},{7,11},{8,4},{9,5},... | collective-permute-start | bytes 442376 | tf_op jit(solution)/shard_map/ppermute | solution.py:287
  88.7 16.9 %collective-permute-start.27 = (bf16[1,18,16,256]{3,2,1,0:T(8,128)(2,1)S(1)}, bf16[1,18,16,256]{3,2,1,0:T(8,128)(2,1)S(1)}, u32[]{:S(2)}, u32[]{:S(2)}) collective-permute-start(bf16[1,18,16,256]{3,2,1,0:T(8,128)(2,1)S(1)} %add_convert_fusion.1), channel_id=1, source_target_pairs={{0,8},{1,9},{2,10},{3,11},{4,12},{5,13},{6,14},{7,15},{8,0},{9,1},... | collective-permute-start | bytes 442376 | tf_op jit(solution)/shard_map/ppermute | solution.py:287
  95.4 10.2 %collective-permute-start.26 = (bf16[1,18,16,256]{3,2,1,0:T(8,128)(2,1)S(1)}, bf16[1,18,16,256]{3,2,1,0:T(8,128)(2,1)S(1)}, u32[]{:S(2)}, u32[]{:S(2)}) collective-permute-start(bf16[1,18,16,256]{3,2,1,0:T(8,128)(2,1)S(1)} %add_convert_fusion.1), channel_id=1, source_target_pairs={{0,4},{1,5},{2,6},{3,7},{4,0},{5,1},{6,2},{7,3},{8,12},{9,13},{10,... | collective-permute-start | bytes 442376 | tf_op jit(solution)/shard_map/ppermute | solution.py:287
  95.6 3.9 %collective-permute-start.29 = (bf16[1,9,16,256]{3,2,1,0:T(8,128)(2,1)S(1)}, bf16[1,9,16,256]{3,2,1,0:T(8,128)(2,1)S(1)}, u32[]{:S(2)}, u32[]{:S(2)}) collective-permute-start(bf16[1,9,16,256]{3,2,1,0:T(8,128)(2,1)S(1)} %add_convert_fusion.8), channel_id=1, source_target_pairs={{0,2},{1,3},{2,0},{3,1},{4,6},{5,7},{6,4},{7,5},{8,10},{9,11},{10,... | collective-permute-start | bytes 221192 | tf_op jit(solution)/shard_map/ppermute | solution.py:287
  105.6 16.0 %collective-permute-start.30 = (bf16[4,18,16,256]{3,2,1,0:T(8,128)(2,1)S(1)}, bf16[4,18,16,256]{3,2,1,0:T(8,128)(2,1)S(1)}, u32[]{:S(2)}, u32[]{:S(2)}) collective-permute-start(bf16[4,18,16,256]{3,2,1,0:T(8,128)(2,1)S(1)} %constant_dynamic-update-slice_fusion), channel_id=1, source_target_pairs={{0,2},{1,3},{2,0},{3,1},{4,6},{5,7},{6,4},{7,5},{8,10},{9,11},{10,... | collective-permute-start | bytes 1769480 | tf_op jit(solution)/shard_map/ppermute | solution.py:287
  107.7 6.1 %collective-permute-start.33 = (bf16[2,9,16,256]{3,2,1,0:T(8,128)(2,1)S(1)}, bf16[2,9,16,256]{3,2,1,0:T(8,128)(2,1)S(1)}, u32[]{:S(2)}, u32[]{:S(2)}) collective-permute-start(bf16[2,9,16,256]{3,2,1,0:T(8,128)(2,1)S(1)} %constant_dynamic-update-slice_fusion.4), channel_id=1, source_target_pairs={{0,12},{1,13},{2,14},{3,15},{4,8},{5,9},{6,10},{7,11},{8,4},{9,5},... | collective-permute-start | bytes 442376 | tf_op jit(solution)/shard_map/ppermute | solution.py:287
  108.9 12.8 %collective-permute-start.32 = (bf16[2,9,16,256]{3,2,1,0:T(8,128)(2,1)S(1)}, bf16[2,9,16,256]{3,2,1,0:T(8,128)(2,1)S(1)}, u32[]{:S(2)}, u32[]{:S(2)}) collective-permute-start(bf16[2,9,16,256]{3,2,1,0:T(8,128)(2,1)S(1)} %constant_dynamic-update-slice_fusion.4), channel_id=1, source_target_pairs={{0,8},{1,9},{2,10},{3,11},{4,12},{5,13},{6,14},{7,15},{8,0},{9,1},... | collective-permute-start | bytes 442376 | tf_op jit(solution)/shard_map/ppermute | solution.py:287
  108.9 12.8 %collective-permute-start.31 = (bf16[2,9,16,256]{3,2,1,0:T(8,128)(2,1)S(1)}, bf16[2,9,16,256]{3,2,1,0:T(8,128)(2,1)S(1)}, u32[]{:S(2)}, u32[]{:S(2)}) collective-permute-start(bf16[2,9,16,256]{3,2,1,0:T(8,128)(2,1)S(1)} %constant_dynamic-update-slice_fusion.4), channel_id=1, source_target_pairs={{0,4},{1,5},{2,6},{3,7},{4,0},{5,1},{6,2},{7,3},{8,12},{9,13},{10,... | collective-permute-start | bytes 442376 | tf_op jit(solution)/shard_map/ppermute | solution.py:287
  121.8 4.1 %collective-permute-start.34 = (bf16[8,18,16,256]{3,2,1,0:T(8,128)(2,1)S(1)}, bf16[8,18,16,256]{3,2,1,0:T(8,128)(2,1)S(1)}, u32[]{:S(2)}, u32[]{:S(2)}) collective-permute-start(bf16[8,18,16,256]{3,2,1,0:T(8,128)(2,1)S(1)} %constant_dynamic-update-slice_fusion.6.one), channel_id=1, source_target_pairs={{0,1},{1,0},{2,3},{3,2},{4,5},{5,4},{6,7},{7,6},{8,9},{9,8},{10,11... | collective-permute-start | bytes 3538952 | tf_op jit(solution)/shard_map/ppermute | solution.py:287
  (21 other events, 118.9 us)

commit v6 on v5

--- a/solution.py
+++ b/solution.py
@@ -10,7 +10,8 @@
 K = 27
 BLOCK = 128
 GROUP = 9
-K_ONE = 18
+HALF = 13
+K_ONE = 9
 EPSILON = 1e-05
 F32 = jnp.float32
 BF16 = jnp.bfloat16
@@ -157,53 +158,10 @@
     )
 
 
-def kernel_gradient(first, place, map_ref, window_ref, grad, keep_any, send_any, scratch):
-    index, picked, product, keep, send, out_sem = scratch
-    half, count, rows = keep.shape[:3]
-    index[...] = transposed_map(map_ref)
-    slots = lax.broadcasted_iota(jnp.int32, (BLOCK, 3 * BLOCK), 1)
-
-    def store(g):
-        here = pl.ds(g * GROUP, GROUP)
-        return [
-            pltpu.make_async_copy(keep.at[:, here], keep_any.at[:, here], out_sem.at[0, g]),
-            pltpu.make_async_copy(send.at[:, here], send_any.at[:, here], out_sem.at[1, g]),
-        ]
-
-    def group(g, carry):
-        local = pltpu.roll(index[...], lax.rem(BLOCK - first - g * GROUP, BLOCK), 1)
-        for j in range(GROUP):
-            for b in range(grad.shape[0] // BLOCK):
-                here = slice(b * BLOCK, (b + 1) * BLOCK)
-                slot = local[here, j : j + 1] - (grad.shape[0] + (b - 1) * BLOCK)
-                tile = window_ref[b * BLOCK : (b + 3) * BLOCK, :]
-                chosen = chosen_slots(slot, slots)
-                picked[j, here, :] = dot(chosen, tile, ((1,), (0,))).astype(BF16)
-        for j in range(GROUP):
-            product[j] = dot(picked[j], grad[...], ((0,), (0,)))
-            for piece in range(16):
-                start = pl.multiple_of(lax.bitwise_xor(jnp.int32(piece), place) * rows, rows)
-                value = product[j, pl.ds(start, rows), :]
-                if piece < half:
-                    keep[piece, g * GROUP + j] = value
-                else:
-                    send[piece - half, g * GROUP + j] = value.astype(BF16)
-        for copy in store(g):
-            copy.start()
-        return carry
-
-    lax.fori_loop(0, count // GROUP, group, 0)
-    for g in range(count // GROUP):
-        for copy in store(g):
-            copy.wait()
-
-
-def first_gradient_kernel(
-    parts, filled_ref, place_ref, inner_ref, outer_ref, gain_ref, shift_ref, cotangent_ref,
-    map_ref, window_ref, *refs,
+def grad_conv_kernel(
+    parts, filled_ref, inner_ref, outer_ref, gain_ref, shift_ref, cotangent_ref, *refs
 ):
-    stats_refs, grads_refs, refs = refs[:parts], refs[parts : 2 * parts], refs[2 * parts :]
-    grad_ref, sums_ref, keep_any, send_any, *scratch = refs
+    stats_refs, grads_refs, (grad_ref, sums_ref) = refs[:parts], refs[parts:-2], refs[-2:]
     occupied, normed, _, upstream, inverse, total = normalised(
         filled_ref[0], inner_ref, outer_ref, stats_refs, gain_ref, shift_ref, cotangent_ref
     )
@@ -213,15 +171,77 @@
         upstream - sums[1:2, :] / total - normed * sums[0:1, :] / total
     )
     grad_ref[...] = jnp.where(occupied, grad_conv, 0.0).astype(BF16)
-    kernel_gradient(0, place_ref[0], map_ref, window_ref, grad_ref, keep_any, send_any, scratch)
-
-
-def second_gradient_kernel(
-    place_ref, grad_ref, map_ref, window_ref, keep_any, send_any, *scratch
+
+
+def gradient_kernel(
+    place_ref, grad_own, grad_mate, map_own, map_mate, window_own, window_mate, *refs
 ):
-    kernel_gradient(
-        K_ONE, place_ref[0], map_ref, window_ref, grad_ref, keep_any, send_any, scratch
-    )
+    outs, scratch = refs[:6], refs[6:]
+    index, picked, grad, product, *staged, out_sem = scratch
+    keep_one, send_one, keep_two, *sends_two = staged
+    rows, channels = grad_own.shape
+    core = place_ref[0]
+    slots = lax.broadcasted_iota(jnp.int32, (BLOCK, 3 * BLOCK), 1)
+    sides = ((map_own, window_own), (map_mate, window_mate))
+    grad[0:rows, :] = grad_own[...]
+    grad[rows:, :] = grad_mate[...]
+    for side, (map_ref, _) in enumerate(sides):
+        index[side] = transposed_map(map_ref)
+
+    def gradient(j, slot_of):
+        for side, (_, window) in enumerate(sides):
+            for b in range(rows // BLOCK):
+                here = slice(b * BLOCK, (b + 1) * BLOCK)
+                chosen = chosen_slots(slot_of(side)[here] - (rows + (b - 1) * BLOCK), slots)
+                tile = window[b * BLOCK : (b + 3) * BLOCK, :]
+                at = slice(side * rows + b * BLOCK, side * rows + (b + 1) * BLOCK)
+                picked[j, at, :] = dot(chosen, tile, ((1,), (0,))).astype(BF16)
+        product[j] = dot(picked[j], grad[...], ((0,), (0,)))
+
+    def stored(staged, out, n):
+        return pltpu.make_async_copy(staged, out, out_sem.at[n])
+
+    shift = lax.rem(BLOCK - core * (HALF + 1), BLOCK)
+    local = [pltpu.roll(index[side], shift, 1) for side in range(2)]
+    size = channels // 8
+
+    def rows_of(piece, place, size, first):
+        at = lax.bitwise_xor(jnp.int32(piece), place) * size + first
+        return pl.ds(pl.multiple_of(at, 16), size)
+
+    for j in range(K_ONE):
+        gradient(j, lambda side: local[side][:, j : j + 1])
+        here = slice(j * size, (j + 1) * size)
+        for piece in range(8):
+            value = product[j, rows_of(piece, place_ref[1], size, 0), :]
+            if piece < 4:
+                keep_one[piece, here, :] = value
+            else:
+                send_one[piece - 4, here, :] = value.astype(BF16)
+    copies = [stored(keep_one, outs[0], 0), stored(send_one, outs[1], 1)]
+    for copy in copies:
+        copy.start()
+    for j in range(HALF - K_ONE + 1):
+        whole_offset = j < HALF - K_ONE
+        if whole_offset:
+            gradient(j, lambda side: local[side][:, K_ONE + j : K_ONE + j + 1])
+        else:
+            gradient(j, lambda side: index[side][:, HALF : HALF + 1])
+        count = size if whole_offset else size // 2
+        first = 0 if whole_offset else core * (channels // 2)
+        here = slice(j * size, j * size + count)
+        for piece in range(8):
+            value = product[j, rows_of(piece, place_ref[2], count, first), :]
+            if piece < 2:
+                keep_two[piece, here, :] = value
+            else:
+                sends_two[piece // 2 - 1][piece % 2, here, :] = value.astype(BF16)
+    late = [stored(keep_two, outs[2], 2)]
+    late += [stored(sends_two[n], outs[3 + n], 3 + n) for n in range(3)]
+    for copy in late:
+        copy.start()
+    for copy in copies + late:
+        copy.wait()
 
 
 def push_kernel(grad_ref, index_ref, weight_ref, before_ref, own_ref, after_ref, sink):
@@ -261,21 +281,24 @@
 
 def place_kernel(other, places_ref, one, two, *refs):
     out_ref, sems = refs[-2:]
-    half, split, rows = one.shape[:3]
+    core = lax.bitwise_xor(places_ref[0], jnp.int32(other))
+    first = core * (HALF + 1)
+    size = out_ref.shape[1] // 8
     copies = []
-    for piece in range(half):
-        for part, source in enumerate((one, two)):
-            relative = jnp.int32(piece + half * other)
-            place = lax.bitwise_xor(relative, places_ref[part])
-            start = pl.multiple_of(place * rows, rows)
-            first = 0 if part == 0 else split
-            copies.append(
-                pltpu.make_async_copy(
-                    source.at[piece],
-                    out_ref.at[pl.ds(first, source.shape[1]), pl.ds(start, rows), :],
-                    sems.at[len(copies)],
-                )
-            )
+
+    def put(source, out, part, piece, count, base):
+        at = lax.bitwise_xor(jnp.int32(piece), places_ref[part]) * count + base
+        here = pl.ds(pl.multiple_of(at, 16), count)
+        copies.append(pltpu.make_async_copy(source, out.at[:, here, :], sems.at[len(copies)]))
+
+    for piece in range(8):
+        put(one.at[piece], out_ref.at[pl.ds(first, K_ONE)], 1, piece, size, 0)
+        for j in range(HALF - K_ONE):
+            source = two.at[pl.ds(piece, 1), pl.ds(j * size, size)]
+            put(source, out_ref.at[pl.ds(first + K_ONE + j, 1)], 2, piece, size, 0)
+        source = two.at[pl.ds(piece, 1), pl.ds((HALF - K_ONE) * size, size // 2)]
+        base = core * (out_ref.shape[1] // 2)
+        put(source, out_ref.at[pl.ds(HALF, 1)], 2, piece, size // 2, base)
     for copy in copies:
         copy.start()
     for copy in copies:
@@ -312,8 +335,7 @@
 
 
 def summed_over_devices(one, two, grad_conv, push, spread):
-    parts = [split(one, "x"), split(two, "z")]
-    parts, grad_conv = lax.optimization_barrier((parts, grad_conv))
+    parts, grad_conv = lax.optimization_barrier(((one, two), grad_conv))
     received = [swapped(sends, stage) for (_, sends), stage in zip(parts, "xz")]
     received, sinks = lax.optimization_barrier((received, push(grad_conv)))
     parts = [
@@ -371,6 +393,7 @@
 
     even, other = neighbours_swap(features[:BLOCK], features[rows - BLOCK :])
     map_rows = jnp.transpose(kernel_map)
+    map_mate = swap(map_rows, 1)
     odd_flag = odd.reshape(1)
 
     gain = bn_gain.reshape(1, channels)
@@ -421,6 +444,7 @@
         name="conv_outer",
     )(occupancy, odd_flag, map_rows, features, even, other, inner, in_hbm(weights))
 
+    window_mate = swap(window, 1)
     stats = exchanged(stats, stacked_moments)
 
     block_out, sums = pl.pallas_call(
@@ -437,51 +461,43 @@
 
     grads = exchanged(sums, jnp.add)
 
-    core, lane, depth = me & 1, (me >> 1) & 1, (me >> 2) & 3
-    place_one = (core * 8 + lane * 4 + depth).reshape(1)
-    place_two = (core * 8 + depth * 2 + lane).reshape(1)
-    piece_rows = channels // 16
-
-    def gradient(kernel, count, in_specs, out_specs, out_shape, name):
-        shape = (8, count, piece_rows, channels)
-        return pl.pallas_call(
-            kernel,
-            in_specs=in_specs,
-            out_specs=out_specs + [anywhere, anywhere],
-            out_shape=out_shape
-            + [jax.ShapeDtypeStruct(shape, F32), jax.ShapeDtypeStruct(shape, BF16)],
-            scratch_shapes=[
-                pltpu.VMEM((rows, BLOCK), jnp.int32),
-                pltpu.VMEM((GROUP, rows, channels), BF16),
-                pltpu.VMEM((GROUP, channels, channels), F32),
-                pltpu.VMEM(shape, F32),
-                pltpu.VMEM(shape, BF16),
-                pltpu.SemaphoreType.DMA((2, count // GROUP)),
-            ],
-            compiler_params=params(LIMIT),
-            cost_estimate=cost(work * count / K, count * channels * channels * 6),
-            name=name,
-        )
-
-    grad_conv, sums, *pair_one = gradient(
-        functools.partial(first_gradient_kernel, len(stats)),
-        K_ONE,
-        [smem, smem] + [vmem] * 15,
-        [vmem, vmem],
-        [
+    grad_conv, sums = pl.pallas_call(
+        functools.partial(grad_conv_kernel, len(stats)),
+        in_specs=[smem] + [vmem] * 13,
+        out_shape=[
             jax.ShapeDtypeStruct((rows, channels), BF16),
             jax.ShapeDtypeStruct((2, channels), F32),
         ],
-        "weight_gradient_one",
-    )(
-        occupancy, place_one, inner, outer, gain, shift, cotangent, map_rows, window,
-        *stats, *grads,
-    )
-    one = [pair_one[0], swap(pair_one[1], 1)]
-    pair_two = gradient(
-        second_gradient_kernel, K - K_ONE, [smem] + [vmem] * 3, [], [], "weight_gradient_two"
-    )(place_two, grad_conv, map_rows, window)
-    two = [pair_two[0], swap(pair_two[1], 1)]
+        compiler_params=params(LIMIT),
+        cost_estimate=cost(rows * channels * 20, rows * channels * 8),
+        name="grad_conv",
+    )(occupancy, inner, outer, gain, shift, cotangent, *stats, *grads)
+    grad_mate = swap(grad_conv, 1)
+
+    core, lane, depth = me & 1, (me >> 1) & 1, (me >> 2) & 3
+    places = jnp.stack([core, lane * 4 + depth, depth * 2 + lane])
+    size = channels // 8
+    rows_one, rows_two = K_ONE * size, (HALF - K_ONE) * size + size // 2
+    shapes = [((4, rows_one, channels), F32), ((4, rows_one, channels), BF16)]
+    shapes += [((2, rows_two, channels), F32)] + [((2, rows_two, channels), BF16)] * 3
+    keep_one, send_one, keep_two, *sends_two = pl.pallas_call(
+        gradient_kernel,
+        in_specs=[smem] + [vmem] * 6,
+        out_specs=[anywhere] * 6,
+        out_shape=[jax.ShapeDtypeStruct(*shape) for shape in shapes],
+        scratch_shapes=[
+            pltpu.VMEM((2, rows, BLOCK), jnp.int32),
+            pltpu.VMEM((K_ONE, 2 * rows, channels), BF16),
+            pltpu.VMEM((2 * rows, channels), BF16),
+            pltpu.VMEM((K_ONE, channels, channels), F32),
+        ]
+        + [pltpu.VMEM(*shape) for shape in shapes]
+        + [pltpu.SemaphoreType.DMA((6,))],
+        compiler_params=params(LIMIT),
+        cost_estimate=cost(work, K * channels * channels * 6),
+        name="weight_gradient",
+    )(places, grad_conv, grad_mate, map_rows, map_mate, window, window_mate)
+    one, two = (keep_one, [send_one]), (keep_two, sends_two)
 
     weight_spec = pl.BlockSpec((GROUP, channels, channels), lambda s: (s, 0, 0))
 
@@ -521,7 +537,6 @@
         axis=0,
     )
     grad_features = (jnp.where(occupied, cotangent.astype(F32), 0.0) + received).astype(BF16)
-    places = jnp.concatenate([place_one, place_two])
 
     def placed(other, sources, *into):
         return pl.pallas_call(
@@ -529,12 +544,12 @@
             in_specs=[smem, anywhere, anywhere] + [hbm] * len(into),
             out_specs=hbm,
             out_shape=jax.ShapeDtypeStruct(weights.shape, BF16),
-            scratch_shapes=[pltpu.SemaphoreType.DMA((16,))],
+            scratch_shapes=[pltpu.SemaphoreType.DMA((8 * (HALF - K_ONE + 2),))],
             input_output_aliases={3: 0} if into else {},
             compiler_params=params(LIMIT),
             cost_estimate=cost(0, K * channels * channels * 2),
             name="place",
-        )(places, *sources, *into)
+        )(places, sources[0].reshape(8, K_ONE, size, channels), sources[1], *into)
 
     others = [swap(own_one, 1), swap(own_two, 1)]
     grad_weights = placed(1, others, placed(0, (own_one, own_two)))

time: 129 us -> 125 us (0.969)
  other arithmetic: 4.27 us -> 2.25 us
  local copies, waits for them, and re-layouts: 2.81 us -> 0.81 us
  Pallas kernels: 34 us -> 35.4 us
    convert_element_type x4 -> x2, other arithmetic: 2.27 us -> 0.25 us  [split(): part(terms, (i + 1) * size, size).astype(BF16)]
    unnamed x26 -> x20, local copies, waits for them, and re-layouts: 2.15 us -> 0.15 us
    ppermute x32 -> x33, waiting for transfers between devices: 31.4 us -> 30.3 us  [swap(): return lax.ppermute(value, 'dp', [(i, i ^ by) for i in range(peers)])]
    ppermute x32 -> x33, starting transfers between devices: 43.3 us -> 43.4 us  [swap(): return lax.ppermute(value, 'dp', [(i, i ^ by) for i in range(peers)])]
  transfers between devices with their start and end apart: 36 -> 37, of which waited for: 18 -> 18; matrix products, arithmetic and copies ran while one was open for 1% -> 1% of each run, Pallas kernels for 15% -> 14%
where the time goes in v6:
time: 125 us; the launch traced here: 124 us
  starting transfers between devices  52.1 us (42%)
  Pallas kernels  35.4 us (28%)
  waiting for transfers between devices  32 us (26%)
  other arithmetic  2.25 us (2%)
  between operations  1.78 us (1%)
    ppermute x33, starting transfers between devices, swap(): return lax.ppermute(value, 'dp', [(i, i ^ by) for i in range(peers)])  43.4 us
    ppermute x33, waiting for transfers between devices, swap(): return lax.ppermute(value, 'dp', [(i, i ^ by) for i in range(peers)])  30.3 us
    pallas_call x1, Pallas kernels, per_device(): pl.pallas_call(gradient_kernel, in_specs=[smem] + [vmem] * 6, out_specs=[...  9.89 us
    pallas_call x1, Pallas kernels, push(): pl.pallas_call(push_kernel, grid=(groups,), in_specs=[full((rows, channel...  9.26 us
    ppermute x2, starting transfers between devices, neighbours_swap(): lax.ppermute(jnp.where(odd == 1, to_after, to_before), 'dp', other_pairs)  8.63 us
    pallas_call x1, Pallas kernels, per_device(): pl.pallas_call(inner_kernel, in_specs=[vmem, vmem, hbm], out_specs=vmem,...  5.73 us
    pallas_call x1, Pallas kernels, per_device(): pl.pallas_call(outer_kernel, in_specs=[smem, smem, vmem, vmem, vmem, vmem...  4.92 us
    pallas_call x2, Pallas kernels, placed(): pl.pallas_call(functools.partial(place_kernel, other), in_specs=[smem, an...  4.32 us
  transfers between devices with their start and end apart: 37, of which 18 were waited for; matrix products, arithmetic and copies ran while one was open for 1% of the time, Pallas kernels for 14%

profile of v6, /device:TPU:1, one launch (start us, length us, event | category | flops | bytes accessed | tf_op | source)
XLA Modules:
  0.0 124.4 jit_solution(2327775852071560906)
XLA Ops:
  1.5 4.5 %collective-permute-start.1 = (bf16[128,256]{1,0:T(8,128)(2,1)S(1)}, bf16[128,256]{1,0:T(8,128)(2,1)S(1)}, u32[]{:S(2)}, u32[]{:S(2)}) collective-permute-start(bf16[128,256]{1,0:T(8,128)(2,1)S(1)} %get-tuple-element.131), channel_id=1, source_target_pairs={{1,2},{2,1},{3,4},{4,3},{5,6},{6,5},{7,8},{8,7},{9,10},{10,9},{11,... | collective-permute-start | bytes 196616 | tf_op jit(solution)/shard_map/ppermute | solution.py:391
  6.1 5.7 %conv_inner.1.inner_ref = f32[256,256]{1,0:T(8,128)S(1)} custom-call(s32[27,512]{1,0:T(8,128)} %bitcast.13, bf16[512,256]{1,0:T(8,128)(2,1)} %feature_ref.1, bf16[27,256,256]{2,1,0:T(8,128)(2,1)} %weight_ref.1), custom_call_target="tpu_custom_call" | custom-call | flops 2264924160 | bytes 10616832 | tf_op jit(solution)/shard_map/conv_inner/pallas_call | solution.py:421
  12.6 4.9 %conv_outer.1 = (f32[256,256]{1,0:T(8,128)S(1)}, f32[3,256]{1,0:T(4,128)S(1)}, bf16[768,256]{1,0:T(8,128)(2,1)S(1)}) custom-call(s32[1]{0:T(128)S(6)} %copy.22.filled_ref, s32[1]{0:T(128)} %bitcast.1.odd_ref, s32[27,512]{1,0:T(8,128)S(1)} %bitcast.14, bf16[512,256]{1,0:T(8,128)(2,1)S(1)} %copy-done.2, bf16[128,256]{1,0:T(8,128)(2,1)S(1)} %collective-permute-done.even_ref, ...), custom_call_target="tpu_custom_call" | custom-call | flops 2264924160 | bytes 10616832 | tf_op jit(solution)/shard_map/conv_outer/pallas_call | solution.py:432
  21.7 2.4 %collective-permute-start.7 = (f32[3,256]{1,0:T(4,128)S(1)}, f32[3,256]{1,0:T(4,128)S(1)}, u32[]{:S(2)}, u32[]{:S(2)}) collective-permute-start(f32[3,256]{1,0:T(4,128)S(1)} %pad_maximum_fusion.refs_0_), channel_id=1, source_target_pairs={{0,12},{1,13},{2,14},{3,15},{4,8},{5,9},{6,10},{7,11},{8,4},{9,5},... | collective-permute-start | bytes 9224 | tf_op jit(solution)/shard_map/ppermute | solution.py:310
  26.1 1.7 %collective-permute-done.6.refs_2_ = f32[3,256]{1,0:T(4,128)S(1)} collective-permute-done((f32[3,256]{1,0:T(4,128)S(1)}, f32[3,256]{1,0:T(4,128)S(1)}, u32[]{:S(2)}, u32[]{:S(2)}) %collective-permute-start.6) | collective-permute-done | bytes 3104 | tf_op jit(solution)/shard_map/ppermute | solution.py:310
  28.8 3.4 %collective-permute-start.10 = (f32[2,256]{1,0:T(2,128)S(1)}, f32[2,256]{1,0:T(2,128)S(1)}, u32[]{:S(2)}, u32[]{:S(2)}) collective-permute-start(f32[2,256]{1,0:T(2,128)S(1)} %get-tuple-element.66), channel_id=1, source_target_pairs={{0,3},{1,2},{2,1},{3,0},{4,7},{5,6},{6,5},{7,4},{8,11},{9,10},{10,... | collective-permute-start | bytes 6152 | tf_op jit(solution)/shard_map/ppermute | solution.py:310
  42.9 9.9 %weight_gradient.1 = (f32[4,288,256]{2,1,0:T(8,128)S(1)}, bf16[4,288,256]{2,1,0:T(8,128)(2,1)S(1)}, f32[2,144,256]{2,1,0:T(8,128)S(1)}, bf16[2,144,256]{2,1,0:T(...) custom-call(s32[3]{0:T(128)S(1)} %pad_add_fusion.place_ref.places_ref, ...), custom_call_target="tpu_custom_call" | custom-call | flops 4529848320 | bytes 10616832 | tf_op jit(solution)/shard_map/weight_gradient/pallas_call | solution.py:483
  53.6 1.7 %collective-permute-start.18 = (bf16[2,144,256]{2,1,0:T(8,128)(2,1)S(1)}, bf16[2,144,256]{2,1,0:T(8,128)(2,1)S(1)}, u32[]{:S(2)}, u32[]{:S(2)}) collective-permute-start(bf16[2,144,256]{2,1,0:T(8,128)(2,1)S(1)} %get-tuple-element.77), channel_id=1, source_target_pairs={{0,4},{1,5},{2,6},{3,7},{4,0},{5,1},{6,2},{7,3},{8,12},{9,13},{10,... | collective-permute-start | bytes 442376 | tf_op jit(solution)/shard_map/ppermute | solution.py:310
  57.4 9.3 %push.1 = (bf16[128,256]{1,0:T(8,128)(2,1)S(1)}, f32[512,256]{1,0:T(8,128)S(1)}, bf16[128,256]{1,0:T(8,128)(2,1)S(1)}) custom-call(bf16[512,256]{1,0:T(8,128)(2,1)S(1)} %get-tuple-element.80.grad_own.grad_ref, s32[27,512]{1,0:T(8,128)S(1)} %bitcast.17, bf16[27,256,256]{2,1,0:T(8,128)(2,1)S(1)} %copy-done), custom_call_target="tpu_custom_call" | custom-call | flops 1000 | bytes 1000 | tf_op jit(solution)/shard_map/push/pallas_call | solution.py:505
  67.7 3.3 %collective-permute-start.21 = (bf16[1,288,256]{2,1,0:T(8,128)(2,1)S(1)}, bf16[1,288,256]{2,1,0:T(8,128)(2,1)S(1)}, u32[]{:S(2)}, u32[]{:S(2)}) collective-permute-start(bf16[1,288,256]{2,1,0:T(8,128)(2,1)S(1)} %get-tuple-element.92), channel_id=1, source_target_pairs={{0,4},{1,5},{2,6},{3,7},{4,0},{5,1},{6,2},{7,3},{8,12},{9,13},{10,... | collective-permute-start | bytes 442376 | tf_op jit(solution)/shard_map/ppermute | solution.py:310
  71.0 2.2 %collective-permute-start.23 = (bf16[1,288,256]{2,1,0:T(8,128)(2,1)S(1)}, bf16[1,288,256]{2,1,0:T(8,128)(2,1)S(1)}, u32[]{:S(2)}, u32[]{:S(2)}) collective-permute-start(bf16[1,288,256]{2,1,0:T(8,128)(2,1)S(1)} %get-tuple-element.94), channel_id=1, source_target_pairs={{0,12},{1,13},{2,14},{3,15},{4,8},{5,9},{6,10},{7,11},{8,4},{9,5},... | collective-permute-start | bytes 442376 | tf_op jit(solution)/shard_map/ppermute | solution.py:310
  73.2 4.1 %collective-permute-start.26 = (bf16[128,256]{1,0:T(8,128)(2,1)S(1)}, bf16[128,256]{1,0:T(8,128)(2,1)S(1)}, u32[]{:S(2)}, u32[]{:S(2)}) collective-permute-start(bf16[128,256]{1,0:T(8,128)(2,1)S(1)} %get-tuple-element.133), channel_id=1, source_target_pairs={{1,2},{2,1},{3,4},{4,3},{5,6},{6,5},{7,8},{8,7},{9,10},{10,9},{11,... | collective-permute-start | bytes 196616 | tf_op jit(solution)/shard_map/ppermute | solution.py:391
  77.3 1.8 %collective-permute-start.24 = (bf16[1,144,256]{2,1,0:T(8,128)(2,1)S(1)}, bf16[1,144,256]{2,1,0:T(8,128)(2,1)S(1)}, u32[]{:S(2)}, u32[]{:S(2)}) collective-permute-start(bf16[1,144,256]{2,1,0:T(8,128)(2,1)S(1)} %get-tuple-element.95), channel_id=1, source_target_pairs={{0,2},{1,3},{2,0},{3,1},{4,6},{5,7},{6,4},{7,5},{8,10},{9,11},{10,... | collective-permute-start | bytes 221192 | tf_op jit(solution)/shard_map/ppermute | solution.py:310
  81.1 2.0 %collective-permute-done.22 = bf16[1,288,256]{2,1,0:T(8,128)(2,1)S(1)} collective-permute-done((bf16[1,288,256]{2,1,0:T(8,128)(2,1)S(1)}, bf16[1,288,256]{2,1,0:T(8,128)(2,1)S(1)}, u32[]{:S(2)}, u32[]{:S(2)}) %collective-permute-start.22) | collective-permute-done | bytes 147488 | tf_op jit(solution)/shard_map/ppermute | solution.py:310
  84.4 7.0 %collective-permute-start.28 = (bf16[1,288,256]{2,1,0:T(8,128)(2,1)S(1)}, bf16[1,288,256]{2,1,0:T(8,128)(2,1)S(1)}, u32[]{:S(2)}, u32[]{:S(2)}) collective-permute-start(bf16[1,288,256]{2,1,0:T(8,128)(2,1)S(1)} %add_convert_fusion), channel_id=1, source_target_pairs={{0,8},{1,9},{2,10},{3,11},{4,12},{5,13},{6,14},{7,15},{8,0},{9,1},... | collective-permute-start | bytes 442376 | tf_op jit(solution)/shard_map/ppermute | solution.py:310
  91.6 1.8 %collective-permute-start.30 = (bf16[1,144,256]{2,1,0:T(8,128)(2,1)S(1)}, bf16[1,144,256]{2,1,0:T(8,128)(2,1)S(1)}, u32[]{:S(2)}, u32[]{:S(2)}) collective-permute-start(bf16[1,144,256]{2,1,0:T(8,128)(2,1)S(1)} %add_convert_fusion.4), channel_id=1, source_target_pairs={{0,2},{1,3},{2,0},{3,1},{4,6},{5,7},{6,4},{7,5},{8,10},{9,11},{10,... | collective-permute-start | bytes 221192 | tf_op jit(solution)/shard_map/ppermute | solution.py:310
  93.4 2.0 %collective-permute-done.30 = bf16[1,144,256]{2,1,0:T(8,128)(2,1)S(1)} collective-permute-done((bf16[1,144,256]{2,1,0:T(8,128)(2,1)S(1)}, bf16[1,144,256]{2,1,0:T(8,128)(2,1)S(1)}, u32[]{:S(2)}, u32[]{:S(2)}) %collective-permute-start.30) | collective-permute-done | bytes 73760 | tf_op jit(solution)/shard_map/ppermute | solution.py:310
  95.4 6.1 %collective-permute-done.28 = bf16[1,288,256]{2,1,0:T(8,128)(2,1)S(1)} collective-permute-done((bf16[1,288,256]{2,1,0:T(8,128)(2,1)S(1)}, bf16[1,288,256]{2,1,0:T(8,128)(2,1)S(1)}, u32[]{:S(2)}, u32[]{:S(2)}) %collective-permute-start.28) | collective-permute-done | bytes 147488 | tf_op jit(solution)/shard_map/ppermute | solution.py:310
  101.6 2.0 %collective-permute-start.31 = (bf16[4,288,256]{2,1,0:T(8,128)(2,1)S(1)}, bf16[4,288,256]{2,1,0:T(8,128)(2,1)S(1)}, u32[]{:S(2)}, u32[]{:S(2)}) collective-permute-start(bf16[4,288,256]{2,1,0:T(8,128)(2,1)S(1)} %constant_dynamic-update-slice_fusion), channel_id=1, source_target_pairs={{0,2},{1,3},{2,0},{3,1},{4,6},{5,7},{6,4},{7,5},{8,10},{9,11},{10,... | collective-permute-start | bytes 1769480 | tf_op jit(solution)/shard_map/ppermute | solution.py:310
  104.8 2.4 %collective-permute-start.32 = (bf16[2,144,256]{2,1,0:T(8,128)(2,1)S(1)}, bf16[2,144,256]{2,1,0:T(8,128)(2,1)S(1)}, u32[]{:S(2)}, u32[]{:S(2)}) collective-permute-start(bf16[2,144,256]{2,1,0:T(8,128)(2,1)S(1)} %constant_dynamic-update-slice_fusion.4), channel_id=1, source_target_pairs={{0,4},{1,5},{2,6},{3,7},{4,0},{5,1},{6,2},{7,3},{8,12},{9,13},{10,... | collective-permute-start | bytes 442376 | tf_op jit(solution)/shard_map/ppermute | solution.py:310
  107.2 2.4 %collective-permute-done.34 = bf16[2,144,256]{2,1,0:T(8,128)(2,1)S(1)} collective-permute-done((bf16[2,144,256]{2,1,0:T(8,128)(2,1)S(1)}, bf16[2,144,256]{2,1,0:T(8,128)(2,1)S(1)}, u32[]{:S(2)}, u32[]{:S(2)}) %collective-permute-start.34) | collective-permute-done | bytes 147488 | tf_op jit(solution)/shard_map/ppermute | solution.py:310
  109.7 7.9 %collective-permute-done.33 = bf16[2,144,256]{2,1,0:T(8,128)(2,1)S(1)} collective-permute-done((bf16[2,144,256]{2,1,0:T(8,128)(2,1)S(1)}, bf16[2,144,256]{2,1,0:T(8,128)(2,1)S(1)}, u32[]{:S(2)}, u32[]{:S(2)}) %collective-permute-start.33) | collective-permute-done | bytes 147488 | tf_op jit(solution)/shard_map/ppermute | solution.py:310
  119.9 2.2 %place.2.refs_0_ = bf16[27,256,256]{2,1,0:T(8,128)(2,1)} custom-call(s32[3]{0:T(128)S(1)} %pad_add_fusion.place_ref.places_ref, bf16[8,9,32,256]{3,2,1,0:T(8,128)(2,1)S(1)} %bitcast.11, bf16[8,144,256]{2,1,0:T(8,128)(2,1)S(1)} %constant_dynamic-update-slice_fusion.8.two), custom_call_target="tpu_custom_call" | custom-call | bytes 3538944 | tf_op jit(solution)/shard_map/place/pallas_call | solution.py:542
  122.1 2.2 %place.3 = bf16[27,256,256]{2,1,0:T(8,128)(2,1)} custom-call(s32[3]{0:T(128)S(1)} %pad_add_fusion.place_ref.places_ref, bf16[8,9,32,256]{3,2,1,0:T(8,128)(2,1)S(1)} %bitcast.12, bf16[8,144,256]{2,1,0:T(8,128)(2,1)S(1)} %collective-permute-done.36.two, bf16[27,256,256]{2,1,0:T(8,128)(2,1)} %place.2.refs_0_), custom_call_target="tpu_custom_call", output_to_operand_aliasing={{}: (3, {})} | custom-call | bytes 3538944 | tf_op jit(solution)/shard_map/place/pallas_call | solution.py:542
  (97 shorter events, 29.7 us)
Async XLA Ops:
  1.5 11.0 %collective-permute-start.1 = (bf16[128,256]{1,0:T(8,128)(2,1)S(1)}, bf16[128,256]{1,0:T(8,128)(2,1)S(1)}, u32[]{:S(2)}, u32[]{:S(2)}) collective-permute-start(bf16[128,256]{1,0:T(8,128)(2,1)S(1)} %get-tuple-element.131), channel_id=1, source_target_pairs={{1,2},{2,1},{3,4},{4,3},{5,6},{6,5},{7,8},{8,7},{9,10},{10,9},{11,... | collective-permute-start | bytes 196616 | tf_op jit(solution)/shard_map/ppermute | solution.py:391
  6.0 6.5 %collective-permute-start = (bf16[128,256]{1,0:T(8,128)(2,1)S(1)}, bf16[128,256]{1,0:T(8,128)(2,1)S(1)}, u32[]{:S(2)}, u32[]{:S(2)}) collective-permute-start(bf16[128,256]{1,0:T(8,128)(2,1)S(1)} %get-tuple-element.132), channel_id=1, source_target_pairs={{0,1},{1,0},{2,3},{3,2},{4,5},{5,4},{6,7},{7,6},{8,9},{9,8},{10,11... | collective-permute-start | bytes 196616 | tf_op jit(solution)/shard_map/ppermute | solution.py:390
  21.7 4.3 %collective-permute-start.7 = (f32[3,256]{1,0:T(4,128)S(1)}, f32[3,256]{1,0:T(4,128)S(1)}, u32[]{:S(2)}, u32[]{:S(2)}) collective-permute-start(f32[3,256]{1,0:T(4,128)S(1)} %pad_maximum_fusion.refs_0_), channel_id=1, source_target_pairs={{0,12},{1,13},{2,14},{3,15},{4,8},{5,9},{6,10},{7,11},{8,4},{9,5},... | collective-permute-start | bytes 9224 | tf_op jit(solution)/shard_map/ppermute | solution.py:310
  28.8 4.8 %collective-permute-start.10 = (f32[2,256]{1,0:T(2,128)S(1)}, f32[2,256]{1,0:T(2,128)S(1)}, u32[]{:S(2)}, u32[]{:S(2)}) collective-permute-start(f32[2,256]{1,0:T(2,128)S(1)} %get-tuple-element.66), channel_id=1, source_target_pairs={{0,3},{1,2},{2,1},{3,0},{4,7},{5,6},{6,5},{7,4},{8,11},{9,10},{10,... | collective-permute-start | bytes 6152 | tf_op jit(solution)/shard_map/ppermute | solution.py:310
  32.6 10.3 %collective-permute-start.16 = (bf16[768,256]{1,0:T(8,128)(2,1)S(1)}, bf16[768,256]{1,0:T(8,128)(2,1)S(1)}, u32[]{:S(2)}, u32[]{:S(2)}) collective-permute-start(bf16[768,256]{1,0:T(8,128)(2,1)S(1)} %get-tuple-element.68.window_own), channel_id=1, source_target_pairs={{0,1},{1,0},{2,3},{3,2},{4,5},{5,4},{6,7},{7,6},{8,9},{9,8},{10,11... | collective-permute-start | bytes 1179656 | tf_op jit(solution)/shard_map/ppermute | solution.py:310
  34.6 4.3 %collective-permute-start.13 = (f32[2,256]{1,0:T(2,128)S(1)}, f32[2,256]{1,0:T(2,128)S(1)}, u32[]{:S(2)}, u32[]{:S(2)}) collective-permute-start(f32[2,256]{1,0:T(2,128)S(1)} %add_add_fusion.refs_4_), channel_id=1, source_target_pairs={{0,12},{1,13},{2,14},{3,15},{4,8},{5,9},{6,10},{7,11},{8,4},{9,5},... | collective-permute-start | bytes 6152 | tf_op jit(solution)/shard_map/ppermute | solution.py:310
  52.8 14.6 %collective-permute-start.17 = (bf16[4,288,256]{2,1,0:T(8,128)(2,1)S(1)}, bf16[4,288,256]{2,1,0:T(8,128)(2,1)S(1)}, u32[]{:S(2)}, u32[]{:S(2)}) collective-permute-start(bf16[4,288,256]{2,1,0:T(8,128)(2,1)S(1)} %get-tuple-element.76), channel_id=1, source_target_pairs={{0,2},{1,3},{2,0},{3,1},{4,6},{5,7},{6,4},{7,5},{8,10},{9,11},{10,... | collective-permute-start | bytes 1769480 | tf_op jit(solution)/shard_map/ppermute | solution.py:310
  53.6 13.1 %collective-permute-start.18 = (bf16[2,144,256]{2,1,0:T(8,128)(2,1)S(1)}, bf16[2,144,256]{2,1,0:T(8,128)(2,1)S(1)}, u32[]{:S(2)}, u32[]{:S(2)}) collective-permute-start(bf16[2,144,256]{2,1,0:T(8,128)(2,1)S(1)} %get-tuple-element.77), channel_id=1, source_target_pairs={{0,4},{1,5},{2,6},{3,7},{4,0},{5,1},{6,2},{7,3},{8,12},{9,13},{10,... | collective-permute-start | bytes 442376 | tf_op jit(solution)/shard_map/ppermute | solution.py:310
  55.3 11.4 %collective-permute-start.19 = (bf16[2,144,256]{2,1,0:T(8,128)(2,1)S(1)}, bf16[2,144,256]{2,1,0:T(8,128)(2,1)S(1)}, u32[]{:S(2)}, u32[]{:S(2)}) collective-permute-start(bf16[2,144,256]{2,1,0:T(8,128)(2,1)S(1)} %get-tuple-element.78), channel_id=1, source_target_pairs={{0,8},{1,9},{2,10},{3,11},{4,12},{5,13},{6,14},{7,15},{8,0},{9,1},... | collective-permute-start | bytes 442376 | tf_op jit(solution)/shard_map/ppermute | solution.py:310
  56.1 10.5 %collective-permute-start.20 = (bf16[2,144,256]{2,1,0:T(8,128)(2,1)S(1)}, bf16[2,144,256]{2,1,0:T(8,128)(2,1)S(1)}, u32[]{:S(2)}, u32[]{:S(2)}) collective-permute-start(bf16[2,144,256]{2,1,0:T(8,128)(2,1)S(1)} %get-tuple-element.79), channel_id=1, source_target_pairs={{0,12},{1,13},{2,14},{3,15},{4,8},{5,9},{6,10},{7,11},{8,4},{9,5},... | collective-permute-start | bytes 442376 | tf_op jit(solution)/shard_map/ppermute | solution.py:310
  67.7 13.5 %collective-permute-start.21 = (bf16[1,288,256]{2,1,0:T(8,128)(2,1)S(1)}, bf16[1,288,256]{2,1,0:T(8,128)(2,1)S(1)}, u32[]{:S(2)}, u32[]{:S(2)}) collective-permute-start(bf16[1,288,256]{2,1,0:T(8,128)(2,1)S(1)} %get-tuple-element.92), channel_id=1, source_target_pairs={{0,4},{1,5},{2,6},{3,7},{4,0},{5,1},{6,2},{7,3},{8,12},{9,13},{10,... | collective-permute-start | bytes 442376 | tf_op jit(solution)/shard_map/ppermute | solution.py:310
  71.0 12.1 %collective-permute-start.22 = (bf16[1,288,256]{2,1,0:T(8,128)(2,1)S(1)}, bf16[1,288,256]{2,1,0:T(8,128)(2,1)S(1)}, u32[]{:S(2)}, u32[]{:S(2)}) collective-permute-start(bf16[1,288,256]{2,1,0:T(8,128)(2,1)S(1)} %get-tuple-element.93), channel_id=1, source_target_pairs={{0,8},{1,9},{2,10},{3,11},{4,12},{5,13},{6,14},{7,15},{8,0},{9,1},... | collective-permute-start | bytes 442376 | tf_op jit(solution)/shard_map/ppermute | solution.py:310
  71.0 12.1 %collective-permute-start.23 = (bf16[1,288,256]{2,1,0:T(8,128)(2,1)S(1)}, bf16[1,288,256]{2,1,0:T(8,128)(2,1)S(1)}, u32[]{:S(2)}, u32[]{:S(2)}) collective-permute-start(bf16[1,288,256]{2,1,0:T(8,128)(2,1)S(1)} %get-tuple-element.94), channel_id=1, source_target_pairs={{0,12},{1,13},{2,14},{3,15},{4,8},{5,9},{6,10},{7,11},{8,4},{9,5},... | collective-permute-start | bytes 442376 | tf_op jit(solution)/shard_map/ppermute | solution.py:310
  73.2 6.4 %collective-permute-start.26 = (bf16[128,256]{1,0:T(8,128)(2,1)S(1)}, bf16[128,256]{1,0:T(8,128)(2,1)S(1)}, u32[]{:S(2)}, u32[]{:S(2)}) collective-permute-start(bf16[128,256]{1,0:T(8,128)(2,1)S(1)} %get-tuple-element.133), channel_id=1, source_target_pairs={{1,2},{2,1},{3,4},{4,3},{5,6},{6,5},{7,8},{8,7},{9,10},{10,9},{11,... | collective-permute-start | bytes 196616 | tf_op jit(solution)/shard_map/ppermute | solution.py:391
  77.3 3.9 %collective-permute-start.24 = (bf16[1,144,256]{2,1,0:T(8,128)(2,1)S(1)}, bf16[1,144,256]{2,1,0:T(8,128)(2,1)S(1)}, u32[]{:S(2)}, u32[]{:S(2)}) collective-permute-start(bf16[1,144,256]{2,1,0:T(8,128)(2,1)S(1)} %get-tuple-element.95), channel_id=1, source_target_pairs={{0,2},{1,3},{2,0},{3,1},{4,6},{5,7},{6,4},{7,5},{8,10},{9,11},{10,... | collective-permute-start | bytes 221192 | tf_op jit(solution)/shard_map/ppermute | solution.py:310
  83.2 12.2 %collective-permute-start.29 = (bf16[1,288,256]{2,1,0:T(8,128)(2,1)S(1)}, bf16[1,288,256]{2,1,0:T(8,128)(2,1)S(1)}, u32[]{:S(2)}, u32[]{:S(2)}) collective-permute-start(bf16[1,288,256]{2,1,0:T(8,128)(2,1)S(1)} %add_convert_fusion), channel_id=1, source_target_pairs={{0,12},{1,13},{2,14},{3,15},{4,8},{5,9},{6,10},{7,11},{8,4},{9,5},... | collective-permute-start | bytes 442376 | tf_op jit(solution)/shard_map/ppermute | solution.py:310
  84.4 17.2 %collective-permute-start.28 = (bf16[1,288,256]{2,1,0:T(8,128)(2,1)S(1)}, bf16[1,288,256]{2,1,0:T(8,128)(2,1)S(1)}, u32[]{:S(2)}, u32[]{:S(2)}) collective-permute-start(bf16[1,288,256]{2,1,0:T(8,128)(2,1)S(1)} %add_convert_fusion), channel_id=1, source_target_pairs={{0,8},{1,9},{2,10},{3,11},{4,12},{5,13},{6,14},{7,15},{8,0},{9,1},... | collective-permute-start | bytes 442376 | tf_op jit(solution)/shard_map/ppermute | solution.py:310
  91.4 10.2 %collective-permute-start.27 = (bf16[1,288,256]{2,1,0:T(8,128)(2,1)S(1)}, bf16[1,288,256]{2,1,0:T(8,128)(2,1)S(1)}, u32[]{:S(2)}, u32[]{:S(2)}) collective-permute-start(bf16[1,288,256]{2,1,0:T(8,128)(2,1)S(1)} %add_convert_fusion), channel_id=1, source_target_pairs={{0,4},{1,5},{2,6},{3,7},{4,0},{5,1},{6,2},{7,3},{8,12},{9,13},{10,... | collective-permute-start | bytes 442376 | tf_op jit(solution)/shard_map/ppermute | solution.py:310
  91.6 3.8 %collective-permute-start.30 = (bf16[1,144,256]{2,1,0:T(8,128)(2,1)S(1)}, bf16[1,144,256]{2,1,0:T(8,128)(2,1)S(1)}, u32[]{:S(2)}, u32[]{:S(2)}) collective-permute-start(bf16[1,144,256]{2,1,0:T(8,128)(2,1)S(1)} %add_convert_fusion.4), channel_id=1, source_target_pairs={{0,2},{1,3},{2,0},{3,1},{4,6},{5,7},{6,4},{7,5},{8,10},{9,11},{10,... | collective-permute-start | bytes 221192 | tf_op jit(solution)/shard_map/ppermute | solution.py:310
  101.6 15.9 %collective-permute-start.31 = (bf16[4,288,256]{2,1,0:T(8,128)(2,1)S(1)}, bf16[4,288,256]{2,1,0:T(8,128)(2,1)S(1)}, u32[]{:S(2)}, u32[]{:S(2)}) collective-permute-start(bf16[4,288,256]{2,1,0:T(8,128)(2,1)S(1)} %constant_dynamic-update-slice_fusion), channel_id=1, source_target_pairs={{0,2},{1,3},{2,0},{3,1},{4,6},{5,7},{6,4},{7,5},{8,10},{9,11},{10,... | collective-permute-start | bytes 1769480 | tf_op jit(solution)/shard_map/ppermute | solution.py:310
  103.6 6.1 %collective-permute-start.34 = (bf16[2,144,256]{2,1,0:T(8,128)(2,1)S(1)}, bf16[2,144,256]{2,1,0:T(8,128)(2,1)S(1)}, u32[]{:S(2)}, u32[]{:S(2)}) collective-permute-start(bf16[2,144,256]{2,1,0:T(8,128)(2,1)S(1)} %constant_dynamic-update-slice_fusion.4), channel_id=1, source_target_pairs={{0,12},{1,13},{2,14},{3,15},{4,8},{5,9},{6,10},{7,11},{8,4},{9,5},... | collective-permute-start | bytes 442376 | tf_op jit(solution)/shard_map/ppermute | solution.py:310
  104.8 12.8 %collective-permute-start.33 = (bf16[2,144,256]{2,1,0:T(8,128)(2,1)S(1)}, bf16[2,144,256]{2,1,0:T(8,128)(2,1)S(1)}, u32[]{:S(2)}, u32[]{:S(2)}) collective-permute-start(bf16[2,144,256]{2,1,0:T(8,128)(2,1)S(1)} %constant_dynamic-update-slice_fusion.4), channel_id=1, source_target_pairs={{0,8},{1,9},{2,10},{3,11},{4,12},{5,13},{6,14},{7,15},{8,0},{9,1},... | collective-permute-start | bytes 442376 | tf_op jit(solution)/shard_map/ppermute | solution.py:310
  104.8 12.8 %collective-permute-start.32 = (bf16[2,144,256]{2,1,0:T(8,128)(2,1)S(1)}, bf16[2,144,256]{2,1,0:T(8,128)(2,1)S(1)}, u32[]{:S(2)}, u32[]{:S(2)}) collective-permute-start(bf16[2,144,256]{2,1,0:T(8,128)(2,1)S(1)} %constant_dynamic-update-slice_fusion.4), channel_id=1, source_target_pairs={{0,4},{1,5},{2,6},{3,7},{4,0},{5,1},{6,2},{7,3},{8,12},{9,13},{10,... | collective-permute-start | bytes 442376 | tf_op jit(solution)/shard_map/ppermute | solution.py:310
  117.7 4.4 %collective-permute-start.35 = (bf16[8,288,256]{2,1,0:T(8,128)(2,1)S(1)}, bf16[8,288,256]{2,1,0:T(8,128)(2,1)S(1)}, u32[]{:S(2)}, u32[]{:S(2)}) collective-permute-start(bf16[8,288,256]{2,1,0:T(8,128)(2,1)S(1)} %constant_dynamic-update-slice_fusion.6), channel_id=1, source_target_pairs={{0,1},{1,0},{2,3},{3,2},{4,5},{5,4},{6,7},{7,6},{8,9},{9,8},{10,11... | collective-permute-start | bytes 3538952 | tf_op jit(solution)/shard_map/ppermute | solution.py:310
  (19 other events, 108.7 us)

commit v7 on v6

--- a/solution.py
+++ b/solution.py
@@ -244,45 +244,59 @@
         copy.wait()
 
 
-def push_kernel(grad_ref, index_ref, weight_ref, before_ref, own_ref, after_ref, sink):
-    step = pl.program_id(0)
-
-    @pl.when(step == 0)
-    def _():
-        sink[...] = jnp.zeros_like(sink)
-
-    blocks = grad_ref.shape[0] // BLOCK
-    here = jnp.concatenate([index_ref[step * GROUP + j, :][None] for j in range(GROUP)], axis=0)
-    block_of = lax.broadcasted_iota(jnp.int32, here.shape, 1) // BLOCK
-    local = here - (3 + block_of) * BLOCK
-    slots = lax.broadcasted_iota(jnp.int32, (3 * BLOCK, BLOCK), 0)
-    pushed = [
-        dot(grad_ref[...], weight_ref[j], ((1,), (1,))).astype(BF16) for j in range(GROUP)
-    ]
-    for b in range(blocks):
+def scatter(step, grad_ref, first_row, map_ref, weight_ref, windows):
+    pushed = [dot(grad_ref[...], weight_ref[j], ((1,), (1,))).astype(BF16) for j in range(GROUP)]
+    named = [map_ref[step * GROUP + j, :][None] for j in range(GROUP)]
+    for b, first_slot, sink in windows:
         rows = slice(b * BLOCK, (b + 1) * BLOCK)
+        at = slice(first_row(b), first_row(b) + BLOCK)
+        slots = lax.broadcasted_iota(jnp.int32, (sink.shape[0], BLOCK), 0) + first_slot
         chosen = jnp.concatenate(
-            [
-                jnp.where(local[j : j + 1, rows] == slots, 1.0, 0.0).astype(BF16)
-                for j in range(GROUP)
-            ],
+            [chosen_slots(named[j][:, at], slots) for j in range(GROUP)],
             axis=1,
         )
         stacked = jnp.concatenate([pushed[j][rows] for j in range(GROUP)], axis=0)
-        window = slice(b * BLOCK, (b + 3) * BLOCK)
-        sink[window, :] = sink[window, :] + dot(chosen, stacked, ((1,), (0,)))
+        sink[...] = sink[...] + dot(chosen, stacked, ((1,), (0,)))
+
+
+def edge_push_kernel(grad_ref, map_ref, weight_ref, before_ref, after_ref, before, after):
+    step = pl.program_id(0)
+    rows = map_ref.shape[1]
+
+    @pl.when(step == 0)
+    def _():
+        before[...] = jnp.zeros_like(before)
+        after[...] = jnp.zeros_like(after)
+
+    def first_row(b):
+        return b * (rows - BLOCK)
+
+    windows = [(0, rows - BLOCK, before), (1, 2 * rows, after)]
+    scatter(step, grad_ref, first_row, map_ref, weight_ref, windows)
 
     @pl.when(step == pl.num_programs(0) - 1)
     def _():
-        before_ref[...] = sink[0:BLOCK, :].astype(BF16)
-        own_ref[...] = sink[BLOCK : (blocks + 1) * BLOCK, :]
-        after_ref[...] = sink[(blocks + 1) * BLOCK :, :].astype(BF16)
-
-
-def place_kernel(other, places_ref, one, two, *refs):
+        before_ref[...] = before[...].astype(BF16)
+        after_ref[...] = after[...].astype(BF16)
+
+
+def push_kernel(grad_ref, map_ref, weight_ref, own_ref):
+    step = pl.program_id(0)
+    rows = map_ref.shape[1]
+
+    @pl.when(step == 0)
+    def _():
+        own_ref[...] = jnp.zeros_like(own_ref)
+
+    windows = []
+    for b in range(rows // BLOCK):
+        start, stop = max(b - 1, 0) * BLOCK, min((b + 2) * BLOCK, rows)
+        windows.append((b, rows + start, own_ref.at[start:stop]))
+    scatter(step, grad_ref, lambda b: b * BLOCK, map_ref, weight_ref, windows)
+
+
+def place_kernel(layout, places_ref, *refs):
     out_ref, sems = refs[-2:]
-    core = lax.bitwise_xor(places_ref[0], jnp.int32(other))
-    first = core * (HALF + 1)
     size = out_ref.shape[1] // 8
     copies = []
 
@@ -291,14 +305,20 @@
         here = pl.ds(pl.multiple_of(at, 16), count)
         copies.append(pltpu.make_async_copy(source, out.at[:, here, :], sems.at[len(copies)]))
 
-    for piece in range(8):
-        put(one.at[piece], out_ref.at[pl.ds(first, K_ONE)], 1, piece, size, 0)
-        for j in range(HALF - K_ONE):
-            source = two.at[pl.ds(piece, 1), pl.ds(j * size, size)]
-            put(source, out_ref.at[pl.ds(first + K_ONE + j, 1)], 2, piece, size, 0)
-        source = two.at[pl.ds(piece, 1), pl.ds((HALF - K_ONE) * size, size // 2)]
-        base = core * (out_ref.shape[1] // 2)
-        put(source, out_ref.at[pl.ds(HALF, 1)], 2, piece, size // 2, base)
+    for n, (other, first_one, first_two) in enumerate(layout):
+        one, two = refs[2 * n : 2 * n + 2]
+        core = lax.bitwise_xor(places_ref[0], jnp.int32(other))
+        first = core * (HALF + 1)
+        for i in range(one.shape[0]):
+            put(one.at[i], out_ref.at[pl.ds(first, K_ONE)], 1, first_one + i, size, 0)
+        for i in range(two.shape[0]):
+            piece = first_two + i
+            for j in range(HALF - K_ONE):
+                source = two.at[pl.ds(i, 1), pl.ds(j * size, size)]
+                put(source, out_ref.at[pl.ds(first + K_ONE + j, 1)], 2, piece, size, 0)
+            source = two.at[pl.ds(i, 1), pl.ds((HALF - K_ONE) * size, size // 2)]
+            base = core * (out_ref.shape[1] // 2)
+            put(source, out_ref.at[pl.ds(HALF, 1)], 2, piece, size // 2, base)
     for copy in copies:
         copy.start()
     for copy in copies:
@@ -334,30 +354,35 @@
     return [swap(piece, by) for by in STAGES[stage]]
 
 
-def summed_over_devices(one, two, grad_conv, push, spread):
+def summed_over_devices(one, two, grad_conv, edge_push, push, spread, finish, place):
     parts, grad_conv = lax.optimization_barrier(((one, two), grad_conv))
     received = [swapped(sends, stage) for (_, sends), stage in zip(parts, "xz")]
-    received, sinks = lax.optimization_barrier((received, push(grad_conv)))
+    received[1][0], edge_grad = lax.optimization_barrier((received[1][0], grad_conv))
+    halo = spread(*edge_push(edge_grad))
+    received, halo = lax.optimization_barrier((received, halo))
     parts = [
         split([kept] + got, stage) for (kept, _), got, stage in zip(parts, received, "zx")
     ]
-    parts, sinks = lax.optimization_barrier((parts, sinks))
+    parts, grad_conv = lax.optimization_barrier((parts, grad_conv))
     received = [swapped(sends, stage) for (_, sends), stage in zip(parts, "zx")]
-    halo = spread(sinks)
-    received, halo = lax.optimization_barrier((received, halo))
+    received, sink = lax.optimization_barrier((received, push(grad_conv)))
     pieces = [part([kept] + got, 0, 1) for (kept, _), got in zip(parts, received)]
     by = 16
     while by < lax.axis_size("dp"):
         pieces = [piece + swap(piece, by) for piece in pieces]
         by *= 2
     pieces = [piece.astype(BF16) for piece in pieces]
-    for stages in ("zx", "xz"):
-        received = [gather_start(piece, stage) for piece, stage in zip(pieces, stages)]
-        received, pieces = lax.optimization_barrier((received, pieces))
-        pieces = [
-            jnp.concatenate([piece] + got, axis=0) for piece, got in zip(pieces, received)
-        ]
-    return pieces, halo
+    pieces, sink = lax.optimization_barrier((pieces, sink))
+    results = finish(sink, halo)
+    received = [gather_start(piece, stage) for piece, stage in zip(pieces, "zx")]
+    received, pieces, results = lax.optimization_barrier((received, pieces, results))
+    early = [jnp.concatenate([piece] + got, axis=0) for piece, got in zip(pieces, received)]
+    early_other = [swap(piece, 1) for piece in early]
+    received = [gather_start(piece, stage) for piece, stage in zip(early, "xz")]
+    received, results = lax.optimization_barrier((received, (results, place(early, early_other))))
+    late = [jnp.concatenate(got, axis=0) for got in received]
+    late_other = [swap(piece, 1) for piece in late]
+    return late, late_other, results
 
 
 def exchanged(value, merge):
@@ -501,59 +526,81 @@
 
     weight_spec = pl.BlockSpec((GROUP, channels, channels), lambda s: (s, 0, 0))
 
+    push_grid = dict(
+        grid=(groups,),
+        compiler_params=params(LIMIT),
+        cost_estimate=cost(1000, 1000),
+    )
+
+    def edge_push(grad_conv):
+        edges = jnp.concatenate([grad_conv[:BLOCK], grad_conv[rows - BLOCK :]], axis=0)
+        edge = jax.ShapeDtypeStruct((BLOCK, channels), BF16)
+        before, after = pl.pallas_call(
+            edge_push_kernel,
+            in_specs=[full((2 * BLOCK, channels)), full((K, rows)), weight_spec],
+            out_specs=[full((BLOCK, channels))] * 2,
+            out_shape=[edge, edge],
+            scratch_shapes=[pltpu.VMEM((BLOCK, channels), F32)] * 2,
+            name="push_edges",
+            **push_grid,
+        )(edges, map_rows, weights)
+        return before, after
+
     def push(grad_conv):
         return pl.pallas_call(
             push_kernel,
-            grid=(groups,),
             in_specs=[full((rows, channels)), full((K, rows)), weight_spec],
-            out_specs=[full((BLOCK, channels)), full((rows, channels)), full((BLOCK, channels))],
-            out_shape=[
-                jax.ShapeDtypeStruct((BLOCK, channels), BF16),
-                jax.ShapeDtypeStruct((rows, channels), F32),
-                jax.ShapeDtypeStruct((BLOCK, channels), BF16),
+            out_specs=full((rows, channels)),
+            out_shape=jax.ShapeDtypeStruct((rows, channels), F32),
+            name="push",
+            **push_grid,
+        )(grad_conv, map_rows, weights)
+
+    def finish(sink, halo):
+        even, other = halo
+        from_prev = jnp.where(odd == 1, even, other).astype(F32)
+        from_next = jnp.where(odd == 1, other, even).astype(F32)
+        occupied = occupied_rows(occupancy[0], rows)
+        received = jnp.concatenate(
+            [
+                sink[:BLOCK] + from_prev,
+                sink[BLOCK : rows - BLOCK],
+                sink[rows - BLOCK :] + from_next,
             ],
-            scratch_shapes=[pltpu.VMEM((rows + 2 * BLOCK, channels), F32)],
-            compiler_params=params(LIMIT),
-            cost_estimate=cost(1000, 1000),
-            name="push",
-        )(grad_conv, map_rows, weights)
-
-    def spread_gradient(sinks):
-        sink_before, sink_own, sink_after = sinks
-        return neighbours_swap(sink_before, sink_after), sink_own
-
-    (own_one, own_two), ((even, other), sink_own) = summed_over_devices(
-        one, two, grad_conv, push, spread_gradient
-    )
-    from_prev = jnp.where(odd == 1, even, other).astype(F32)
-    from_next = jnp.where(odd == 1, other, even).astype(F32)
-    occupied = occupied_rows(occupancy[0], rows)
-    received = jnp.concatenate(
-        [
-            sink_own[:BLOCK] + from_prev,
-            sink_own[BLOCK : rows - BLOCK],
-            sink_own[rows - BLOCK :] + from_next,
-        ],
-        axis=0,
-    )
-    grad_features = (jnp.where(occupied, cotangent.astype(F32), 0.0) + received).astype(BF16)
-
-    def placed(other, sources, *into):
+            axis=0,
+        )
+        total = jnp.where(occupied, cotangent.astype(F32), 0.0) + received
+        return total.astype(BF16), sums[0], sums[1]
+
+
+    def placed(layout, sources, *into):
+        count = sum(one.shape[0] + two.shape[0] * (HALF - K_ONE + 1) for one, two in sources)
+        operands = []
+        for one, two in sources:
+            operands += [one.reshape(one.shape[0], K_ONE, size, channels), two]
         return pl.pallas_call(
-            functools.partial(place_kernel, other),
-            in_specs=[smem, anywhere, anywhere] + [hbm] * len(into),
+            functools.partial(place_kernel, layout),
+            in_specs=[smem] + [anywhere] * len(operands) + [hbm] * len(into),
             out_specs=hbm,
             out_shape=jax.ShapeDtypeStruct(weights.shape, BF16),
-            scratch_shapes=[pltpu.SemaphoreType.DMA((8 * (HALF - K_ONE + 2),))],
-            input_output_aliases={3: 0} if into else {},
+            scratch_shapes=[pltpu.SemaphoreType.DMA((count,))],
+            input_output_aliases={len(operands) + 1: 0} if into else {},
             compiler_params=params(LIMIT),
             cost_estimate=cost(0, K * channels * channels * 2),
             name="place",
-        )(places, sources[0].reshape(8, K_ONE, size, channels), sources[1], *into)
-
-    others = [swap(own_one, 1), swap(own_two, 1)]
-    grad_weights = placed(1, others, placed(0, (own_one, own_two)))
-    return block_out, grad_features, grad_weights, sums[0], sums[1]
+        )(places, *operands, *into)
+
+    def place_early(own, other):
+        return placed(((0, 0, 0), (1, 0, 0)), (own, other))
+
+    late, late_other, results = summed_over_devices(
+        one, two, grad_conv, edge_push, push, neighbours_swap, finish, place_early
+    )
+    (grad_features, grad_gain, grad_shift), grad_weights = results
+    first_late = (8 - late[0].shape[0], 8 - late[1].shape[0])
+    grad_weights = placed(((0, *first_late),), (late,), grad_weights)
+    grad_weights = placed(((1, *first_late),), (late_other,), grad_weights)
+    return block_out, grad_features, grad_weights, grad_gain, grad_shift
 
 
 def solution(mesh):

time: 125 us -> 124 us (level)
  starting transfers between devices: 52.1 us -> 48.5 us
  Pallas kernels: 35.4 us -> 37.4 us
    ppermute x33 -> x35, starting transfers between devices: 43.4 us -> 37.8 us  [swap(): return lax.ppermute(value, 'dp', [(i, i ^ by) for i in range(peers)])]
    pallas_call x3 -> x5, Pallas kernels: 13.6 us -> 15.6 us  [the longest x1 7.97 us: push(): pl.pallas_call(push_kernel, in_specs=[full((rows, channels)), full((K, ro...]
    ppermute x2, starting transfers between devices: 8.63 us -> 10.5 us  [neighbours_swap(): lax.ppermute(jnp.where(odd == 1, to_after, to_before), 'dp', other_pairs)]
    ppermute x2, waiting for transfers between devices: 0.42 us -> 1.82 us  [neighbours_swap(): lax.ppermute(jnp.where(odd == 1, to_after, to_before), 'dp', other_pairs)]
    ppermute x33 -> x35, waiting for transfers between devices: 30.3 us -> 30.8 us  [swap(): return lax.ppermute(value, 'dp', [(i, i ^ by) for i in range(peers)])]
  transfers between devices with their start and end apart: 37 -> 39, of which waited for: 18 -> 16; matrix products, arithmetic and copies ran while one was open for 1% -> 1% of each run, Pallas kernels for 14% -> 16%
where the time goes in v7:
time: 124 us; the launch traced here: 123 us
  starting transfers between devices  48.5 us (39%)
  Pallas kernels  37.4 us (30%)
  waiting for transfers between devices  32.7 us (26%)
  other arithmetic  2.26 us (2%)
  between operations  1.82 us (1%)
    ppermute x35, starting transfers between devices, swap(): return lax.ppermute(value, 'dp', [(i, i ^ by) for i in range(peers)])  37.8 us
    ppermute x35, waiting for transfers between devices, swap(): return lax.ppermute(value, 'dp', [(i, i ^ by) for i in range(peers)])  30.8 us
    ppermute x2, starting transfers between devices, neighbours_swap(): lax.ppermute(jnp.where(odd == 1, to_after, to_before), 'dp', other_pairs)  10.5 us
    pallas_call x1, Pallas kernels, per_device(): pl.pallas_call(gradient_kernel, in_specs=[smem] + [vmem] * 6, out_specs=[...  9.89 us
    pallas_call x1, Pallas kernels, push(): pl.pallas_call(push_kernel, in_specs=[full((rows, channels)), full((K, ro...  7.97 us
    pallas_call x1, Pallas kernels, per_device(): pl.pallas_call(inner_kernel, in_specs=[vmem, vmem, hbm], out_specs=vmem,...  5.73 us
    pallas_call x3, Pallas kernels, placed(): pl.pallas_call(functools.partial(place_kernel, layout), in_specs=[smem] +...  5.45 us
    pallas_call x1, Pallas kernels, per_device(): pl.pallas_call(outer_kernel, in_specs=[smem, smem, vmem, vmem, vmem, vmem...  4.92 us
  transfers between devices with their start and end apart: 39, of which 16 were waited for; matrix products, arithmetic and copies ran while one was open for 1% of the time, Pallas kernels for 16%

profile of v7, /device:TPU:1, one launch (start us, length us, event | category | flops | bytes accessed | tf_op | source)
XLA Modules:
  0.0 123.3 jit_solution(14150243644144382192)
XLA Ops:
  1.5 4.5 %collective-permute-start.1 = (bf16[128,256]{1,0:T(8,128)(2,1)S(1)}, bf16[128,256]{1,0:T(8,128)(2,1)S(1)}, u32[]{:S(2)}, u32[]{:S(2)}) collective-permute-start(bf16[128,256]{1,0:T(8,128)(2,1)S(1)} %get-tuple-element.141), channel_id=1, source_target_pairs={{1,2},{2,1},{3,4},{4,3},{5,6},{6,5},{7,8},{8,7},{9,10},{10,9},{11,... | collective-permute-start | bytes 196616 | tf_op jit(solution)/shard_map/ppermute | solution.py:416
  6.1 5.7 %conv_inner.1.inner_ref = f32[256,256]{1,0:T(8,128)S(1)} custom-call(s32[27,512]{1,0:T(8,128)} %bitcast.17, bf16[512,256]{1,0:T(8,128)(2,1)} %feature_ref.1, bf16[27,256,256]{2,1,0:T(8,128)(2,1)} %weight_ref.3), custom_call_target="tpu_custom_call" | custom-call | flops 2264924160 | bytes 10616832 | tf_op jit(solution)/shard_map/conv_inner/pallas_call | solution.py:446
  12.6 4.9 %conv_outer.1 = (f32[256,256]{1,0:T(8,128)S(1)}, f32[3,256]{1,0:T(4,128)S(1)}, bf16[768,256]{1,0:T(8,128)(2,1)S(1)}) custom-call(s32[1]{0:T(128)S(6)} %copy.22.filled_ref, s32[1]{0:T(128)} %bitcast.1.odd_ref, s32[27,512]{1,0:T(8,128)S(1)} %bitcast.18, bf16[512,256]{1,0:T(8,128)(2,1)S(1)} %copy-done.2, bf16[128,256]{1,0:T(8,128)(2,1)S(1)} %collective-permute-done.even_ref, ...), custom_call_target="tpu_custom_call" | custom-call | flops 2264924160 | bytes 10616832 | tf_op jit(solution)/shard_map/conv_outer/pallas_call | solution.py:457
  17.5 1.7 %collective-permute-start.4 = (f32[3,256]{1,0:T(4,128)S(1)}, f32[3,256]{1,0:T(4,128)S(1)}, u32[]{:S(2)}, u32[]{:S(2)}) collective-permute-start(f32[3,256]{1,0:T(4,128)S(1)} %get-tuple-element.68), channel_id=1, source_target_pairs={{0,3},{1,2},{2,1},{3,0},{4,7},{5,6},{6,5},{7,4},{8,11},{9,10},{10,... | collective-permute-start | bytes 9224 | tf_op jit(solution)/shard_map/ppermute | solution.py:330
  21.7 2.4 %collective-permute-start.7 = (f32[3,256]{1,0:T(4,128)S(1)}, f32[3,256]{1,0:T(4,128)S(1)}, u32[]{:S(2)}, u32[]{:S(2)}) collective-permute-start(f32[3,256]{1,0:T(4,128)S(1)} %pad_maximum_fusion.1.refs_0_), channel_id=1, source_target_pairs={{0,12},{1,13},{2,14},{3,15},{4,8},{5,9},{6,10},{7,11},{8,4},{9,5},... | collective-permute-start | bytes 9224 | tf_op jit(solution)/shard_map/ppermute | solution.py:330
  26.1 1.7 %collective-permute-done.6.refs_2_ = f32[3,256]{1,0:T(4,128)S(1)} collective-permute-done((f32[3,256]{1,0:T(4,128)S(1)}, f32[3,256]{1,0:T(4,128)S(1)}, u32[]{:S(2)}, u32[]{:S(2)}) %collective-permute-start.6) | collective-permute-done | bytes 3104 | tf_op jit(solution)/shard_map/ppermute | solution.py:330
  28.8 3.4 %collective-permute-start.10 = (f32[2,256]{1,0:T(2,128)S(1)}, f32[2,256]{1,0:T(2,128)S(1)}, u32[]{:S(2)}, u32[]{:S(2)}) collective-permute-start(f32[2,256]{1,0:T(2,128)S(1)} %get-tuple-element.70), channel_id=1, source_target_pairs={{0,3},{1,2},{2,1},{3,0},{4,7},{5,6},{6,5},{7,4},{8,11},{9,10},{10,... | collective-permute-start | bytes 6152 | tf_op jit(solution)/shard_map/ppermute | solution.py:330
  36.5 1.7 %collective-permute-start.11 = (f32[2,256]{1,0:T(2,128)S(1)}, f32[2,256]{1,0:T(2,128)S(1)}, u32[]{:S(2)}, u32[]{:S(2)}) collective-permute-start(f32[2,256]{1,0:T(2,128)S(1)} %add_add_fusion.refs_4_), channel_id=1, source_target_pairs={{0,4},{1,5},{2,6},{3,7},{4,0},{5,1},{6,2},{7,3},{8,12},{9,13},{10,... | collective-permute-start | bytes 6152 | tf_op jit(solution)/shard_map/ppermute | solution.py:330
  42.9 9.9 %weight_gradient.1 = (f32[4,288,256]{2,1,0:T(8,128)S(1)}, bf16[4,288,256]{2,1,0:T(8,128)(2,1)S(1)}, f32[2,144,256]{2,1,0:T(8,128)S(1)}, bf16[2,144,256]{2,1,0:T(...) custom-call(s32[3]{0:T(128)S(1)} %pad_add_fusion.place_ref.places_ref, ...), custom_call_target="tpu_custom_call" | custom-call | flops 4529848320 | bytes 10616832 | tf_op jit(solution)/shard_map/weight_gradient/pallas_call | solution.py:508
  56.1 3.8 %collective-permute-done.18 = bf16[2,144,256]{2,1,0:T(8,128)(2,1)S(1)} collective-permute-done((bf16[2,144,256]{2,1,0:T(8,128)(2,1)S(1)}, bf16[2,144,256]{2,1,0:T(8,128)(2,1)S(1)}, u32[]{:S(2)}, u32[]{:S(2)}) %collective-permute-start.18) | collective-permute-done | bytes 147488 | tf_op jit(solution)/shard_map/ppermute | solution.py:330
  61.2 2.1 %push_edges.1 = (bf16[128,256]{1,0:T(8,128)(2,1)S(1)}, bf16[128,256]{1,0:T(8,128)(2,1)S(1)}) custom-call(bf16[256,256]{1,0:T(8,128)(2,1)S(1)} %pad_maximum_fusion.grad_ref, s32[27,512]{1,0:T(8,128)S(1)} %bitcast.21, bf16[27,256,256]{2,1,0:T(8,128)(2,1)S(1)} %copy-done), custom_call_target="tpu_custom_call" | custom-call | flops 1000 | bytes 1000 | tf_op jit(solution)/shard_map/push_edges/pallas_call | solution.py:538
  63.4 6.0 %collective-permute-start.22 = (bf16[128,256]{1,0:T(8,128)(2,1)S(1)}, bf16[128,256]{1,0:T(8,128)(2,1)S(1)}, u32[]{:S(2)}, u32[]{:S(2)}) collective-permute-start(bf16[128,256]{1,0:T(8,128)(2,1)S(1)} %get-tuple-element.143), channel_id=1, source_target_pairs={{1,2},{2,1},{3,4},{4,3},{5,6},{6,5},{7,8},{8,7},{9,10},{10,9},{11,... | collective-permute-start | bytes 196616 | tf_op jit(solution)/shard_map/ppermute | solution.py:416
  69.5 1.8 %collective-permute-done.22 = bf16[128,256]{1,0:T(8,128)(2,1)S(1)} collective-permute-done((bf16[128,256]{1,0:T(8,128)(2,1)S(1)}, bf16[128,256]{1,0:T(8,128)(2,1)S(1)}, u32[]{:S(2)}, u32[]{:S(2)}) %collective-permute-start.22) | collective-permute-done | bytes 65568 | tf_op jit(solution)/shard_map/ppermute | solution.py:416
  73.3 3.2 %collective-permute-start.25 = (bf16[1,288,256]{2,1,0:T(8,128)(2,1)S(1)}, bf16[1,288,256]{2,1,0:T(8,128)(2,1)S(1)}, u32[]{:S(2)}, u32[]{:S(2)}) collective-permute-start(bf16[1,288,256]{2,1,0:T(8,128)(2,1)S(1)} %get-tuple-element.97), channel_id=1, source_target_pairs={{0,12},{1,13},{2,14},{3,15},{4,8},{5,9},{6,10},{7,11},{8,4},{9,5},... | collective-permute-start | bytes 442376 | tf_op jit(solution)/shard_map/ppermute | solution.py:330
  77.1 8.0 %push.1 = f32[512,256]{1,0:T(8,128)S(1)} custom-call(bf16[512,256]{1,0:T(8,128)(2,1)S(1)} %get-tuple-element.99.grad_own.grad_ref, s32[27,512]{1,0:T(8,128)S(1)} %bitcast.22, bf16[27,256,256]{2,1,0:T(8,128)(2,1)S(1)} %copy-done), custom_call_target="tpu_custom_call" | custom-call | flops 1000 | bytes 1000 | tf_op jit(solution)/shard_map/push/pallas_call | solution.py:550
  85.3 4.1 %collective-permute-start.28 = (bf16[1,288,256]{2,1,0:T(8,128)(2,1)S(1)}, bf16[1,288,256]{2,1,0:T(8,128)(2,1)S(1)}, u32[]{:S(2)}, u32[]{:S(2)}) collective-permute-start(bf16[1,288,256]{2,1,0:T(8,128)(2,1)S(1)} %add_convert_fusion), channel_id=1, source_target_pairs={{0,8},{1,9},{2,10},{3,11},{4,12},{5,13},{6,14},{7,15},{8,0},{9,1},... | collective-permute-start | bytes 442376 | tf_op jit(solution)/shard_map/ppermute | solution.py:330
  89.4 1.9 %collective-permute-start.30 = (bf16[1,144,256]{2,1,0:T(8,128)(2,1)S(1)}, bf16[1,144,256]{2,1,0:T(8,128)(2,1)S(1)}, u32[]{:S(2)}, u32[]{:S(2)}) collective-permute-start(bf16[1,144,256]{2,1,0:T(8,128)(2,1)S(1)} %add_convert_fusion.4), channel_id=1, source_target_pairs={{0,2},{1,3},{2,0},{3,1},{4,6},{5,7},{6,4},{7,5},{8,10},{9,11},{10,... | collective-permute-start | bytes 221192 | tf_op jit(solution)/shard_map/ppermute | solution.py:330
  93.3 8.3 %collective-permute-done.28 = bf16[1,288,256]{2,1,0:T(8,128)(2,1)S(1)} collective-permute-done((bf16[1,288,256]{2,1,0:T(8,128)(2,1)S(1)}, bf16[1,288,256]{2,1,0:T(8,128)(2,1)S(1)}, u32[]{:S(2)}, u32[]{:S(2)}) %collective-permute-start.28) | collective-permute-done | bytes 147488 | tf_op jit(solution)/shard_map/ppermute | solution.py:330
  106.0 2.1 %collective-permute-start.32 = (bf16[2,144,256]{2,1,0:T(8,128)(2,1)S(1)}, bf16[2,144,256]{2,1,0:T(8,128)(2,1)S(1)}, u32[]{:S(2)}, u32[]{:S(2)}) collective-permute-start(bf16[2,144,256]{2,1,0:T(8,128)(2,1)S(1)} %constant_dynamic-update-slice_fusion.4.refs_1_), channel_id=1, source_target_pairs={{0,4},{1,5},{2,6},{3,7},{4,0},{5,1},{6,2},{7,3},{8,12},{9,13},{10,... | collective-permute-start | bytes 442376 | tf_op jit(solution)/shard_map/ppermute | solution.py:330
  108.1 1.9 %place.3.refs_2_ = bf16[27,256,256]{2,1,0:T(8,128)(2,1)} custom-call(s32[3]{0:T(128)S(1)} %pad_add_fusion.place_ref.places_ref, bf16[4,9,32,256]{3,2,1,0:T(8,128)(2,1)S(1)} %bitcast.13, bf16[2,144,256]{2,1,0:T(8,128)(2,1)S(1)} %constant_dynamic-update-slice_fusion.4.refs_1_, bf16[4,9,32,256]{3,2,1,0:T(8,128)(2,1)S(1)} %bitcast.16, ...), custom_call_target="tpu_custom_call" | custom-call | bytes 3538944 | tf_op jit(solution)/shard_map/place/pallas_call | solution.py:581
  110.0 1.7 %collective-permute-done.34 = bf16[2,144,256]{2,1,0:T(8,128)(2,1)S(1)} collective-permute-done((bf16[2,144,256]{2,1,0:T(8,128)(2,1)S(1)}, bf16[2,144,256]{2,1,0:T(8,128)(2,1)S(1)}, u32[]{:S(2)}, u32[]{:S(2)}) %collective-permute-start.34) | collective-permute-done | bytes 147488 | tf_op jit(solution)/shard_map/ppermute | solution.py:330
  111.7 6.8 %collective-permute-done.33 = bf16[2,144,256]{2,1,0:T(8,128)(2,1)S(1)} collective-permute-done((bf16[2,144,256]{2,1,0:T(8,128)(2,1)S(1)}, bf16[2,144,256]{2,1,0:T(8,128)(2,1)S(1)}, u32[]{:S(2)}, u32[]{:S(2)}) %collective-permute-start.33) | collective-permute-done | bytes 147488 | tf_op jit(solution)/shard_map/ppermute | solution.py:330
  119.2 1.8 %place.4.refs_2_ = bf16[27,256,256]{2,1,0:T(8,128)(2,1)} custom-call(s32[3]{0:T(128)S(1)} %pad_add_fusion.place_ref.places_ref, bf16[4,9,32,256]{3,2,1,0:T(8,128)(2,1)S(1)} %bitcast.14, bf16[6,144,256]{2,1,0:T(8,128)(2,1)S(1)} %constant_dynamic-update-slice_fusion.6.refs_1_, bf16[27,256,256]{2,1,0:T(8,128)(2,1)} %place.3.refs_2_), custom_call_target="tpu_custom_call", output_to_operand_aliasing={{}: (3, {})} | custom-call | bytes 3538944 | tf_op jit(solution)/shard_map/place/pallas_call | solution.py:581
  121.4 1.8 %place.5 = bf16[27,256,256]{2,1,0:T(8,128)(2,1)} custom-call(s32[3]{0:T(128)S(1)} %pad_add_fusion.place_ref.places_ref, bf16[4,9,32,256]{3,2,1,0:T(8,128)(2,1)S(1)} %bitcast.15, bf16[6,144,256]{2,1,0:T(8,128)(2,1)S(1)} %collective-permute-done.38.refs_1_, bf16[27,256,256]{2,1,0:T(8,128)(2,1)} %place.4.refs_2_), custom_call_target="tpu_custom_call", output_to_operand_aliasing={{}: (3, {})} | custom-call | bytes 3538944 | tf_op jit(solution)/shard_map/place/pallas_call | solution.py:581
  (102 shorter events, 30.1 us)
Async XLA Ops:
  1.5 11.0 %collective-permute-start.1 = (bf16[128,256]{1,0:T(8,128)(2,1)S(1)}, bf16[128,256]{1,0:T(8,128)(2,1)S(1)}, u32[]{:S(2)}, u32[]{:S(2)}) collective-permute-start(bf16[128,256]{1,0:T(8,128)(2,1)S(1)} %get-tuple-element.141), channel_id=1, source_target_pairs={{1,2},{2,1},{3,4},{4,3},{5,6},{6,5},{7,8},{8,7},{9,10},{10,9},{11,... | collective-permute-start | bytes 196616 | tf_op jit(solution)/shard_map/ppermute | solution.py:416
  6.0 6.5 %collective-permute-start = (bf16[128,256]{1,0:T(8,128)(2,1)S(1)}, bf16[128,256]{1,0:T(8,128)(2,1)S(1)}, u32[]{:S(2)}, u32[]{:S(2)}) collective-permute-start(bf16[128,256]{1,0:T(8,128)(2,1)S(1)} %get-tuple-element.142), channel_id=1, source_target_pairs={{0,1},{1,0},{2,3},{3,2},{4,5},{5,4},{6,7},{7,6},{8,9},{9,8},{10,11... | collective-permute-start | bytes 196616 | tf_op jit(solution)/shard_map/ppermute | solution.py:415
  21.7 4.3 %collective-permute-start.7 = (f32[3,256]{1,0:T(4,128)S(1)}, f32[3,256]{1,0:T(4,128)S(1)}, u32[]{:S(2)}, u32[]{:S(2)}) collective-permute-start(f32[3,256]{1,0:T(4,128)S(1)} %pad_maximum_fusion.1.refs_0_), channel_id=1, source_target_pairs={{0,12},{1,13},{2,14},{3,15},{4,8},{5,9},{6,10},{7,11},{8,4},{9,5},... | collective-permute-start | bytes 9224 | tf_op jit(solution)/shard_map/ppermute | solution.py:330
  28.8 4.8 %collective-permute-start.10 = (f32[2,256]{1,0:T(2,128)S(1)}, f32[2,256]{1,0:T(2,128)S(1)}, u32[]{:S(2)}, u32[]{:S(2)}) collective-permute-start(f32[2,256]{1,0:T(2,128)S(1)} %get-tuple-element.70), channel_id=1, source_target_pairs={{0,3},{1,2},{2,1},{3,0},{4,7},{5,6},{6,5},{7,4},{8,11},{9,10},{10,... | collective-permute-start | bytes 6152 | tf_op jit(solution)/shard_map/ppermute | solution.py:330
  32.6 10.3 %collective-permute-start.16 = (bf16[768,256]{1,0:T(8,128)(2,1)S(1)}, bf16[768,256]{1,0:T(8,128)(2,1)S(1)}, u32[]{:S(2)}, u32[]{:S(2)}) collective-permute-start(bf16[768,256]{1,0:T(8,128)(2,1)S(1)} %get-tuple-element.72.window_own), channel_id=1, source_target_pairs={{0,1},{1,0},{2,3},{3,2},{4,5},{5,4},{6,7},{7,6},{8,9},{9,8},{10,11... | collective-permute-start | bytes 1179656 | tf_op jit(solution)/shard_map/ppermute | solution.py:330
  34.6 4.3 %collective-permute-start.13 = (f32[2,256]{1,0:T(2,128)S(1)}, f32[2,256]{1,0:T(2,128)S(1)}, u32[]{:S(2)}, u32[]{:S(2)}) collective-permute-start(f32[2,256]{1,0:T(2,128)S(1)} %add_add_fusion.refs_4_), channel_id=1, source_target_pairs={{0,12},{1,13},{2,14},{3,15},{4,8},{5,9},{6,10},{7,11},{8,4},{9,5},... | collective-permute-start | bytes 6152 | tf_op jit(solution)/shard_map/ppermute | solution.py:330
  52.8 7.2 %collective-permute-start.18 = (bf16[2,144,256]{2,1,0:T(8,128)(2,1)S(1)}, bf16[2,144,256]{2,1,0:T(8,128)(2,1)S(1)}, u32[]{:S(2)}, u32[]{:S(2)}) collective-permute-start(bf16[2,144,256]{2,1,0:T(8,128)(2,1)S(1)} %get-tuple-element.81), channel_id=1, source_target_pairs={{0,4},{1,5},{2,6},{3,7},{4,0},{5,1},{6,2},{7,3},{8,12},{9,13},{10,... | collective-permute-start | bytes 442376 | tf_op jit(solution)/shard_map/ppermute | solution.py:330
  54.0 15.5 %collective-permute-start.19 = (bf16[2,144,256]{2,1,0:T(8,128)(2,1)S(1)}, bf16[2,144,256]{2,1,0:T(8,128)(2,1)S(1)}, u32[]{:S(2)}, u32[]{:S(2)}) collective-permute-start(bf16[2,144,256]{2,1,0:T(8,128)(2,1)S(1)} %get-tuple-element.84), channel_id=1, source_target_pairs={{0,8},{1,9},{2,10},{3,11},{4,12},{5,13},{6,14},{7,15},{8,0},{9,1},... | collective-permute-start | bytes 442376 | tf_op jit(solution)/shard_map/ppermute | solution.py:330
  54.8 16.5 %collective-permute-start.17 = (bf16[4,288,256]{2,1,0:T(8,128)(2,1)S(1)}, bf16[4,288,256]{2,1,0:T(8,128)(2,1)S(1)}, u32[]{:S(2)}, u32[]{:S(2)}) collective-permute-start(bf16[4,288,256]{2,1,0:T(8,128)(2,1)S(1)} %get-tuple-element.80), channel_id=1, source_target_pairs={{0,2},{1,3},{2,0},{3,1},{4,6},{5,7},{6,4},{7,5},{8,10},{9,11},{10,... | collective-permute-start | bytes 1769480 | tf_op jit(solution)/shard_map/ppermute | solution.py:330
  60.0 9.5 %collective-permute-start.20 = (bf16[2,144,256]{2,1,0:T(8,128)(2,1)S(1)}, bf16[2,144,256]{2,1,0:T(8,128)(2,1)S(1)}, u32[]{:S(2)}, u32[]{:S(2)}) collective-permute-start(bf16[2,144,256]{2,1,0:T(8,128)(2,1)S(1)} %get-tuple-element.85), channel_id=1, source_target_pairs={{0,12},{1,13},{2,14},{3,15},{4,8},{5,9},{6,10},{7,11},{8,4},{9,5},... | collective-permute-start | bytes 442376 | tf_op jit(solution)/shard_map/ppermute | solution.py:330
  63.4 8.0 %collective-permute-start.22 = (bf16[128,256]{1,0:T(8,128)(2,1)S(1)}, bf16[128,256]{1,0:T(8,128)(2,1)S(1)}, u32[]{:S(2)}, u32[]{:S(2)}) collective-permute-start(bf16[128,256]{1,0:T(8,128)(2,1)S(1)} %get-tuple-element.143), channel_id=1, source_target_pairs={{1,2},{2,1},{3,4},{4,3},{5,6},{6,5},{7,8},{8,7},{9,10},{10,9},{11,... | collective-permute-start | bytes 196616 | tf_op jit(solution)/shard_map/ppermute | solution.py:416
  71.6 13.4 %collective-permute-start.26 = (bf16[1,144,256]{2,1,0:T(8,128)(2,1)S(1)}, bf16[1,144,256]{2,1,0:T(8,128)(2,1)S(1)}, u32[]{:S(2)}, u32[]{:S(2)}) collective-permute-start(bf16[1,144,256]{2,1,0:T(8,128)(2,1)S(1)} %get-tuple-element.98), channel_id=1, source_target_pairs={{0,2},{1,3},{2,0},{3,1},{4,6},{5,7},{6,4},{7,5},{8,10},{9,11},{10,... | collective-permute-start | bytes 221192 | tf_op jit(solution)/shard_map/ppermute | solution.py:330
  72.9 12.1 %collective-permute-start.23 = (bf16[1,288,256]{2,1,0:T(8,128)(2,1)S(1)}, bf16[1,288,256]{2,1,0:T(8,128)(2,1)S(1)}, u32[]{:S(2)}, u32[]{:S(2)}) collective-permute-start(bf16[1,288,256]{2,1,0:T(8,128)(2,1)S(1)} %get-tuple-element.95), channel_id=1, source_target_pairs={{0,4},{1,5},{2,6},{3,7},{4,0},{5,1},{6,2},{7,3},{8,12},{9,13},{10,... | collective-permute-start | bytes 442376 | tf_op jit(solution)/shard_map/ppermute | solution.py:330
  73.0 12.1 %collective-permute-start.24 = (bf16[1,288,256]{2,1,0:T(8,128)(2,1)S(1)}, bf16[1,288,256]{2,1,0:T(8,128)(2,1)S(1)}, u32[]{:S(2)}, u32[]{:S(2)}) collective-permute-start(bf16[1,288,256]{2,1,0:T(8,128)(2,1)S(1)} %get-tuple-element.96), channel_id=1, source_target_pairs={{0,8},{1,9},{2,10},{3,11},{4,12},{5,13},{6,14},{7,15},{8,0},{9,1},... | collective-permute-start | bytes 442376 | tf_op jit(solution)/shard_map/ppermute | solution.py:330
  73.3 11.8 %collective-permute-start.25 = (bf16[1,288,256]{2,1,0:T(8,128)(2,1)S(1)}, bf16[1,288,256]{2,1,0:T(8,128)(2,1)S(1)}, u32[]{:S(2)}, u32[]{:S(2)}) collective-permute-start(bf16[1,288,256]{2,1,0:T(8,128)(2,1)S(1)} %get-tuple-element.97), channel_id=1, source_target_pairs={{0,12},{1,13},{2,14},{3,15},{4,8},{5,9},{6,10},{7,11},{8,4},{9,5},... | collective-permute-start | bytes 442376 | tf_op jit(solution)/shard_map/ppermute | solution.py:330
  85.2 8.2 %collective-permute-start.29 = (bf16[1,288,256]{2,1,0:T(8,128)(2,1)S(1)}, bf16[1,288,256]{2,1,0:T(8,128)(2,1)S(1)}, u32[]{:S(2)}, u32[]{:S(2)}) collective-permute-start(bf16[1,288,256]{2,1,0:T(8,128)(2,1)S(1)} %add_convert_fusion), channel_id=1, source_target_pairs={{0,12},{1,13},{2,14},{3,15},{4,8},{5,9},{6,10},{7,11},{8,4},{9,5},... | collective-permute-start | bytes 442376 | tf_op jit(solution)/shard_map/ppermute | solution.py:330
  85.3 16.3 %collective-permute-start.28 = (bf16[1,288,256]{2,1,0:T(8,128)(2,1)S(1)}, bf16[1,288,256]{2,1,0:T(8,128)(2,1)S(1)}, u32[]{:S(2)}, u32[]{:S(2)}) collective-permute-start(bf16[1,288,256]{2,1,0:T(8,128)(2,1)S(1)} %add_convert_fusion), channel_id=1, source_target_pairs={{0,8},{1,9},{2,10},{3,11},{4,12},{5,13},{6,14},{7,15},{8,0},{9,1},... | collective-permute-start | bytes 442376 | tf_op jit(solution)/shard_map/ppermute | solution.py:330
  89.4 12.3 %collective-permute-start.27 = (bf16[1,288,256]{2,1,0:T(8,128)(2,1)S(1)}, bf16[1,288,256]{2,1,0:T(8,128)(2,1)S(1)}, u32[]{:S(2)}, u32[]{:S(2)}) collective-permute-start(bf16[1,288,256]{2,1,0:T(8,128)(2,1)S(1)} %add_convert_fusion), channel_id=1, source_target_pairs={{0,4},{1,5},{2,6},{3,7},{4,0},{5,1},{6,2},{7,3},{8,12},{9,13},{10,... | collective-permute-start | bytes 442376 | tf_op jit(solution)/shard_map/ppermute | solution.py:330
  89.4 4.0 %collective-permute-start.30 = (bf16[1,144,256]{2,1,0:T(8,128)(2,1)S(1)}, bf16[1,144,256]{2,1,0:T(8,128)(2,1)S(1)}, u32[]{:S(2)}, u32[]{:S(2)}) collective-permute-start(bf16[1,144,256]{2,1,0:T(8,128)(2,1)S(1)} %add_convert_fusion.4), channel_id=1, source_target_pairs={{0,2},{1,3},{2,0},{3,1},{4,6},{5,7},{6,4},{7,5},{8,10},{9,11},{10,... | collective-permute-start | bytes 221192 | tf_op jit(solution)/shard_map/ppermute | solution.py:330
  101.7 6.4 %collective-permute-start.35 = (bf16[4,288,256]{2,1,0:T(8,128)(2,1)S(1)}, bf16[4,288,256]{2,1,0:T(8,128)(2,1)S(1)}, u32[]{:S(2)}, u32[]{:S(2)}) collective-permute-start(bf16[4,288,256]{2,1,0:T(8,128)(2,1)S(1)} %constant_dynamic-update-slice_fusion), channel_id=1, source_target_pairs={{0,1},{1,0},{2,3},{3,2},{4,5},{5,4},{6,7},{7,6},{8,9},{9,8},{10,11... | collective-permute-start | bytes 1769480 | tf_op jit(solution)/shard_map/ppermute | solution.py:330
  102.9 15.6 %collective-permute-start.31 = (bf16[4,288,256]{2,1,0:T(8,128)(2,1)S(1)}, bf16[4,288,256]{2,1,0:T(8,128)(2,1)S(1)}, u32[]{:S(2)}, u32[]{:S(2)}) collective-permute-start(bf16[4,288,256]{2,1,0:T(8,128)(2,1)S(1)} %constant_dynamic-update-slice_fusion), channel_id=1, source_target_pairs={{0,2},{1,3},{2,0},{3,1},{4,6},{5,7},{6,4},{7,5},{8,10},{9,11},{10,... | collective-permute-start | bytes 1769480 | tf_op jit(solution)/shard_map/ppermute | solution.py:330
  104.6 7.1 %collective-permute-start.34 = (bf16[2,144,256]{2,1,0:T(8,128)(2,1)S(1)}, bf16[2,144,256]{2,1,0:T(8,128)(2,1)S(1)}, u32[]{:S(2)}, u32[]{:S(2)}) collective-permute-start(bf16[2,144,256]{2,1,0:T(8,128)(2,1)S(1)} %constant_dynamic-update-slice_fusion.4.refs_1_), channel_id=1, source_target_pairs={{0,12},{1,13},{2,14},{3,15},{4,8},{5,9},{6,10},{7,11},{8,4},{9,5},... | collective-permute-start | bytes 442376 | tf_op jit(solution)/shard_map/ppermute | solution.py:330
  106.0 12.5 %collective-permute-start.33 = (bf16[2,144,256]{2,1,0:T(8,128)(2,1)S(1)}, bf16[2,144,256]{2,1,0:T(8,128)(2,1)S(1)}, u32[]{:S(2)}, u32[]{:S(2)}) collective-permute-start(bf16[2,144,256]{2,1,0:T(8,128)(2,1)S(1)} %constant_dynamic-update-slice_fusion.4.refs_1_), channel_id=1, source_target_pairs={{0,8},{1,9},{2,10},{3,11},{4,12},{5,13},{6,14},{7,15},{8,0},{9,1},... | collective-permute-start | bytes 442376 | tf_op jit(solution)/shard_map/ppermute | solution.py:330
  106.0 12.5 %collective-permute-start.32 = (bf16[2,144,256]{2,1,0:T(8,128)(2,1)S(1)}, bf16[2,144,256]{2,1,0:T(8,128)(2,1)S(1)}, u32[]{:S(2)}, u32[]{:S(2)}) collective-permute-start(bf16[2,144,256]{2,1,0:T(8,128)(2,1)S(1)} %constant_dynamic-update-slice_fusion.4.refs_1_), channel_id=1, source_target_pairs={{0,4},{1,5},{2,6},{3,7},{4,0},{5,1},{6,2},{7,3},{8,12},{9,13},{10,... | collective-permute-start | bytes 442376 | tf_op jit(solution)/shard_map/ppermute | solution.py:330
  (21 other events, 117.5 us)

commit v8 on v7

--- a/solution.py
+++ b/solution.py
@@ -357,15 +357,15 @@
 def summed_over_devices(one, two, grad_conv, edge_push, push, spread, finish, place):
     parts, grad_conv = lax.optimization_barrier(((one, two), grad_conv))
     received = [swapped(sends, stage) for (_, sends), stage in zip(parts, "xz")]
-    received[1][0], edge_grad = lax.optimization_barrier((received[1][0], grad_conv))
-    halo = spread(*edge_push(edge_grad))
-    received, halo = lax.optimization_barrier((received, halo))
+    edges, sink = edge_push(grad_conv), push(grad_conv)
+    received, edges, sink = lax.optimization_barrier((received, edges, sink))
     parts = [
         split([kept] + got, stage) for (kept, _), got, stage in zip(parts, received, "zx")
     ]
-    parts, grad_conv = lax.optimization_barrier((parts, grad_conv))
+    parts, edges = lax.optimization_barrier((parts, edges))
     received = [swapped(sends, stage) for (_, sends), stage in zip(parts, "zx")]
-    received, sink = lax.optimization_barrier((received, push(grad_conv)))
+    halo = spread(*edges)
+    received, sink = lax.optimization_barrier((received, sink))
     pieces = [part([kept] + got, 0, 1) for (kept, _), got in zip(parts, received)]
     by = 16
     while by < lax.axis_size("dp"):

time: 124 us -> 123 us (level)
  waiting for transfers between devices: 32.7 us -> 28.3 us
  starting transfers between devices: 48.5 us -> 51.5 us
    ppermute x35, starting transfers between devices: 37.8 us -> 41.3 us  [swap(): return lax.ppermute(value, 'dp', [(i, i ^ by) for i in range(peers)])]
    ppermute x2, starting transfers between devices: 10.5 us -> 7.58 us  [neighbours_swap(): lax.ppermute(jnp.where(odd == 1, to_after, to_before), 'dp', other_pairs)]
    ppermute x35, waiting for transfers between devices: 30.8 us -> 28.3 us  [swap(): return lax.ppermute(value, 'dp', [(i, i ^ by) for i in range(peers)])]
    ppermute x2, starting transfers between devices: 0.14 us -> 2.59 us  [neighbours_swap(): lax.ppermute(jnp.where(odd == 1, to_before, to_after), 'dp', even_pairs)]
    ppermute x2, waiting for transfers between devices: 1.82 us -> 0.01 us  [neighbours_swap(): lax.ppermute(jnp.where(odd == 1, to_after, to_before), 'dp', other_pairs)]
where the time goes in v8:
time: 123 us; the launch traced here: 122 us
  starting transfers between devices  51.5 us (42%)
  Pallas kernels  37.4 us (30%)
  waiting for transfers between devices  28.3 us (23%)
  other arithmetic  2.25 us (2%)
  between operations  1.8 us (1%)
    ppermute x35, starting transfers between devices, swap(): return lax.ppermute(value, 'dp', [(i, i ^ by) for i in range(peers)])  41.3 us
    ppermute x35, waiting for transfers between devices, swap(): return lax.ppermute(value, 'dp', [(i, i ^ by) for i in range(peers)])  28.3 us
    pallas_call x1, Pallas kernels, per_device(): pl.pallas_call(gradient_kernel, in_specs=[smem] + [vmem] * 6, out_specs=[...  9.89 us
    pallas_call x1, Pallas kernels, push(): pl.pallas_call(push_kernel, in_specs=[full((rows, channels)), full((K, ro...  7.97 us
    ppermute x2, starting transfers between devices, neighbours_swap(): lax.ppermute(jnp.where(odd == 1, to_after, to_before), 'dp', other_pairs)  7.58 us
    pallas_call x1, Pallas kernels, per_device(): pl.pallas_call(inner_kernel, in_specs=[vmem, vmem, hbm], out_specs=vmem,...  5.73 us
    pallas_call x3, Pallas kernels, placed(): pl.pallas_call(functools.partial(place_kernel, layout), in_specs=[smem] +...  5.45 us
    pallas_call x1, Pallas kernels, per_device(): pl.pallas_call(outer_kernel, in_specs=[smem, smem, vmem, vmem, vmem, vmem...  4.92 us
  transfers between devices with their start and end apart: 39, of which 16 were waited for; matrix products, arithmetic and copies ran while one was open for 1% of the time, Pallas kernels for 16%

profile of v8, /device:TPU:1, one launch (start us, length us, event | category | flops | bytes accessed | tf_op | source)
XLA Modules:
  0.0 122.0 jit_solution(7245166746103448370)
XLA Ops:
  1.5 4.5 %collective-permute-start.1 = (bf16[128,256]{1,0:T(8,128)(2,1)S(1)}, bf16[128,256]{1,0:T(8,128)(2,1)S(1)}, u32[]{:S(2)}, u32[]{:S(2)}) collective-permute-start(bf16[128,256]{1,0:T(8,128)(2,1)S(1)} %get-tuple-element.141), channel_id=1, source_target_pairs={{1,2},{2,1},{3,4},{4,3},{5,6},{6,5},{7,8},{8,7},{9,10},{10,9},{11,... | collective-permute-start | bytes 196616 | tf_op jit(solution)/shard_map/ppermute | solution.py:416
  6.1 5.7 %conv_inner.1.inner_ref = f32[256,256]{1,0:T(8,128)S(1)} custom-call(s32[27,512]{1,0:T(8,128)} %bitcast.17, bf16[512,256]{1,0:T(8,128)(2,1)} %feature_ref.1, bf16[27,256,256]{2,1,0:T(8,128)(2,1)} %weight_ref.3), custom_call_target="tpu_custom_call" | custom-call | flops 2264924160 | bytes 10616832 | tf_op jit(solution)/shard_map/conv_inner/pallas_call | solution.py:446
  12.6 4.9 %conv_outer.1 = (f32[256,256]{1,0:T(8,128)S(1)}, f32[3,256]{1,0:T(4,128)S(1)}, bf16[768,256]{1,0:T(8,128)(2,1)S(1)}) custom-call(s32[1]{0:T(128)S(6)} %copy.22.filled_ref, s32[1]{0:T(128)} %bitcast.1.odd_ref, s32[27,512]{1,0:T(8,128)S(1)} %bitcast.18, bf16[512,256]{1,0:T(8,128)(2,1)S(1)} %copy-done.2, bf16[128,256]{1,0:T(8,128)(2,1)S(1)} %collective-permute-done.even_ref, ...), custom_call_target="tpu_custom_call" | custom-call | flops 2264924160 | bytes 10616832 | tf_op jit(solution)/shard_map/conv_outer/pallas_call | solution.py:457
  21.7 2.4 %collective-permute-start.7 = (f32[3,256]{1,0:T(4,128)S(1)}, f32[3,256]{1,0:T(4,128)S(1)}, u32[]{:S(2)}, u32[]{:S(2)}) collective-permute-start(f32[3,256]{1,0:T(4,128)S(1)} %pad_maximum_fusion.1.refs_0_), channel_id=1, source_target_pairs={{0,12},{1,13},{2,14},{3,15},{4,8},{5,9},{6,10},{7,11},{8,4},{9,5},... | collective-permute-start | bytes 9224 | tf_op jit(solution)/shard_map/ppermute | solution.py:330
  26.1 1.7 %collective-permute-done.6.refs_2_ = f32[3,256]{1,0:T(4,128)S(1)} collective-permute-done((f32[3,256]{1,0:T(4,128)S(1)}, f32[3,256]{1,0:T(4,128)S(1)}, u32[]{:S(2)}, u32[]{:S(2)}) %collective-permute-start.6) | collective-permute-done | bytes 3104 | tf_op jit(solution)/shard_map/ppermute | solution.py:330
  28.8 3.4 %collective-permute-start.10 = (f32[2,256]{1,0:T(2,128)S(1)}, f32[2,256]{1,0:T(2,128)S(1)}, u32[]{:S(2)}, u32[]{:S(2)}) collective-permute-start(f32[2,256]{1,0:T(2,128)S(1)} %get-tuple-element.70), channel_id=1, source_target_pairs={{0,3},{1,2},{2,1},{3,0},{4,7},{5,6},{6,5},{7,4},{8,11},{9,10},{10,... | collective-permute-start | bytes 6152 | tf_op jit(solution)/shard_map/ppermute | solution.py:330
  36.5 1.7 %collective-permute-start.11 = (f32[2,256]{1,0:T(2,128)S(1)}, f32[2,256]{1,0:T(2,128)S(1)}, u32[]{:S(2)}, u32[]{:S(2)}) collective-permute-start(f32[2,256]{1,0:T(2,128)S(1)} %add_add_fusion.refs_4_), channel_id=1, source_target_pairs={{0,4},{1,5},{2,6},{3,7},{4,0},{5,1},{6,2},{7,3},{8,12},{9,13},{10,... | collective-permute-start | bytes 6152 | tf_op jit(solution)/shard_map/ppermute | solution.py:330
  42.9 9.9 %weight_gradient.1 = (f32[4,288,256]{2,1,0:T(8,128)S(1)}, bf16[4,288,256]{2,1,0:T(8,128)(2,1)S(1)}, f32[2,144,256]{2,1,0:T(8,128)S(1)}, bf16[2,144,256]{2,1,0:T(...) custom-call(s32[3]{0:T(128)S(1)} %pad_add_fusion.place_ref.places_ref, ...), custom_call_target="tpu_custom_call" | custom-call | flops 4529848320 | bytes 10616832 | tf_op jit(solution)/shard_map/weight_gradient/pallas_call | solution.py:508
  53.6 1.7 %collective-permute-start.18 = (bf16[2,144,256]{2,1,0:T(8,128)(2,1)S(1)}, bf16[2,144,256]{2,1,0:T(8,128)(2,1)S(1)}, u32[]{:S(2)}, u32[]{:S(2)}) collective-permute-start(bf16[2,144,256]{2,1,0:T(8,128)(2,1)S(1)} %get-tuple-element.81), channel_id=1, source_target_pairs={{0,4},{1,5},{2,6},{3,7},{4,0},{5,1},{6,2},{7,3},{8,12},{9,13},{10,... | collective-permute-start | bytes 442376 | tf_op jit(solution)/shard_map/ppermute | solution.py:330
  58.1 8.0 %push.1 = f32[512,256]{1,0:T(8,128)S(1)} custom-call(bf16[512,256]{1,0:T(8,128)(2,1)S(1)} %get-tuple-element.84.grad_own.grad_ref, s32[27,512]{1,0:T(8,128)S(1)} %bitcast.21, bf16[27,256,256]{2,1,0:T(8,128)(2,1)S(1)} %copy-done), custom_call_target="tpu_custom_call" | custom-call | flops 1000 | bytes 1000 | tf_op jit(solution)/shard_map/push/pallas_call | solution.py:550
  66.0 2.2 %push_edges.1 = (bf16[128,256]{1,0:T(8,128)(2,1)S(1)}, bf16[128,256]{1,0:T(8,128)(2,1)S(1)}) custom-call(bf16[256,256]{1,0:T(8,128)(2,1)S(1)} %pad_maximum_fusion.grad_ref, s32[27,512]{1,0:T(8,128)S(1)} %bitcast.22, bf16[27,256,256]{2,1,0:T(8,128)(2,1)S(1)} %copy-done), custom_call_target="tpu_custom_call" | custom-call | flops 1000 | bytes 1000 | tf_op jit(solution)/shard_map/push_edges/pallas_call | solution.py:538
  69.0 2.0 %collective-permute-start.21 = (bf16[1,288,256]{2,1,0:T(8,128)(2,1)S(1)}, bf16[1,288,256]{2,1,0:T(8,128)(2,1)S(1)}, u32[]{:S(2)}, u32[]{:S(2)}) collective-permute-start(bf16[1,288,256]{2,1,0:T(8,128)(2,1)S(1)} %get-tuple-element.95), channel_id=1, source_target_pairs={{0,4},{1,5},{2,6},{3,7},{4,0},{5,1},{6,2},{7,3},{8,12},{9,13},{10,... | collective-permute-start | bytes 442376 | tf_op jit(solution)/shard_map/ppermute | solution.py:330
  73.2 2.5 %collective-permute-start.29 = (bf16[128,256]{1,0:T(8,128)(2,1)S(1)}, bf16[128,256]{1,0:T(8,128)(2,1)S(1)}, u32[]{:S(2)}, u32[]{:S(2)}) collective-permute-start(bf16[128,256]{1,0:T(8,128)(2,1)S(1)} %get-tuple-element.143), channel_id=1, source_target_pairs={{0,1},{1,0},{2,3},{3,2},{4,5},{5,4},{6,7},{7,6},{8,9},{9,8},{10,11... | collective-permute-start | bytes 196616 | tf_op jit(solution)/shard_map/ppermute | solution.py:415
  75.8 3.1 %collective-permute-start.30 = (bf16[128,256]{1,0:T(8,128)(2,1)S(1)}, bf16[128,256]{1,0:T(8,128)(2,1)S(1)}, u32[]{:S(2)}, u32[]{:S(2)}) collective-permute-start(bf16[128,256]{1,0:T(8,128)(2,1)S(1)} %get-tuple-element.144), channel_id=1, source_target_pairs={{1,2},{2,1},{3,4},{4,3},{5,6},{6,5},{7,8},{8,7},{9,10},{10,9},{11,... | collective-permute-start | bytes 196616 | tf_op jit(solution)/shard_map/ppermute | solution.py:416
  78.9 2.0 %collective-permute-done.23 = bf16[1,288,256]{2,1,0:T(8,128)(2,1)S(1)} collective-permute-done((bf16[1,288,256]{2,1,0:T(8,128)(2,1)S(1)}, bf16[1,288,256]{2,1,0:T(8,128)(2,1)S(1)}, u32[]{:S(2)}, u32[]{:S(2)}) %collective-permute-start.23) | collective-permute-done | bytes 147488 | tf_op jit(solution)/shard_map/ppermute | solution.py:330
  82.4 6.7 %collective-permute-start.26 = (bf16[1,288,256]{2,1,0:T(8,128)(2,1)S(1)}, bf16[1,288,256]{2,1,0:T(8,128)(2,1)S(1)}, u32[]{:S(2)}, u32[]{:S(2)}) collective-permute-start(bf16[1,288,256]{2,1,0:T(8,128)(2,1)S(1)} %add_convert_fusion), channel_id=1, source_target_pairs={{0,8},{1,9},{2,10},{3,11},{4,12},{5,13},{6,14},{7,15},{8,0},{9,1},... | collective-permute-start | bytes 442376 | tf_op jit(solution)/shard_map/ppermute | solution.py:330
  90.3 2.1 %collective-permute-done.28 = bf16[1,144,256]{2,1,0:T(8,128)(2,1)S(1)} collective-permute-done((bf16[1,144,256]{2,1,0:T(8,128)(2,1)S(1)}, bf16[1,144,256]{2,1,0:T(8,128)(2,1)S(1)}, u32[]{:S(2)}, u32[]{:S(2)}) %collective-permute-start.28) | collective-permute-done | bytes 73760 | tf_op jit(solution)/shard_map/ppermute | solution.py:330
  92.4 6.5 %collective-permute-done.26 = bf16[1,288,256]{2,1,0:T(8,128)(2,1)S(1)} collective-permute-done((bf16[1,288,256]{2,1,0:T(8,128)(2,1)S(1)}, bf16[1,288,256]{2,1,0:T(8,128)(2,1)S(1)}, u32[]{:S(2)}, u32[]{:S(2)}) %collective-permute-start.26) | collective-permute-done | bytes 147488 | tf_op jit(solution)/shard_map/ppermute | solution.py:330
  99.0 2.9 %collective-permute-start.35 = (bf16[4,288,256]{2,1,0:T(8,128)(2,1)S(1)}, bf16[4,288,256]{2,1,0:T(8,128)(2,1)S(1)}, u32[]{:S(2)}, u32[]{:S(2)}) collective-permute-start(bf16[4,288,256]{2,1,0:T(8,128)(2,1)S(1)} %constant_dynamic-update-slice_fusion), channel_id=1, source_target_pairs={{0,1},{1,0},{2,3},{3,2},{4,5},{5,4},{6,7},{7,6},{8,9},{9,8},{10,11... | collective-permute-start | bytes 1769480 | tf_op jit(solution)/shard_map/ppermute | solution.py:330
  104.2 2.2 %collective-permute-start.32 = (bf16[2,144,256]{2,1,0:T(8,128)(2,1)S(1)}, bf16[2,144,256]{2,1,0:T(8,128)(2,1)S(1)}, u32[]{:S(2)}, u32[]{:S(2)}) collective-permute-start(bf16[2,144,256]{2,1,0:T(8,128)(2,1)S(1)} %constant_dynamic-update-slice_fusion.4.refs_1_), channel_id=1, source_target_pairs={{0,4},{1,5},{2,6},{3,7},{4,0},{5,1},{6,2},{7,3},{8,12},{9,13},{10,... | collective-permute-start | bytes 442376 | tf_op jit(solution)/shard_map/ppermute | solution.py:330
  106.4 1.9 %place.3.refs_2_ = bf16[27,256,256]{2,1,0:T(8,128)(2,1)} custom-call(s32[3]{0:T(128)S(1)} %pad_add_fusion.place_ref.places_ref, bf16[4,9,32,256]{3,2,1,0:T(8,128)(2,1)S(1)} %bitcast.13, bf16[2,144,256]{2,1,0:T(8,128)(2,1)S(1)} %constant_dynamic-update-slice_fusion.4.refs_1_, bf16[4,9,32,256]{3,2,1,0:T(8,128)(2,1)S(1)} %bitcast.16, ...), custom_call_target="tpu_custom_call" | custom-call | bytes 3538944 | tf_op jit(solution)/shard_map/place/pallas_call | solution.py:581
  110.0 6.8 %collective-permute-done.33 = bf16[2,144,256]{2,1,0:T(8,128)(2,1)S(1)} collective-permute-done((bf16[2,144,256]{2,1,0:T(8,128)(2,1)S(1)}, bf16[2,144,256]{2,1,0:T(8,128)(2,1)S(1)}, u32[]{:S(2)}, u32[]{:S(2)}) %collective-permute-start.33) | collective-permute-done | bytes 147488 | tf_op jit(solution)/shard_map/ppermute | solution.py:330
  117.9 1.8 %place.4.refs_2_ = bf16[27,256,256]{2,1,0:T(8,128)(2,1)} custom-call(s32[3]{0:T(128)S(1)} %pad_add_fusion.place_ref.places_ref, bf16[4,9,32,256]{3,2,1,0:T(8,128)(2,1)S(1)} %bitcast.14, bf16[6,144,256]{2,1,0:T(8,128)(2,1)S(1)} %constant_dynamic-update-slice_fusion.6.refs_1_, bf16[27,256,256]{2,1,0:T(8,128)(2,1)} %place.3.refs_2_), custom_call_target="tpu_custom_call", output_to_operand_aliasing={{}: (3, {})} | custom-call | bytes 3538944 | tf_op jit(solution)/shard_map/place/pallas_call | solution.py:581
  120.1 1.8 %place.5 = bf16[27,256,256]{2,1,0:T(8,128)(2,1)} custom-call(s32[3]{0:T(128)S(1)} %pad_add_fusion.place_ref.places_ref, bf16[4,9,32,256]{3,2,1,0:T(8,128)(2,1)S(1)} %bitcast.15, bf16[6,144,256]{2,1,0:T(8,128)(2,1)S(1)} %collective-permute-done.38.refs_1_, bf16[27,256,256]{2,1,0:T(8,128)(2,1)} %place.4.refs_2_), custom_call_target="tpu_custom_call", output_to_operand_aliasing={{}: (3, {})} | custom-call | bytes 3538944 | tf_op jit(solution)/shard_map/place/pallas_call | solution.py:581
  (102 shorter events, 31.6 us)
Async XLA Ops:
  1.5 11.0 %collective-permute-start.1 = (bf16[128,256]{1,0:T(8,128)(2,1)S(1)}, bf16[128,256]{1,0:T(8,128)(2,1)S(1)}, u32[]{:S(2)}, u32[]{:S(2)}) collective-permute-start(bf16[128,256]{1,0:T(8,128)(2,1)S(1)} %get-tuple-element.141), channel_id=1, source_target_pairs={{1,2},{2,1},{3,4},{4,3},{5,6},{6,5},{7,8},{8,7},{9,10},{10,9},{11,... | collective-permute-start | bytes 196616 | tf_op jit(solution)/shard_map/ppermute | solution.py:416
  6.0 6.5 %collective-permute-start = (bf16[128,256]{1,0:T(8,128)(2,1)S(1)}, bf16[128,256]{1,0:T(8,128)(2,1)S(1)}, u32[]{:S(2)}, u32[]{:S(2)}) collective-permute-start(bf16[128,256]{1,0:T(8,128)(2,1)S(1)} %get-tuple-element.142), channel_id=1, source_target_pairs={{0,1},{1,0},{2,3},{3,2},{4,5},{5,4},{6,7},{7,6},{8,9},{9,8},{10,11... | collective-permute-start | bytes 196616 | tf_op jit(solution)/shard_map/ppermute | solution.py:415
  21.7 4.3 %collective-permute-start.7 = (f32[3,256]{1,0:T(4,128)S(1)}, f32[3,256]{1,0:T(4,128)S(1)}, u32[]{:S(2)}, u32[]{:S(2)}) collective-permute-start(f32[3,256]{1,0:T(4,128)S(1)} %pad_maximum_fusion.1.refs_0_), channel_id=1, source_target_pairs={{0,12},{1,13},{2,14},{3,15},{4,8},{5,9},{6,10},{7,11},{8,4},{9,5},... | collective-permute-start | bytes 9224 | tf_op jit(solution)/shard_map/ppermute | solution.py:330
  28.8 4.8 %collective-permute-start.10 = (f32[2,256]{1,0:T(2,128)S(1)}, f32[2,256]{1,0:T(2,128)S(1)}, u32[]{:S(2)}, u32[]{:S(2)}) collective-permute-start(f32[2,256]{1,0:T(2,128)S(1)} %get-tuple-element.70), channel_id=1, source_target_pairs={{0,3},{1,2},{2,1},{3,0},{4,7},{5,6},{6,5},{7,4},{8,11},{9,10},{10,... | collective-permute-start | bytes 6152 | tf_op jit(solution)/shard_map/ppermute | solution.py:330
  32.6 10.3 %collective-permute-start.16 = (bf16[768,256]{1,0:T(8,128)(2,1)S(1)}, bf16[768,256]{1,0:T(8,128)(2,1)S(1)}, u32[]{:S(2)}, u32[]{:S(2)}) collective-permute-start(bf16[768,256]{1,0:T(8,128)(2,1)S(1)} %get-tuple-element.72.window_own), channel_id=1, source_target_pairs={{0,1},{1,0},{2,3},{3,2},{4,5},{5,4},{6,7},{7,6},{8,9},{9,8},{10,11... | collective-permute-start | bytes 1179656 | tf_op jit(solution)/shard_map/ppermute | solution.py:330
  34.6 4.3 %collective-permute-start.13 = (f32[2,256]{1,0:T(2,128)S(1)}, f32[2,256]{1,0:T(2,128)S(1)}, u32[]{:S(2)}, u32[]{:S(2)}) collective-permute-start(f32[2,256]{1,0:T(2,128)S(1)} %add_add_fusion.refs_4_), channel_id=1, source_target_pairs={{0,12},{1,13},{2,14},{3,15},{4,8},{5,9},{6,10},{7,11},{8,4},{9,5},... | collective-permute-start | bytes 6152 | tf_op jit(solution)/shard_map/ppermute | solution.py:330
  52.8 15.4 %collective-permute-start.17 = (bf16[4,288,256]{2,1,0:T(8,128)(2,1)S(1)}, bf16[4,288,256]{2,1,0:T(8,128)(2,1)S(1)}, u32[]{:S(2)}, u32[]{:S(2)}) collective-permute-start(bf16[4,288,256]{2,1,0:T(8,128)(2,1)S(1)} %get-tuple-element.80), channel_id=1, source_target_pairs={{0,2},{1,3},{2,0},{3,1},{4,6},{5,7},{6,4},{7,5},{8,10},{9,11},{10,... | collective-permute-start | bytes 1769480 | tf_op jit(solution)/shard_map/ppermute | solution.py:330
  53.6 14.7 %collective-permute-start.18 = (bf16[2,144,256]{2,1,0:T(8,128)(2,1)S(1)}, bf16[2,144,256]{2,1,0:T(8,128)(2,1)S(1)}, u32[]{:S(2)}, u32[]{:S(2)}) collective-permute-start(bf16[2,144,256]{2,1,0:T(8,128)(2,1)S(1)} %get-tuple-element.81), channel_id=1, source_target_pairs={{0,4},{1,5},{2,6},{3,7},{4,0},{5,1},{6,2},{7,3},{8,12},{9,13},{10,... | collective-permute-start | bytes 442376 | tf_op jit(solution)/shard_map/ppermute | solution.py:330
  55.3 12.9 %collective-permute-start.19 = (bf16[2,144,256]{2,1,0:T(8,128)(2,1)S(1)}, bf16[2,144,256]{2,1,0:T(8,128)(2,1)S(1)}, u32[]{:S(2)}, u32[]{:S(2)}) collective-permute-start(bf16[2,144,256]{2,1,0:T(8,128)(2,1)S(1)} %get-tuple-element.82), channel_id=1, source_target_pairs={{0,8},{1,9},{2,10},{3,11},{4,12},{5,13},{6,14},{7,15},{8,0},{9,1},... | collective-permute-start | bytes 442376 | tf_op jit(solution)/shard_map/ppermute | solution.py:330
  56.1 12.1 %collective-permute-start.20 = (bf16[2,144,256]{2,1,0:T(8,128)(2,1)S(1)}, bf16[2,144,256]{2,1,0:T(8,128)(2,1)S(1)}, u32[]{:S(2)}, u32[]{:S(2)}) collective-permute-start(bf16[2,144,256]{2,1,0:T(8,128)(2,1)S(1)} %get-tuple-element.83), channel_id=1, source_target_pairs={{0,12},{1,13},{2,14},{3,15},{4,8},{5,9},{6,10},{7,11},{8,4},{9,5},... | collective-permute-start | bytes 442376 | tf_op jit(solution)/shard_map/ppermute | solution.py:330
  68.5 7.2 %collective-permute-start.24 = (bf16[1,144,256]{2,1,0:T(8,128)(2,1)S(1)}, bf16[1,144,256]{2,1,0:T(8,128)(2,1)S(1)}, u32[]{:S(2)}, u32[]{:S(2)}) collective-permute-start(bf16[1,144,256]{2,1,0:T(8,128)(2,1)S(1)} %get-tuple-element.98), channel_id=1, source_target_pairs={{0,2},{1,3},{2,0},{3,1},{4,6},{5,7},{6,4},{7,5},{8,10},{9,11},{10,... | collective-permute-start | bytes 221192 | tf_op jit(solution)/shard_map/ppermute | solution.py:330
  69.0 9.8 %collective-permute-start.21 = (bf16[1,288,256]{2,1,0:T(8,128)(2,1)S(1)}, bf16[1,288,256]{2,1,0:T(8,128)(2,1)S(1)}, u32[]{:S(2)}, u32[]{:S(2)}) collective-permute-start(bf16[1,288,256]{2,1,0:T(8,128)(2,1)S(1)} %get-tuple-element.95), channel_id=1, source_target_pairs={{0,4},{1,5},{2,6},{3,7},{4,0},{5,1},{6,2},{7,3},{8,12},{9,13},{10,... | collective-permute-start | bytes 442376 | tf_op jit(solution)/shard_map/ppermute | solution.py:330
  71.1 7.8 %collective-permute-start.22 = (bf16[1,288,256]{2,1,0:T(8,128)(2,1)S(1)}, bf16[1,288,256]{2,1,0:T(8,128)(2,1)S(1)}, u32[]{:S(2)}, u32[]{:S(2)}) collective-permute-start(bf16[1,288,256]{2,1,0:T(8,128)(2,1)S(1)} %get-tuple-element.96), channel_id=1, source_target_pairs={{0,8},{1,9},{2,10},{3,11},{4,12},{5,13},{6,14},{7,15},{8,0},{9,1},... | collective-permute-start | bytes 442376 | tf_op jit(solution)/shard_map/ppermute | solution.py:330
  71.7 9.1 %collective-permute-start.23 = (bf16[1,288,256]{2,1,0:T(8,128)(2,1)S(1)}, bf16[1,288,256]{2,1,0:T(8,128)(2,1)S(1)}, u32[]{:S(2)}, u32[]{:S(2)}) collective-permute-start(bf16[1,288,256]{2,1,0:T(8,128)(2,1)S(1)} %get-tuple-element.97), channel_id=1, source_target_pairs={{0,12},{1,13},{2,14},{3,15},{4,8},{5,9},{6,10},{7,11},{8,4},{9,5},... | collective-permute-start | bytes 442376 | tf_op jit(solution)/shard_map/ppermute | solution.py:330
  73.2 15.9 %collective-permute-start.29 = (bf16[128,256]{1,0:T(8,128)(2,1)S(1)}, bf16[128,256]{1,0:T(8,128)(2,1)S(1)}, u32[]{:S(2)}, u32[]{:S(2)}) collective-permute-start(bf16[128,256]{1,0:T(8,128)(2,1)S(1)} %get-tuple-element.143), channel_id=1, source_target_pairs={{0,1},{1,0},{2,3},{3,2},{4,5},{5,4},{6,7},{7,6},{8,9},{9,8},{10,11... | collective-permute-start | bytes 196616 | tf_op jit(solution)/shard_map/ppermute | solution.py:415
  75.8 13.7 %collective-permute-start.30 = (bf16[128,256]{1,0:T(8,128)(2,1)S(1)}, bf16[128,256]{1,0:T(8,128)(2,1)S(1)}, u32[]{:S(2)}, u32[]{:S(2)}) collective-permute-start(bf16[128,256]{1,0:T(8,128)(2,1)S(1)} %get-tuple-element.144), channel_id=1, source_target_pairs={{1,2},{2,1},{3,4},{4,3},{5,6},{6,5},{7,8},{8,7},{9,10},{10,9},{11,... | collective-permute-start | bytes 196616 | tf_op jit(solution)/shard_map/ppermute | solution.py:416
  81.0 11.4 %collective-permute-start.27 = (bf16[1,288,256]{2,1,0:T(8,128)(2,1)S(1)}, bf16[1,288,256]{2,1,0:T(8,128)(2,1)S(1)}, u32[]{:S(2)}, u32[]{:S(2)}) collective-permute-start(bf16[1,288,256]{2,1,0:T(8,128)(2,1)S(1)} %add_convert_fusion), channel_id=1, source_target_pairs={{0,12},{1,13},{2,14},{3,15},{4,8},{5,9},{6,10},{7,11},{8,4},{9,5},... | collective-permute-start | bytes 442376 | tf_op jit(solution)/shard_map/ppermute | solution.py:330
  82.4 16.6 %collective-permute-start.26 = (bf16[1,288,256]{2,1,0:T(8,128)(2,1)S(1)}, bf16[1,288,256]{2,1,0:T(8,128)(2,1)S(1)}, u32[]{:S(2)}, u32[]{:S(2)}) collective-permute-start(bf16[1,288,256]{2,1,0:T(8,128)(2,1)S(1)} %add_convert_fusion), channel_id=1, source_target_pairs={{0,8},{1,9},{2,10},{3,11},{4,12},{5,13},{6,14},{7,15},{8,0},{9,1},... | collective-permute-start | bytes 442376 | tf_op jit(solution)/shard_map/ppermute | solution.py:330
  89.1 9.8 %collective-permute-start.25 = (bf16[1,288,256]{2,1,0:T(8,128)(2,1)S(1)}, bf16[1,288,256]{2,1,0:T(8,128)(2,1)S(1)}, u32[]{:S(2)}, u32[]{:S(2)}) collective-permute-start(bf16[1,288,256]{2,1,0:T(8,128)(2,1)S(1)} %add_convert_fusion), channel_id=1, source_target_pairs={{0,4},{1,5},{2,6},{3,7},{4,0},{5,1},{6,2},{7,3},{8,12},{9,13},{10,... | collective-permute-start | bytes 442376 | tf_op jit(solution)/shard_map/ppermute | solution.py:330
  99.0 7.4 %collective-permute-start.35 = (bf16[4,288,256]{2,1,0:T(8,128)(2,1)S(1)}, bf16[4,288,256]{2,1,0:T(8,128)(2,1)S(1)}, u32[]{:S(2)}, u32[]{:S(2)}) collective-permute-start(bf16[4,288,256]{2,1,0:T(8,128)(2,1)S(1)} %constant_dynamic-update-slice_fusion), channel_id=1, source_target_pairs={{0,1},{1,0},{2,3},{3,2},{4,5},{5,4},{6,7},{7,6},{8,9},{9,8},{10,11... | collective-permute-start | bytes 1769480 | tf_op jit(solution)/shard_map/ppermute | solution.py:330
  102.0 14.9 %collective-permute-start.31 = (bf16[4,288,256]{2,1,0:T(8,128)(2,1)S(1)}, bf16[4,288,256]{2,1,0:T(8,128)(2,1)S(1)}, u32[]{:S(2)}, u32[]{:S(2)}) collective-permute-start(bf16[4,288,256]{2,1,0:T(8,128)(2,1)S(1)} %constant_dynamic-update-slice_fusion), channel_id=1, source_target_pairs={{0,2},{1,3},{2,0},{3,1},{4,6},{5,7},{6,4},{7,5},{8,10},{9,11},{10,... | collective-permute-start | bytes 1769480 | tf_op jit(solution)/shard_map/ppermute | solution.py:330
  102.9 7.1 %collective-permute-start.34 = (bf16[2,144,256]{2,1,0:T(8,128)(2,1)S(1)}, bf16[2,144,256]{2,1,0:T(8,128)(2,1)S(1)}, u32[]{:S(2)}, u32[]{:S(2)}) collective-permute-start(bf16[2,144,256]{2,1,0:T(8,128)(2,1)S(1)} %constant_dynamic-update-slice_fusion.4.refs_1_), channel_id=1, source_target_pairs={{0,12},{1,13},{2,14},{3,15},{4,8},{5,9},{6,10},{7,11},{8,4},{9,5},... | collective-permute-start | bytes 442376 | tf_op jit(solution)/shard_map/ppermute | solution.py:330
  104.2 12.6 %collective-permute-start.33 = (bf16[2,144,256]{2,1,0:T(8,128)(2,1)S(1)}, bf16[2,144,256]{2,1,0:T(8,128)(2,1)S(1)}, u32[]{:S(2)}, u32[]{:S(2)}) collective-permute-start(bf16[2,144,256]{2,1,0:T(8,128)(2,1)S(1)} %constant_dynamic-update-slice_fusion.4.refs_1_), channel_id=1, source_target_pairs={{0,8},{1,9},{2,10},{3,11},{4,12},{5,13},{6,14},{7,15},{8,0},{9,1},... | collective-permute-start | bytes 442376 | tf_op jit(solution)/shard_map/ppermute | solution.py:330
  104.2 12.6 %collective-permute-start.32 = (bf16[2,144,256]{2,1,0:T(8,128)(2,1)S(1)}, bf16[2,144,256]{2,1,0:T(8,128)(2,1)S(1)}, u32[]{:S(2)}, u32[]{:S(2)}) collective-permute-start(bf16[2,144,256]{2,1,0:T(8,128)(2,1)S(1)} %constant_dynamic-update-slice_fusion.4.refs_1_), channel_id=1, source_target_pairs={{0,4},{1,5},{2,6},{3,7},{4,0},{5,1},{6,2},{7,3},{8,12},{9,13},{10,... | collective-permute-start | bytes 442376 | tf_op jit(solution)/shard_map/ppermute | solution.py:330
  (21 other events, 115.9 us)

commit v9 on v8

--- a/solution.py
+++ b/solution.py
@@ -244,8 +244,8 @@
         copy.wait()
 
 
-def scatter(step, grad_ref, first_row, map_ref, weight_ref, windows):
-    pushed = [dot(grad_ref[...], weight_ref[j], ((1,), (1,))).astype(BF16) for j in range(GROUP)]
+def scatter(step, grad, first_row, map_ref, weight_ref, windows):
+    pushed = [dot(grad, weight_ref[j], ((1,), (1,))).astype(BF16) for j in range(GROUP)]
     named = [map_ref[step * GROUP + j, :][None] for j in range(GROUP)]
     for b, first_slot, sink in windows:
         rows = slice(b * BLOCK, (b + 1) * BLOCK)
@@ -272,7 +272,8 @@
         return b * (rows - BLOCK)
 
     windows = [(0, rows - BLOCK, before), (1, 2 * rows, after)]
-    scatter(step, grad_ref, first_row, map_ref, weight_ref, windows)
+    grad = jnp.concatenate([grad_ref[0:BLOCK, :], grad_ref[rows - BLOCK :, :]], axis=0)
+    scatter(step, grad, first_row, map_ref, weight_ref, windows)
 
     @pl.when(step == pl.num_programs(0) - 1)
     def _():
@@ -292,7 +293,7 @@
     for b in range(rows // BLOCK):
         start, stop = max(b - 1, 0) * BLOCK, min((b + 2) * BLOCK, rows)
         windows.append((b, rows + start, own_ref.at[start:stop]))
-    scatter(step, grad_ref, lambda b: b * BLOCK, map_ref, weight_ref, windows)
+    scatter(step, grad_ref[...], lambda b: b * BLOCK, map_ref, weight_ref, windows)
 
 
 def place_kernel(layout, places_ref, *refs):
@@ -313,9 +314,9 @@
             put(one.at[i], out_ref.at[pl.ds(first, K_ONE)], 1, first_one + i, size, 0)
         for i in range(two.shape[0]):
             piece = first_two + i
-            for j in range(HALF - K_ONE):
-                source = two.at[pl.ds(i, 1), pl.ds(j * size, size)]
-                put(source, out_ref.at[pl.ds(first + K_ONE + j, 1)], 2, piece, size, 0)
+            source = two.at[i, pl.ds(0, (HALF - K_ONE) * size)]
+            source = source.reshape(HALF - K_ONE, size, two.shape[2])
+            put(source, out_ref.at[pl.ds(first + K_ONE, HALF - K_ONE)], 2, piece, size, 0)
             source = two.at[pl.ds(i, 1), pl.ds((HALF - K_ONE) * size, size // 2)]
             base = core * (out_ref.shape[1] // 2)
             put(source, out_ref.at[pl.ds(HALF, 1)], 2, piece, size // 2, base)
@@ -377,12 +378,11 @@
     received = [gather_start(piece, stage) for piece, stage in zip(pieces, "zx")]
     received, pieces, results = lax.optimization_barrier((received, pieces, results))
     early = [jnp.concatenate([piece] + got, axis=0) for piece, got in zip(pieces, received)]
-    early_other = [swap(piece, 1) for piece in early]
     received = [gather_start(piece, stage) for piece, stage in zip(early, "xz")]
-    received, results = lax.optimization_barrier((received, (results, place(early, early_other))))
+    received, results = lax.optimization_barrier((received, (results, place(early))))
     late = [jnp.concatenate(got, axis=0) for got in received]
-    late_other = [swap(piece, 1) for piece in late]
-    return late, late_other, results
+    other = [swap(jnp.concatenate(pair, axis=0), 1) for pair in zip(early, late)]
+    return late, other, results
 
 
 def exchanged(value, merge):
@@ -533,17 +533,16 @@
     )
 
     def edge_push(grad_conv):
-        edges = jnp.concatenate([grad_conv[:BLOCK], grad_conv[rows - BLOCK :]], axis=0)
         edge = jax.ShapeDtypeStruct((BLOCK, channels), BF16)
         before, after = pl.pallas_call(
             edge_push_kernel,
-            in_specs=[full((2 * BLOCK, channels)), full((K, rows)), weight_spec],
+            in_specs=[full((rows, channels)), full((K, rows)), weight_spec],
             out_specs=[full((BLOCK, channels))] * 2,
             out_shape=[edge, edge],
             scratch_shapes=[pltpu.VMEM((BLOCK, channels), F32)] * 2,
             name="push_edges",
             **push_grid,
-        )(edges, map_rows, weights)
+        )(grad_conv, map_rows, weights)
         return before, after
 
     def push(grad_conv):
@@ -574,7 +573,7 @@
 
 
     def placed(layout, sources, *into):
-        count = sum(one.shape[0] + two.shape[0] * (HALF - K_ONE + 1) for one, two in sources)
+        count = sum(one.shape[0] + two.shape[0] * 2 for one, two in sources)
         operands = []
         for one, two in sources:
             operands += [one.reshape(one.shape[0], K_ONE, size, channels), two]
@@ -590,16 +589,16 @@
             name="place",
         )(places, *operands, *into)
 
-    def place_early(own, other):
-        return placed(((0, 0, 0), (1, 0, 0)), (own, other))
-
-    late, late_other, results = summed_over_devices(
+    def place_early(own):
+        return placed(((0, 0, 0),), (own,))
+
+    late, other_pieces, results = summed_over_devices(
         one, two, grad_conv, edge_push, push, neighbours_swap, finish, place_early
     )
     (grad_features, grad_gain, grad_shift), grad_weights = results
     first_late = (8 - late[0].shape[0], 8 - late[1].shape[0])
     grad_weights = placed(((0, *first_late),), (late,), grad_weights)
-    grad_weights = placed(((1, *first_late),), (late_other,), grad_weights)
+    grad_weights = placed(((1, 0, 0),), (other_pieces,), grad_weights)
     return block_out, grad_features, grad_weights, grad_gain, grad_shift
 
 

time: 123 us -> 122 us (level)
  starting transfers between devices: 51.5 us -> 49.5 us
  waiting for transfers between devices: 28.3 us -> 29.8 us
    ppermute x35 -> x33, starting transfers between devices: 41.3 us -> 39.3 us  [swap(): return lax.ppermute(value, 'dp', [(i, i ^ by) for i in range(peers)])]
    ppermute x35 -> x33, waiting for transfers between devices: 28.3 us -> 29.8 us  [swap(): return lax.ppermute(value, 'dp', [(i, i ^ by) for i in range(peers)])]
  transfers between devices with their start and end apart: 39 -> 37, of which waited for: 16 -> 15; matrix products, arithmetic and copies ran while one was open for 1% -> 1% of each run, Pallas kernels for 16% -> 16%
where the time goes in v9:
time: 122 us; the launch traced here: 121 us
  starting transfers between devices  49.5 us (41%)
  Pallas kernels  37 us (30%)
  waiting for transfers between devices  29.8 us (24%)
  other arithmetic  2.28 us (2%)
  between operations  1.81 us (1%)
    ppermute x33, starting transfers between devices, swap(): return lax.ppermute(value, 'dp', [(i, i ^ by) for i in range(peers)])  39.3 us
    ppermute x33, waiting for transfers between devices, swap(): return lax.ppermute(value, 'dp', [(i, i ^ by) for i in range(peers)])  29.8 us
    pallas_call x1, Pallas kernels, per_device(): pl.pallas_call(gradient_kernel, in_specs=[smem] + [vmem] * 6, out_specs=[...  9.89 us
    pallas_call x1, Pallas kernels, push(): pl.pallas_call(push_kernel, in_specs=[full((rows, channels)), full((K, ro...  7.98 us
    ppermute x2, starting transfers between devices, neighbours_swap(): lax.ppermute(jnp.where(odd == 1, to_after, to_before), 'dp', other_pairs)  7.59 us
    pallas_call x1, Pallas kernels, per_device(): pl.pallas_call(inner_kernel, in_specs=[vmem, vmem, hbm], out_specs=vmem,...  5.73 us
    pallas_call x3, Pallas kernels, placed(): pl.pallas_call(functools.partial(place_kernel, layout), in_specs=[smem] +...  5.05 us
    pallas_call x1, Pallas kernels, per_device(): pl.pallas_call(outer_kernel, in_specs=[smem, smem, vmem, vmem, vmem, vmem...  4.92 us
  transfers between devices with their start and end apart: 37, of which 15 were waited for; matrix products, arithmetic and copies ran while one was open for 1% of the time, Pallas kernels for 16%

profile of v9, /device:TPU:1, one launch (start us, length us, event | category | flops | bytes accessed | tf_op | source)
XLA Modules:
  0.0 121.2 jit_solution(14718647267012992052)
XLA Ops:
  1.5 4.5 %collective-permute-start.1 = (bf16[128,256]{1,0:T(8,128)(2,1)S(1)}, bf16[128,256]{1,0:T(8,128)(2,1)S(1)}, u32[]{:S(2)}, u32[]{:S(2)}) collective-permute-start(bf16[128,256]{1,0:T(8,128)(2,1)S(1)} %get-tuple-element.139), channel_id=1, source_target_pairs={{1,2},{2,1},{3,4},{4,3},{5,6},{6,5},{7,8},{8,7},{9,10},{10,9},{11,... | collective-permute-start | bytes 196616 | tf_op jit(solution)/shard_map/ppermute | solution.py:416
  6.1 5.7 %conv_inner.1.inner_ref = f32[256,256]{1,0:T(8,128)S(1)} custom-call(s32[27,512]{1,0:T(8,128)} %bitcast.15, bf16[512,256]{1,0:T(8,128)(2,1)} %feature_ref.1, bf16[27,256,256]{2,1,0:T(8,128)(2,1)} %weight_ref.3), custom_call_target="tpu_custom_call" | custom-call | flops 2264924160 | bytes 10616832 | tf_op jit(solution)/shard_map/conv_inner/pallas_call | solution.py:446
  12.6 4.9 %conv_outer.1 = (f32[256,256]{1,0:T(8,128)S(1)}, f32[3,256]{1,0:T(4,128)S(1)}, bf16[768,256]{1,0:T(8,128)(2,1)S(1)}) custom-call(s32[1]{0:T(128)S(6)} %copy.28.filled_ref, s32[1]{0:T(128)} %bitcast.1.odd_ref, s32[27,512]{1,0:T(8,128)S(1)} %bitcast.16, bf16[512,256]{1,0:T(8,128)(2,1)S(1)} %copy-done.2, bf16[128,256]{1,0:T(8,128)(2,1)S(1)} %collective-permute-done.even_ref, ...), custom_call_target="tpu_custom_call" | custom-call | flops 2264924160 | bytes 10616832 | tf_op jit(solution)/shard_map/conv_outer/pallas_call | solution.py:457
  17.5 1.7 %collective-permute-start.4 = (f32[3,256]{1,0:T(4,128)S(1)}, f32[3,256]{1,0:T(4,128)S(1)}, u32[]{:S(2)}, u32[]{:S(2)}) collective-permute-start(f32[3,256]{1,0:T(4,128)S(1)} %get-tuple-element.68), channel_id=1, source_target_pairs={{0,3},{1,2},{2,1},{3,0},{4,7},{5,6},{6,5},{7,4},{8,11},{9,10},{10,... | collective-permute-start | bytes 9224 | tf_op jit(solution)/shard_map/ppermute | solution.py:331
  21.7 2.4 %collective-permute-start.7 = (f32[3,256]{1,0:T(4,128)S(1)}, f32[3,256]{1,0:T(4,128)S(1)}, u32[]{:S(2)}, u32[]{:S(2)}) collective-permute-start(f32[3,256]{1,0:T(4,128)S(1)} %pad_maximum_fusion.1.refs_0_), channel_id=1, source_target_pairs={{0,12},{1,13},{2,14},{3,15},{4,8},{5,9},{6,10},{7,11},{8,4},{9,5},... | collective-permute-start | bytes 9224 | tf_op jit(solution)/shard_map/ppermute | solution.py:331
  26.1 1.7 %collective-permute-done.6.refs_2_ = f32[3,256]{1,0:T(4,128)S(1)} collective-permute-done((f32[3,256]{1,0:T(4,128)S(1)}, f32[3,256]{1,0:T(4,128)S(1)}, u32[]{:S(2)}, u32[]{:S(2)}) %collective-permute-start.6) | collective-permute-done | bytes 3104 | tf_op jit(solution)/shard_map/ppermute | solution.py:331
  28.8 3.4 %collective-permute-start.10 = (f32[2,256]{1,0:T(2,128)S(1)}, f32[2,256]{1,0:T(2,128)S(1)}, u32[]{:S(2)}, u32[]{:S(2)}) collective-permute-start(f32[2,256]{1,0:T(2,128)S(1)} %get-tuple-element.70), channel_id=1, source_target_pairs={{0,3},{1,2},{2,1},{3,0},{4,7},{5,6},{6,5},{7,4},{8,11},{9,10},{10,... | collective-permute-start | bytes 6152 | tf_op jit(solution)/shard_map/ppermute | solution.py:331
  36.5 1.7 %collective-permute-start.11 = (f32[2,256]{1,0:T(2,128)S(1)}, f32[2,256]{1,0:T(2,128)S(1)}, u32[]{:S(2)}, u32[]{:S(2)}) collective-permute-start(f32[2,256]{1,0:T(2,128)S(1)} %add_add_fusion.refs_4_), channel_id=1, source_target_pairs={{0,4},{1,5},{2,6},{3,7},{4,0},{5,1},{6,2},{7,3},{8,12},{9,13},{10,... | collective-permute-start | bytes 6152 | tf_op jit(solution)/shard_map/ppermute | solution.py:331
  40.0 1.7 %collective-permute-start.14 = (bf16[512,256]{1,0:T(8,128)(2,1)S(1)}, bf16[512,256]{1,0:T(8,128)(2,1)S(1)}, u32[]{:S(2)}, u32[]{:S(2)}) collective-permute-start(bf16[512,256]{1,0:T(8,128)(2,1)S(1)} %get-tuple-element.84.grad_own.grad_ref), channel_id=1, source_target_pairs={{0,1},{1,0},{2,3},{3,2},{4,5},{5,4},{6,7},{7,6},{8,9},{9,8},{10,11... | collective-permute-start | bytes 786440 | tf_op jit(solution)/shard_map/ppermute | solution.py:331
  42.9 9.9 %weight_gradient.1 = (f32[4,288,256]{2,1,0:T(8,128)S(1)}, bf16[4,288,256]{2,1,0:T(8,128)(2,1)S(1)}, f32[2,144,256]{2,1,0:T(8,128)S(1)}, bf16[2,144,256]{2,1,0:T(...) custom-call(s32[3]{0:T(128)S(1)} %pad_add_fusion.place_ref.places_ref, ...), custom_call_target="tpu_custom_call" | custom-call | flops 4529848320 | bytes 10616832 | tf_op jit(solution)/shard_map/weight_gradient/pallas_call | solution.py:508
  53.6 1.7 %collective-permute-start.18 = (bf16[2,144,256]{2,1,0:T(8,128)(2,1)S(1)}, bf16[2,144,256]{2,1,0:T(8,128)(2,1)S(1)}, u32[]{:S(2)}, u32[]{:S(2)}) collective-permute-start(bf16[2,144,256]{2,1,0:T(8,128)(2,1)S(1)} %get-tuple-element.81), channel_id=1, source_target_pairs={{0,4},{1,5},{2,6},{3,7},{4,0},{5,1},{6,2},{7,3},{8,12},{9,13},{10,... | collective-permute-start | bytes 442376 | tf_op jit(solution)/shard_map/ppermute | solution.py:331
  58.0 2.1 %push_edges.1 = (bf16[128,256]{1,0:T(8,128)(2,1)S(1)}, bf16[128,256]{1,0:T(8,128)(2,1)S(1)}) custom-call(bf16[512,256]{1,0:T(8,128)(2,1)S(1)} %get-tuple-element.84.grad_own.grad_ref, s32[27,512]{1,0:T(8,128)S(1)} %bitcast.19, bf16[27,256,256]{2,1,0:T(8,128)(2,1)S(1)} %copy-done), custom_call_target="tpu_custom_call" | custom-call | flops 1000 | bytes 1000 | tf_op jit(solution)/shard_map/push_edges/pallas_call | solution.py:537
  60.2 8.0 %push.1 = f32[512,256]{1,0:T(8,128)S(1)} custom-call(bf16[512,256]{1,0:T(8,128)(2,1)S(1)} %get-tuple-element.84.grad_own.grad_ref, s32[27,512]{1,0:T(8,128)S(1)} %bitcast.20, bf16[27,256,256]{2,1,0:T(8,128)(2,1)S(1)} %copy-done), custom_call_target="tpu_custom_call" | custom-call | flops 1000 | bytes 1000 | tf_op jit(solution)/shard_map/push/pallas_call | solution.py:549
  69.0 2.1 %collective-permute-start.21 = (bf16[1,288,256]{2,1,0:T(8,128)(2,1)S(1)}, bf16[1,288,256]{2,1,0:T(8,128)(2,1)S(1)}, u32[]{:S(2)}, u32[]{:S(2)}) collective-permute-start(bf16[1,288,256]{2,1,0:T(8,128)(2,1)S(1)} %get-tuple-element.95), channel_id=1, source_target_pairs={{0,4},{1,5},{2,6},{3,7},{4,0},{5,1},{6,2},{7,3},{8,12},{9,13},{10,... | collective-permute-start | bytes 442376 | tf_op jit(solution)/shard_map/ppermute | solution.py:331
  73.2 2.5 %collective-permute-start.29 = (bf16[128,256]{1,0:T(8,128)(2,1)S(1)}, bf16[128,256]{1,0:T(8,128)(2,1)S(1)}, u32[]{:S(2)}, u32[]{:S(2)}) collective-permute-start(bf16[128,256]{1,0:T(8,128)(2,1)S(1)} %get-tuple-element.149), channel_id=1, source_target_pairs={{0,1},{1,0},{2,3},{3,2},{4,5},{5,4},{6,7},{7,6},{8,9},{9,8},{10,11... | collective-permute-start | bytes 196616 | tf_op jit(solution)/shard_map/ppermute | solution.py:415
  75.8 3.1 %collective-permute-start.30 = (bf16[128,256]{1,0:T(8,128)(2,1)S(1)}, bf16[128,256]{1,0:T(8,128)(2,1)S(1)}, u32[]{:S(2)}, u32[]{:S(2)}) collective-permute-start(bf16[128,256]{1,0:T(8,128)(2,1)S(1)} %get-tuple-element.150), channel_id=1, source_target_pairs={{1,2},{2,1},{3,4},{4,3},{5,6},{6,5},{7,8},{8,7},{9,10},{10,9},{11,... | collective-permute-start | bytes 196616 | tf_op jit(solution)/shard_map/ppermute | solution.py:416
  78.9 2.0 %collective-permute-done.23 = bf16[1,288,256]{2,1,0:T(8,128)(2,1)S(1)} collective-permute-done((bf16[1,288,256]{2,1,0:T(8,128)(2,1)S(1)}, bf16[1,288,256]{2,1,0:T(8,128)(2,1)S(1)}, u32[]{:S(2)}, u32[]{:S(2)}) %collective-permute-start.23) | collective-permute-done | bytes 147488 | tf_op jit(solution)/shard_map/ppermute | solution.py:331
  82.4 6.7 %collective-permute-start.26 = (bf16[1,288,256]{2,1,0:T(8,128)(2,1)S(1)}, bf16[1,288,256]{2,1,0:T(8,128)(2,1)S(1)}, u32[]{:S(2)}, u32[]{:S(2)}) collective-permute-start(bf16[1,288,256]{2,1,0:T(8,128)(2,1)S(1)} %add_convert_fusion), channel_id=1, source_target_pairs={{0,8},{1,9},{2,10},{3,11},{4,12},{5,13},{6,14},{7,15},{8,0},{9,1},... | collective-permute-start | bytes 442376 | tf_op jit(solution)/shard_map/ppermute | solution.py:331
  90.3 2.1 %collective-permute-done.28 = bf16[1,144,256]{2,1,0:T(8,128)(2,1)S(1)} collective-permute-done((bf16[1,144,256]{2,1,0:T(8,128)(2,1)S(1)}, bf16[1,144,256]{2,1,0:T(8,128)(2,1)S(1)}, u32[]{:S(2)}, u32[]{:S(2)}) %collective-permute-start.28) | collective-permute-done | bytes 73760 | tf_op jit(solution)/shard_map/ppermute | solution.py:331
  92.4 6.5 %collective-permute-done.26 = bf16[1,288,256]{2,1,0:T(8,128)(2,1)S(1)} collective-permute-done((bf16[1,288,256]{2,1,0:T(8,128)(2,1)S(1)}, bf16[1,288,256]{2,1,0:T(8,128)(2,1)S(1)}, u32[]{:S(2)}, u32[]{:S(2)}) %collective-permute-start.26) | collective-permute-done | bytes 147488 | tf_op jit(solution)/shard_map/ppermute | solution.py:331
  99.1 2.0 %collective-permute-start.31 = (bf16[4,288,256]{2,1,0:T(8,128)(2,1)S(1)}, bf16[4,288,256]{2,1,0:T(8,128)(2,1)S(1)}, u32[]{:S(2)}, u32[]{:S(2)}) collective-permute-start(bf16[4,288,256]{2,1,0:T(8,128)(2,1)S(1)} %get-tuple-element.142), channel_id=1, source_target_pairs={{0,2},{1,3},{2,0},{3,1},{4,6},{5,7},{6,4},{7,5},{8,10},{9,11},{10,... | collective-permute-start | bytes 1769480 | tf_op jit(solution)/shard_map/ppermute | solution.py:331
  102.3 2.5 %collective-permute-start.32 = (bf16[2,144,256]{2,1,0:T(8,128)(2,1)S(1)}, bf16[2,144,256]{2,1,0:T(8,128)(2,1)S(1)}, u32[]{:S(2)}, u32[]{:S(2)}) collective-permute-start(bf16[2,144,256]{2,1,0:T(8,128)(2,1)S(1)} %get-tuple-element.152.refs_1_), channel_id=1, source_target_pairs={{0,4},{1,5},{2,6},{3,7},{4,0},{5,1},{6,2},{7,3},{8,12},{9,13},{10,... | collective-permute-start | bytes 442376 | tf_op jit(solution)/shard_map/ppermute | solution.py:331
  107.2 7.9 %collective-permute-done.33 = bf16[2,144,256]{2,1,0:T(8,128)(2,1)S(1)} collective-permute-done((bf16[2,144,256]{2,1,0:T(8,128)(2,1)S(1)}, bf16[2,144,256]{2,1,0:T(8,128)(2,1)S(1)}, u32[]{:S(2)}, u32[]{:S(2)}) %collective-permute-start.33) | collective-permute-done | bytes 147488 | tf_op jit(solution)/shard_map/ppermute | solution.py:331
  119.1 2.0 %place.5 = bf16[27,256,256]{2,1,0:T(8,128)(2,1)} custom-call(s32[3]{0:T(128)S(1)} %pad_add_fusion.place_ref.places_ref, bf16[8,9,32,256]{3,2,1,0:T(8,128)(2,1)S(1)} %bitcast.13, bf16[8,144,256]{2,1,0:T(8,128)(2,1)S(1)} %collective-permute-done.36.refs_1_, bf16[27,256,256]{2,1,0:T(8,128)(2,1)} %place.4.refs_2_), custom_call_target="tpu_custom_call", output_to_operand_aliasing={{}: (3, {})} | custom-call | bytes 3538944 | tf_op jit(solution)/shard_map/place/pallas_call | solution.py:580
  (98 shorter events, 30.4 us)
Async XLA Ops:
  1.5 11.0 %collective-permute-start.1 = (bf16[128,256]{1,0:T(8,128)(2,1)S(1)}, bf16[128,256]{1,0:T(8,128)(2,1)S(1)}, u32[]{:S(2)}, u32[]{:S(2)}) collective-permute-start(bf16[128,256]{1,0:T(8,128)(2,1)S(1)} %get-tuple-element.139), channel_id=1, source_target_pairs={{1,2},{2,1},{3,4},{4,3},{5,6},{6,5},{7,8},{8,7},{9,10},{10,9},{11,... | collective-permute-start | bytes 196616 | tf_op jit(solution)/shard_map/ppermute | solution.py:416
  6.0 6.5 %collective-permute-start = (bf16[128,256]{1,0:T(8,128)(2,1)S(1)}, bf16[128,256]{1,0:T(8,128)(2,1)S(1)}, u32[]{:S(2)}, u32[]{:S(2)}) collective-permute-start(bf16[128,256]{1,0:T(8,128)(2,1)S(1)} %get-tuple-element.140), channel_id=1, source_target_pairs={{0,1},{1,0},{2,3},{3,2},{4,5},{5,4},{6,7},{7,6},{8,9},{9,8},{10,11... | collective-permute-start | bytes 196616 | tf_op jit(solution)/shard_map/ppermute | solution.py:415
  21.7 4.3 %collective-permute-start.7 = (f32[3,256]{1,0:T(4,128)S(1)}, f32[3,256]{1,0:T(4,128)S(1)}, u32[]{:S(2)}, u32[]{:S(2)}) collective-permute-start(f32[3,256]{1,0:T(4,128)S(1)} %pad_maximum_fusion.1.refs_0_), channel_id=1, source_target_pairs={{0,12},{1,13},{2,14},{3,15},{4,8},{5,9},{6,10},{7,11},{8,4},{9,5},... | collective-permute-start | bytes 9224 | tf_op jit(solution)/shard_map/ppermute | solution.py:331
  28.8 4.8 %collective-permute-start.10 = (f32[2,256]{1,0:T(2,128)S(1)}, f32[2,256]{1,0:T(2,128)S(1)}, u32[]{:S(2)}, u32[]{:S(2)}) collective-permute-start(f32[2,256]{1,0:T(2,128)S(1)} %get-tuple-element.70), channel_id=1, source_target_pairs={{0,3},{1,2},{2,1},{3,0},{4,7},{5,6},{6,5},{7,4},{8,11},{9,10},{10,... | collective-permute-start | bytes 6152 | tf_op jit(solution)/shard_map/ppermute | solution.py:331
  32.6 10.3 %collective-permute-start.16 = (bf16[768,256]{1,0:T(8,128)(2,1)S(1)}, bf16[768,256]{1,0:T(8,128)(2,1)S(1)}, u32[]{:S(2)}, u32[]{:S(2)}) collective-permute-start(bf16[768,256]{1,0:T(8,128)(2,1)S(1)} %get-tuple-element.72.window_own), channel_id=1, source_target_pairs={{0,1},{1,0},{2,3},{3,2},{4,5},{5,4},{6,7},{7,6},{8,9},{9,8},{10,11... | collective-permute-start | bytes 1179656 | tf_op jit(solution)/shard_map/ppermute | solution.py:331
  34.6 4.3 %collective-permute-start.13 = (f32[2,256]{1,0:T(2,128)S(1)}, f32[2,256]{1,0:T(2,128)S(1)}, u32[]{:S(2)}, u32[]{:S(2)}) collective-permute-start(f32[2,256]{1,0:T(2,128)S(1)} %add_add_fusion.refs_4_), channel_id=1, source_target_pairs={{0,12},{1,13},{2,14},{3,15},{4,8},{5,9},{6,10},{7,11},{8,4},{9,5},... | collective-permute-start | bytes 6152 | tf_op jit(solution)/shard_map/ppermute | solution.py:331
  52.8 15.4 %collective-permute-start.17 = (bf16[4,288,256]{2,1,0:T(8,128)(2,1)S(1)}, bf16[4,288,256]{2,1,0:T(8,128)(2,1)S(1)}, u32[]{:S(2)}, u32[]{:S(2)}) collective-permute-start(bf16[4,288,256]{2,1,0:T(8,128)(2,1)S(1)} %get-tuple-element.80), channel_id=1, source_target_pairs={{0,2},{1,3},{2,0},{3,1},{4,6},{5,7},{6,4},{7,5},{8,10},{9,11},{10,... | collective-permute-start | bytes 1769480 | tf_op jit(solution)/shard_map/ppermute | solution.py:331
  53.6 14.6 %collective-permute-start.18 = (bf16[2,144,256]{2,1,0:T(8,128)(2,1)S(1)}, bf16[2,144,256]{2,1,0:T(8,128)(2,1)S(1)}, u32[]{:S(2)}, u32[]{:S(2)}) collective-permute-start(bf16[2,144,256]{2,1,0:T(8,128)(2,1)S(1)} %get-tuple-element.81), channel_id=1, source_target_pairs={{0,4},{1,5},{2,6},{3,7},{4,0},{5,1},{6,2},{7,3},{8,12},{9,13},{10,... | collective-permute-start | bytes 442376 | tf_op jit(solution)/shard_map/ppermute | solution.py:331
  55.3 12.9 %collective-permute-start.19 = (bf16[2,144,256]{2,1,0:T(8,128)(2,1)S(1)}, bf16[2,144,256]{2,1,0:T(8,128)(2,1)S(1)}, u32[]{:S(2)}, u32[]{:S(2)}) collective-permute-start(bf16[2,144,256]{2,1,0:T(8,128)(2,1)S(1)} %get-tuple-element.82), channel_id=1, source_target_pairs={{0,8},{1,9},{2,10},{3,11},{4,12},{5,13},{6,14},{7,15},{8,0},{9,1},... | collective-permute-start | bytes 442376 | tf_op jit(solution)/shard_map/ppermute | solution.py:331
  56.1 12.0 %collective-permute-start.20 = (bf16[2,144,256]{2,1,0:T(8,128)(2,1)S(1)}, bf16[2,144,256]{2,1,0:T(8,128)(2,1)S(1)}, u32[]{:S(2)}, u32[]{:S(2)}) collective-permute-start(bf16[2,144,256]{2,1,0:T(8,128)(2,1)S(1)} %get-tuple-element.83), channel_id=1, source_target_pairs={{0,12},{1,13},{2,14},{3,15},{4,8},{5,9},{6,10},{7,11},{8,4},{9,5},... | collective-permute-start | bytes 442376 | tf_op jit(solution)/shard_map/ppermute | solution.py:331
  68.5 7.3 %collective-permute-start.24 = (bf16[1,144,256]{2,1,0:T(8,128)(2,1)S(1)}, bf16[1,144,256]{2,1,0:T(8,128)(2,1)S(1)}, u32[]{:S(2)}, u32[]{:S(2)}) collective-permute-start(bf16[1,144,256]{2,1,0:T(8,128)(2,1)S(1)} %get-tuple-element.98), channel_id=1, source_target_pairs={{0,2},{1,3},{2,0},{3,1},{4,6},{5,7},{6,4},{7,5},{8,10},{9,11},{10,... | collective-permute-start | bytes 221192 | tf_op jit(solution)/shard_map/ppermute | solution.py:331
  69.0 9.9 %collective-permute-start.21 = (bf16[1,288,256]{2,1,0:T(8,128)(2,1)S(1)}, bf16[1,288,256]{2,1,0:T(8,128)(2,1)S(1)}, u32[]{:S(2)}, u32[]{:S(2)}) collective-permute-start(bf16[1,288,256]{2,1,0:T(8,128)(2,1)S(1)} %get-tuple-element.95), channel_id=1, source_target_pairs={{0,4},{1,5},{2,6},{3,7},{4,0},{5,1},{6,2},{7,3},{8,12},{9,13},{10,... | collective-permute-start | bytes 442376 | tf_op jit(solution)/shard_map/ppermute | solution.py:331
  71.1 7.8 %collective-permute-start.22 = (bf16[1,288,256]{2,1,0:T(8,128)(2,1)S(1)}, bf16[1,288,256]{2,1,0:T(8,128)(2,1)S(1)}, u32[]{:S(2)}, u32[]{:S(2)}) collective-permute-start(bf16[1,288,256]{2,1,0:T(8,128)(2,1)S(1)} %get-tuple-element.96), channel_id=1, source_target_pairs={{0,8},{1,9},{2,10},{3,11},{4,12},{5,13},{6,14},{7,15},{8,0},{9,1},... | collective-permute-start | bytes 442376 | tf_op jit(solution)/shard_map/ppermute | solution.py:331
  71.7 9.1 %collective-permute-start.23 = (bf16[1,288,256]{2,1,0:T(8,128)(2,1)S(1)}, bf16[1,288,256]{2,1,0:T(8,128)(2,1)S(1)}, u32[]{:S(2)}, u32[]{:S(2)}) collective-permute-start(bf16[1,288,256]{2,1,0:T(8,128)(2,1)S(1)} %get-tuple-element.97), channel_id=1, source_target_pairs={{0,12},{1,13},{2,14},{3,15},{4,8},{5,9},{6,10},{7,11},{8,4},{9,5},... | collective-permute-start | bytes 442376 | tf_op jit(solution)/shard_map/ppermute | solution.py:331
  73.2 15.9 %collective-permute-start.29 = (bf16[128,256]{1,0:T(8,128)(2,1)S(1)}, bf16[128,256]{1,0:T(8,128)(2,1)S(1)}, u32[]{:S(2)}, u32[]{:S(2)}) collective-permute-start(bf16[128,256]{1,0:T(8,128)(2,1)S(1)} %get-tuple-element.149), channel_id=1, source_target_pairs={{0,1},{1,0},{2,3},{3,2},{4,5},{5,4},{6,7},{7,6},{8,9},{9,8},{10,11... | collective-permute-start | bytes 196616 | tf_op jit(solution)/shard_map/ppermute | solution.py:415
  75.8 13.7 %collective-permute-start.30 = (bf16[128,256]{1,0:T(8,128)(2,1)S(1)}, bf16[128,256]{1,0:T(8,128)(2,1)S(1)}, u32[]{:S(2)}, u32[]{:S(2)}) collective-permute-start(bf16[128,256]{1,0:T(8,128)(2,1)S(1)} %get-tuple-element.150), channel_id=1, source_target_pairs={{1,2},{2,1},{3,4},{4,3},{5,6},{6,5},{7,8},{8,7},{9,10},{10,9},{11,... | collective-permute-start | bytes 196616 | tf_op jit(solution)/shard_map/ppermute | solution.py:416
  81.0 11.5 %collective-permute-start.27 = (bf16[1,288,256]{2,1,0:T(8,128)(2,1)S(1)}, bf16[1,288,256]{2,1,0:T(8,128)(2,1)S(1)}, u32[]{:S(2)}, u32[]{:S(2)}) collective-permute-start(bf16[1,288,256]{2,1,0:T(8,128)(2,1)S(1)} %add_convert_fusion), channel_id=1, source_target_pairs={{0,12},{1,13},{2,14},{3,15},{4,8},{5,9},{6,10},{7,11},{8,4},{9,5},... | collective-permute-start | bytes 442376 | tf_op jit(solution)/shard_map/ppermute | solution.py:331
  82.4 16.6 %collective-permute-start.26 = (bf16[1,288,256]{2,1,0:T(8,128)(2,1)S(1)}, bf16[1,288,256]{2,1,0:T(8,128)(2,1)S(1)}, u32[]{:S(2)}, u32[]{:S(2)}) collective-permute-start(bf16[1,288,256]{2,1,0:T(8,128)(2,1)S(1)} %add_convert_fusion), channel_id=1, source_target_pairs={{0,8},{1,9},{2,10},{3,11},{4,12},{5,13},{6,14},{7,15},{8,0},{9,1},... | collective-permute-start | bytes 442376 | tf_op jit(solution)/shard_map/ppermute | solution.py:331
  89.1 9.8 %collective-permute-start.25 = (bf16[1,288,256]{2,1,0:T(8,128)(2,1)S(1)}, bf16[1,288,256]{2,1,0:T(8,128)(2,1)S(1)}, u32[]{:S(2)}, u32[]{:S(2)}) collective-permute-start(bf16[1,288,256]{2,1,0:T(8,128)(2,1)S(1)} %add_convert_fusion), channel_id=1, source_target_pairs={{0,4},{1,5},{2,6},{3,7},{4,0},{5,1},{6,2},{7,3},{8,12},{9,13},{10,... | collective-permute-start | bytes 442376 | tf_op jit(solution)/shard_map/ppermute | solution.py:331
  99.1 16.1 %collective-permute-start.31 = (bf16[4,288,256]{2,1,0:T(8,128)(2,1)S(1)}, bf16[4,288,256]{2,1,0:T(8,128)(2,1)S(1)}, u32[]{:S(2)}, u32[]{:S(2)}) collective-permute-start(bf16[4,288,256]{2,1,0:T(8,128)(2,1)S(1)} %get-tuple-element.142), channel_id=1, source_target_pairs={{0,2},{1,3},{2,0},{3,1},{4,6},{5,7},{6,4},{7,5},{8,10},{9,11},{10,... | collective-permute-start | bytes 1769480 | tf_op jit(solution)/shard_map/ppermute | solution.py:331
  101.2 6.1 %collective-permute-start.34 = (bf16[2,144,256]{2,1,0:T(8,128)(2,1)S(1)}, bf16[2,144,256]{2,1,0:T(8,128)(2,1)S(1)}, u32[]{:S(2)}, u32[]{:S(2)}) collective-permute-start(bf16[2,144,256]{2,1,0:T(8,128)(2,1)S(1)} %get-tuple-element.152.refs_1_), channel_id=1, source_target_pairs={{0,12},{1,13},{2,14},{3,15},{4,8},{5,9},{6,10},{7,11},{8,4},{9,5},... | collective-permute-start | bytes 442376 | tf_op jit(solution)/shard_map/ppermute | solution.py:331
  102.3 12.9 %collective-permute-start.33 = (bf16[2,144,256]{2,1,0:T(8,128)(2,1)S(1)}, bf16[2,144,256]{2,1,0:T(8,128)(2,1)S(1)}, u32[]{:S(2)}, u32[]{:S(2)}) collective-permute-start(bf16[2,144,256]{2,1,0:T(8,128)(2,1)S(1)} %get-tuple-element.152.refs_1_), channel_id=1, source_target_pairs={{0,8},{1,9},{2,10},{3,11},{4,12},{5,13},{6,14},{7,15},{8,0},{9,1},... | collective-permute-start | bytes 442376 | tf_op jit(solution)/shard_map/ppermute | solution.py:331
  102.3 12.9 %collective-permute-start.32 = (bf16[2,144,256]{2,1,0:T(8,128)(2,1)S(1)}, bf16[2,144,256]{2,1,0:T(8,128)(2,1)S(1)}, u32[]{:S(2)}, u32[]{:S(2)}) collective-permute-start(bf16[2,144,256]{2,1,0:T(8,128)(2,1)S(1)} %get-tuple-element.152.refs_1_), channel_id=1, source_target_pairs={{0,4},{1,5},{2,6},{3,7},{4,0},{5,1},{6,2},{7,3},{8,12},{9,13},{10,... | collective-permute-start | bytes 442376 | tf_op jit(solution)/shard_map/ppermute | solution.py:331
  115.2 3.9 %collective-permute-start.35 = (bf16[8,288,256]{2,1,0:T(8,128)(2,1)S(1)}, bf16[8,288,256]{2,1,0:T(8,128)(2,1)S(1)}, u32[]{:S(2)}, u32[]{:S(2)}) collective-permute-start(bf16[8,288,256]{2,1,0:T(8,128)(2,1)S(1)} %constant_dynamic-update-slice_fusion.6), channel_id=1, source_target_pairs={{0,1},{1,0},{2,3},{3,2},{4,5},{5,4},{6,7},{7,6},{8,9},{9,8},{10,11... | collective-permute-start | bytes 3538952 | tf_op jit(solution)/shard_map/ppermute | solution.py:331
  (19 other events, 110.9 us)

commit v10 on v9

--- a/solution.py
+++ b/solution.py
@@ -177,7 +177,7 @@
     place_ref, grad_own, grad_mate, map_own, map_mate, window_own, window_mate, *refs
 ):
     outs, scratch = refs[:6], refs[6:]
-    index, picked, grad, product, *staged, out_sem = scratch
+    index, picked, grad, turned, product, *staged, out_sem = scratch
     keep_one, send_one, keep_two, *sends_two = staged
     rows, channels = grad_own.shape
     core = place_ref[0]
@@ -185,6 +185,7 @@
     sides = ((map_own, window_own), (map_mate, window_mate))
     grad[0:rows, :] = grad_own[...]
     grad[rows:, :] = grad_mate[...]
+    turned[...] = jnp.transpose(grad[...].astype(F32)).astype(BF16)
     for side, (map_ref, _) in enumerate(sides):
         index[side] = transposed_map(map_ref)
 
@@ -196,7 +197,7 @@
                 tile = window[b * BLOCK : (b + 3) * BLOCK, :]
                 at = slice(side * rows + b * BLOCK, side * rows + (b + 1) * BLOCK)
                 picked[j, at, :] = dot(chosen, tile, ((1,), (0,))).astype(BF16)
-        product[j] = dot(picked[j], grad[...], ((0,), (0,)))
+        product[j] = jnp.transpose(dot(turned[...], picked[j], ((1,), (0,))))
 
     def stored(staged, out, n):
         return pltpu.make_async_copy(staged, out, out_sem.at[n])
@@ -514,6 +515,7 @@
             pltpu.VMEM((2, rows, BLOCK), jnp.int32),
             pltpu.VMEM((K_ONE, 2 * rows, channels), BF16),
             pltpu.VMEM((2 * rows, channels), BF16),
+            pltpu.VMEM((channels, 2 * rows), BF16),
             pltpu.VMEM((K_ONE, channels, channels), F32),
         ]
         + [pltpu.VMEM(*shape) for shape in shapes]

time: 122 us -> 121 us (level)
  no operation moved by 1% of the time
where the time goes in v10:
time: 121 us
  starting transfers between devices  49.5 us (41%)
  Pallas kernels  36.3 us (30%)
  waiting for transfers between devices  29.8 us (25%)
  other arithmetic  2.28 us (2%)
  between operations  1.81 us (1%)
    ppermute x33, starting transfers between devices, swap(): return lax.ppermute(value, 'dp', [(i, i ^ by) for i in range(peers)])  39.3 us
    ppermute x33, waiting for transfers between devices, swap(): return lax.ppermute(value, 'dp', [(i, i ^ by) for i in range(peers)])  29.8 us
    pallas_call x1, Pallas kernels, per_device(): pl.pallas_call(gradient_kernel, in_specs=[smem] + [vmem] * 6, out_specs=[...  9.23 us
    pallas_call x1, Pallas kernels, push(): pl.pallas_call(push_kernel, in_specs=[full((rows, channels)), full((K, ro...  7.99 us
    ppermute x2, starting transfers between devices, neighbours_swap(): lax.ppermute(jnp.where(odd == 1, to_after, to_before), 'dp', other_pairs)  7.58 us
    pallas_call x1, Pallas kernels, per_device(): pl.pallas_call(inner_kernel, in_specs=[vmem, vmem, hbm], out_specs=vmem,...  5.73 us
    pallas_call x3, Pallas kernels, placed(): pl.pallas_call(functools.partial(place_kernel, layout), in_specs=[smem] +...  5.05 us
    pallas_call x1, Pallas kernels, per_device(): pl.pallas_call(outer_kernel, in_specs=[smem, smem, vmem, vmem, vmem, vmem...  4.92 us
  transfers between devices with their start and end apart: 37, of which 15 were waited for; matrix products, arithmetic and copies ran while one was open for 1% of the time, Pallas kernels for 16%

profile of v10, /device:TPU:1, one launch (start us, length us, event | category | flops | bytes accessed | tf_op | source)
XLA Modules:
  0.0 120.5 jit_solution(6769689280475848254)
XLA Ops:
  1.5 4.5 %collective-permute-start.1 = (bf16[128,256]{1,0:T(8,128)(2,1)S(1)}, bf16[128,256]{1,0:T(8,128)(2,1)S(1)}, u32[]{:S(2)}, u32[]{:S(2)}) collective-permute-start(bf16[128,256]{1,0:T(8,128)(2,1)S(1)} %get-tuple-element.139), channel_id=1, source_target_pairs={{1,2},{2,1},{3,4},{4,3},{5,6},{6,5},{7,8},{8,7},{9,10},{10,9},{11,... | collective-permute-start | bytes 196616 | tf_op jit(solution)/shard_map/ppermute | solution.py:417
  6.1 5.7 %conv_inner.1.inner_ref = f32[256,256]{1,0:T(8,128)S(1)} custom-call(s32[27,512]{1,0:T(8,128)} %bitcast.15, bf16[512,256]{1,0:T(8,128)(2,1)} %feature_ref.1, bf16[27,256,256]{2,1,0:T(8,128)(2,1)} %weight_ref.3), custom_call_target="tpu_custom_call" | custom-call | flops 2264924160 | bytes 10616832 | tf_op jit(solution)/shard_map/conv_inner/pallas_call | solution.py:447
  12.6 4.9 %conv_outer.1 = (f32[256,256]{1,0:T(8,128)S(1)}, f32[3,256]{1,0:T(4,128)S(1)}, bf16[768,256]{1,0:T(8,128)(2,1)S(1)}) custom-call(s32[1]{0:T(128)S(6)} %copy.28.filled_ref, s32[1]{0:T(128)} %bitcast.1.odd_ref, s32[27,512]{1,0:T(8,128)S(1)} %bitcast.16, bf16[512,256]{1,0:T(8,128)(2,1)S(1)} %copy-done.2, bf16[128,256]{1,0:T(8,128)(2,1)S(1)} %collective-permute-done.even_ref, ...), custom_call_target="tpu_custom_call" | custom-call | flops 2264924160 | bytes 10616832 | tf_op jit(solution)/shard_map/conv_outer/pallas_call | solution.py:458
  17.5 1.7 %collective-permute-start.4 = (f32[3,256]{1,0:T(4,128)S(1)}, f32[3,256]{1,0:T(4,128)S(1)}, u32[]{:S(2)}, u32[]{:S(2)}) collective-permute-start(f32[3,256]{1,0:T(4,128)S(1)} %get-tuple-element.68), channel_id=1, source_target_pairs={{0,3},{1,2},{2,1},{3,0},{4,7},{5,6},{6,5},{7,4},{8,11},{9,10},{10,... | collective-permute-start | bytes 9224 | tf_op jit(solution)/shard_map/ppermute | solution.py:332
  21.7 2.4 %collective-permute-start.7 = (f32[3,256]{1,0:T(4,128)S(1)}, f32[3,256]{1,0:T(4,128)S(1)}, u32[]{:S(2)}, u32[]{:S(2)}) collective-permute-start(f32[3,256]{1,0:T(4,128)S(1)} %pad_maximum_fusion.1.refs_0_), channel_id=1, source_target_pairs={{0,12},{1,13},{2,14},{3,15},{4,8},{5,9},{6,10},{7,11},{8,4},{9,5},... | collective-permute-start | bytes 9224 | tf_op jit(solution)/shard_map/ppermute | solution.py:332
  26.1 1.7 %collective-permute-done.6.refs_2_ = f32[3,256]{1,0:T(4,128)S(1)} collective-permute-done((f32[3,256]{1,0:T(4,128)S(1)}, f32[3,256]{1,0:T(4,128)S(1)}, u32[]{:S(2)}, u32[]{:S(2)}) %collective-permute-start.6) | collective-permute-done | bytes 3104 | tf_op jit(solution)/shard_map/ppermute | solution.py:332
  28.8 3.4 %collective-permute-start.10 = (f32[2,256]{1,0:T(2,128)S(1)}, f32[2,256]{1,0:T(2,128)S(1)}, u32[]{:S(2)}, u32[]{:S(2)}) collective-permute-start(f32[2,256]{1,0:T(2,128)S(1)} %get-tuple-element.70), channel_id=1, source_target_pairs={{0,3},{1,2},{2,1},{3,0},{4,7},{5,6},{6,5},{7,4},{8,11},{9,10},{10,... | collective-permute-start | bytes 6152 | tf_op jit(solution)/shard_map/ppermute | solution.py:332
  36.5 1.7 %collective-permute-start.11 = (f32[2,256]{1,0:T(2,128)S(1)}, f32[2,256]{1,0:T(2,128)S(1)}, u32[]{:S(2)}, u32[]{:S(2)}) collective-permute-start(f32[2,256]{1,0:T(2,128)S(1)} %add_add_fusion.refs_4_), channel_id=1, source_target_pairs={{0,4},{1,5},{2,6},{3,7},{4,0},{5,1},{6,2},{7,3},{8,12},{9,13},{10,... | collective-permute-start | bytes 6152 | tf_op jit(solution)/shard_map/ppermute | solution.py:332
  40.0 1.7 %collective-permute-start.14 = (bf16[512,256]{1,0:T(8,128)(2,1)S(1)}, bf16[512,256]{1,0:T(8,128)(2,1)S(1)}, u32[]{:S(2)}, u32[]{:S(2)}) collective-permute-start(bf16[512,256]{1,0:T(8,128)(2,1)S(1)} %get-tuple-element.84.grad_own.grad_ref), channel_id=1, source_target_pairs={{0,1},{1,0},{2,3},{3,2},{4,5},{5,4},{6,7},{7,6},{8,9},{9,8},{10,11... | collective-permute-start | bytes 786440 | tf_op jit(solution)/shard_map/ppermute | solution.py:332
  42.9 9.2 %weight_gradient.1 = (f32[4,288,256]{2,1,0:T(8,128)S(1)}, bf16[4,288,256]{2,1,0:T(8,128)(2,1)S(1)}, f32[2,144,256]{2,1,0:T(8,128)S(1)}, bf16[2,144,256]{2,1,0:T(...) custom-call(s32[3]{0:T(128)S(1)} %pad_add_fusion.place_ref.places_ref, ...), custom_call_target="tpu_custom_call" | custom-call | flops 4529848320 | bytes 10616832 | tf_op jit(solution)/shard_map/weight_gradient/pallas_call | solution.py:509
  52.9 1.7 %collective-permute-start.18 = (bf16[2,144,256]{2,1,0:T(8,128)(2,1)S(1)}, bf16[2,144,256]{2,1,0:T(8,128)(2,1)S(1)}, u32[]{:S(2)}, u32[]{:S(2)}) collective-permute-start(bf16[2,144,256]{2,1,0:T(8,128)(2,1)S(1)} %get-tuple-element.81), channel_id=1, source_target_pairs={{0,4},{1,5},{2,6},{3,7},{4,0},{5,1},{6,2},{7,3},{8,12},{9,13},{10,... | collective-permute-start | bytes 442376 | tf_op jit(solution)/shard_map/ppermute | solution.py:332
  57.4 2.1 %push_edges.1 = (bf16[128,256]{1,0:T(8,128)(2,1)S(1)}, bf16[128,256]{1,0:T(8,128)(2,1)S(1)}) custom-call(bf16[512,256]{1,0:T(8,128)(2,1)S(1)} %get-tuple-element.84.grad_own.grad_ref, s32[27,512]{1,0:T(8,128)S(1)} %bitcast.19, bf16[27,256,256]{2,1,0:T(8,128)(2,1)S(1)} %copy-done), custom_call_target="tpu_custom_call" | custom-call | flops 1000 | bytes 1000 | tf_op jit(solution)/shard_map/push_edges/pallas_call | solution.py:539
  59.5 8.0 %push.1 = f32[512,256]{1,0:T(8,128)S(1)} custom-call(bf16[512,256]{1,0:T(8,128)(2,1)S(1)} %get-tuple-element.84.grad_own.grad_ref, s32[27,512]{1,0:T(8,128)S(1)} %bitcast.20, bf16[27,256,256]{2,1,0:T(8,128)(2,1)S(1)} %copy-done), custom_call_target="tpu_custom_call" | custom-call | flops 1000 | bytes 1000 | tf_op jit(solution)/shard_map/push/pallas_call | solution.py:551
  68.3 2.1 %collective-permute-start.21 = (bf16[1,288,256]{2,1,0:T(8,128)(2,1)S(1)}, bf16[1,288,256]{2,1,0:T(8,128)(2,1)S(1)}, u32[]{:S(2)}, u32[]{:S(2)}) collective-permute-start(bf16[1,288,256]{2,1,0:T(8,128)(2,1)S(1)} %get-tuple-element.95), channel_id=1, source_target_pairs={{0,4},{1,5},{2,6},{3,7},{4,0},{5,1},{6,2},{7,3},{8,12},{9,13},{10,... | collective-permute-start | bytes 442376 | tf_op jit(solution)/shard_map/ppermute | solution.py:332
  72.6 2.5 %collective-permute-start.29 = (bf16[128,256]{1,0:T(8,128)(2,1)S(1)}, bf16[128,256]{1,0:T(8,128)(2,1)S(1)}, u32[]{:S(2)}, u32[]{:S(2)}) collective-permute-start(bf16[128,256]{1,0:T(8,128)(2,1)S(1)} %get-tuple-element.149), channel_id=1, source_target_pairs={{0,1},{1,0},{2,3},{3,2},{4,5},{5,4},{6,7},{7,6},{8,9},{9,8},{10,11... | collective-permute-start | bytes 196616 | tf_op jit(solution)/shard_map/ppermute | solution.py:416
  75.1 3.1 %collective-permute-start.30 = (bf16[128,256]{1,0:T(8,128)(2,1)S(1)}, bf16[128,256]{1,0:T(8,128)(2,1)S(1)}, u32[]{:S(2)}, u32[]{:S(2)}) collective-permute-start(bf16[128,256]{1,0:T(8,128)(2,1)S(1)} %get-tuple-element.150), channel_id=1, source_target_pairs={{1,2},{2,1},{3,4},{4,3},{5,6},{6,5},{7,8},{8,7},{9,10},{10,9},{11,... | collective-permute-start | bytes 196616 | tf_op jit(solution)/shard_map/ppermute | solution.py:417
  78.2 2.0 %collective-permute-done.23 = bf16[1,288,256]{2,1,0:T(8,128)(2,1)S(1)} collective-permute-done((bf16[1,288,256]{2,1,0:T(8,128)(2,1)S(1)}, bf16[1,288,256]{2,1,0:T(8,128)(2,1)S(1)}, u32[]{:S(2)}, u32[]{:S(2)}) %collective-permute-start.23) | collective-permute-done | bytes 147488 | tf_op jit(solution)/shard_map/ppermute | solution.py:332
  81.7 6.7 %collective-permute-start.26 = (bf16[1,288,256]{2,1,0:T(8,128)(2,1)S(1)}, bf16[1,288,256]{2,1,0:T(8,128)(2,1)S(1)}, u32[]{:S(2)}, u32[]{:S(2)}) collective-permute-start(bf16[1,288,256]{2,1,0:T(8,128)(2,1)S(1)} %add_convert_fusion), channel_id=1, source_target_pairs={{0,8},{1,9},{2,10},{3,11},{4,12},{5,13},{6,14},{7,15},{8,0},{9,1},... | collective-permute-start | bytes 442376 | tf_op jit(solution)/shard_map/ppermute | solution.py:332
  89.7 2.1 %collective-permute-done.28 = bf16[1,144,256]{2,1,0:T(8,128)(2,1)S(1)} collective-permute-done((bf16[1,144,256]{2,1,0:T(8,128)(2,1)S(1)}, bf16[1,144,256]{2,1,0:T(8,128)(2,1)S(1)}, u32[]{:S(2)}, u32[]{:S(2)}) %collective-permute-start.28) | collective-permute-done | bytes 73760 | tf_op jit(solution)/shard_map/ppermute | solution.py:332
  91.7 6.5 %collective-permute-done.26 = bf16[1,288,256]{2,1,0:T(8,128)(2,1)S(1)} collective-permute-done((bf16[1,288,256]{2,1,0:T(8,128)(2,1)S(1)}, bf16[1,288,256]{2,1,0:T(8,128)(2,1)S(1)}, u32[]{:S(2)}, u32[]{:S(2)}) %collective-permute-start.26) | collective-permute-done | bytes 147488 | tf_op jit(solution)/shard_map/ppermute | solution.py:332
  98.4 2.1 %collective-permute-start.31 = (bf16[4,288,256]{2,1,0:T(8,128)(2,1)S(1)}, bf16[4,288,256]{2,1,0:T(8,128)(2,1)S(1)}, u32[]{:S(2)}, u32[]{:S(2)}) collective-permute-start(bf16[4,288,256]{2,1,0:T(8,128)(2,1)S(1)} %get-tuple-element.142), channel_id=1, source_target_pairs={{0,2},{1,3},{2,0},{3,1},{4,6},{5,7},{6,4},{7,5},{8,10},{9,11},{10,... | collective-permute-start | bytes 1769480 | tf_op jit(solution)/shard_map/ppermute | solution.py:332
  101.7 2.4 %collective-permute-start.32 = (bf16[2,144,256]{2,1,0:T(8,128)(2,1)S(1)}, bf16[2,144,256]{2,1,0:T(8,128)(2,1)S(1)}, u32[]{:S(2)}, u32[]{:S(2)}) collective-permute-start(bf16[2,144,256]{2,1,0:T(8,128)(2,1)S(1)} %get-tuple-element.152.refs_1_), channel_id=1, source_target_pairs={{0,4},{1,5},{2,6},{3,7},{4,0},{5,1},{6,2},{7,3},{8,12},{9,13},{10,... | collective-permute-start | bytes 442376 | tf_op jit(solution)/shard_map/ppermute | solution.py:332
  106.6 8.0 %collective-permute-done.33 = bf16[2,144,256]{2,1,0:T(8,128)(2,1)S(1)} collective-permute-done((bf16[2,144,256]{2,1,0:T(8,128)(2,1)S(1)}, bf16[2,144,256]{2,1,0:T(8,128)(2,1)S(1)}, u32[]{:S(2)}, u32[]{:S(2)}) %collective-permute-start.33) | collective-permute-done | bytes 147488 | tf_op jit(solution)/shard_map/ppermute | solution.py:332
  118.4 2.0 %place.5 = bf16[27,256,256]{2,1,0:T(8,128)(2,1)} custom-call(s32[3]{0:T(128)S(1)} %pad_add_fusion.place_ref.places_ref, bf16[8,9,32,256]{3,2,1,0:T(8,128)(2,1)S(1)} %bitcast.13, bf16[8,144,256]{2,1,0:T(8,128)(2,1)S(1)} %collective-permute-done.36.refs_1_, bf16[27,256,256]{2,1,0:T(8,128)(2,1)} %place.4.refs_2_), custom_call_target="tpu_custom_call", output_to_operand_aliasing={{}: (3, {})} | custom-call | bytes 3538944 | tf_op jit(solution)/shard_map/place/pallas_call | solution.py:582
  (98 shorter events, 30.4 us)
Async XLA Ops:
  1.5 11.0 %collective-permute-start.1 = (bf16[128,256]{1,0:T(8,128)(2,1)S(1)}, bf16[128,256]{1,0:T(8,128)(2,1)S(1)}, u32[]{:S(2)}, u32[]{:S(2)}) collective-permute-start(bf16[128,256]{1,0:T(8,128)(2,1)S(1)} %get-tuple-element.139), channel_id=1, source_target_pairs={{1,2},{2,1},{3,4},{4,3},{5,6},{6,5},{7,8},{8,7},{9,10},{10,9},{11,... | collective-permute-start | bytes 196616 | tf_op jit(solution)/shard_map/ppermute | solution.py:417
  6.0 6.5 %collective-permute-start = (bf16[128,256]{1,0:T(8,128)(2,1)S(1)}, bf16[128,256]{1,0:T(8,128)(2,1)S(1)}, u32[]{:S(2)}, u32[]{:S(2)}) collective-permute-start(bf16[128,256]{1,0:T(8,128)(2,1)S(1)} %get-tuple-element.140), channel_id=1, source_target_pairs={{0,1},{1,0},{2,3},{3,2},{4,5},{5,4},{6,7},{7,6},{8,9},{9,8},{10,11... | collective-permute-start | bytes 196616 | tf_op jit(solution)/shard_map/ppermute | solution.py:416
  21.7 4.3 %collective-permute-start.7 = (f32[3,256]{1,0:T(4,128)S(1)}, f32[3,256]{1,0:T(4,128)S(1)}, u32[]{:S(2)}, u32[]{:S(2)}) collective-permute-start(f32[3,256]{1,0:T(4,128)S(1)} %pad_maximum_fusion.1.refs_0_), channel_id=1, source_target_pairs={{0,12},{1,13},{2,14},{3,15},{4,8},{5,9},{6,10},{7,11},{8,4},{9,5},... | collective-permute-start | bytes 9224 | tf_op jit(solution)/shard_map/ppermute | solution.py:332
  28.8 4.8 %collective-permute-start.10 = (f32[2,256]{1,0:T(2,128)S(1)}, f32[2,256]{1,0:T(2,128)S(1)}, u32[]{:S(2)}, u32[]{:S(2)}) collective-permute-start(f32[2,256]{1,0:T(2,128)S(1)} %get-tuple-element.70), channel_id=1, source_target_pairs={{0,3},{1,2},{2,1},{3,0},{4,7},{5,6},{6,5},{7,4},{8,11},{9,10},{10,... | collective-permute-start | bytes 6152 | tf_op jit(solution)/shard_map/ppermute | solution.py:332
  32.6 10.3 %collective-permute-start.16 = (bf16[768,256]{1,0:T(8,128)(2,1)S(1)}, bf16[768,256]{1,0:T(8,128)(2,1)S(1)}, u32[]{:S(2)}, u32[]{:S(2)}) collective-permute-start(bf16[768,256]{1,0:T(8,128)(2,1)S(1)} %get-tuple-element.72.window_own), channel_id=1, source_target_pairs={{0,1},{1,0},{2,3},{3,2},{4,5},{5,4},{6,7},{7,6},{8,9},{9,8},{10,11... | collective-permute-start | bytes 1179656 | tf_op jit(solution)/shard_map/ppermute | solution.py:332
  34.6 4.3 %collective-permute-start.13 = (f32[2,256]{1,0:T(2,128)S(1)}, f32[2,256]{1,0:T(2,128)S(1)}, u32[]{:S(2)}, u32[]{:S(2)}) collective-permute-start(f32[2,256]{1,0:T(2,128)S(1)} %add_add_fusion.refs_4_), channel_id=1, source_target_pairs={{0,12},{1,13},{2,14},{3,15},{4,8},{5,9},{6,10},{7,11},{8,4},{9,5},... | collective-permute-start | bytes 6152 | tf_op jit(solution)/shard_map/ppermute | solution.py:332
  52.2 15.4 %collective-permute-start.17 = (bf16[4,288,256]{2,1,0:T(8,128)(2,1)S(1)}, bf16[4,288,256]{2,1,0:T(8,128)(2,1)S(1)}, u32[]{:S(2)}, u32[]{:S(2)}) collective-permute-start(bf16[4,288,256]{2,1,0:T(8,128)(2,1)S(1)} %get-tuple-element.80), channel_id=1, source_target_pairs={{0,2},{1,3},{2,0},{3,1},{4,6},{5,7},{6,4},{7,5},{8,10},{9,11},{10,... | collective-permute-start | bytes 1769480 | tf_op jit(solution)/shard_map/ppermute | solution.py:332
  52.9 14.6 %collective-permute-start.18 = (bf16[2,144,256]{2,1,0:T(8,128)(2,1)S(1)}, bf16[2,144,256]{2,1,0:T(8,128)(2,1)S(1)}, u32[]{:S(2)}, u32[]{:S(2)}) collective-permute-start(bf16[2,144,256]{2,1,0:T(8,128)(2,1)S(1)} %get-tuple-element.81), channel_id=1, source_target_pairs={{0,4},{1,5},{2,6},{3,7},{4,0},{5,1},{6,2},{7,3},{8,12},{9,13},{10,... | collective-permute-start | bytes 442376 | tf_op jit(solution)/shard_map/ppermute | solution.py:332
  54.6 12.9 %collective-permute-start.19 = (bf16[2,144,256]{2,1,0:T(8,128)(2,1)S(1)}, bf16[2,144,256]{2,1,0:T(8,128)(2,1)S(1)}, u32[]{:S(2)}, u32[]{:S(2)}) collective-permute-start(bf16[2,144,256]{2,1,0:T(8,128)(2,1)S(1)} %get-tuple-element.82), channel_id=1, source_target_pairs={{0,8},{1,9},{2,10},{3,11},{4,12},{5,13},{6,14},{7,15},{8,0},{9,1},... | collective-permute-start | bytes 442376 | tf_op jit(solution)/shard_map/ppermute | solution.py:332
  55.5 12.0 %collective-permute-start.20 = (bf16[2,144,256]{2,1,0:T(8,128)(2,1)S(1)}, bf16[2,144,256]{2,1,0:T(8,128)(2,1)S(1)}, u32[]{:S(2)}, u32[]{:S(2)}) collective-permute-start(bf16[2,144,256]{2,1,0:T(8,128)(2,1)S(1)} %get-tuple-element.83), channel_id=1, source_target_pairs={{0,12},{1,13},{2,14},{3,15},{4,8},{5,9},{6,10},{7,11},{8,4},{9,5},... | collective-permute-start | bytes 442376 | tf_op jit(solution)/shard_map/ppermute | solution.py:332
  67.8 7.3 %collective-permute-start.24 = (bf16[1,144,256]{2,1,0:T(8,128)(2,1)S(1)}, bf16[1,144,256]{2,1,0:T(8,128)(2,1)S(1)}, u32[]{:S(2)}, u32[]{:S(2)}) collective-permute-start(bf16[1,144,256]{2,1,0:T(8,128)(2,1)S(1)} %get-tuple-element.98), channel_id=1, source_target_pairs={{0,2},{1,3},{2,0},{3,1},{4,6},{5,7},{6,4},{7,5},{8,10},{9,11},{10,... | collective-permute-start | bytes 221192 | tf_op jit(solution)/shard_map/ppermute | solution.py:332
  68.3 9.9 %collective-permute-start.21 = (bf16[1,288,256]{2,1,0:T(8,128)(2,1)S(1)}, bf16[1,288,256]{2,1,0:T(8,128)(2,1)S(1)}, u32[]{:S(2)}, u32[]{:S(2)}) collective-permute-start(bf16[1,288,256]{2,1,0:T(8,128)(2,1)S(1)} %get-tuple-element.95), channel_id=1, source_target_pairs={{0,4},{1,5},{2,6},{3,7},{4,0},{5,1},{6,2},{7,3},{8,12},{9,13},{10,... | collective-permute-start | bytes 442376 | tf_op jit(solution)/shard_map/ppermute | solution.py:332
  70.4 7.8 %collective-permute-start.22 = (bf16[1,288,256]{2,1,0:T(8,128)(2,1)S(1)}, bf16[1,288,256]{2,1,0:T(8,128)(2,1)S(1)}, u32[]{:S(2)}, u32[]{:S(2)}) collective-permute-start(bf16[1,288,256]{2,1,0:T(8,128)(2,1)S(1)} %get-tuple-element.96), channel_id=1, source_target_pairs={{0,8},{1,9},{2,10},{3,11},{4,12},{5,13},{6,14},{7,15},{8,0},{9,1},... | collective-permute-start | bytes 442376 | tf_op jit(solution)/shard_map/ppermute | solution.py:332
  71.1 9.1 %collective-permute-start.23 = (bf16[1,288,256]{2,1,0:T(8,128)(2,1)S(1)}, bf16[1,288,256]{2,1,0:T(8,128)(2,1)S(1)}, u32[]{:S(2)}, u32[]{:S(2)}) collective-permute-start(bf16[1,288,256]{2,1,0:T(8,128)(2,1)S(1)} %get-tuple-element.97), channel_id=1, source_target_pairs={{0,12},{1,13},{2,14},{3,15},{4,8},{5,9},{6,10},{7,11},{8,4},{9,5},... | collective-permute-start | bytes 442376 | tf_op jit(solution)/shard_map/ppermute | solution.py:332
  72.6 15.9 %collective-permute-start.29 = (bf16[128,256]{1,0:T(8,128)(2,1)S(1)}, bf16[128,256]{1,0:T(8,128)(2,1)S(1)}, u32[]{:S(2)}, u32[]{:S(2)}) collective-permute-start(bf16[128,256]{1,0:T(8,128)(2,1)S(1)} %get-tuple-element.149), channel_id=1, source_target_pairs={{0,1},{1,0},{2,3},{3,2},{4,5},{5,4},{6,7},{7,6},{8,9},{9,8},{10,11... | collective-permute-start | bytes 196616 | tf_op jit(solution)/shard_map/ppermute | solution.py:416
  75.1 13.7 %collective-permute-start.30 = (bf16[128,256]{1,0:T(8,128)(2,1)S(1)}, bf16[128,256]{1,0:T(8,128)(2,1)S(1)}, u32[]{:S(2)}, u32[]{:S(2)}) collective-permute-start(bf16[128,256]{1,0:T(8,128)(2,1)S(1)} %get-tuple-element.150), channel_id=1, source_target_pairs={{1,2},{2,1},{3,4},{4,3},{5,6},{6,5},{7,8},{8,7},{9,10},{10,9},{11,... | collective-permute-start | bytes 196616 | tf_op jit(solution)/shard_map/ppermute | solution.py:417
  80.3 11.4 %collective-permute-start.27 = (bf16[1,288,256]{2,1,0:T(8,128)(2,1)S(1)}, bf16[1,288,256]{2,1,0:T(8,128)(2,1)S(1)}, u32[]{:S(2)}, u32[]{:S(2)}) collective-permute-start(bf16[1,288,256]{2,1,0:T(8,128)(2,1)S(1)} %add_convert_fusion), channel_id=1, source_target_pairs={{0,12},{1,13},{2,14},{3,15},{4,8},{5,9},{6,10},{7,11},{8,4},{9,5},... | collective-permute-start | bytes 442376 | tf_op jit(solution)/shard_map/ppermute | solution.py:332
  81.7 16.5 %collective-permute-start.26 = (bf16[1,288,256]{2,1,0:T(8,128)(2,1)S(1)}, bf16[1,288,256]{2,1,0:T(8,128)(2,1)S(1)}, u32[]{:S(2)}, u32[]{:S(2)}) collective-permute-start(bf16[1,288,256]{2,1,0:T(8,128)(2,1)S(1)} %add_convert_fusion), channel_id=1, source_target_pairs={{0,8},{1,9},{2,10},{3,11},{4,12},{5,13},{6,14},{7,15},{8,0},{9,1},... | collective-permute-start | bytes 442376 | tf_op jit(solution)/shard_map/ppermute | solution.py:332
  88.4 9.8 %collective-permute-start.25 = (bf16[1,288,256]{2,1,0:T(8,128)(2,1)S(1)}, bf16[1,288,256]{2,1,0:T(8,128)(2,1)S(1)}, u32[]{:S(2)}, u32[]{:S(2)}) collective-permute-start(bf16[1,288,256]{2,1,0:T(8,128)(2,1)S(1)} %add_convert_fusion), channel_id=1, source_target_pairs={{0,4},{1,5},{2,6},{3,7},{4,0},{5,1},{6,2},{7,3},{8,12},{9,13},{10,... | collective-permute-start | bytes 442376 | tf_op jit(solution)/shard_map/ppermute | solution.py:332
  98.4 16.2 %collective-permute-start.31 = (bf16[4,288,256]{2,1,0:T(8,128)(2,1)S(1)}, bf16[4,288,256]{2,1,0:T(8,128)(2,1)S(1)}, u32[]{:S(2)}, u32[]{:S(2)}) collective-permute-start(bf16[4,288,256]{2,1,0:T(8,128)(2,1)S(1)} %get-tuple-element.142), channel_id=1, source_target_pairs={{0,2},{1,3},{2,0},{3,1},{4,6},{5,7},{6,4},{7,5},{8,10},{9,11},{10,... | collective-permute-start | bytes 1769480 | tf_op jit(solution)/shard_map/ppermute | solution.py:332
  100.5 6.1 %collective-permute-start.34 = (bf16[2,144,256]{2,1,0:T(8,128)(2,1)S(1)}, bf16[2,144,256]{2,1,0:T(8,128)(2,1)S(1)}, u32[]{:S(2)}, u32[]{:S(2)}) collective-permute-start(bf16[2,144,256]{2,1,0:T(8,128)(2,1)S(1)} %get-tuple-element.152.refs_1_), channel_id=1, source_target_pairs={{0,12},{1,13},{2,14},{3,15},{4,8},{5,9},{6,10},{7,11},{8,4},{9,5},... | collective-permute-start | bytes 442376 | tf_op jit(solution)/shard_map/ppermute | solution.py:332
  101.7 12.9 %collective-permute-start.33 = (bf16[2,144,256]{2,1,0:T(8,128)(2,1)S(1)}, bf16[2,144,256]{2,1,0:T(8,128)(2,1)S(1)}, u32[]{:S(2)}, u32[]{:S(2)}) collective-permute-start(bf16[2,144,256]{2,1,0:T(8,128)(2,1)S(1)} %get-tuple-element.152.refs_1_), channel_id=1, source_target_pairs={{0,8},{1,9},{2,10},{3,11},{4,12},{5,13},{6,14},{7,15},{8,0},{9,1},... | collective-permute-start | bytes 442376 | tf_op jit(solution)/shard_map/ppermute | solution.py:332
  101.7 12.9 %collective-permute-start.32 = (bf16[2,144,256]{2,1,0:T(8,128)(2,1)S(1)}, bf16[2,144,256]{2,1,0:T(8,128)(2,1)S(1)}, u32[]{:S(2)}, u32[]{:S(2)}) collective-permute-start(bf16[2,144,256]{2,1,0:T(8,128)(2,1)S(1)} %get-tuple-element.152.refs_1_), channel_id=1, source_target_pairs={{0,4},{1,5},{2,6},{3,7},{4,0},{5,1},{6,2},{7,3},{8,12},{9,13},{10,... | collective-permute-start | bytes 442376 | tf_op jit(solution)/shard_map/ppermute | solution.py:332
  114.6 3.8 %collective-permute-start.35 = (bf16[8,288,256]{2,1,0:T(8,128)(2,1)S(1)}, bf16[8,288,256]{2,1,0:T(8,128)(2,1)S(1)}, u32[]{:S(2)}, u32[]{:S(2)}) collective-permute-start(bf16[8,288,256]{2,1,0:T(8,128)(2,1)S(1)} %constant_dynamic-update-slice_fusion.6), channel_id=1, source_target_pairs={{0,1},{1,0},{2,3},{3,2},{4,5},{5,4},{6,7},{7,6},{8,9},{9,8},{10,11... | collective-permute-start | bytes 3538952 | tf_op jit(solution)/shard_map/ppermute | solution.py:332
  (19 other events, 110.3 us)

commit v11 on v10

--- a/solution.py
+++ b/solution.py
@@ -52,7 +52,8 @@
 
 
 def chosen_slots(slot, slots):
-    return jnp.where(slot == slots, 1.0, 0.0).astype(BF16)
+    one = jnp.ones((), BF16 if slots.dtype == jnp.int16 else F32)
+    return jnp.where(slot == slots, one, jnp.zeros_like(one)).astype(BF16)
 
 
 def transposed_map(map_ref):
@@ -181,7 +182,7 @@
     keep_one, send_one, keep_two, *sends_two = staged
     rows, channels = grad_own.shape
     core = place_ref[0]
-    slots = lax.broadcasted_iota(jnp.int32, (BLOCK, 3 * BLOCK), 1)
+    slots = lax.broadcasted_iota(jnp.int32, (BLOCK, 3 * BLOCK), 1).astype(jnp.int16)
     sides = ((map_own, window_own), (map_mate, window_mate))
     grad[0:rows, :] = grad_own[...]
     grad[rows:, :] = grad_mate[...]
@@ -193,7 +194,8 @@
         for side, (_, window) in enumerate(sides):
             for b in range(rows // BLOCK):
                 here = slice(b * BLOCK, (b + 1) * BLOCK)
-                chosen = chosen_slots(slot_of(side)[here] - (rows + (b - 1) * BLOCK), slots)
+                slot = slot_of(side)[here] - (rows + (b - 1) * BLOCK)
+                chosen = chosen_slots(slot.astype(jnp.int16), slots)
                 tile = window[b * BLOCK : (b + 3) * BLOCK, :]
                 at = slice(side * rows + b * BLOCK, side * rows + (b + 1) * BLOCK)
                 picked[j, at, :] = dot(chosen, tile, ((1,), (0,))).astype(BF16)
@@ -356,7 +358,7 @@
     return [swap(piece, by) for by in STAGES[stage]]
 
 
-def summed_over_devices(one, two, grad_conv, edge_push, push, spread, finish, place):
+def summed_over_devices(one, two, grad_conv, sums, edge_push, push, spread, finish, place):
     parts, grad_conv = lax.optimization_barrier(((one, two), grad_conv))
     received = [swapped(sends, stage) for (_, sends), stage in zip(parts, "xz")]
     edges, sink = edge_push(grad_conv), push(grad_conv)
@@ -367,7 +369,7 @@
     parts, edges = lax.optimization_barrier((parts, edges))
     received = [swapped(sends, stage) for (_, sends), stage in zip(parts, "zx")]
     halo = spread(*edges)
-    received, sink = lax.optimization_barrier((received, sink))
+    received, sink, sums = lax.optimization_barrier((received, sink, sums))
     pieces = [part([kept] + got, 0, 1) for (kept, _), got in zip(parts, received)]
     by = 16
     while by < lax.axis_size("dp"):
@@ -375,7 +377,7 @@
         by *= 2
     pieces = [piece.astype(BF16) for piece in pieces]
     pieces, sink = lax.optimization_barrier((pieces, sink))
-    results = finish(sink, halo)
+    results = finish(sink, halo, sums)
     received = [gather_start(piece, stage) for piece, stage in zip(pieces, "zx")]
     received, pieces, results = lax.optimization_barrier((received, pieces, results))
     early = [jnp.concatenate([piece] + got, axis=0) for piece, got in zip(pieces, received)]
@@ -557,7 +559,7 @@
             **push_grid,
         )(grad_conv, map_rows, weights)
 
-    def finish(sink, halo):
+    def finish(sink, halo, sums):
         even, other = halo
         from_prev = jnp.where(odd == 1, even, other).astype(F32)
         from_next = jnp.where(odd == 1, other, even).astype(F32)
@@ -595,7 +597,7 @@
         return placed(((0, 0, 0),), (own,))
 
     late, other_pieces, results = summed_over_devices(
-        one, two, grad_conv, edge_push, push, neighbours_swap, finish, place_early
+        one, two, grad_conv, sums, edge_push, push, neighbours_swap, finish, place_early
     )
     (grad_features, grad_gain, grad_shift), grad_weights = results
     first_late = (8 - late[0].shape[0], 8 - late[1].shape[0])

time: 121 us -> 121 us (level)
  no operation moved by 1% of the time
where the time goes in v11:
time: 121 us; the launch traced here: 120 us
  starting transfers between devices  49.9 us (41%)
  Pallas kernels  36.4 us (30%)
  waiting for transfers between devices  29.2 us (24%)
  other arithmetic  2.29 us (2%)
  between operations  1.81 us (1%)
    ppermute x33, starting transfers between devices, swap(): return lax.ppermute(value, 'dp', [(i, i ^ by) for i in range(peers)])  39.7 us
    ppermute x33, waiting for transfers between devices, swap(): return lax.ppermute(value, 'dp', [(i, i ^ by) for i in range(peers)])  29.2 us
    pallas_call x1, Pallas kernels, per_device(): pl.pallas_call(gradient_kernel, in_specs=[smem] + [vmem] * 6, out_specs=[...  9.08 us
    pallas_call x1, Pallas kernels, push(): pl.pallas_call(push_kernel, in_specs=[full((rows, channels)), full((K, ro...  7.98 us
    ppermute x2, starting transfers between devices, neighbours_swap(): lax.ppermute(jnp.where(odd == 1, to_after, to_before), 'dp', other_pairs)  7.58 us
    pallas_call x1, Pallas kernels, per_device(): pl.pallas_call(inner_kernel, in_specs=[vmem, vmem, hbm], out_specs=vmem,...  5.73 us
    pallas_call x3, Pallas kernels, placed(): pl.pallas_call(functools.partial(place_kernel, layout), in_specs=[smem] +...  5.05 us
    pallas_call x1, Pallas kernels, per_device(): pl.pallas_call(outer_kernel, in_specs=[smem, smem, vmem, vmem, vmem, vmem...  4.92 us
  transfers between devices with their start and end apart: 37, of which 15 were waited for; matrix products, arithmetic and copies ran while one was open for 1% of the time, Pallas kernels for 16%

profile of v11, /device:TPU:1, one launch (start us, length us, event | category | flops | bytes accessed | tf_op | source)
XLA Modules:
  0.0 120.4 jit_solution(17324464719120807304)
XLA Ops:
  1.5 4.5 %collective-permute-start.1 = (bf16[128,256]{1,0:T(8,128)(2,1)S(1)}, bf16[128,256]{1,0:T(8,128)(2,1)S(1)}, u32[]{:S(2)}, u32[]{:S(2)}) collective-permute-start(bf16[128,256]{1,0:T(8,128)(2,1)S(1)} %get-tuple-element.141), channel_id=1, source_target_pairs={{1,2},{2,1},{3,4},{4,3},{5,6},{6,5},{7,8},{8,7},{9,10},{10,9},{11,... | collective-permute-start | bytes 196616 | tf_op jit(solution)/shard_map/ppermute | solution.py:419
  6.1 5.7 %conv_inner.1.inner_ref = f32[256,256]{1,0:T(8,128)S(1)} custom-call(s32[27,512]{1,0:T(8,128)} %bitcast.15, bf16[512,256]{1,0:T(8,128)(2,1)} %feature_ref.1, bf16[27,256,256]{2,1,0:T(8,128)(2,1)} %weight_ref.3), custom_call_target="tpu_custom_call" | custom-call | flops 2264924160 | bytes 10616832 | tf_op jit(solution)/shard_map/conv_inner/pallas_call | solution.py:449
  12.6 4.9 %conv_outer.1 = (f32[256,256]{1,0:T(8,128)S(1)}, f32[3,256]{1,0:T(4,128)S(1)}, bf16[768,256]{1,0:T(8,128)(2,1)S(1)}) custom-call(s32[1]{0:T(128)S(6)} %copy.28.filled_ref, s32[1]{0:T(128)} %bitcast.1.odd_ref, s32[27,512]{1,0:T(8,128)S(1)} %bitcast.16, bf16[512,256]{1,0:T(8,128)(2,1)S(1)} %copy-done.2, bf16[128,256]{1,0:T(8,128)(2,1)S(1)} %collective-permute-done.even_ref, ...), custom_call_target="tpu_custom_call" | custom-call | flops 2264924160 | bytes 10616832 | tf_op jit(solution)/shard_map/conv_outer/pallas_call | solution.py:460
  17.5 1.7 %collective-permute-start.4 = (f32[3,256]{1,0:T(4,128)S(1)}, f32[3,256]{1,0:T(4,128)S(1)}, u32[]{:S(2)}, u32[]{:S(2)}) collective-permute-start(f32[3,256]{1,0:T(4,128)S(1)} %get-tuple-element.69), channel_id=1, source_target_pairs={{0,3},{1,2},{2,1},{3,0},{4,7},{5,6},{6,5},{7,4},{8,11},{9,10},{10,... | collective-permute-start | bytes 9224 | tf_op jit(solution)/shard_map/ppermute | solution.py:334
  21.7 2.4 %collective-permute-start.7 = (f32[3,256]{1,0:T(4,128)S(1)}, f32[3,256]{1,0:T(4,128)S(1)}, u32[]{:S(2)}, u32[]{:S(2)}) collective-permute-start(f32[3,256]{1,0:T(4,128)S(1)} %pad_maximum_fusion.1.refs_0_), channel_id=1, source_target_pairs={{0,12},{1,13},{2,14},{3,15},{4,8},{5,9},{6,10},{7,11},{8,4},{9,5},... | collective-permute-start | bytes 9224 | tf_op jit(solution)/shard_map/ppermute | solution.py:334
  26.1 1.7 %collective-permute-done.6.refs_2_ = f32[3,256]{1,0:T(4,128)S(1)} collective-permute-done((f32[3,256]{1,0:T(4,128)S(1)}, f32[3,256]{1,0:T(4,128)S(1)}, u32[]{:S(2)}, u32[]{:S(2)}) %collective-permute-start.6) | collective-permute-done | bytes 3104 | tf_op jit(solution)/shard_map/ppermute | solution.py:334
  28.8 3.4 %collective-permute-start.10 = (f32[2,256]{1,0:T(2,128)S(1)}, f32[2,256]{1,0:T(2,128)S(1)}, u32[]{:S(2)}, u32[]{:S(2)}) collective-permute-start(f32[2,256]{1,0:T(2,128)S(1)} %get-tuple-element.71), channel_id=1, source_target_pairs={{0,3},{1,2},{2,1},{3,0},{4,7},{5,6},{6,5},{7,4},{8,11},{9,10},{10,... | collective-permute-start | bytes 6152 | tf_op jit(solution)/shard_map/ppermute | solution.py:334
  36.5 1.7 %collective-permute-start.11 = (f32[2,256]{1,0:T(2,128)S(1)}, f32[2,256]{1,0:T(2,128)S(1)}, u32[]{:S(2)}, u32[]{:S(2)}) collective-permute-start(f32[2,256]{1,0:T(2,128)S(1)} %add_add_fusion.refs_4_), channel_id=1, source_target_pairs={{0,4},{1,5},{2,6},{3,7},{4,0},{5,1},{6,2},{7,3},{8,12},{9,13},{10,... | collective-permute-start | bytes 6152 | tf_op jit(solution)/shard_map/ppermute | solution.py:334
  40.0 1.7 %collective-permute-start.14 = (bf16[512,256]{1,0:T(8,128)(2,1)S(1)}, bf16[512,256]{1,0:T(8,128)(2,1)S(1)}, u32[]{:S(2)}, u32[]{:S(2)}) collective-permute-start(bf16[512,256]{1,0:T(8,128)(2,1)S(1)} %get-tuple-element.85.grad_own.grad_ref), channel_id=1, source_target_pairs={{0,1},{1,0},{2,3},{3,2},{4,5},{5,4},{6,7},{7,6},{8,9},{9,8},{10,11... | collective-permute-start | bytes 786440 | tf_op jit(solution)/shard_map/ppermute | solution.py:334
  42.9 9.1 %weight_gradient.1 = (f32[4,288,256]{2,1,0:T(8,128)S(1)}, bf16[4,288,256]{2,1,0:T(8,128)(2,1)S(1)}, f32[2,144,256]{2,1,0:T(8,128)S(1)}, bf16[2,144,256]{2,1,0:T(...) custom-call(s32[3]{0:T(128)S(1)} %pad_add_fusion.place_ref.places_ref, ...), custom_call_target="tpu_custom_call" | custom-call | flops 4529848320 | bytes 10616832 | tf_op jit(solution)/shard_map/weight_gradient/pallas_call | solution.py:511
  52.7 1.7 %collective-permute-start.18 = (bf16[2,144,256]{2,1,0:T(8,128)(2,1)S(1)}, bf16[2,144,256]{2,1,0:T(8,128)(2,1)S(1)}, u32[]{:S(2)}, u32[]{:S(2)}) collective-permute-start(bf16[2,144,256]{2,1,0:T(8,128)(2,1)S(1)} %get-tuple-element.82), channel_id=1, source_target_pairs={{0,4},{1,5},{2,6},{3,7},{4,0},{5,1},{6,2},{7,3},{8,12},{9,13},{10,... | collective-permute-start | bytes 442376 | tf_op jit(solution)/shard_map/ppermute | solution.py:334
  56.6 2.3 %push_edges.1 = (bf16[128,256]{1,0:T(8,128)(2,1)S(1)}, bf16[128,256]{1,0:T(8,128)(2,1)S(1)}) custom-call(bf16[512,256]{1,0:T(8,128)(2,1)S(1)} %get-tuple-element.85.grad_own.grad_ref, s32[27,512]{1,0:T(8,128)S(1)} %bitcast.19, bf16[27,256,256]{2,1,0:T(8,128)(2,1)S(1)} %copy-done), custom_call_target="tpu_custom_call" | custom-call | flops 1000 | bytes 1000 | tf_op jit(solution)/shard_map/push_edges/pallas_call | solution.py:541
  58.9 8.0 %push.1 = f32[512,256]{1,0:T(8,128)S(1)} custom-call(bf16[512,256]{1,0:T(8,128)(2,1)S(1)} %get-tuple-element.85.grad_own.grad_ref, s32[27,512]{1,0:T(8,128)S(1)} %bitcast.20, bf16[27,256,256]{2,1,0:T(8,128)(2,1)S(1)} %copy-done), custom_call_target="tpu_custom_call" | custom-call | flops 1000 | bytes 1000 | tf_op jit(solution)/shard_map/push/pallas_call | solution.py:553
  67.8 2.4 %collective-permute-start.21 = (bf16[1,288,256]{2,1,0:T(8,128)(2,1)S(1)}, bf16[1,288,256]{2,1,0:T(8,128)(2,1)S(1)}, u32[]{:S(2)}, u32[]{:S(2)}) collective-permute-start(bf16[1,288,256]{2,1,0:T(8,128)(2,1)S(1)} %get-tuple-element.96), channel_id=1, source_target_pairs={{0,4},{1,5},{2,6},{3,7},{4,0},{5,1},{6,2},{7,3},{8,12},{9,13},{10,... | collective-permute-start | bytes 442376 | tf_op jit(solution)/shard_map/ppermute | solution.py:334
  72.4 2.5 %collective-permute-start.29 = (bf16[128,256]{1,0:T(8,128)(2,1)S(1)}, bf16[128,256]{1,0:T(8,128)(2,1)S(1)}, u32[]{:S(2)}, u32[]{:S(2)}) collective-permute-start(bf16[128,256]{1,0:T(8,128)(2,1)S(1)} %get-tuple-element.151), channel_id=1, source_target_pairs={{0,1},{1,0},{2,3},{3,2},{4,5},{5,4},{6,7},{7,6},{8,9},{9,8},{10,11... | collective-permute-start | bytes 196616 | tf_op jit(solution)/shard_map/ppermute | solution.py:418
  74.9 3.1 %collective-permute-start.30 = (bf16[128,256]{1,0:T(8,128)(2,1)S(1)}, bf16[128,256]{1,0:T(8,128)(2,1)S(1)}, u32[]{:S(2)}, u32[]{:S(2)}) collective-permute-start(bf16[128,256]{1,0:T(8,128)(2,1)S(1)} %get-tuple-element.152), channel_id=1, source_target_pairs={{1,2},{2,1},{3,4},{4,3},{5,6},{6,5},{7,8},{8,7},{9,10},{10,9},{11,... | collective-permute-start | bytes 196616 | tf_op jit(solution)/shard_map/ppermute | solution.py:419
  78.0 2.0 %collective-permute-done.23 = bf16[1,288,256]{2,1,0:T(8,128)(2,1)S(1)} collective-permute-done((bf16[1,288,256]{2,1,0:T(8,128)(2,1)S(1)}, bf16[1,288,256]{2,1,0:T(8,128)(2,1)S(1)}, u32[]{:S(2)}, u32[]{:S(2)}) %collective-permute-start.23) | collective-permute-done | bytes 147488 | tf_op jit(solution)/shard_map/ppermute | solution.py:334
  81.6 6.7 %collective-permute-start.26 = (bf16[1,288,256]{2,1,0:T(8,128)(2,1)S(1)}, bf16[1,288,256]{2,1,0:T(8,128)(2,1)S(1)}, u32[]{:S(2)}, u32[]{:S(2)}) collective-permute-start(bf16[1,288,256]{2,1,0:T(8,128)(2,1)S(1)} %add_convert_fusion), channel_id=1, source_target_pairs={{0,8},{1,9},{2,10},{3,11},{4,12},{5,13},{6,14},{7,15},{8,0},{9,1},... | collective-permute-start | bytes 442376 | tf_op jit(solution)/shard_map/ppermute | solution.py:334
  91.6 6.6 %collective-permute-done.26 = bf16[1,288,256]{2,1,0:T(8,128)(2,1)S(1)} collective-permute-done((bf16[1,288,256]{2,1,0:T(8,128)(2,1)S(1)}, bf16[1,288,256]{2,1,0:T(8,128)(2,1)S(1)}, u32[]{:S(2)}, u32[]{:S(2)}) %collective-permute-start.26) | collective-permute-done | bytes 147488 | tf_op jit(solution)/shard_map/ppermute | solution.py:334
  98.3 2.0 %collective-permute-start.31 = (bf16[4,288,256]{2,1,0:T(8,128)(2,1)S(1)}, bf16[4,288,256]{2,1,0:T(8,128)(2,1)S(1)}, u32[]{:S(2)}, u32[]{:S(2)}) collective-permute-start(bf16[4,288,256]{2,1,0:T(8,128)(2,1)S(1)} %get-tuple-element.144), channel_id=1, source_target_pairs={{0,2},{1,3},{2,0},{3,1},{4,6},{5,7},{6,4},{7,5},{8,10},{9,11},{10,... | collective-permute-start | bytes 1769480 | tf_op jit(solution)/shard_map/ppermute | solution.py:334
  101.4 2.5 %collective-permute-start.32 = (bf16[2,144,256]{2,1,0:T(8,128)(2,1)S(1)}, bf16[2,144,256]{2,1,0:T(8,128)(2,1)S(1)}, u32[]{:S(2)}, u32[]{:S(2)}) collective-permute-start(bf16[2,144,256]{2,1,0:T(8,128)(2,1)S(1)} %get-tuple-element.154.refs_1_), channel_id=1, source_target_pairs={{0,4},{1,5},{2,6},{3,7},{4,0},{5,1},{6,2},{7,3},{8,12},{9,13},{10,... | collective-permute-start | bytes 442376 | tf_op jit(solution)/shard_map/ppermute | solution.py:334
  106.4 7.9 %collective-permute-done.33 = bf16[2,144,256]{2,1,0:T(8,128)(2,1)S(1)} collective-permute-done((bf16[2,144,256]{2,1,0:T(8,128)(2,1)S(1)}, bf16[2,144,256]{2,1,0:T(8,128)(2,1)S(1)}, u32[]{:S(2)}, u32[]{:S(2)}) %collective-permute-start.33) | collective-permute-done | bytes 147488 | tf_op jit(solution)/shard_map/ppermute | solution.py:334
  115.1 1.6 %place.4.refs_2_ = bf16[27,256,256]{2,1,0:T(8,128)(2,1)} custom-call(s32[3]{0:T(128)S(1)} %pad_add_fusion.place_ref.places_ref, bf16[4,9,32,256]{3,2,1,0:T(8,128)(2,1)S(1)} %bitcast.12, bf16[6,144,256]{2,1,0:T(8,128)(2,1)S(1)} %pad_maximum_fusion.refs_1_, bf16[27,256,256]{2,1,0:T(8,128)(2,1)} %place.3.refs_2_), custom_call_target="tpu_custom_call", output_to_operand_aliasing={{}: (3, {})} | custom-call | bytes 3538944 | tf_op jit(solution)/shard_map/place/pallas_call | solution.py:584
  118.2 2.0 %place.5 = bf16[27,256,256]{2,1,0:T(8,128)(2,1)} custom-call(s32[3]{0:T(128)S(1)} %pad_add_fusion.place_ref.places_ref, bf16[8,9,32,256]{3,2,1,0:T(8,128)(2,1)S(1)} %bitcast.13, bf16[8,144,256]{2,1,0:T(8,128)(2,1)S(1)} %collective-permute-done.36.refs_1_, bf16[27,256,256]{2,1,0:T(8,128)(2,1)} %place.4.refs_2_), custom_call_target="tpu_custom_call", output_to_operand_aliasing={{}: (3, {})} | custom-call | bytes 3538944 | tf_op jit(solution)/shard_map/place/pallas_call | solution.py:584
  (98 shorter events, 30.3 us)
Async XLA Ops:
  1.5 11.0 %collective-permute-start.1 = (bf16[128,256]{1,0:T(8,128)(2,1)S(1)}, bf16[128,256]{1,0:T(8,128)(2,1)S(1)}, u32[]{:S(2)}, u32[]{:S(2)}) collective-permute-start(bf16[128,256]{1,0:T(8,128)(2,1)S(1)} %get-tuple-element.141), channel_id=1, source_target_pairs={{1,2},{2,1},{3,4},{4,3},{5,6},{6,5},{7,8},{8,7},{9,10},{10,9},{11,... | collective-permute-start | bytes 196616 | tf_op jit(solution)/shard_map/ppermute | solution.py:419
  6.0 6.5 %collective-permute-start = (bf16[128,256]{1,0:T(8,128)(2,1)S(1)}, bf16[128,256]{1,0:T(8,128)(2,1)S(1)}, u32[]{:S(2)}, u32[]{:S(2)}) collective-permute-start(bf16[128,256]{1,0:T(8,128)(2,1)S(1)} %get-tuple-element.142), channel_id=1, source_target_pairs={{0,1},{1,0},{2,3},{3,2},{4,5},{5,4},{6,7},{7,6},{8,9},{9,8},{10,11... | collective-permute-start | bytes 196616 | tf_op jit(solution)/shard_map/ppermute | solution.py:418
  21.7 4.3 %collective-permute-start.7 = (f32[3,256]{1,0:T(4,128)S(1)}, f32[3,256]{1,0:T(4,128)S(1)}, u32[]{:S(2)}, u32[]{:S(2)}) collective-permute-start(f32[3,256]{1,0:T(4,128)S(1)} %pad_maximum_fusion.1.refs_0_), channel_id=1, source_target_pairs={{0,12},{1,13},{2,14},{3,15},{4,8},{5,9},{6,10},{7,11},{8,4},{9,5},... | collective-permute-start | bytes 9224 | tf_op jit(solution)/shard_map/ppermute | solution.py:334
  28.8 4.8 %collective-permute-start.10 = (f32[2,256]{1,0:T(2,128)S(1)}, f32[2,256]{1,0:T(2,128)S(1)}, u32[]{:S(2)}, u32[]{:S(2)}) collective-permute-start(f32[2,256]{1,0:T(2,128)S(1)} %get-tuple-element.71), channel_id=1, source_target_pairs={{0,3},{1,2},{2,1},{3,0},{4,7},{5,6},{6,5},{7,4},{8,11},{9,10},{10,... | collective-permute-start | bytes 6152 | tf_op jit(solution)/shard_map/ppermute | solution.py:334
  32.6 10.3 %collective-permute-start.16 = (bf16[768,256]{1,0:T(8,128)(2,1)S(1)}, bf16[768,256]{1,0:T(8,128)(2,1)S(1)}, u32[]{:S(2)}, u32[]{:S(2)}) collective-permute-start(bf16[768,256]{1,0:T(8,128)(2,1)S(1)} %get-tuple-element.73.window_own), channel_id=1, source_target_pairs={{0,1},{1,0},{2,3},{3,2},{4,5},{5,4},{6,7},{7,6},{8,9},{9,8},{10,11... | collective-permute-start | bytes 1179656 | tf_op jit(solution)/shard_map/ppermute | solution.py:334
  34.6 4.3 %collective-permute-start.13 = (f32[2,256]{1,0:T(2,128)S(1)}, f32[2,256]{1,0:T(2,128)S(1)}, u32[]{:S(2)}, u32[]{:S(2)}) collective-permute-start(f32[2,256]{1,0:T(2,128)S(1)} %add_add_fusion.refs_4_), channel_id=1, source_target_pairs={{0,12},{1,13},{2,14},{3,15},{4,8},{5,9},{6,10},{7,11},{8,4},{9,5},... | collective-permute-start | bytes 6152 | tf_op jit(solution)/shard_map/ppermute | solution.py:334
  52.0 14.9 %collective-permute-start.17 = (bf16[4,288,256]{2,1,0:T(8,128)(2,1)S(1)}, bf16[4,288,256]{2,1,0:T(8,128)(2,1)S(1)}, u32[]{:S(2)}, u32[]{:S(2)}) collective-permute-start(bf16[4,288,256]{2,1,0:T(8,128)(2,1)S(1)} %get-tuple-element.81), channel_id=1, source_target_pairs={{0,2},{1,3},{2,0},{3,1},{4,6},{5,7},{6,4},{7,5},{8,10},{9,11},{10,... | collective-permute-start | bytes 1769480 | tf_op jit(solution)/shard_map/ppermute | solution.py:334
  52.7 14.1 %collective-permute-start.18 = (bf16[2,144,256]{2,1,0:T(8,128)(2,1)S(1)}, bf16[2,144,256]{2,1,0:T(8,128)(2,1)S(1)}, u32[]{:S(2)}, u32[]{:S(2)}) collective-permute-start(bf16[2,144,256]{2,1,0:T(8,128)(2,1)S(1)} %get-tuple-element.82), channel_id=1, source_target_pairs={{0,4},{1,5},{2,6},{3,7},{4,0},{5,1},{6,2},{7,3},{8,12},{9,13},{10,... | collective-permute-start | bytes 442376 | tf_op jit(solution)/shard_map/ppermute | solution.py:334
  54.5 12.4 %collective-permute-start.19 = (bf16[2,144,256]{2,1,0:T(8,128)(2,1)S(1)}, bf16[2,144,256]{2,1,0:T(8,128)(2,1)S(1)}, u32[]{:S(2)}, u32[]{:S(2)}) collective-permute-start(bf16[2,144,256]{2,1,0:T(8,128)(2,1)S(1)} %get-tuple-element.83), channel_id=1, source_target_pairs={{0,8},{1,9},{2,10},{3,11},{4,12},{5,13},{6,14},{7,15},{8,0},{9,1},... | collective-permute-start | bytes 442376 | tf_op jit(solution)/shard_map/ppermute | solution.py:334
  55.3 11.6 %collective-permute-start.20 = (bf16[2,144,256]{2,1,0:T(8,128)(2,1)S(1)}, bf16[2,144,256]{2,1,0:T(8,128)(2,1)S(1)}, u32[]{:S(2)}, u32[]{:S(2)}) collective-permute-start(bf16[2,144,256]{2,1,0:T(8,128)(2,1)S(1)} %get-tuple-element.84), channel_id=1, source_target_pairs={{0,12},{1,13},{2,14},{3,15},{4,8},{5,9},{6,10},{7,11},{8,4},{9,5},... | collective-permute-start | bytes 442376 | tf_op jit(solution)/shard_map/ppermute | solution.py:334
  67.2 7.7 %collective-permute-start.24 = (bf16[1,144,256]{2,1,0:T(8,128)(2,1)S(1)}, bf16[1,144,256]{2,1,0:T(8,128)(2,1)S(1)}, u32[]{:S(2)}, u32[]{:S(2)}) collective-permute-start(bf16[1,144,256]{2,1,0:T(8,128)(2,1)S(1)} %get-tuple-element.99), channel_id=1, source_target_pairs={{0,2},{1,3},{2,0},{3,1},{4,6},{5,7},{6,4},{7,5},{8,10},{9,11},{10,... | collective-permute-start | bytes 221192 | tf_op jit(solution)/shard_map/ppermute | solution.py:334
  67.8 10.2 %collective-permute-start.21 = (bf16[1,288,256]{2,1,0:T(8,128)(2,1)S(1)}, bf16[1,288,256]{2,1,0:T(8,128)(2,1)S(1)}, u32[]{:S(2)}, u32[]{:S(2)}) collective-permute-start(bf16[1,288,256]{2,1,0:T(8,128)(2,1)S(1)} %get-tuple-element.96), channel_id=1, source_target_pairs={{0,4},{1,5},{2,6},{3,7},{4,0},{5,1},{6,2},{7,3},{8,12},{9,13},{10,... | collective-permute-start | bytes 442376 | tf_op jit(solution)/shard_map/ppermute | solution.py:334
  70.2 7.8 %collective-permute-start.22 = (bf16[1,288,256]{2,1,0:T(8,128)(2,1)S(1)}, bf16[1,288,256]{2,1,0:T(8,128)(2,1)S(1)}, u32[]{:S(2)}, u32[]{:S(2)}) collective-permute-start(bf16[1,288,256]{2,1,0:T(8,128)(2,1)S(1)} %get-tuple-element.97), channel_id=1, source_target_pairs={{0,8},{1,9},{2,10},{3,11},{4,12},{5,13},{6,14},{7,15},{8,0},{9,1},... | collective-permute-start | bytes 442376 | tf_op jit(solution)/shard_map/ppermute | solution.py:334
  70.9 9.1 %collective-permute-start.23 = (bf16[1,288,256]{2,1,0:T(8,128)(2,1)S(1)}, bf16[1,288,256]{2,1,0:T(8,128)(2,1)S(1)}, u32[]{:S(2)}, u32[]{:S(2)}) collective-permute-start(bf16[1,288,256]{2,1,0:T(8,128)(2,1)S(1)} %get-tuple-element.98), channel_id=1, source_target_pairs={{0,12},{1,13},{2,14},{3,15},{4,8},{5,9},{6,10},{7,11},{8,4},{9,5},... | collective-permute-start | bytes 442376 | tf_op jit(solution)/shard_map/ppermute | solution.py:334
  72.4 15.9 %collective-permute-start.29 = (bf16[128,256]{1,0:T(8,128)(2,1)S(1)}, bf16[128,256]{1,0:T(8,128)(2,1)S(1)}, u32[]{:S(2)}, u32[]{:S(2)}) collective-permute-start(bf16[128,256]{1,0:T(8,128)(2,1)S(1)} %get-tuple-element.151), channel_id=1, source_target_pairs={{0,1},{1,0},{2,3},{3,2},{4,5},{5,4},{6,7},{7,6},{8,9},{9,8},{10,11... | collective-permute-start | bytes 196616 | tf_op jit(solution)/shard_map/ppermute | solution.py:418
  74.9 13.7 %collective-permute-start.30 = (bf16[128,256]{1,0:T(8,128)(2,1)S(1)}, bf16[128,256]{1,0:T(8,128)(2,1)S(1)}, u32[]{:S(2)}, u32[]{:S(2)}) collective-permute-start(bf16[128,256]{1,0:T(8,128)(2,1)S(1)} %get-tuple-element.152), channel_id=1, source_target_pairs={{1,2},{2,1},{3,4},{4,3},{5,6},{6,5},{7,8},{8,7},{9,10},{10,9},{11,... | collective-permute-start | bytes 196616 | tf_op jit(solution)/shard_map/ppermute | solution.py:419
  80.2 11.5 %collective-permute-start.27 = (bf16[1,288,256]{2,1,0:T(8,128)(2,1)S(1)}, bf16[1,288,256]{2,1,0:T(8,128)(2,1)S(1)}, u32[]{:S(2)}, u32[]{:S(2)}) collective-permute-start(bf16[1,288,256]{2,1,0:T(8,128)(2,1)S(1)} %add_convert_fusion), channel_id=1, source_target_pairs={{0,12},{1,13},{2,14},{3,15},{4,8},{5,9},{6,10},{7,11},{8,4},{9,5},... | collective-permute-start | bytes 442376 | tf_op jit(solution)/shard_map/ppermute | solution.py:334
  81.6 16.6 %collective-permute-start.26 = (bf16[1,288,256]{2,1,0:T(8,128)(2,1)S(1)}, bf16[1,288,256]{2,1,0:T(8,128)(2,1)S(1)}, u32[]{:S(2)}, u32[]{:S(2)}) collective-permute-start(bf16[1,288,256]{2,1,0:T(8,128)(2,1)S(1)} %add_convert_fusion), channel_id=1, source_target_pairs={{0,8},{1,9},{2,10},{3,11},{4,12},{5,13},{6,14},{7,15},{8,0},{9,1},... | collective-permute-start | bytes 442376 | tf_op jit(solution)/shard_map/ppermute | solution.py:334
  88.3 9.9 %collective-permute-start.25 = (bf16[1,288,256]{2,1,0:T(8,128)(2,1)S(1)}, bf16[1,288,256]{2,1,0:T(8,128)(2,1)S(1)}, u32[]{:S(2)}, u32[]{:S(2)}) collective-permute-start(bf16[1,288,256]{2,1,0:T(8,128)(2,1)S(1)} %add_convert_fusion), channel_id=1, source_target_pairs={{0,4},{1,5},{2,6},{3,7},{4,0},{5,1},{6,2},{7,3},{8,12},{9,13},{10,... | collective-permute-start | bytes 442376 | tf_op jit(solution)/shard_map/ppermute | solution.py:334
  98.3 16.0 %collective-permute-start.31 = (bf16[4,288,256]{2,1,0:T(8,128)(2,1)S(1)}, bf16[4,288,256]{2,1,0:T(8,128)(2,1)S(1)}, u32[]{:S(2)}, u32[]{:S(2)}) collective-permute-start(bf16[4,288,256]{2,1,0:T(8,128)(2,1)S(1)} %get-tuple-element.144), channel_id=1, source_target_pairs={{0,2},{1,3},{2,0},{3,1},{4,6},{5,7},{6,4},{7,5},{8,10},{9,11},{10,... | collective-permute-start | bytes 1769480 | tf_op jit(solution)/shard_map/ppermute | solution.py:334
  100.4 6.1 %collective-permute-start.34 = (bf16[2,144,256]{2,1,0:T(8,128)(2,1)S(1)}, bf16[2,144,256]{2,1,0:T(8,128)(2,1)S(1)}, u32[]{:S(2)}, u32[]{:S(2)}) collective-permute-start(bf16[2,144,256]{2,1,0:T(8,128)(2,1)S(1)} %get-tuple-element.154.refs_1_), channel_id=1, source_target_pairs={{0,12},{1,13},{2,14},{3,15},{4,8},{5,9},{6,10},{7,11},{8,4},{9,5},... | collective-permute-start | bytes 442376 | tf_op jit(solution)/shard_map/ppermute | solution.py:334
  101.4 12.9 %collective-permute-start.33 = (bf16[2,144,256]{2,1,0:T(8,128)(2,1)S(1)}, bf16[2,144,256]{2,1,0:T(8,128)(2,1)S(1)}, u32[]{:S(2)}, u32[]{:S(2)}) collective-permute-start(bf16[2,144,256]{2,1,0:T(8,128)(2,1)S(1)} %get-tuple-element.154.refs_1_), channel_id=1, source_target_pairs={{0,8},{1,9},{2,10},{3,11},{4,12},{5,13},{6,14},{7,15},{8,0},{9,1},... | collective-permute-start | bytes 442376 | tf_op jit(solution)/shard_map/ppermute | solution.py:334
  101.4 12.9 %collective-permute-start.32 = (bf16[2,144,256]{2,1,0:T(8,128)(2,1)S(1)}, bf16[2,144,256]{2,1,0:T(8,128)(2,1)S(1)}, u32[]{:S(2)}, u32[]{:S(2)}) collective-permute-start(bf16[2,144,256]{2,1,0:T(8,128)(2,1)S(1)} %get-tuple-element.154.refs_1_), channel_id=1, source_target_pairs={{0,4},{1,5},{2,6},{3,7},{4,0},{5,1},{6,2},{7,3},{8,12},{9,13},{10,... | collective-permute-start | bytes 442376 | tf_op jit(solution)/shard_map/ppermute | solution.py:334
  114.4 3.9 %collective-permute-start.35 = (bf16[8,288,256]{2,1,0:T(8,128)(2,1)S(1)}, bf16[8,288,256]{2,1,0:T(8,128)(2,1)S(1)}, u32[]{:S(2)}, u32[]{:S(2)}) collective-permute-start(bf16[8,288,256]{2,1,0:T(8,128)(2,1)S(1)} %constant_dynamic-update-slice_fusion.6), channel_id=1, source_target_pairs={{0,1},{1,0},{2,3},{3,2},{4,5},{5,4},{6,7},{7,6},{8,9},{9,8},{10,11... | collective-permute-start | bytes 3538952 | tf_op jit(solution)/shard_map/ppermute | solution.py:334
  (19 other events, 109.5 us)
